TPU v7x, 32 devices: a whole 2x2x4 slice. The times are simulated.
32 devices in a mesh: parts: 2 (over x), seq: 16 (over z, y, core).
Axes of the slice: x: 2, y: 2, z: 4, core: 2. Of those that a mesh axis runs over, the one named last changes fastest.
Arguments:
- fresh_qkv: bfloat16 [2432, 3, 2048], P(('parts', 'seq')), parts along dimension 0, may hold values from -6 to 6
- slot_rows: int32 [2432], P(('parts', 'seq')), parts along dimension 0, may hold values from 0 to 128, as said below
- k_cache: bfloat16 [4096, 2048], P(('parts', 'seq')), parts along dimension 0, may hold values from -6 to 6
- v_cache: bfloat16 [4096, 2048], P(('parts', 'seq')), parts along dimension 0, may hold values from -6 to 6
- attn_cache: bfloat16 [4096, 2048], P(('parts', 'seq')), parts along dimension 0, may hold values from -6 to 6
- text_k: bfloat16 [512, 2048], P('parts'), parts along dimension 0, may hold values from -6 to 6
- text_v: bfloat16 [512, 2048], P('parts'), parts along dimension 0, may hold values from -6 to 6
- q_gain: float32 [128], replicated, may hold values from 1 to 2.2
- k_gain: float32 [128], replicated, may hold values from 1 to 2.2
Outputs:
- attn_out: bfloat16 [4096, 2048], P(('parts', 'seq')), parts along dimension 0
There are 2 independent parts, one for each index of `parts`. A program takes and returns all parts, laid end to end along the dimension named above; an argument that names none is the same for every part. Nothing has to cross between parts.
Inputs may be any that keep to these rules, and one draw needn't show every extreme that they name: `slot_rows`: entries s * 76 to s * 76 + 75 belong to sequence shard s: the local indices of that shard's fresh tokens in increasing order, then 128 in every slot left empty. A shard holds at most 76 fresh tokens and some shard exactly 76; the shards of a sample hold exactly 608 fresh tokens together.
All inputs are finite; a program needn't handle non-finite values.
Results may differ from a plain program's by a relative error of at most 0.0025.
Values may be sent and summed in bfloat16 or wider, within the bound.
No kernel may reach another device: no remote copies, remote signals or barrier semaphores. Data moves between devices by JAX's collectives and lax.ppermute only.
A program may use at most 64 MiB of HBM per device.

v0:
```python
import jax
import jax.numpy as jnp
from jax import lax
from jax.sharding import PartitionSpec as P


def normalize(entries, scales):
    mean_square = jnp.mean(entries * entries, axis=-1, keepdims=True)
    return entries * lax.rsqrt(mean_square + 1e-06) * scales


def attend(queries, key_rows, value_rows, text_keys, text_values):
    query_count = queries.shape[0]
    head_size = queries.shape[1]
    factor = head_size ** (-0.5)

    def add_block(running, block_pair):
        numerator, denominator = running
        key_block, value_block = block_pair
        scores = (
            lax.dot_general(
                queries, key_block, (((1,), (1,)), ((), ())), preferred_element_type=jnp.float32
            )
            * factor
        )
        expd = jnp.exp(scores)
        denominator = denominator + jnp.sum(expd, axis=1)
        numerator = numerator + jnp.dot(
            expd.astype(jnp.bfloat16), value_block, preferred_element_type=jnp.float32
        )
        return ((numerator, denominator), None)

    initial = (
        jnp.zeros((query_count, head_size), jnp.float32),
        jnp.zeros((query_count,), jnp.float32),
    )
    running = add_block(initial, (text_keys, text_values))[0]
    key_count = key_rows.shape[0]
    block_rows = min(key_count, max(512, key_count // 16))
    turns = key_count // block_rows
    running, unused = lax.scan(
        add_block,
        running,
        (
            key_rows.reshape(turns, block_rows, head_size),
            value_rows.reshape(turns, block_rows, head_size),
        ),
    )
    return running


def shards(fresh_qkv, slot_rows, k_cache, v_cache, attn_cache, text_k, text_v, q_gain, k_gain):
    seq_count = lax.axis_size("seq")
    my_index = lax.axis_index("seq")
    slot_count = slot_rows.shape[0]
    tokens = k_cache.shape[0]
    row_width = k_cache.shape[1]
    head_size = q_gain.shape[0]
    head_count = row_width // head_size
    groups = seq_count // head_count
    per_group = slot_count // groups
    my_head = my_index // groups
    one_hot = slot_rows[:, None] == jnp.arange(tokens, dtype=jnp.int32)[None, :]
    is_fresh = jnp.any(one_hot, axis=0)
    one_hot = one_hot.astype(jnp.bfloat16)

    def spread(row_data):
        return lax.dot_general(
            one_hot, row_data, (((0,), (0,)), ((), ())), preferred_element_type=jnp.float32
        ).astype(jnp.bfloat16)

    fresh_kv = spread(fresh_qkv[:, 1:].reshape(slot_count, 2 * row_width))
    keys_raw = jnp.where(is_fresh[:, None], fresh_kv[:, :row_width], k_cache)
    values = jnp.where(is_fresh[:, None], fresh_kv[:, row_width:], v_cache)
    key_rows = normalize(
        keys_raw.astype(jnp.float32).reshape(tokens, head_count, head_size), k_gain
    ).astype(jnp.bfloat16)
    queries = normalize(
        fresh_qkv[:, 0].astype(jnp.float32).reshape(slot_count, head_count, head_size), q_gain
    ).astype(jnp.bfloat16)
    head_text_k = lax.dynamic_slice_in_dim(text_k, my_head * head_size, head_size, 1)
    head_text_v = lax.dynamic_slice_in_dim(text_v, my_head * head_size, head_size, 1)
    text_keys = normalize(head_text_k.astype(jnp.float32), k_gain).astype(jnp.bfloat16)
    paired = jnp.concatenate([key_rows, values.reshape(tokens, head_count, head_size)], axis=2)
    outgoing_kv = jnp.transpose(paired, (1, 0, 2))
    outgoing_kv = jnp.broadcast_to(
        outgoing_kv[:, None], (head_count, groups, tokens, 2 * head_size)
    ).reshape(seq_count, tokens, 2 * head_size)
    arrived = lax.all_to_all(outgoing_kv, "seq", split_axis=0, concat_axis=1, tiled=True)[0]
    outgoing = (
        queries.reshape(per_group, groups, head_count, head_size)
        .transpose(2, 1, 0, 3)
        .reshape(seq_count, per_group, head_size)
    )
    received = lax.all_to_all(outgoing, "seq", split_axis=0, concat_axis=1, tiled=True)[0]
    numerator, denominator = attend(
        received, arrived[:, :head_size], arrived[:, head_size:], text_keys, head_text_v
    )
    result = (
        (numerator / denominator[:, None])
        .astype(jnp.bfloat16)
        .reshape(1, seq_count * per_group, head_size)
    )
    returned = lax.all_to_all(result, "seq", split_axis=1, concat_axis=0, tiled=True)
    slot_out = (
        returned.reshape(head_count, groups, per_group, head_size)
        .transpose(2, 1, 0, 3)
        .reshape(slot_count, row_width)
    )
    placed = spread(slot_out)
    return jnp.where(is_fresh[:, None], placed, attn_cache)


def solution(mesh):
    return jax.shard_map(
        shards,
        mesh=mesh,
        in_specs=(
            P(("parts", "seq"), None, None),
            P(("parts", "seq")),
            P(("parts", "seq"), None),
            P(("parts", "seq"), None),
            P(("parts", "seq"), None),
            P("parts", None),
            P("parts", None),
            P(),
            P(),
        ),
        out_specs=P(("parts", "seq"), None),
        check_vma=False,
    )
```

profile of v0, /device:TPU:0, one launch (start us, length us, event | category | flops | bytes accessed | tf_op | source)
XLA Modules:
  0.0 99.9 jit_solution(17249691891320374705)
XLA Ops:
  0.0 1.1 %slice_convert_fusion = f32[76,1,2048]{2,0,1:T(8,128)S(1)} fusion(bf16[76,3,2048]{2,0,1:T(8,128)(2,1)} %param.11), kind=kLoop, calls=%fused_computation.35 | loop fusion | flops 155648 | bytes 933888 | tf_op jit(solution)/shard_map/convert_element_type | solution.py:79
  1.1 1.0 %fusion.22 = f32[76,1,2048]{2,0,1:T(8,128)S(1)} fusion(bf16[76,3,2048]{2,0,1:T(8,128)(2,1)} %param.11), kind=kLoop, calls=%fused_computation.43 | loop fusion | flops 311296 | bytes 933888 | tf_op jit(solution)/shard_map/mul | solution.py:8
  2.5 0.2 slice_reduce_fusion
  2.8 0.2 copy-done.10
  3.0 1.0 %fusion.17 = bf16[16,76,128]{2,1,0:T(8,128)(2,1)} fusion(f32[76,1,16,128]{3,2,0,1:T(8,128)S(1)} %slice_bitcast_fusion, f32[128]{0:T(128)S(1)} %copy-done.10, f32[76,16]{0,1:T(8,128)S(1)} %add_rsqrt_fusion.1), kind=kLoop, calls=%fused_computation.34 | loop fusion | flops 466944 | bytes 939264 | tf_op jit(solution)/shard_map/reshape | solution.py:93
  4.0 7.4 %all-to-all-start = ((bf16[16,76,128]{2,1,0:T(8,128)(2,1)}), bf16[16,76,128]{2,1,0:T(8,128)(2,1)S(1)}, u32[]{:S(2)}, u32[]{:S(2)}) async-start(bf16[16,76,128]{2,1,0:T(8,128)(2,1)} %fusion.17), calls=%async_computation | async-start | bytes 655360 | tf_op jit(solution)/shard_map/all_to_all | solution.py:95
  11.5 0.6 copy.41
  12.2 0.5 pad.2
  12.7 0.2 copy.52
  12.9 0.5 convolution_convert_fusion
  13.5 0.2 copy-done.1
  13.9 0.2 convert_bitcast_fusion.1
  14.1 0.2 copy.53
  14.3 0.3 multiply_reduce_fusion
  15.0 0.3 fusion.11
  15.3 1.1 %maximum_bitcast_fusion = bf16[16,128,256]{2,1,0:T(8,128)(2,1)} fusion(bf16[128,16,128]{2,0,1:T(8,128)(2,1)S(1)} %bitcast.88, bf16[128,16,128]{2,0,1:T(8,128)(2,1)S(1)} %fusion.11), kind=kLoop, calls=%fused_computation.20 | loop fusion | flops 2097152 | bytes 2097152 | tf_op jit(solution)/shard_map/transpose | solution.py:85
  16.4 6.0 %all-to-all-done = bf16[16,76,128]{2,1,0:T(8,128)(2,1)S(1)} async-done(((bf16[16,76,128]{2,1,0:T(8,128)(2,1)}), bf16[16,76,128]{2,1,0:T(8,128)(2,1)S(1)}, u32[]{:S(2)}, u32[]{:S(2)}) %all-to-all-start) | async-done | bytes 311328 | tf_op jit(solution)/shard_map/all_to_all | solution.py:95
  22.5 3.8 %all-to-all-start.1 = ((bf16[16,128,256]{2,1,0:T(8,128)(2,1)}), bf16[16,128,256]{2,1,0:T(8,128)(2,1)S(1)}, u32[]{:S(2)}, u32[]{:S(2)}) async-start(bf16[16,128,256]{2,1,0:T(8,128)(2,1)} %maximum_bitcast_fusion), calls=%async_computation.1 | async-start | bytes 2097152 | tf_op jit(solution)/shard_map/all_to_all | solution.py:89
  26.3 1.0 fusion.19
  27.4 2.0 %fusion.35 = (f32[1216]{0:T(1024)}, bf16[1216,256]{1,0:T(8,128)(2,1)S(1)}) fusion(bf16[1216,128]{1,0:T(8,128)(2,1)S(1)} %squeeze.14, f32[128]{0:T(128)S(1)} %copy-done.11, f32[256]{0:T(256)S(1)} %add_rsqrt_fusion.2, bf16[256,2048]{1,0:T(8,128)(2,1)} %param.16, s32[]{:T(128)S(6)} %select_n.17), kind=kOutput, calls=%fused_computation.59 | convolution fusion | flops 80755520 | bytes 1005828 | tf_op jit(solution)/shard_map/dot_general | solution.py:21
  29.4 0.3 fusion.14
  29.7 19.4 %all-to-all-done.1 = bf16[16,128,256]{2,1,0:T(8,128)(2,1)S(1)} async-done(((bf16[16,128,256]{2,1,0:T(8,128)(2,1)}), bf16[16,128,256]{2,1,0:T(8,128)(2,1)S(1)}, u32[]{:S(2)}, u32[]{:S(2)}) %all-to-all-start.1) | async-done | bytes 1048608 | tf_op jit(solution)/shard_map/all_to_all | solution.py:89
  49.0 0.9 fusion.34
  49.9 11.3 %while.12 = (s32[]{:T(128)}, f32[1216,128]{1,0:T(8,128)S(1)}, f32[1216]{0:T(1024)}, bf16[4,512,128]{2,1,0:T(8,128)(2,1)}, bf16[1216,128]{1,0:T(8,128)(2,1)S(1)}, /*index=5*/bf16[4,512,128]{2,1,0:T(8,128)(2,1)S(1)}, s32[]{:T(128)}) while((s32[]{:T(128)}, f32[1216,128]{1,0:T(8,128)S(1)}, f32[1216]{0:T(1024)}, bf16[4,512,128]{2,1,0:T(8,128)(2,1)}, ...), condition=%wide.region_7.8_spmd, body=%wide.region_5.7_spmd.sunk | while | flops 320790528 | bytes 4368009 | solution.py:41
  49.9 1.5 %fusion.49 = (f32[1216]{0:T(1024)S(1)}, bf16[512,1216]{0,1:T(8,128)(2,1)S(1)}) fusion(bf16[1216,128]{1,0:T(8,128)(2,1)S(1)} %get-tuple-element.124, bf16[4,512,128]{2,1,0:T(8,128)(2,1)} %get-tuple-element.123, s32[]{:T(128)} %get-tuple-element.113), kind=kOutput, calls=%fused_computation.57.clone.1 | convolution fusion | flops 161250112 | bytes 1692928 | tf_op jit(solution)/shard_map/while/body/eval_jaxpr/dot_general | solution.py:21
  51.4 0.5 convolution_add_fusion.2
  52.0 0.2 copy-done.4
  52.1 0.6 copy-done.5
  52.7 1.5 %fusion.49 = (f32[1216]{0:T(1024)S(1)}, bf16[512,1216]{0,1:T(8,128)(2,1)S(1)}) fusion(bf16[1216,128]{1,0:T(8,128)(2,1)S(1)} %get-tuple-element.124, bf16[4,512,128]{2,1,0:T(8,128)(2,1)} %get-tuple-element.123, s32[]{:T(128)} %get-tuple-element.113), kind=kOutput, calls=%fused_computation.57.clone.1 | convolution fusion | flops 161250112 | bytes 1692928 | tf_op jit(solution)/shard_map/while/body/eval_jaxpr/dot_general | solution.py:21
  54.3 0.5 convolution_add_fusion.2
  55.0 0.6 copy-done.5
  55.6 1.5 %fusion.49 = (f32[1216]{0:T(1024)S(1)}, bf16[512,1216]{0,1:T(8,128)(2,1)S(1)}) fusion(bf16[1216,128]{1,0:T(8,128)(2,1)S(1)} %get-tuple-element.124, bf16[4,512,128]{2,1,0:T(8,128)(2,1)} %get-tuple-element.123, s32[]{:T(128)} %get-tuple-element.113), kind=kOutput, calls=%fused_computation.57.clone.1 | convolution fusion | flops 161250112 | bytes 1692928 | tf_op jit(solution)/shard_map/while/body/eval_jaxpr/dot_general | solution.py:21
  57.1 0.5 convolution_add_fusion.2
  57.6 0.2 copy-done.4
  57.8 0.6 copy-done.5
  58.4 1.5 %fusion.49 = (f32[1216]{0:T(1024)S(1)}, bf16[512,1216]{0,1:T(8,128)(2,1)S(1)}) fusion(bf16[1216,128]{1,0:T(8,128)(2,1)S(1)} %get-tuple-element.124, bf16[4,512,128]{2,1,0:T(8,128)(2,1)} %get-tuple-element.123, s32[]{:T(128)} %get-tuple-element.113), kind=kOutput, calls=%fused_computation.57.clone.1 | convolution fusion | flops 161250112 | bytes 1692928 | tf_op jit(solution)/shard_map/while/body/eval_jaxpr/dot_general | solution.py:21
  60.0 0.5 convolution_add_fusion.2
  60.5 0.2 copy-done.4
  60.7 0.6 copy-done.5
  61.3 0.9 fusion.18
  62.2 4.9 %copy.68 = bf16[1,1216,128]{2,0,1:T(2,128)(2,1)S(1)} copy(bf16[1,1216,128]{2,1,0:T(8,128)(2,1)S(1)} %fusion.18) | data formatting | bytes 622592 | tf_op jit(solution)/shard_map/reshape | solution.py:102
  67.0 0.5 broadcast.61
  67.6 7.1 %reduce.3 = bf16[1216,128]{1,0:T(8,128)(2,1)S(1)} reduce(bf16[1216,1,128]{2,1,0:T(2,128)(2,1)S(1)} %bitcast.87, bf16[]{:T(256)} %broadcast.61), dimensions={1}, to_apply=%bitcast.69.reduce_sub_computation | reduce | bytes 622594
  74.8 17.5 %all_to_all.12 = bf16[16,2,4864]{2,1,0:T(2,128)(2,1)S(1)} all-to-all(bf16[16,2,4864]{2,1,0:T(2,128)(2,1)S(1)} %reshape.114), channel_id=1, replica_groups=mesh['parts'=2,'seq'=16] {'seq'}, dimensions={0} | all-to-all | bytes 622592 | tf_op jit(solution)/shard_map/all_to_all | solution.py:104
  92.2 0.3 reshape.115
  92.5 5.2 %bitcast_reduce_fusion = bf16[1216,128]{1,0:T(8,128)(2,1)S(1)} fusion(bf16[1216,1,128]{2,1,0:T(2,128)(2,1)S(1)} %reshape.115), kind=kLoop, calls=%fused_computation.60 | loop fusion | bytes 622592 | tf_op jit(solution)/shard_map/all_to_all | solution.py:104
  98.0 0.7 copy-done.3
  98.7 1.2 %fusion.9 = bf16[128,2048]{1,0:T(8,128)(2,1)} fusion(bf16[128,2048]{1,0:T(8,128)(2,1)S(1)} %copy-done.3, bf16[76,2048]{1,0:T(8,128)(2,1)S(1)} %bitcast.91, pred[128]{0:T(512)(128)(4,1)S(1)} %copy-done.9, s32[76]{0:T(128)S(1)} %copy-done.7), kind=kOutput, calls=%fused_computation.14 | convolution fusion | flops 40379904 | bytes 1360304 | tf_op jit(solution)/shard_map/dot_general | solution.py:68
  (48 shorter events, 1.5 us)
Async XLA Ops:
  0.0 29.4 %copy-start = (bf16[256,2048]{1,0:T(8,128)(2,1)S(1)}, bf16[256,2048]{1,0:T(8,128)(2,1)}, u32[]{:S(2)}) copy-start(bf16[256,2048]{1,0:T(8,128)(2,1)} %param.17) | copy-start | bytes 3145732
  2.3 0.7 copy-start.10
  3.0 8.4 %copy-start.6 = (s32[76]{0:T(128)S(1)}, s32[76]{0:T(128)}, u32[]{:S(2)}) copy-start(s32[76]{0:T(128)} %param.12) | copy-start | bytes 916
  3.0 8.5 %slice-start = ((bf16[76,3,2048]{2,0,1:T(8,128)(2,1)}), bf16[76,2,2048]{2,0,1:T(8,128)(2,1)S(1)}, s32[]{:S(2)}) async-start(bf16[76,3,2048]{2,0,1:T(8,128)(2,1)} %param.11), calls=%async_computation.3 | async-start | bytes 1310720 | tf_op jit(solution)/shard_map/slice | solution.py:72
  4.0 18.5 %all-to-all-start = ((bf16[16,76,128]{2,1,0:T(8,128)(2,1)}), bf16[16,76,128]{2,1,0:T(8,128)(2,1)S(1)}, u32[]{:S(2)}, u32[]{:S(2)}) async-start(bf16[16,76,128]{2,1,0:T(8,128)(2,1)} %fusion.17), calls=%async_computation | async-start | bytes 655360 | tf_op jit(solution)/shard_map/all_to_all | solution.py:95
  11.5 2.0 %copy-start.8 = (pred[128]{0:T(512)(128)(4,1)}, pred[128]{0:T(512)(128)(4,1)S(1)}, u32[]{:S(2)}) copy-start(pred[128]{0:T(512)(128)(4,1)S(1)} %fusion.28) | copy-start | bytes 388
  12.7 1.0 %copy-start.1 = (bf16[128,2048]{1,0:T(8,128)(2,1)S(1)}, bf16[128,2048]{1,0:T(8,128)(2,1)}, u32[]{:S(2)}) copy-start(bf16[128,2048]{1,0:T(8,128)(2,1)} %param.13) | copy-start | bytes 1572868
  12.7 1.2 %copy-start.2 = (bf16[128,2048]{1,0:T(8,128)(2,1)S(1)}, bf16[128,2048]{1,0:T(8,128)(2,1)}, u32[]{:S(2)}) copy-start(bf16[128,2048]{1,0:T(8,128)(2,1)} %param.14) | copy-start | bytes 1572868
  14.3 0.7 copy-start.11
  22.5 26.6 %all-to-all-start.1 = ((bf16[16,128,256]{2,1,0:T(8,128)(2,1)}), bf16[16,128,256]{2,1,0:T(8,128)(2,1)S(1)}, u32[]{:S(2)}, u32[]{:S(2)}) async-start(bf16[16,128,256]{2,1,0:T(8,128)(2,1)} %maximum_bitcast_fusion), calls=%async_computation.1 | async-start | bytes 2097152 | tf_op jit(solution)/shard_map/all_to_all | solution.py:89
  51.4 0.7 copy-start.4
  52.1 0.6 copy-start.5
  54.3 0.7 copy-start.4
  55.0 0.6 copy-start.5
  57.1 0.7 copy-start.4
  57.8 0.6 copy-start.5
  60.0 0.7 copy-start.4
  60.7 0.6 copy-start.5
  97.7 1.0 %copy-start.3 = (bf16[128,2048]{1,0:T(8,128)(2,1)S(1)}, bf16[128,2048]{1,0:T(8,128)(2,1)}, u32[]{:S(2)}) copy-start(bf16[128,2048]{1,0:T(8,128)(2,1)} %param.15) | copy-start | bytes 1572868
  97.7 1.0 %copy-start.7 = (s32[76]{0:T(128)S(1)}, s32[76]{0:T(128)}, u32[]{:S(2)}) copy-start(s32[76]{0:T(128)} %param.12) | copy-start | bytes 916
  97.7 1.0 %copy-start.9 = (pred[128]{0:T(512)(128)(4,1)S(1)}, pred[128]{0:T(512)(128)(4,1)}, u32[]{:S(2)}) copy-start(pred[128]{0:T(512)(128)(4,1)} %copy-done.8) | copy-start | bytes 388
where the time goes:
time: 101 us; the launch traced here: 99.9 us
  waiting for transfers between devices  25.4 us (25%)
  local copies, waits for them, and re-layouts  18.7 us (19%)
  blocking collectives  17.5 us (17%)
  other arithmetic  14.5 us (14%)
  matrix products  12.3 us (12%)
  starting transfers between devices  11.2 us (11%)
    all_to_all x1, waiting for transfers between devices, shards(): lax.all_to_all(outgoing_kv, 'seq', split_axis=0, concat_axis=1, tiled=True)  19.4 us
    all_to_all x1, blocking collectives, shards(): lax.all_to_all(result, 'seq', split_axis=1, concat_axis=0, tiled=True)  17.5 us
    dot_general x5, matrix products, add_block(): lax.dot_general(queries, key_block, (((1,), (1,)), ((), ())), preferred_e...  8.14 us
    all_to_all x1, starting transfers between devices, shards(): lax.all_to_all(outgoing, 'seq', split_axis=0, concat_axis=1, tiled=True)[0]  7.39 us
    unnamed x2, other arithmetic  7.34 us
    all_to_all x1, waiting for transfers between devices, shards(): lax.all_to_all(outgoing, 'seq', split_axis=0, concat_axis=1, tiled=True)[0]  6.04 us
    all_to_all x1, local copies, waits for them, and re-layouts, shards(): lax.all_to_all(result, 'seq', split_axis=1, concat_axis=0, tiled=True)  5.21 us
    reshape x1, local copies, waits for them, and re-layouts, shards(): result = (numerator / denominator[:, None]).astype(jnp.bfloat16).reshape(...  4.86 us
  transfers between devices with their start and end apart: 2, of which 2 were waited for; matrix products, arithmetic and copies ran while one was open for 8% of the time, Pallas kernels for 0%

commit v1 on v0

v1 whole, which is shorter than its diff:
```python
import math

import jax
import jax.numpy as jnp
from jax import lax
from jax.experimental import pallas as pl
from jax.experimental.pallas import tpu as pltpu
from jax.sharding import PartitionSpec as P

LOG2E = math.log2(math.e)


def round_up(count, step):
    return (count + step - 1) // step * step


def normalize(entries, scales):
    mean_square = jnp.mean(entries * entries, axis=-1, keepdims=True)
    return entries * lax.rsqrt(mean_square + 1e-06) * scales


def place(slots, tokens):
    owner = lax.broadcasted_iota(jnp.int32, (tokens, slots.shape[1]), 0)
    return owner == slots


def prepare_kernel(
    per_group, padded, slots_ref, qkv_ref, k_ref, v_ref, q_gain_ref, k_gain_ref, out_ref
):
    tokens = k_ref.shape[0]
    head_size = q_gain_ref.shape[1]
    groups = qkv_ref.shape[1] // per_group
    heads = k_ref.shape[1] // head_size
    mine = place(slots_ref[...], tokens)
    is_fresh = jnp.max(mine.astype(jnp.float32), axis=1, keepdims=True) > 0.5
    one_hot = mine.astype(jnp.bfloat16)
    q_gain = q_gain_ref[...]
    k_gain = k_gain_ref[...]

    def merged(part, cache_ref):
        spread = jnp.dot(one_hot, qkv_ref[part], preferred_element_type=jnp.float32)
        return jnp.where(is_fresh, spread, cache_ref[...].astype(jnp.float32))

    keys_raw = merged(1, k_ref)
    values = merged(2, v_ref).astype(jnp.bfloat16)
    raw_queries = qkv_ref[0].astype(jnp.float32)
    for head in range(heads):
        columns = slice(head * head_size, (head + 1) * head_size)
        keys = normalize(keys_raw[:, columns], k_gain).astype(jnp.bfloat16)
        queries = normalize(raw_queries[:, columns], q_gain)
        for group in range(groups):
            at = head * groups + group
            out_ref[at, :tokens] = keys
            out_ref[at, tokens : 2 * tokens] = values[:, columns]
            share = queries[group * per_group : (group + 1) * per_group]
            if padded > per_group:
                empty = jnp.zeros((padded - per_group, head_size), jnp.float32)
                share = jnp.concatenate([share, empty], axis=0)
            out_ref[at, 2 * tokens :] = share.astype(jnp.bfloat16)


def attend_kernel(
    tokens,
    query_sources,
    key_sources,
    head_ref,
    arrived_ref,
    text_k_ref,
    text_v_ref,
    k_gain_ref,
    out_ref,
    text_keys,
    weights,
):
    del head_ref
    sources, rows, head_size = arrived_ref.shape
    padded = rows - 2 * tokens
    factor = head_size ** (-0.5) * LOG2E
    text_keys[...] = normalize(text_k_ref[...].astype(jnp.float32), k_gain_ref[...]).astype(
        jnp.bfloat16
    )
    text = text_keys.shape[0]
    query_rows = query_sources * padded
    key_rows = key_sources * tokens

    def keys_of(turn):
        if turn == 0:
            return text_keys[...]
        first = (turn - 1) * key_sources
        return arrived_ref[first : first + key_sources, :tokens].reshape(key_rows, head_size)

    def values_of(turn):
        if turn == 0:
            rows_of = text_v_ref[...]
        else:
            first = (turn - 1) * key_sources
            rows_of = arrived_ref[first : first + key_sources, tokens : 2 * tokens].reshape(
                key_rows, head_size
            )
        return jnp.concatenate([rows_of, jnp.ones_like(rows_of)], axis=1)

    turns = 1 + sources // key_sources

    def columns_of(turn):
        if turn == 0:
            return slice(0, text)
        return slice(text + (turn - 1) * key_rows, text + turn * key_rows)

    def add_queries(step, carry):
        first = step * query_sources
        queries = arrived_ref[pl.ds(first, query_sources), 2 * tokens :].reshape(
            query_rows, head_size
        )
        for turn in range(turns):
            scores = lax.dot_general(
                queries,
                keys_of(turn),
                (((1,), (1,)), ((), ())),
                preferred_element_type=jnp.float32,
            )
            weights[:, columns_of(turn)] = jnp.exp2(scores * factor).astype(jnp.bfloat16)
        sums = jnp.zeros((query_rows, 2 * head_size), jnp.float32)
        for turn in range(turns):
            sums = sums + jnp.dot(
                weights[:, columns_of(turn)],
                values_of(turn),
                preferred_element_type=jnp.float32,
            )
        result = (sums[:, :head_size] / sums[:, head_size:]).astype(jnp.bfloat16)
        out_ref[pl.ds(first, query_sources)] = result.reshape(query_sources, padded, head_size)
        return carry

    lax.fori_loop(0, sources // query_sources, add_queries, 0)


def finish_kernel(per_group, slots_ref, returned_ref, cache_ref, out_ref):
    tokens = cache_ref.shape[0]
    head_size = returned_ref.shape[2]
    groups = slots_ref.shape[0]
    heads = cache_ref.shape[1] // head_size
    mine = [place(slots_ref[group : group + 1], tokens) for group in range(groups)]
    count = sum(jnp.sum(m.astype(jnp.float32), axis=1, keepdims=True) for m in mine)
    is_fresh = count > 0.5
    one_hot = [m.astype(jnp.bfloat16) for m in mine]
    for head in range(heads):
        columns = slice(head * head_size, (head + 1) * head_size)
        placed = sum(
            jnp.dot(
                one_hot[group],
                returned_ref[head * groups + group],
                preferred_element_type=jnp.float32,
            )
            for group in range(groups)
        )
        out_ref[:, columns] = jnp.where(
            is_fresh, placed, cache_ref[:, columns].astype(jnp.float32)
        ).astype(out_ref.dtype)


def shards(fresh_qkv, slot_rows, k_cache, v_cache, attn_cache, text_k, text_v, q_gain, k_gain):
    seq_count = lax.axis_size("seq")
    my_index = lax.axis_index("seq")
    slot_count = slot_rows.shape[0]
    tokens, row_width = k_cache.shape
    text = text_k.shape[0]
    head_size = q_gain.shape[0]
    head_count = row_width // head_size
    groups = seq_count // head_count
    per_group = slot_count // groups
    padded = round_up(per_group, 16)
    rows = 2 * tokens + padded
    my_head = my_index // groups
    q_gain = q_gain.reshape(1, head_size)
    k_gain = k_gain.reshape(1, head_size)
    qkv = jnp.transpose(fresh_qkv, (1, 0, 2))
    slots = slot_rows.reshape(1, slot_count)
    padded_slots = jnp.pad(
        slot_rows.reshape(groups, per_group),
        ((0, 0), (0, padded - per_group)),
        constant_values=tokens,
    )

    steps = 4
    width = row_width // steps
    step_heads = head_count // steps
    outgoing = pl.pallas_call(
        lambda *refs: prepare_kernel(per_group, padded, *refs),
        out_shape=jax.ShapeDtypeStruct((seq_count, rows, head_size), jnp.bfloat16),
        grid=(steps,),
        in_specs=[
            pl.BlockSpec((1, slot_count), lambda i: (0, 0)),
            pl.BlockSpec((3, slot_count, width), lambda i: (0, 0, i)),
            pl.BlockSpec((tokens, width), lambda i: (0, i)),
            pl.BlockSpec((tokens, width), lambda i: (0, i)),
            pl.BlockSpec((1, head_size), lambda i: (0, 0)),
            pl.BlockSpec((1, head_size), lambda i: (0, 0)),
        ],
        out_specs=pl.BlockSpec((step_heads * groups, rows, head_size), lambda i: (i, 0, 0)),
        compiler_params=pltpu.CompilerParams(vmem_limit_bytes=32 * 2**20),
        name="prepare",
    )(slots, qkv, k_cache, v_cache, q_gain, k_gain)

    arrived = lax.all_to_all(outgoing, "seq", split_axis=0, concat_axis=0, tiled=True)

    query_sources = 4
    result = pl.pallas_call(
        lambda *refs: attend_kernel(tokens, query_sources, 4, *refs),
        out_shape=jax.ShapeDtypeStruct((seq_count, padded, head_size), jnp.bfloat16),
        grid_spec=pltpu.PrefetchScalarGridSpec(
            num_scalar_prefetch=1,
            grid=(1,),
            in_specs=[
                pl.BlockSpec((seq_count, rows, head_size), lambda i, head: (0, 0, 0)),
                pl.BlockSpec((text, head_size), lambda i, head: (0, head[0])),
                pl.BlockSpec((text, head_size), lambda i, head: (0, head[0])),
                pl.BlockSpec((1, head_size), lambda i, head: (0, 0)),
            ],
            out_specs=pl.BlockSpec((seq_count, padded, head_size), lambda i, head: (0, 0, 0)),
            scratch_shapes=[
                pltpu.VMEM((text, head_size), jnp.bfloat16),
                pltpu.VMEM((query_sources * padded, text + seq_count * tokens), jnp.bfloat16),
            ],
        ),
        compiler_params=pltpu.CompilerParams(vmem_limit_bytes=40 * 2**20),
        name="attend",
    )(my_head.reshape(1), arrived, text_k, text_v, k_gain)

    returned = lax.all_to_all(result, "seq", split_axis=0, concat_axis=0, tiled=True)

    return pl.pallas_call(
        lambda *refs: finish_kernel(per_group, *refs),
        out_shape=jax.ShapeDtypeStruct((tokens, row_width), attn_cache.dtype),
        grid=(steps,),
        in_specs=[
            pl.BlockSpec((groups, padded), lambda i: (0, 0)),
            pl.BlockSpec((step_heads * groups, padded, head_size), lambda i: (i, 0, 0)),
            pl.BlockSpec((tokens, width), lambda i: (0, i)),
        ],
        out_specs=pl.BlockSpec((tokens, width), lambda i: (0, i)),
        compiler_params=pltpu.CompilerParams(vmem_limit_bytes=32 * 2**20),
        name="finish",
    )(padded_slots, returned, attn_cache)


def solution(mesh):
    return jax.shard_map(
        shards,
        mesh=mesh,
        in_specs=(
            P(("parts", "seq"), None, None),
            P(("parts", "seq")),
            P(("parts", "seq"), None),
            P(("parts", "seq"), None),
            P(("parts", "seq"), None),
            P("parts", None),
            P("parts", None),
            P(),
            P(),
        ),
        out_specs=P(("parts", "seq"), None),
        check_vma=False,
    )
```

time: 101 us -> 72.1 us (0.71)
  blocking collectives: 17.5 us -> 0 us
  other arithmetic: 14.5 us -> 0 us
  waiting for transfers between devices: 25.4 us -> 39.6 us
  local copies, waits for them, and re-layouts: 18.7 us -> 6.31 us
  matrix products: 12.3 us -> 0 us
  Pallas kernels: 0 us -> 9.85 us
  starting transfers between devices: 11.2 us -> 15.8 us
    all_to_all x1 -> x0, blocking collectives: 17.5 us -> none  [shards(): lax.all_to_all(result, 'seq', split_axis=1, concat_axis=0, tiled=True)]
    all_to_all x2, waiting for transfers between devices: 25.4 us -> 39.6 us  [the longest x1 28.6 us: shards(): lax.all_to_all(outgoing, 'seq', split_axis=0, concat_axis=0, tiled=True)]
    dot_general x12 -> x0, matrix products: 12.3 us -> none  [the longest x5 8.14 us: add_block(): lax.dot_general(queries, key_block, (((1,), (1,)), ((), ())), preferred_e...]
    pallas_call x0 -> x3, Pallas kernels: none -> 9.85 us  [the longest x1 5.42 us: shards(): pl.pallas_call(lambda *refs: attend_kernel(tokens, query_sources, 4, *ref...]
    unnamed x2 -> x0, other arithmetic: 7.34 us -> none
    all_to_all x1 -> x0, local copies, waits for them, and re-layouts: 5.21 us -> none  [shards(): lax.all_to_all(result, 'seq', split_axis=1, concat_axis=0, tiled=True)]
    reshape x3 -> x0, local copies, waits for them, and re-layouts: 5.06 us -> none  [the longest x1 4.86 us: shards(): result = (numerator / denominator[:, None]).astype(jnp.bfloat16).reshape(...]
    all_to_all x2, starting transfers between devices: 11.2 us -> 15.8 us  [the longest x1 8.28 us: shards(): lax.all_to_all(result, 'seq', split_axis=0, concat_axis=0, tiled=True)]
  transfers between devices with their start and end apart: 2 -> 2, of which waited for: 2 -> 2; matrix products, arithmetic and copies ran while one was open for 8% -> 0% of each run, Pallas kernels for 0% -> 0%
where the time goes in v1:
time: 72.1 us; the launch traced here: 71.6 us
  waiting for transfers between devices  39.6 us (55%)
  starting transfers between devices  15.8 us (22%)
  Pallas kernels  9.85 us (14%)
  local copies, waits for them, and re-layouts  6.31 us (9%)
    all_to_all x1, waiting for transfers between devices, shards(): lax.all_to_all(outgoing, 'seq', split_axis=0, concat_axis=0, tiled=True)  28.6 us
    all_to_all x1, waiting for transfers between devices, shards(): lax.all_to_all(result, 'seq', split_axis=0, concat_axis=0, tiled=True)  11.1 us
    all_to_all x1, starting transfers between devices, shards(): lax.all_to_all(result, 'seq', split_axis=0, concat_axis=0, tiled=True)  8.28 us
    all_to_all x1, starting transfers between devices, shards(): lax.all_to_all(outgoing, 'seq', split_axis=0, concat_axis=0, tiled=True)  7.52 us
    unnamed x22, local copies, waits for them, and re-layouts  6.31 us
    pallas_call x1, Pallas kernels, shards(): pl.pallas_call(lambda *refs: attend_kernel(tokens, query_sources, 4, *ref...  5.42 us
    pallas_call x1, Pallas kernels, shards(): pl.pallas_call(lambda *refs: prepare_kernel(per_group, padded, *refs), ou...  2.54 us
    pallas_call x1, Pallas kernels, shards(): pl.pallas_call(lambda *refs: finish_kernel(per_group, *refs), out_shape=j...  1.88 us
  transfers between devices with their start and end apart: 2, of which 2 were waited for; matrix products, arithmetic and copies ran while one was open for 0% of the time, Pallas kernels for 0%

profile of v1, /device:TPU:0, one launch (start us, length us, event | category | flops | bytes accessed | tf_op | source)
XLA Modules:
  0.0 71.6 jit_solution(8128624687343348686)
XLA Ops:
  0.0 0.0 copy-start.2
  0.0 1.2 %copy-done.2 = bf16[76,3,2048]{2,0,1:T(8,128)(2,1)S(1)} copy-done((bf16[76,3,2048]{2,0,1:T(8,128)(2,1)S(1)}, bf16[76,3,2048]{2,0,1:T(8,128)(2,1)}, u32[]{:S(2)}) %copy-start.2) | copy-done | bytes 933912
  1.2 0.0 copy-start.4
  1.2 1.0 %copy-done.4 = bf16[128,2048]{1,0:T(8,128)(2,1)S(1)} copy-done((bf16[128,2048]{1,0:T(8,128)(2,1)S(1)}, bf16[128,2048]{1,0:T(8,128)(2,1)}, u32[]{:S(2)}) %copy-start.4) | copy-done | bytes 524312
  2.2 0.0 copy-start.5
  2.2 1.0 %copy-done.5 = bf16[128,2048]{1,0:T(8,128)(2,1)S(1)} copy-done((bf16[128,2048]{1,0:T(8,128)(2,1)S(1)}, bf16[128,2048]{1,0:T(8,128)(2,1)}, u32[]{:S(2)}) %copy-start.5) | copy-done | bytes 524312
  3.3 0.0 copy-start.6
  3.3 0.7 copy-done.6
  3.9 0.0 copy-start.8
  3.9 0.7 copy-done.8
  4.6 0.0 copy-start.9
  4.6 0.7 copy-done.9
  5.3 2.5 %prepare.1 = bf16[16,336,128]{2,1,0:T(8,128)(2,1)} custom-call(s32[1,76]{1,0:T(1,128)S(1)} %bitcast.9, bf16[3,76,2048]{2,1,0:T(8,128)(2,1)S(1)} %bitcast.5, bf16[128,2048]{1,0:T(8,128)(2,1)S(1)} %copy-done.4, bf16[128,2048]{1,0:T(8,128)(2,1)S(1)} %copy-done.5, f32[1,128]{1,0:T(1,128)S(1)} %bitcast.8, f32[1,128]{1,0:T(1,128)S(1)} %bitcast.6), custom_call_target="tpu_custom_call" | custom-call | tf_op jit(solution)/shard_map/prepare/pallas_call | solution.py:186
  7.8 0.0 copy-start
  7.8 0.0 copy-start.1
  7.8 0.0 copy-start.7
  7.8 7.5 %all-to-all-start = ((bf16[16,336,128]{2,1,0:T(8,128)(2,1)}), bf16[16,336,128]{2,1,0:T(8,128)(2,1)S(1)}, u32[]{:S(2)}, u32[]{:S(2)}) async-start(bf16[16,336,128]{2,1,0:T(8,128)(2,1)} %prepare.1), calls=%async_computation | async-start | bytes 2752512 | tf_op jit(solution)/shard_map/all_to_all | solution.py:203
  15.3 28.6 %all-to-all-done.refs_1_ = bf16[16,336,128]{2,1,0:T(8,128)(2,1)S(1)} async-done(((bf16[16,336,128]{2,1,0:T(8,128)(2,1)}), bf16[16,336,128]{2,1,0:T(8,128)(2,1)S(1)}, u32[]{:S(2)}, u32[]{:S(2)}) %all-to-all-start) | async-done | bytes 1376288 | tf_op jit(solution)/shard_map/all_to_all | solution.py:203
  43.9 0.0 copy-done
  43.9 0.0 copy-done.1
  43.9 0.0 copy-done.7
  43.9 0.0 copy-start.10
  43.9 5.4 %attend.1 = bf16[16,80,128]{2,1,0:T(8,128)(2,1)} custom-call(s32[1]{0:T(128)} %bitcast.1.refs_0_, bf16[16,336,128]{2,1,0:T(8,128)(2,1)S(1)} %all-to-all-done.refs_1_, bf16[256,2048]{1,0:T(8,128)(2,1)S(1)} %copy-done, bf16[256,2048]{1,0:T(8,128)(2,1)S(1)} %copy-done.1, f32[1,128]{1,0:T(1,128)S(1)} %bitcast.7), custom_call_target="tpu_custom_call" | custom-call | tf_op jit(solution)/shard_map/attend/pallas_call | solution.py:206
  49.3 8.3 %all-to-all-start.1 = ((bf16[16,80,128]{2,1,0:T(8,128)(2,1)}), bf16[16,80,128]{2,1,0:T(8,128)(2,1)S(1)}, u32[]{:S(2)}, u32[]{:S(2)}) async-start(bf16[16,80,128]{2,1,0:T(8,128)(2,1)} %attend.1), calls=%async_computation.1 | async-start | bytes 655360 | tf_op jit(solution)/shard_map/all_to_all | solution.py:228
  57.6 0.0 copy-done.10
  57.6 11.1 %all-to-all-done.1.refs_1_ = bf16[16,80,128]{2,1,0:T(8,128)(2,1)S(1)} async-done(((bf16[16,80,128]{2,1,0:T(8,128)(2,1)}), bf16[16,80,128]{2,1,0:T(8,128)(2,1)S(1)}, u32[]{:S(2)}, u32[]{:S(2)}) %all-to-all-start.1) | async-done | bytes 327712 | tf_op jit(solution)/shard_map/all_to_all | solution.py:228
  68.7 0.0 copy-start.3
  68.7 1.0 %copy-done.3 = bf16[128,2048]{1,0:T(8,128)(2,1)S(1)} copy-done((bf16[128,2048]{1,0:T(8,128)(2,1)S(1)}, bf16[128,2048]{1,0:T(8,128)(2,1)}, u32[]{:S(2)}) %copy-start.3) | copy-done | bytes 524312
  69.8 1.9 %finish.1 = bf16[128,2048]{1,0:T(8,128)(2,1)} custom-call(s32[1,80]{1,0:T(1,128)S(1)} %pad.4.refs_0_, bf16[16,80,128]{2,1,0:T(8,128)(2,1)S(1)} %all-to-all-done.1.refs_1_, bf16[128,2048]{1,0:T(8,128)(2,1)S(1)} %copy-done.3), custom_call_target="tpu_custom_call" | custom-call | tf_op jit(solution)/shard_map/finish/pallas_call | solution.py:230
  (1 shorter events, 0.0 us)
Async XLA Ops:
  0.0 1.2 %copy-start.2 = (bf16[76,3,2048]{2,0,1:T(8,128)(2,1)S(1)}, bf16[76,3,2048]{2,0,1:T(8,128)(2,1)}, u32[]{:S(2)}) copy-start(bf16[76,3,2048]{2,0,1:T(8,128)(2,1)} %param.9) | copy-start | bytes 2801668
  1.2 1.0 %copy-start.4 = (bf16[128,2048]{1,0:T(8,128)(2,1)S(1)}, bf16[128,2048]{1,0:T(8,128)(2,1)}, u32[]{:S(2)}) copy-start(bf16[128,2048]{1,0:T(8,128)(2,1)} %refs_2_.3) | copy-start | bytes 1572868
  2.2 1.0 %copy-start.5 = (bf16[128,2048]{1,0:T(8,128)(2,1)S(1)}, bf16[128,2048]{1,0:T(8,128)(2,1)}, u32[]{:S(2)}) copy-start(bf16[128,2048]{1,0:T(8,128)(2,1)} %refs_3_.2) | copy-start | bytes 1572868
  3.3 0.7 copy-start.6
  3.9 0.7 copy-start.8
  4.6 0.7 copy-start.9
  7.8 36.1 %copy-start = (bf16[256,2048]{1,0:T(8,128)(2,1)S(1)}, bf16[256,2048]{1,0:T(8,128)(2,1)}, u32[]{:S(2)}) copy-start(bf16[256,2048]{1,0:T(8,128)(2,1)} %refs_2_.4) | copy-start | bytes 3145732
  7.8 36.1 %copy-start.1 = (bf16[256,2048]{1,0:T(8,128)(2,1)S(1)}, bf16[256,2048]{1,0:T(8,128)(2,1)}, u32[]{:S(2)}) copy-start(bf16[256,2048]{1,0:T(8,128)(2,1)} %refs_3_.3) | copy-start | bytes 3145732
  7.8 36.1 %copy-start.7 = (f32[128]{0:T(128)S(1)}, f32[128]{0:T(128)}, u32[]{:S(2)}) copy-start(f32[128]{0:T(128)} %param.17) | copy-start | bytes 1540
  7.8 36.1 %all-to-all-start = ((bf16[16,336,128]{2,1,0:T(8,128)(2,1)}), bf16[16,336,128]{2,1,0:T(8,128)(2,1)S(1)}, u32[]{:S(2)}, u32[]{:S(2)}) async-start(bf16[16,336,128]{2,1,0:T(8,128)(2,1)} %prepare.1), calls=%async_computation | async-start | bytes 2752512 | tf_op jit(solution)/shard_map/all_to_all | solution.py:203
  43.9 13.7 %copy-start.10 = (s32[76]{0:T(128)S(1)}, s32[76]{0:T(128)}, u32[]{:S(2)}) copy-start(s32[76]{0:T(128)} %param.10) | copy-start | bytes 916
  49.3 19.4 %all-to-all-start.1 = ((bf16[16,80,128]{2,1,0:T(8,128)(2,1)}), bf16[16,80,128]{2,1,0:T(8,128)(2,1)S(1)}, u32[]{:S(2)}, u32[]{:S(2)}) async-start(bf16[16,80,128]{2,1,0:T(8,128)(2,1)} %attend.1), calls=%async_computation.1 | async-start | bytes 655360 | tf_op jit(solution)/shard_map/all_to_all | solution.py:228
  68.7 1.0 %copy-start.3 = (bf16[128,2048]{1,0:T(8,128)(2,1)S(1)}, bf16[128,2048]{1,0:T(8,128)(2,1)}, u32[]{:S(2)}) copy-start(bf16[128,2048]{1,0:T(8,128)(2,1)} %refs_2_.5) | copy-start | bytes 1572868

commit v2 on v1

v2 whole, which is shorter than its diff:
```python
import math

import jax
import jax.numpy as jnp
from jax import lax
from jax.experimental import pallas as pl
from jax.experimental.pallas import tpu as pltpu
from jax.sharding import PartitionSpec as P

LOG2E = math.log2(math.e)


def round_up(count, step):
    return (count + step - 1) // step * step


def normalize(entries, scales):
    mean_square = jnp.mean(entries * entries, axis=-1, keepdims=True)
    return entries * lax.rsqrt(mean_square + 1e-06) * scales


def place(slots, tokens):
    owner = lax.broadcasted_iota(jnp.int32, (tokens, slots.shape[1]), 0)
    return owner == slots


def prepare_kernel(
    per_group, padded, me_ref, slots_ref, qkv_ref, k_ref, v_ref, q_gain_ref, k_gain_ref, *rest
):
    outs, queries_ref = rest[:-1], rest[-1]
    tokens = k_ref.shape[0]
    head_size = q_gain_ref.shape[1]
    groups = qkv_ref.shape[1] // per_group
    mine = place(slots_ref[...], tokens)
    is_fresh = jnp.max(mine.astype(jnp.float32), axis=1, keepdims=True) > 0.5
    one_hot = mine.astype(jnp.bfloat16)
    q_gain = q_gain_ref[...]
    k_gain = k_gain_ref[...]
    me = me_ref[0]

    for high in range(len(outs) // groups):
        head = lax.bitwise_xor(me // groups, high)
        columns = pl.ds(pl.multiple_of(head * head_size, head_size), head_size)

        def merged(part, cache_ref):
            spread = jnp.dot(
                one_hot, qkv_ref[part, :, columns], preferred_element_type=jnp.float32
            )
            return jnp.where(is_fresh, spread, cache_ref[:, columns].astype(jnp.float32))

        keys = normalize(merged(1, k_ref), k_gain).astype(jnp.bfloat16)
        values = merged(2, v_ref).astype(jnp.bfloat16)
        queries = normalize(qkv_ref[0, :, columns].astype(jnp.float32), q_gain)
        empty = jnp.zeros((padded - per_group, head_size), jnp.float32)
        for group in range(groups):
            share = queries[group * per_group : (group + 1) * per_group]
            if padded > per_group:
                share = jnp.concatenate([share, empty], axis=0)
            queries_ref[group] = share.astype(jnp.bfloat16)
        for low in range(groups):
            out_ref = outs[high * groups + low]
            group = lax.bitwise_xor(me % groups, low)
            out_ref[:tokens] = keys
            out_ref[tokens : 2 * tokens] = values
            out_ref[2 * tokens :] = queries_ref[group]


def attend_kernel(tokens, query_rows, key_rows, count, me_ref, *rest):
    del me_ref
    arrived = rest[:count]
    text_k_ref, text_v_ref, k_gain_ref = rest[count : count + 3]
    outs = rest[count + 3 : 2 * count + 3]
    queries_ref, keys_ref, values_ref, weights_ref, result_ref = rest[2 * count + 3 :]
    head_size = text_k_ref.shape[1]
    padded = arrived[0].shape[0] - 2 * tokens
    factor = head_size ** (-0.5) * LOG2E
    text = text_k_ref.shape[0]
    text_keys = normalize(text_k_ref[...].astype(jnp.float32), k_gain_ref[...])
    keys_ref[:text] = text_keys.astype(jnp.bfloat16)
    values_ref[:text, :head_size] = text_v_ref[...]
    values_ref[:, head_size:] = jnp.ones((values_ref.shape[0], head_size), jnp.bfloat16)
    for step in range(count):
        first = text + step * tokens
        keys_ref[first : first + tokens] = arrived[step][:tokens]
        values_ref[first : first + tokens, :head_size] = arrived[step][tokens : 2 * tokens]
        queries_ref[step * padded : (step + 1) * padded] = arrived[step][2 * tokens :]

    def add_queries(step, carry):
        mine = pl.ds(pl.multiple_of(step * query_rows, 16), query_rows)
        queries = queries_ref[mine]
        for first in range(0, keys_ref.shape[0], key_rows):
            scores = lax.dot_general(
                queries,
                keys_ref[first : first + key_rows],
                (((1,), (1,)), ((), ())),
                preferred_element_type=jnp.float32,
            )
            weights_ref[:, first : first + key_rows] = jnp.exp2(scores * factor).astype(
                jnp.bfloat16
            )
        sums = jnp.dot(weights_ref[...], values_ref[...], preferred_element_type=jnp.float32)
        result_ref[mine] = (sums[:, :head_size] / sums[:, head_size:]).astype(jnp.bfloat16)
        return carry

    lax.fori_loop(0, queries_ref.shape[0] // query_rows, add_queries, 0)
    for step in range(count):
        outs[step][...] = result_ref[step * padded : (step + 1) * padded]


def finish_kernel(count, me_ref, slots_ref, cache_ref, *rest):
    returned, out_ref = rest[:count], rest[count]
    tokens = cache_ref.shape[0]
    head_size = returned[0].shape[1]
    groups = slots_ref.shape[0]
    me = me_ref[0]
    one_hot = []
    owned = jnp.zeros((tokens, 1), jnp.float32)
    for low in range(groups):
        group = lax.bitwise_xor(me % groups, low)
        mine = place(slots_ref[pl.ds(group, 1)], tokens).astype(jnp.float32)
        owned = owned + jnp.sum(mine, axis=1, keepdims=True)
        one_hot.append(mine.astype(jnp.bfloat16))
    is_fresh = owned > 0.5
    for high in range(count // groups):
        head = lax.bitwise_xor(me // groups, high)
        columns = pl.ds(pl.multiple_of(head * head_size, head_size), head_size)
        placed = jnp.zeros((tokens, head_size), jnp.float32)
        for low in range(groups):
            placed = placed + jnp.dot(
                one_hot[low], returned[high * groups + low][...], preferred_element_type=jnp.float32
            )
        out_ref[:, columns] = jnp.where(
            is_fresh, placed, cache_ref[:, columns].astype(jnp.float32)
        ).astype(out_ref.dtype)


def whole(shape):
    return pl.BlockSpec(shape, lambda i, me: (0,) * len(shape))


def exchange(blocks):
    count = len(blocks)
    arrived = list(blocks)
    for step in reversed(range(1, count)):
        arrived[step] = lax.ppermute(blocks[step], "seq", [(a, a ^ step) for a in range(count)])
    return arrived


def shards(fresh_qkv, slot_rows, k_cache, v_cache, attn_cache, text_k, text_v, q_gain, k_gain):
    seq_count = lax.axis_size("seq")
    me = lax.axis_index("seq").reshape(1)
    slot_count = slot_rows.shape[0]
    tokens, row_width = k_cache.shape
    text = text_k.shape[0]
    head_size = q_gain.shape[0]
    head_count = row_width // head_size
    groups = seq_count // head_count
    per_group = slot_count // groups
    padded = round_up(per_group, 16)
    rows = 2 * tokens + padded
    q_gain = q_gain.reshape(1, head_size)
    k_gain = k_gain.reshape(1, head_size)
    qkv = jnp.transpose(fresh_qkv, (1, 0, 2))
    slots = slot_rows.reshape(1, slot_count)
    padded_slots = jnp.pad(
        slot_rows.reshape(groups, per_group),
        ((0, 0), (0, padded - per_group)),
        constant_values=tokens,
    )

    outgoing = pl.pallas_call(
        lambda *refs: prepare_kernel(per_group, padded, *refs),
        out_shape=[jax.ShapeDtypeStruct((rows, head_size), jnp.bfloat16)] * seq_count,
        grid_spec=pltpu.PrefetchScalarGridSpec(
            num_scalar_prefetch=1,
            grid=(1,),
            in_specs=[
                whole((1, slot_count)),
                whole((3, slot_count, row_width)),
                whole((tokens, row_width)),
                whole((tokens, row_width)),
                whole((1, head_size)),
                whole((1, head_size)),
            ],
            out_specs=[whole((rows, head_size))] * seq_count,
            scratch_shapes=[pltpu.VMEM((groups, padded, head_size), jnp.bfloat16)],
        ),
        name="prepare",
    )(me, slots, qkv, k_cache, v_cache, q_gain, k_gain)

    arrived = exchange(outgoing)

    query_rows = 4 * padded
    all_keys = text + seq_count * tokens
    result = pl.pallas_call(
        lambda *refs: attend_kernel(tokens, query_rows, 256, seq_count, *refs),
        out_shape=[jax.ShapeDtypeStruct((padded, head_size), jnp.bfloat16)] * seq_count,
        grid_spec=pltpu.PrefetchScalarGridSpec(
            num_scalar_prefetch=1,
            grid=(1,),
            in_specs=[whole((rows, head_size))] * seq_count
            + [pl.BlockSpec((text, head_size), lambda i, me: (0, me[0] // groups))] * 2
            + [whole((1, head_size))],
            out_specs=[whole((padded, head_size))] * seq_count,
            scratch_shapes=[
                pltpu.VMEM((seq_count * padded, head_size), jnp.bfloat16),
                pltpu.VMEM((all_keys, head_size), jnp.bfloat16),
                pltpu.VMEM((all_keys, 2 * head_size), jnp.bfloat16),
                pltpu.VMEM((query_rows, all_keys), jnp.bfloat16),
                pltpu.VMEM((seq_count * padded, head_size), jnp.bfloat16),
            ],
        ),
        compiler_params=pltpu.CompilerParams(vmem_limit_bytes=40 * 2**20),
        name="attend",
    )(me, *arrived, text_k, text_v, k_gain)

    returned = exchange(result)

    return pl.pallas_call(
        lambda *refs: finish_kernel(seq_count, *refs),
        out_shape=jax.ShapeDtypeStruct((tokens, row_width), attn_cache.dtype),
        grid_spec=pltpu.PrefetchScalarGridSpec(
            num_scalar_prefetch=1,
            grid=(1,),
            in_specs=[whole((groups, padded)), whole((tokens, row_width))]
            + [whole((padded, head_size))] * seq_count,
            out_specs=whole((tokens, row_width)),
        ),
        compiler_params=pltpu.CompilerParams(vmem_limit_bytes=32 * 2**20),
        name="finish",
    )(me, padded_slots, attn_cache, *returned)


def solution(mesh):
    return jax.shard_map(
        shards,
        mesh=mesh,
        in_specs=(
            P(("parts", "seq"), None, None),
            P(("parts", "seq")),
            P(("parts", "seq"), None),
            P(("parts", "seq"), None),
            P(("parts", "seq"), None),
            P("parts", None),
            P("parts", None),
            P(),
            P(),
        ),
        out_specs=P(("parts", "seq"), None),
        check_vma=False,
    )
```

time: 72.1 us -> 79.8 us (1.11)
  starting transfers between devices: 15.8 us -> 49.3 us
  waiting for transfers between devices: 39.6 us -> 18.8 us
  local copies, waits for them, and re-layouts: 6.31 us -> 2.13 us
    ppermute x0 -> x30, starting transfers between devices: none -> 49.3 us  [exchange(): lax.ppermute(blocks[step], 'seq', [(a, a ^ step) for a in range(count)])]
    all_to_all x2 -> x0, waiting for transfers between devices: 39.6 us -> none  [the longest x1 28.6 us: shards(): lax.all_to_all(outgoing, 'seq', split_axis=0, concat_axis=0, tiled=True)]
    ppermute x0 -> x30, waiting for transfers between devices: none -> 18.8 us  [exchange(): lax.ppermute(blocks[step], 'seq', [(a, a ^ step) for a in range(count)])]
    all_to_all x2 -> x0, starting transfers between devices: 15.8 us -> none  [the longest x1 8.28 us: shards(): lax.all_to_all(result, 'seq', split_axis=0, concat_axis=0, tiled=True)]
    unnamed x22 -> x12, local copies, waits for them, and re-layouts: 6.31 us -> 2.13 us
    pallas_call x2, Pallas kernels: 7.3 us -> 5.64 us  [the longest x1 4.51 us: shards(): pl.pallas_call(lambda *refs: attend_kernel(tokens, query_rows, 256, seq_c...]
    pallas_call x1, Pallas kernels: 2.54 us -> 3.57 us  [shards(): pl.pallas_call(lambda *refs: prepare_kernel(per_group, padded, *refs), ou...]
  transfers between devices with their start and end apart: 2 -> 30, of which waited for: 2 -> 7; matrix products, arithmetic and copies ran while one was open for 0% -> 0% of each run, Pallas kernels for 0% -> 0%
where the time goes in v2:
time: 79.8 us; the launch traced here: 79.6 us
  starting transfers between devices  49.3 us (62%)
  waiting for transfers between devices  18.8 us (24%)
  Pallas kernels  9.21 us (12%)
  local copies, waits for them, and re-layouts  2.13 us (3%)
    ppermute x30, starting transfers between devices, exchange(): lax.ppermute(blocks[step], 'seq', [(a, a ^ step) for a in range(count)])  49.3 us
    ppermute x30, waiting for transfers between devices, exchange(): lax.ppermute(blocks[step], 'seq', [(a, a ^ step) for a in range(count)])  18.8 us
    pallas_call x1, Pallas kernels, shards(): pl.pallas_call(lambda *refs: attend_kernel(tokens, query_rows, 256, seq_c...  4.51 us
    pallas_call x1, Pallas kernels, shards(): pl.pallas_call(lambda *refs: prepare_kernel(per_group, padded, *refs), ou...  3.57 us
    unnamed x12, local copies, waits for them, and re-layouts  2.13 us
  transfers between devices with their start and end apart: 30, of which 7 were waited for; matrix products, arithmetic and copies ran while one was open for 0% of the time, Pallas kernels for 0%

profile of v2, /device:TPU:0, one launch (start us, length us, event | category | flops | bytes accessed | tf_op | source)
XLA Modules:
  0.0 79.6 jit_solution(15860563138729549220)
XLA Ops:
  0.0 3.6 %prepare.1 = (bf16[336,128]{1,0:T(8,128)(2,1)}, bf16[336,128]{1,0:T(8,128)(2,1)}, bf16[336,128]{1,0:T(8,128)(2,1)}, bf16[336,128]{1,0:T(8,128)(2,1)}, bf16[336,1...) custom-call(s32[1]{0:T(128)} %bitcast.refs_0_, ...), custom_call_target="tpu_custom_call" | custom-call | tf_op jit(solution)/shard_map/prepare/pallas_call | solution.py:171
  3.6 0.5 collective-permute-start
  4.0 2.6 %collective-permute-start.1 = (bf16[336,128]{1,0:T(8,128)(2,1)}, bf16[336,128]{1,0:T(8,128)(2,1)S(1)}, u32[]{:S(2)}, u32[]{:S(2)}) collective-permute-start(bf16[336,128]{1,0:T(8,128)(2,1)} %get-tuple-element.39), channel_id=1, source_target_pairs={{0,2},{1,3},{2,0},{3,1},{4,6},{5,7},{6,4},{7,5},{8,10},{9,11},{10,... | collective-permute-start | bytes 258056 | tf_op jit(solution)/shard_map/ppermute | solution.py:145
  6.6 2.3 %collective-permute-start.10 = (bf16[336,128]{1,0:T(8,128)(2,1)}, bf16[336,128]{1,0:T(8,128)(2,1)S(1)}, u32[]{:S(2)}, u32[]{:S(2)}) collective-permute-start(bf16[336,128]{1,0:T(8,128)(2,1)} %get-tuple-element.48), channel_id=1, source_target_pairs={{0,11},{1,10},{2,9},{3,8},{4,15},{5,14},{6,13},{7,12},{8,3},{9,2},... | collective-permute-start | bytes 258056 | tf_op jit(solution)/shard_map/ppermute | solution.py:145
  8.9 1.4 %collective-permute-start.11 = (bf16[336,128]{1,0:T(8,128)(2,1)}, bf16[336,128]{1,0:T(8,128)(2,1)S(1)}, u32[]{:S(2)}, u32[]{:S(2)}) collective-permute-start(bf16[336,128]{1,0:T(8,128)(2,1)} %get-tuple-element.49), channel_id=1, source_target_pairs={{0,12},{1,13},{2,14},{3,15},{4,8},{5,9},{6,10},{7,11},{8,4},{9,5},... | collective-permute-start | bytes 258056 | tf_op jit(solution)/shard_map/ppermute | solution.py:145
  10.3 2.1 %collective-permute-start.12 = (bf16[336,128]{1,0:T(8,128)(2,1)}, bf16[336,128]{1,0:T(8,128)(2,1)S(1)}, u32[]{:S(2)}, u32[]{:S(2)}) collective-permute-start(bf16[336,128]{1,0:T(8,128)(2,1)} %get-tuple-element.50), channel_id=1, source_target_pairs={{0,13},{1,12},{2,15},{3,14},{4,9},{5,8},{6,11},{7,10},{8,5},{9,4},... | collective-permute-start | bytes 258056 | tf_op jit(solution)/shard_map/ppermute | solution.py:145
  12.4 0.0 collective-permute-done.refs_2_
  12.4 2.3 %collective-permute-start.13 = (bf16[336,128]{1,0:T(8,128)(2,1)}, bf16[336,128]{1,0:T(8,128)(2,1)S(1)}, u32[]{:S(2)}, u32[]{:S(2)}) collective-permute-start(bf16[336,128]{1,0:T(8,128)(2,1)} %get-tuple-element.51), channel_id=1, source_target_pairs={{0,14},{1,15},{2,12},{3,13},{4,10},{5,11},{6,8},{7,9},{8,6},{9,7},... | collective-permute-start | bytes 258056 | tf_op jit(solution)/shard_map/ppermute | solution.py:145
  14.8 0.0 collective-permute-done.1.refs_3_
  14.8 2.2 %collective-permute-start.14 = (bf16[336,128]{1,0:T(8,128)(2,1)}, bf16[336,128]{1,0:T(8,128)(2,1)S(1)}, u32[]{:S(2)}, u32[]{:S(2)}) collective-permute-start(bf16[336,128]{1,0:T(8,128)(2,1)} %get-tuple-element.52), channel_id=1, source_target_pairs={{0,15},{1,14},{2,13},{3,12},{4,11},{5,10},{6,9},{7,8},{8,7},{9,6},... | collective-permute-start | bytes 258056 | tf_op jit(solution)/shard_map/ppermute | solution.py:145
  16.9 3.7 %collective-permute-done.10.refs_12_ = bf16[336,128]{1,0:T(8,128)(2,1)S(1)} collective-permute-done((bf16[336,128]{1,0:T(8,128)(2,1)}, bf16[336,128]{1,0:T(8,128)(2,1)S(1)}, u32[]{:S(2)}, u32[]{:S(2)}) %collective-permute-start.10) | collective-permute-done | bytes 86048 | tf_op jit(solution)/shard_map/ppermute | solution.py:145
  20.6 3.8 %collective-permute-start.3 = (bf16[336,128]{1,0:T(8,128)(2,1)}, bf16[336,128]{1,0:T(8,128)(2,1)S(1)}, u32[]{:S(2)}, u32[]{:S(2)}) collective-permute-start(bf16[336,128]{1,0:T(8,128)(2,1)} %get-tuple-element.41), channel_id=1, source_target_pairs={{0,4},{1,5},{2,6},{3,7},{4,0},{5,1},{6,2},{7,3},{8,12},{9,13},{10,... | collective-permute-start | bytes 258056 | tf_op jit(solution)/shard_map/ppermute | solution.py:145
  24.4 1.6 %collective-permute-start.4 = (bf16[336,128]{1,0:T(8,128)(2,1)}, bf16[336,128]{1,0:T(8,128)(2,1)S(1)}, u32[]{:S(2)}, u32[]{:S(2)}) collective-permute-start(bf16[336,128]{1,0:T(8,128)(2,1)} %get-tuple-element.42), channel_id=1, source_target_pairs={{0,5},{1,4},{2,7},{3,6},{4,1},{5,0},{6,3},{7,2},{8,13},{9,12},{10,... | collective-permute-start | bytes 258056 | tf_op jit(solution)/shard_map/ppermute | solution.py:145
  25.9 3.1 %collective-permute-start.5 = (bf16[336,128]{1,0:T(8,128)(2,1)}, bf16[336,128]{1,0:T(8,128)(2,1)S(1)}, u32[]{:S(2)}, u32[]{:S(2)}) collective-permute-start(bf16[336,128]{1,0:T(8,128)(2,1)} %get-tuple-element.43), channel_id=1, source_target_pairs={{0,6},{1,7},{2,4},{3,5},{4,2},{5,3},{6,0},{7,1},{8,14},{9,15},{10,... | collective-permute-start | bytes 258056 | tf_op jit(solution)/shard_map/ppermute | solution.py:145
  29.1 0.0 collective-permute-done.14.refs_16_
  29.1 1.5 %collective-permute-start.6 = (bf16[336,128]{1,0:T(8,128)(2,1)}, bf16[336,128]{1,0:T(8,128)(2,1)S(1)}, u32[]{:S(2)}, u32[]{:S(2)}) collective-permute-start(bf16[336,128]{1,0:T(8,128)(2,1)} %get-tuple-element.44), channel_id=1, source_target_pairs={{0,7},{1,6},{2,5},{3,4},{4,3},{5,2},{6,1},{7,0},{8,15},{9,14},{10,... | collective-permute-start | bytes 258056 | tf_op jit(solution)/shard_map/ppermute | solution.py:145
  30.5 2.6 %collective-permute-start.7 = (bf16[336,128]{1,0:T(8,128)(2,1)}, bf16[336,128]{1,0:T(8,128)(2,1)S(1)}, u32[]{:S(2)}, u32[]{:S(2)}) collective-permute-start(bf16[336,128]{1,0:T(8,128)(2,1)} %get-tuple-element.45), channel_id=1, source_target_pairs={{0,8},{1,9},{2,10},{3,11},{4,12},{5,13},{6,14},{7,15},{8,0},{9,1},... | collective-permute-start | bytes 258056 | tf_op jit(solution)/shard_map/ppermute | solution.py:145
  33.2 0.4 collective-permute-start.8
  33.6 0.0 collective-permute-done.4.refs_6_
  33.6 2.5 %collective-permute-start.9 = (bf16[336,128]{1,0:T(8,128)(2,1)}, bf16[336,128]{1,0:T(8,128)(2,1)S(1)}, u32[]{:S(2)}, u32[]{:S(2)}) collective-permute-start(bf16[336,128]{1,0:T(8,128)(2,1)} %get-tuple-element.47), channel_id=1, source_target_pairs={{0,10},{1,11},{2,8},{3,9},{4,14},{5,15},{6,12},{7,13},{8,2},{9,3},... | collective-permute-start | bytes 258056 | tf_op jit(solution)/shard_map/ppermute | solution.py:145
  36.1 0.0 collective-permute-done.5.refs_7_
  36.1 0.0 collective-permute-done.6.refs_8_
  36.1 0.7 collective-permute-done.7.refs_9_
  36.8 7.4 %collective-permute-done.8.refs_10_ = bf16[336,128]{1,0:T(8,128)(2,1)S(1)} collective-permute-done((bf16[336,128]{1,0:T(8,128)(2,1)}, bf16[336,128]{1,0:T(8,128)(2,1)S(1)}, u32[]{:S(2)}, u32[]{:S(2)}) %collective-permute-start.8) | collective-permute-done | bytes 86048 | tf_op jit(solution)/shard_map/ppermute | solution.py:145
  44.2 2.2 %collective-permute-done.9.refs_11_ = bf16[336,128]{1,0:T(8,128)(2,1)S(1)} collective-permute-done((bf16[336,128]{1,0:T(8,128)(2,1)}, bf16[336,128]{1,0:T(8,128)(2,1)S(1)}, u32[]{:S(2)}, u32[]{:S(2)}) %collective-permute-start.9) | collective-permute-done | bytes 86048 | tf_op jit(solution)/shard_map/ppermute | solution.py:145
  46.4 1.2 %copy-done.1 = bf16[256,2048]{1,0:T(8,128)(2,1)S(1)} copy-done((bf16[256,2048]{1,0:T(8,128)(2,1)S(1)}, bf16[256,2048]{1,0:T(8,128)(2,1)}, u32[]{:S(2)}) %copy-start.1) | copy-done | bytes 1048600
  47.6 0.9 %copy-done.3 = bf16[336,128]{1,0:T(8,128)(2,1)S(1)} copy-done((bf16[336,128]{1,0:T(8,128)(2,1)S(1)}, bf16[336,128]{1,0:T(8,128)(2,1)}, u32[]{:S(2)}) %copy-start.3) | copy-done | bytes 86040
  48.5 4.5 %attend.1 = (bf16[80,128]{1,0:T(8,128)(2,1)S(1)}, bf16[80,128]{1,0:T(8,128)(2,1)S(1)}, bf16[80,128]{1,0:T(8,128)(2,1)S(1)}, bf16[80,128]{1,0:T(8,128)(2,1)S(1)},...) custom-call(s32[1]{0:T(128)} %bitcast.refs_0_, ...), custom_call_target="tpu_custom_call" | custom-call | tf_op jit(solution)/shard_map/attend/pallas_call | solution.py:195
  53.0 0.1 collective-permute-start.15
  53.1 1.3 %collective-permute-start.16 = (bf16[80,128]{1,0:T(8,128)(2,1)S(1)}, bf16[80,128]{1,0:T(8,128)(2,1)S(1)}, u32[]{:S(2)}, u32[]{:S(2)}) collective-permute-start(bf16[80,128]{1,0:T(8,128)(2,1)S(1)} %get-tuple-element.55), channel_id=1, source_target_pairs={{0,2},{1,3},{2,0},{3,1},{4,6},{5,7},{6,4},{7,5},{8,10},{9,11},{10,... | collective-permute-start | bytes 61448 | tf_op jit(solution)/shard_map/ppermute | solution.py:145
  54.5 0.5 collective-permute-start.17
  55.0 1.7 %collective-permute-start.19 = (bf16[80,128]{1,0:T(8,128)(2,1)S(1)}, bf16[80,128]{1,0:T(8,128)(2,1)S(1)}, u32[]{:S(2)}, u32[]{:S(2)}) collective-permute-start(bf16[80,128]{1,0:T(8,128)(2,1)S(1)} %get-tuple-element.58), channel_id=1, source_target_pairs={{0,5},{1,4},{2,7},{3,6},{4,1},{5,0},{6,3},{7,2},{8,13},{9,12},{10,... | collective-permute-start | bytes 61448 | tf_op jit(solution)/shard_map/ppermute | solution.py:145
  56.7 0.0 collective-permute-done.15.refs_4_
  56.7 1.1 %collective-permute-start.20 = (bf16[80,128]{1,0:T(8,128)(2,1)S(1)}, bf16[80,128]{1,0:T(8,128)(2,1)S(1)}, u32[]{:S(2)}, u32[]{:S(2)}) collective-permute-start(bf16[80,128]{1,0:T(8,128)(2,1)S(1)} %get-tuple-element.59), channel_id=1, source_target_pairs={{0,6},{1,7},{2,4},{3,5},{4,2},{5,3},{6,0},{7,1},{8,14},{9,15},{10,... | collective-permute-start | bytes 61448 | tf_op jit(solution)/shard_map/ppermute | solution.py:145
  57.7 0.0 collective-permute-done.16.refs_5_
  57.8 1.7 %collective-permute-start.21 = (bf16[80,128]{1,0:T(8,128)(2,1)S(1)}, bf16[80,128]{1,0:T(8,128)(2,1)S(1)}, u32[]{:S(2)}, u32[]{:S(2)}) collective-permute-start(bf16[80,128]{1,0:T(8,128)(2,1)S(1)} %get-tuple-element.60), channel_id=1, source_target_pairs={{0,7},{1,6},{2,5},{3,4},{4,3},{5,2},{6,1},{7,0},{8,15},{9,14},{10,... | collective-permute-start | bytes 61448 | tf_op jit(solution)/shard_map/ppermute | solution.py:145
  59.4 1.6 %collective-permute-start.22 = (bf16[80,128]{1,0:T(8,128)(2,1)S(1)}, bf16[80,128]{1,0:T(8,128)(2,1)S(1)}, u32[]{:S(2)}, u32[]{:S(2)}) collective-permute-start(bf16[80,128]{1,0:T(8,128)(2,1)S(1)} %get-tuple-element.61), channel_id=1, source_target_pairs={{0,8},{1,9},{2,10},{3,11},{4,12},{5,13},{6,14},{7,15},{8,0},{9,1},... | collective-permute-start | bytes 61448 | tf_op jit(solution)/shard_map/ppermute | solution.py:145
  61.0 0.9 %collective-permute-start.23 = (bf16[80,128]{1,0:T(8,128)(2,1)S(1)}, bf16[80,128]{1,0:T(8,128)(2,1)S(1)}, u32[]{:S(2)}, u32[]{:S(2)}) collective-permute-start(bf16[80,128]{1,0:T(8,128)(2,1)S(1)} %get-tuple-element.62), channel_id=1, source_target_pairs={{0,9},{1,8},{2,11},{3,10},{4,13},{5,12},{6,15},{7,14},{8,1},{9,0},... | collective-permute-start | bytes 61448 | tf_op jit(solution)/shard_map/ppermute | solution.py:145
  62.0 2.3 %collective-permute-start.24 = (bf16[80,128]{1,0:T(8,128)(2,1)S(1)}, bf16[80,128]{1,0:T(8,128)(2,1)S(1)}, u32[]{:S(2)}, u32[]{:S(2)}) collective-permute-start(bf16[80,128]{1,0:T(8,128)(2,1)S(1)} %get-tuple-element.63), channel_id=1, source_target_pairs={{0,10},{1,11},{2,8},{3,9},{4,14},{5,15},{6,12},{7,13},{8,2},{9,3},... | collective-permute-start | bytes 61448 | tf_op jit(solution)/shard_map/ppermute | solution.py:145
  64.3 1.3 %collective-permute-start.25 = (bf16[80,128]{1,0:T(8,128)(2,1)S(1)}, bf16[80,128]{1,0:T(8,128)(2,1)S(1)}, u32[]{:S(2)}, u32[]{:S(2)}) collective-permute-start(bf16[80,128]{1,0:T(8,128)(2,1)S(1)} %get-tuple-element.64), channel_id=1, source_target_pairs={{0,11},{1,10},{2,9},{3,8},{4,15},{5,14},{6,13},{7,12},{8,3},{9,2},... | collective-permute-start | bytes 61448 | tf_op jit(solution)/shard_map/ppermute | solution.py:145
  65.6 3.1 %collective-permute-start.26 = (bf16[80,128]{1,0:T(8,128)(2,1)S(1)}, bf16[80,128]{1,0:T(8,128)(2,1)S(1)}, u32[]{:S(2)}, u32[]{:S(2)}) collective-permute-start(bf16[80,128]{1,0:T(8,128)(2,1)S(1)} %get-tuple-element.65), channel_id=1, source_target_pairs={{0,12},{1,13},{2,14},{3,15},{4,8},{5,9},{6,10},{7,11},{8,4},{9,5},... | collective-permute-start | bytes 61448 | tf_op jit(solution)/shard_map/ppermute | solution.py:145
  68.7 0.4 collective-permute-start.27
  69.1 3.4 %collective-permute-start.28 = (bf16[80,128]{1,0:T(8,128)(2,1)S(1)}, bf16[80,128]{1,0:T(8,128)(2,1)S(1)}, u32[]{:S(2)}, u32[]{:S(2)}) collective-permute-start(bf16[80,128]{1,0:T(8,128)(2,1)S(1)} %get-tuple-element.67), channel_id=1, source_target_pairs={{0,14},{1,15},{2,12},{3,13},{4,10},{5,11},{6,8},{7,9},{8,6},{9,7},... | collective-permute-start | bytes 61448 | tf_op jit(solution)/shard_map/ppermute | solution.py:145
  72.5 1.1 %collective-permute-start.29 = (bf16[80,128]{1,0:T(8,128)(2,1)S(1)}, bf16[80,128]{1,0:T(8,128)(2,1)S(1)}, u32[]{:S(2)}, u32[]{:S(2)}) collective-permute-start(bf16[80,128]{1,0:T(8,128)(2,1)S(1)} %get-tuple-element.68), channel_id=1, source_target_pairs={{0,15},{1,14},{2,13},{3,12},{4,11},{5,10},{6,9},{7,8},{8,7},{9,6},... | collective-permute-start | bytes 61448 | tf_op jit(solution)/shard_map/ppermute | solution.py:145
  73.6 0.2 collective-permute-done.27.refs_16_
  73.8 1.8 %collective-permute-done.28.refs_17_ = bf16[80,128]{1,0:T(8,128)(2,1)S(1)} collective-permute-done((bf16[80,128]{1,0:T(8,128)(2,1)S(1)}, bf16[80,128]{1,0:T(8,128)(2,1)S(1)}, u32[]{:S(2)}, u32[]{:S(2)}) %collective-permute-start.28) | collective-permute-done | bytes 20512 | tf_op jit(solution)/shard_map/ppermute | solution.py:145
  75.6 2.9 %collective-permute-done.29.refs_18_ = bf16[80,128]{1,0:T(8,128)(2,1)S(1)} collective-permute-done((bf16[80,128]{1,0:T(8,128)(2,1)S(1)}, bf16[80,128]{1,0:T(8,128)(2,1)S(1)}, u32[]{:S(2)}, u32[]{:S(2)}) %collective-permute-start.29) | collective-permute-done | bytes 20512 | tf_op jit(solution)/shard_map/ppermute | solution.py:145
  78.4 1.1 %finish.1 = bf16[128,2048]{1,0:T(8,128)(2,1)} custom-call(s32[1]{0:T(128)} %bitcast.refs_0_, s32[1,80]{1,0:T(1,128)S(1)} %pad.4.refs_1_, bf16[128,2048]{1,0:T(8,128)(2,1)S(1)} %copy-done.2, bf16[80,128]{1,0:T(8,128)(2,1)S(1)} %get-tuple-element.53.refs_3_, bf16[80,128]{1,0:T(8,128)(2,1)S(1)} %collective-permute-done.15.refs_4_, ...), custom_call_target="tpu_custom_call" | custom-call | tf_op jit(solution)/shard_map/finish/pallas_call | solution.py:219
  (28 shorter events, 0.1 us)
Async XLA Ops:
  0.0 46.4 %copy-start = (bf16[256,2048]{1,0:T(8,128)(2,1)S(1)}, bf16[256,2048]{1,0:T(8,128)(2,1)}, u32[]{:S(2)}) copy-start(bf16[256,2048]{1,0:T(8,128)(2,1)} %refs_17_.1) | copy-start | bytes 3145732
  3.6 8.9 %collective-permute-start = (bf16[336,128]{1,0:T(8,128)(2,1)}, bf16[336,128]{1,0:T(8,128)(2,1)S(1)}, u32[]{:S(2)}, u32[]{:S(2)}) collective-permute-start(bf16[336,128]{1,0:T(8,128)(2,1)} %get-tuple-element.38), channel_id=1, source_target_pairs={{0,1},{1,0},{2,3},{3,2},{4,5},{5,4},{6,7},{7,6},{8,9},{9,8},{10,11... | collective-permute-start | bytes 258056 | tf_op jit(solution)/shard_map/ppermute | solution.py:145
  4.0 10.7 %collective-permute-start.1 = (bf16[336,128]{1,0:T(8,128)(2,1)}, bf16[336,128]{1,0:T(8,128)(2,1)S(1)}, u32[]{:S(2)}, u32[]{:S(2)}) collective-permute-start(bf16[336,128]{1,0:T(8,128)(2,1)} %get-tuple-element.39), channel_id=1, source_target_pairs={{0,2},{1,3},{2,0},{3,1},{4,6},{5,7},{6,4},{7,5},{8,10},{9,11},{10,... | collective-permute-start | bytes 258056 | tf_op jit(solution)/shard_map/ppermute | solution.py:145
  6.6 14.0 %collective-permute-start.10 = (bf16[336,128]{1,0:T(8,128)(2,1)}, bf16[336,128]{1,0:T(8,128)(2,1)S(1)}, u32[]{:S(2)}, u32[]{:S(2)}) collective-permute-start(bf16[336,128]{1,0:T(8,128)(2,1)} %get-tuple-element.48), channel_id=1, source_target_pairs={{0,11},{1,10},{2,9},{3,8},{4,15},{5,14},{6,13},{7,12},{8,3},{9,2},... | collective-permute-start | bytes 258056 | tf_op jit(solution)/shard_map/ppermute | solution.py:145
  8.9 11.7 %collective-permute-start.11 = (bf16[336,128]{1,0:T(8,128)(2,1)}, bf16[336,128]{1,0:T(8,128)(2,1)S(1)}, u32[]{:S(2)}, u32[]{:S(2)}) collective-permute-start(bf16[336,128]{1,0:T(8,128)(2,1)} %get-tuple-element.49), channel_id=1, source_target_pairs={{0,12},{1,13},{2,14},{3,15},{4,8},{5,9},{6,10},{7,11},{8,4},{9,5},... | collective-permute-start | bytes 258056 | tf_op jit(solution)/shard_map/ppermute | solution.py:145
  10.3 14.1 %collective-permute-start.12 = (bf16[336,128]{1,0:T(8,128)(2,1)}, bf16[336,128]{1,0:T(8,128)(2,1)S(1)}, u32[]{:S(2)}, u32[]{:S(2)}) collective-permute-start(bf16[336,128]{1,0:T(8,128)(2,1)} %get-tuple-element.50), channel_id=1, source_target_pairs={{0,13},{1,12},{2,15},{3,14},{4,9},{5,8},{6,11},{7,10},{8,5},{9,4},... | collective-permute-start | bytes 258056 | tf_op jit(solution)/shard_map/ppermute | solution.py:145
  12.4 13.5 %collective-permute-start.13 = (bf16[336,128]{1,0:T(8,128)(2,1)}, bf16[336,128]{1,0:T(8,128)(2,1)S(1)}, u32[]{:S(2)}, u32[]{:S(2)}) collective-permute-start(bf16[336,128]{1,0:T(8,128)(2,1)} %get-tuple-element.51), channel_id=1, source_target_pairs={{0,14},{1,15},{2,12},{3,13},{4,10},{5,11},{6,8},{7,9},{8,6},{9,7},... | collective-permute-start | bytes 258056 | tf_op jit(solution)/shard_map/ppermute | solution.py:145
  14.8 14.3 %collective-permute-start.14 = (bf16[336,128]{1,0:T(8,128)(2,1)}, bf16[336,128]{1,0:T(8,128)(2,1)S(1)}, u32[]{:S(2)}, u32[]{:S(2)}) collective-permute-start(bf16[336,128]{1,0:T(8,128)(2,1)} %get-tuple-element.52), channel_id=1, source_target_pairs={{0,15},{1,14},{2,13},{3,12},{4,11},{5,10},{6,9},{7,8},{8,7},{9,6},... | collective-permute-start | bytes 258056 | tf_op jit(solution)/shard_map/ppermute | solution.py:145
  20.6 9.9 %collective-permute-start.2 = (bf16[336,128]{1,0:T(8,128)(2,1)}, bf16[336,128]{1,0:T(8,128)(2,1)S(1)}, u32[]{:S(2)}, u32[]{:S(2)}) collective-permute-start(bf16[336,128]{1,0:T(8,128)(2,1)} %get-tuple-element.40), channel_id=1, source_target_pairs={{0,3},{1,2},{2,1},{3,0},{4,7},{5,6},{6,5},{7,4},{8,11},{9,10},{10,... | collective-permute-start | bytes 258056 | tf_op jit(solution)/shard_map/ppermute | solution.py:145
  20.6 12.6 %collective-permute-start.3 = (bf16[336,128]{1,0:T(8,128)(2,1)}, bf16[336,128]{1,0:T(8,128)(2,1)S(1)}, u32[]{:S(2)}, u32[]{:S(2)}) collective-permute-start(bf16[336,128]{1,0:T(8,128)(2,1)} %get-tuple-element.41), channel_id=1, source_target_pairs={{0,4},{1,5},{2,6},{3,7},{4,0},{5,1},{6,2},{7,3},{8,12},{9,13},{10,... | collective-permute-start | bytes 258056 | tf_op jit(solution)/shard_map/ppermute | solution.py:145
  24.4 9.2 %collective-permute-start.4 = (bf16[336,128]{1,0:T(8,128)(2,1)}, bf16[336,128]{1,0:T(8,128)(2,1)S(1)}, u32[]{:S(2)}, u32[]{:S(2)}) collective-permute-start(bf16[336,128]{1,0:T(8,128)(2,1)} %get-tuple-element.42), channel_id=1, source_target_pairs={{0,5},{1,4},{2,7},{3,6},{4,1},{5,0},{6,3},{7,2},{8,13},{9,12},{10,... | collective-permute-start | bytes 258056 | tf_op jit(solution)/shard_map/ppermute | solution.py:145
  25.9 10.1 %collective-permute-start.5 = (bf16[336,128]{1,0:T(8,128)(2,1)}, bf16[336,128]{1,0:T(8,128)(2,1)S(1)}, u32[]{:S(2)}, u32[]{:S(2)}) collective-permute-start(bf16[336,128]{1,0:T(8,128)(2,1)} %get-tuple-element.43), channel_id=1, source_target_pairs={{0,6},{1,7},{2,4},{3,5},{4,2},{5,3},{6,0},{7,1},{8,14},{9,15},{10,... | collective-permute-start | bytes 258056 | tf_op jit(solution)/shard_map/ppermute | solution.py:145
  29.1 7.0 %collective-permute-start.6 = (bf16[336,128]{1,0:T(8,128)(2,1)}, bf16[336,128]{1,0:T(8,128)(2,1)S(1)}, u32[]{:S(2)}, u32[]{:S(2)}) collective-permute-start(bf16[336,128]{1,0:T(8,128)(2,1)} %get-tuple-element.44), channel_id=1, source_target_pairs={{0,7},{1,6},{2,5},{3,4},{4,3},{5,2},{6,1},{7,0},{8,15},{9,14},{10,... | collective-permute-start | bytes 258056 | tf_op jit(solution)/shard_map/ppermute | solution.py:145
  30.5 6.3 %collective-permute-start.7 = (bf16[336,128]{1,0:T(8,128)(2,1)}, bf16[336,128]{1,0:T(8,128)(2,1)S(1)}, u32[]{:S(2)}, u32[]{:S(2)}) collective-permute-start(bf16[336,128]{1,0:T(8,128)(2,1)} %get-tuple-element.45), channel_id=1, source_target_pairs={{0,8},{1,9},{2,10},{3,11},{4,12},{5,13},{6,14},{7,15},{8,0},{9,1},... | collective-permute-start | bytes 258056 | tf_op jit(solution)/shard_map/ppermute | solution.py:145
  33.2 11.1 %collective-permute-start.8 = (bf16[336,128]{1,0:T(8,128)(2,1)}, bf16[336,128]{1,0:T(8,128)(2,1)S(1)}, u32[]{:S(2)}, u32[]{:S(2)}) collective-permute-start(bf16[336,128]{1,0:T(8,128)(2,1)} %get-tuple-element.46), channel_id=1, source_target_pairs={{0,9},{1,8},{2,11},{3,10},{4,13},{5,12},{6,15},{7,14},{8,1},{9,0},... | collective-permute-start | bytes 258056 | tf_op jit(solution)/shard_map/ppermute | solution.py:145
  33.6 12.8 %copy-start.4 = (f32[128]{0:T(128)S(1)}, f32[128]{0:T(128)}, u32[]{:S(2)}) copy-start(f32[128]{0:T(128)} %param.17) | copy-start | bytes 1540
  33.6 12.8 %collective-permute-start.9 = (bf16[336,128]{1,0:T(8,128)(2,1)}, bf16[336,128]{1,0:T(8,128)(2,1)S(1)}, u32[]{:S(2)}, u32[]{:S(2)}) collective-permute-start(bf16[336,128]{1,0:T(8,128)(2,1)} %get-tuple-element.47), channel_id=1, source_target_pairs={{0,10},{1,11},{2,8},{3,9},{4,14},{5,15},{6,12},{7,13},{8,2},{9,3},... | collective-permute-start | bytes 258056 | tf_op jit(solution)/shard_map/ppermute | solution.py:145
  46.4 1.2 %copy-start.1 = (bf16[256,2048]{1,0:T(8,128)(2,1)S(1)}, bf16[256,2048]{1,0:T(8,128)(2,1)}, u32[]{:S(2)}) copy-start(bf16[256,2048]{1,0:T(8,128)(2,1)} %refs_18_.1) | copy-start | bytes 3145732
  47.6 0.9 %copy-start.3 = (bf16[336,128]{1,0:T(8,128)(2,1)S(1)}, bf16[336,128]{1,0:T(8,128)(2,1)}, u32[]{:S(2)}) copy-start(bf16[336,128]{1,0:T(8,128)(2,1)} %get-tuple-element.37.refs_1_) | copy-start | bytes 258052
  48.5 29.9 %copy-start.2 = (bf16[128,2048]{1,0:T(8,128)(2,1)S(1)}, bf16[128,2048]{1,0:T(8,128)(2,1)}, u32[]{:S(2)}) copy-start(bf16[128,2048]{1,0:T(8,128)(2,1)} %refs_2_.1) | copy-start | bytes 1572868
  53.0 3.6 %collective-permute-start.15 = (bf16[80,128]{1,0:T(8,128)(2,1)S(1)}, bf16[80,128]{1,0:T(8,128)(2,1)S(1)}, u32[]{:S(2)}, u32[]{:S(2)}) collective-permute-start(bf16[80,128]{1,0:T(8,128)(2,1)S(1)} %get-tuple-element.54), channel_id=1, source_target_pairs={{0,1},{1,0},{2,3},{3,2},{4,5},{5,4},{6,7},{7,6},{8,9},{9,8},{10,11... | collective-permute-start | bytes 61448 | tf_op jit(solution)/shard_map/ppermute | solution.py:145
  53.1 4.6 %collective-permute-start.16 = (bf16[80,128]{1,0:T(8,128)(2,1)S(1)}, bf16[80,128]{1,0:T(8,128)(2,1)S(1)}, u32[]{:S(2)}, u32[]{:S(2)}) collective-permute-start(bf16[80,128]{1,0:T(8,128)(2,1)S(1)} %get-tuple-element.55), channel_id=1, source_target_pairs={{0,2},{1,3},{2,0},{3,1},{4,6},{5,7},{6,4},{7,5},{8,10},{9,11},{10,... | collective-permute-start | bytes 61448 | tf_op jit(solution)/shard_map/ppermute | solution.py:145
  54.5 4.9 %collective-permute-start.17 = (bf16[80,128]{1,0:T(8,128)(2,1)S(1)}, bf16[80,128]{1,0:T(8,128)(2,1)S(1)}, u32[]{:S(2)}, u32[]{:S(2)}) collective-permute-start(bf16[80,128]{1,0:T(8,128)(2,1)S(1)} %get-tuple-element.56), channel_id=1, source_target_pairs={{0,3},{1,2},{2,1},{3,0},{4,7},{5,6},{6,5},{7,4},{8,11},{9,10},{10,... | collective-permute-start | bytes 61448 | tf_op jit(solution)/shard_map/ppermute | solution.py:145
  55.0 6.1 %collective-permute-start.18 = (bf16[80,128]{1,0:T(8,128)(2,1)S(1)}, bf16[80,128]{1,0:T(8,128)(2,1)S(1)}, u32[]{:S(2)}, u32[]{:S(2)}) collective-permute-start(bf16[80,128]{1,0:T(8,128)(2,1)S(1)} %get-tuple-element.57), channel_id=1, source_target_pairs={{0,4},{1,5},{2,6},{3,7},{4,0},{5,1},{6,2},{7,3},{8,12},{9,13},{10,... | collective-permute-start | bytes 61448 | tf_op jit(solution)/shard_map/ppermute | solution.py:145
  55.0 7.0 %collective-permute-start.19 = (bf16[80,128]{1,0:T(8,128)(2,1)S(1)}, bf16[80,128]{1,0:T(8,128)(2,1)S(1)}, u32[]{:S(2)}, u32[]{:S(2)}) collective-permute-start(bf16[80,128]{1,0:T(8,128)(2,1)S(1)} %get-tuple-element.58), channel_id=1, source_target_pairs={{0,5},{1,4},{2,7},{3,6},{4,1},{5,0},{6,3},{7,2},{8,13},{9,12},{10,... | collective-permute-start | bytes 61448 | tf_op jit(solution)/shard_map/ppermute | solution.py:145
  56.7 7.6 %collective-permute-start.20 = (bf16[80,128]{1,0:T(8,128)(2,1)S(1)}, bf16[80,128]{1,0:T(8,128)(2,1)S(1)}, u32[]{:S(2)}, u32[]{:S(2)}) collective-permute-start(bf16[80,128]{1,0:T(8,128)(2,1)S(1)} %get-tuple-element.59), channel_id=1, source_target_pairs={{0,6},{1,7},{2,4},{3,5},{4,2},{5,3},{6,0},{7,1},{8,14},{9,15},{10,... | collective-permute-start | bytes 61448 | tf_op jit(solution)/shard_map/ppermute | solution.py:145
  57.8 7.9 %collective-permute-start.21 = (bf16[80,128]{1,0:T(8,128)(2,1)S(1)}, bf16[80,128]{1,0:T(8,128)(2,1)S(1)}, u32[]{:S(2)}, u32[]{:S(2)}) collective-permute-start(bf16[80,128]{1,0:T(8,128)(2,1)S(1)} %get-tuple-element.60), channel_id=1, source_target_pairs={{0,7},{1,6},{2,5},{3,4},{4,3},{5,2},{6,1},{7,0},{8,15},{9,14},{10,... | collective-permute-start | bytes 61448 | tf_op jit(solution)/shard_map/ppermute | solution.py:145
  59.4 9.3 %collective-permute-start.22 = (bf16[80,128]{1,0:T(8,128)(2,1)S(1)}, bf16[80,128]{1,0:T(8,128)(2,1)S(1)}, u32[]{:S(2)}, u32[]{:S(2)}) collective-permute-start(bf16[80,128]{1,0:T(8,128)(2,1)S(1)} %get-tuple-element.61), channel_id=1, source_target_pairs={{0,8},{1,9},{2,10},{3,11},{4,12},{5,13},{6,14},{7,15},{8,0},{9,1},... | collective-permute-start | bytes 61448 | tf_op jit(solution)/shard_map/ppermute | solution.py:145
  61.0 8.0 %collective-permute-start.23 = (bf16[80,128]{1,0:T(8,128)(2,1)S(1)}, bf16[80,128]{1,0:T(8,128)(2,1)S(1)}, u32[]{:S(2)}, u32[]{:S(2)}) collective-permute-start(bf16[80,128]{1,0:T(8,128)(2,1)S(1)} %get-tuple-element.62), channel_id=1, source_target_pairs={{0,9},{1,8},{2,11},{3,10},{4,13},{5,12},{6,15},{7,14},{8,1},{9,0},... | collective-permute-start | bytes 61448 | tf_op jit(solution)/shard_map/ppermute | solution.py:145
  62.0 10.5 %collective-permute-start.24 = (bf16[80,128]{1,0:T(8,128)(2,1)S(1)}, bf16[80,128]{1,0:T(8,128)(2,1)S(1)}, u32[]{:S(2)}, u32[]{:S(2)}) collective-permute-start(bf16[80,128]{1,0:T(8,128)(2,1)S(1)} %get-tuple-element.63), channel_id=1, source_target_pairs={{0,10},{1,11},{2,8},{3,9},{4,14},{5,15},{6,12},{7,13},{8,2},{9,3},... | collective-permute-start | bytes 61448 | tf_op jit(solution)/shard_map/ppermute | solution.py:145
  64.3 9.3 %collective-permute-start.25 = (bf16[80,128]{1,0:T(8,128)(2,1)S(1)}, bf16[80,128]{1,0:T(8,128)(2,1)S(1)}, u32[]{:S(2)}, u32[]{:S(2)}) collective-permute-start(bf16[80,128]{1,0:T(8,128)(2,1)S(1)} %get-tuple-element.64), channel_id=1, source_target_pairs={{0,11},{1,10},{2,9},{3,8},{4,15},{5,14},{6,13},{7,12},{8,3},{9,2},... | collective-permute-start | bytes 61448 | tf_op jit(solution)/shard_map/ppermute | solution.py:145
  65.6 8.0 %collective-permute-start.26 = (bf16[80,128]{1,0:T(8,128)(2,1)S(1)}, bf16[80,128]{1,0:T(8,128)(2,1)S(1)}, u32[]{:S(2)}, u32[]{:S(2)}) collective-permute-start(bf16[80,128]{1,0:T(8,128)(2,1)S(1)} %get-tuple-element.65), channel_id=1, source_target_pairs={{0,12},{1,13},{2,14},{3,15},{4,8},{5,9},{6,10},{7,11},{8,4},{9,5},... | collective-permute-start | bytes 61448 | tf_op jit(solution)/shard_map/ppermute | solution.py:145
  68.7 5.1 %collective-permute-start.27 = (bf16[80,128]{1,0:T(8,128)(2,1)S(1)}, bf16[80,128]{1,0:T(8,128)(2,1)S(1)}, u32[]{:S(2)}, u32[]{:S(2)}) collective-permute-start(bf16[80,128]{1,0:T(8,128)(2,1)S(1)} %get-tuple-element.66), channel_id=1, source_target_pairs={{0,13},{1,12},{2,15},{3,14},{4,9},{5,8},{6,11},{7,10},{8,5},{9,4},... | collective-permute-start | bytes 61448 | tf_op jit(solution)/shard_map/ppermute | solution.py:145
  69.1 4.5 %copy-start.5 = (s32[76]{0:T(128)S(1)}, s32[76]{0:T(128)}, u32[]{:S(2)}) copy-start(s32[76]{0:T(128)} %param.10) | copy-start | bytes 916
  69.1 6.5 %collective-permute-start.28 = (bf16[80,128]{1,0:T(8,128)(2,1)S(1)}, bf16[80,128]{1,0:T(8,128)(2,1)S(1)}, u32[]{:S(2)}, u32[]{:S(2)}) collective-permute-start(bf16[80,128]{1,0:T(8,128)(2,1)S(1)} %get-tuple-element.67), channel_id=1, source_target_pairs={{0,14},{1,15},{2,12},{3,13},{4,10},{5,11},{6,8},{7,9},{8,6},{9,7},... | collective-permute-start | bytes 61448 | tf_op jit(solution)/shard_map/ppermute | solution.py:145
  72.5 5.9 %collective-permute-start.29 = (bf16[80,128]{1,0:T(8,128)(2,1)S(1)}, bf16[80,128]{1,0:T(8,128)(2,1)S(1)}, u32[]{:S(2)}, u32[]{:S(2)}) collective-permute-start(bf16[80,128]{1,0:T(8,128)(2,1)S(1)} %get-tuple-element.68), channel_id=1, source_target_pairs={{0,15},{1,14},{2,13},{3,12},{4,11},{5,10},{6,9},{7,8},{8,7},{9,6},... | collective-permute-start | bytes 61448 | tf_op jit(solution)/shard_map/ppermute | solution.py:145

commit v3 on v1

--- a/solution.py
+++ b/solution.py
@@ -61,76 +61,55 @@
 
 def attend_kernel(
     tokens,
-    query_sources,
-    key_sources,
+    query_rows,
+    key_rows,
     head_ref,
     arrived_ref,
     text_k_ref,
     text_v_ref,
     k_gain_ref,
     out_ref,
-    text_keys,
-    weights,
+    queries_ref,
+    keys_ref,
+    values_ref,
+    weights_ref,
+    result_ref,
 ):
     del head_ref
-    sources, rows, head_size = arrived_ref.shape
+    count, rows, head_size = arrived_ref.shape
     padded = rows - 2 * tokens
     factor = head_size ** (-0.5) * LOG2E
-    text_keys[...] = normalize(text_k_ref[...].astype(jnp.float32), k_gain_ref[...]).astype(
-        jnp.bfloat16
-    )
-    text = text_keys.shape[0]
-    query_rows = query_sources * padded
-    key_rows = key_sources * tokens
-
-    def keys_of(turn):
-        if turn == 0:
-            return text_keys[...]
-        first = (turn - 1) * key_sources
-        return arrived_ref[first : first + key_sources, :tokens].reshape(key_rows, head_size)
-
-    def values_of(turn):
-        if turn == 0:
-            rows_of = text_v_ref[...]
-        else:
-            first = (turn - 1) * key_sources
-            rows_of = arrived_ref[first : first + key_sources, tokens : 2 * tokens].reshape(
-                key_rows, head_size
-            )
-        return jnp.concatenate([rows_of, jnp.ones_like(rows_of)], axis=1)
-
-    turns = 1 + sources // key_sources
-
-    def columns_of(turn):
-        if turn == 0:
-            return slice(0, text)
-        return slice(text + (turn - 1) * key_rows, text + turn * key_rows)
+    text = text_k_ref.shape[0]
+    text_keys = normalize(text_k_ref[...].astype(jnp.float32), k_gain_ref[...])
+    keys_ref[:text] = text_keys.astype(jnp.bfloat16)
+    values_ref[:text, :head_size] = text_v_ref[...]
+    values_ref[:, head_size:] = jnp.ones((values_ref.shape[0], head_size), jnp.bfloat16)
+    for step in range(count):
+        first = text + step * tokens
+        keys_ref[first : first + tokens] = arrived_ref[step, :tokens]
+        values_ref[first : first + tokens, :head_size] = arrived_ref[step, tokens : 2 * tokens]
+        queries_ref[step * padded : (step + 1) * padded] = arrived_ref[step, 2 * tokens :]
 
     def add_queries(step, carry):
-        first = step * query_sources
-        queries = arrived_ref[pl.ds(first, query_sources), 2 * tokens :].reshape(
-            query_rows, head_size
-        )
-        for turn in range(turns):
+        mine = pl.ds(pl.multiple_of(step * query_rows, 16), query_rows)
+        queries = queries_ref[mine]
+        for first in range(0, keys_ref.shape[0], key_rows):
             scores = lax.dot_general(
                 queries,
-                keys_of(turn),
+                keys_ref[first : first + key_rows],
                 (((1,), (1,)), ((), ())),
                 preferred_element_type=jnp.float32,
             )
-            weights[:, columns_of(turn)] = jnp.exp2(scores * factor).astype(jnp.bfloat16)
-        sums = jnp.zeros((query_rows, 2 * head_size), jnp.float32)
-        for turn in range(turns):
-            sums = sums + jnp.dot(
-                weights[:, columns_of(turn)],
-                values_of(turn),
-                preferred_element_type=jnp.float32,
+            weights_ref[:, first : first + key_rows] = jnp.exp2(scores * factor).astype(
+                jnp.bfloat16
             )
-        result = (sums[:, :head_size] / sums[:, head_size:]).astype(jnp.bfloat16)
-        out_ref[pl.ds(first, query_sources)] = result.reshape(query_sources, padded, head_size)
+        sums = jnp.dot(weights_ref[...], values_ref[...], preferred_element_type=jnp.float32)
+        result_ref[mine] = (sums[:, :head_size] / sums[:, head_size:]).astype(jnp.bfloat16)
         return carry
 
-    lax.fori_loop(0, sources // query_sources, add_queries, 0)
+    lax.fori_loop(0, queries_ref.shape[0] // query_rows, add_queries, 0)
+    for step in range(count):
+        out_ref[step] = result_ref[step * padded : (step + 1) * padded]
 
 
 def finish_kernel(per_group, slots_ref, returned_ref, cache_ref, out_ref):
@@ -196,15 +175,15 @@
             pl.BlockSpec((1, head_size), lambda i: (0, 0)),
         ],
         out_specs=pl.BlockSpec((step_heads * groups, rows, head_size), lambda i: (i, 0, 0)),
-        compiler_params=pltpu.CompilerParams(vmem_limit_bytes=32 * 2**20),
         name="prepare",
     )(slots, qkv, k_cache, v_cache, q_gain, k_gain)
 
     arrived = lax.all_to_all(outgoing, "seq", split_axis=0, concat_axis=0, tiled=True)
 
-    query_sources = 4
+    query_rows = 4 * padded
+    all_keys = text + seq_count * tokens
     result = pl.pallas_call(
-        lambda *refs: attend_kernel(tokens, query_sources, 4, *refs),
+        lambda *refs: attend_kernel(tokens, query_rows, 256, *refs),
         out_shape=jax.ShapeDtypeStruct((seq_count, padded, head_size), jnp.bfloat16),
         grid_spec=pltpu.PrefetchScalarGridSpec(
             num_scalar_prefetch=1,
@@ -217,8 +196,11 @@
             ],
             out_specs=pl.BlockSpec((seq_count, padded, head_size), lambda i, head: (0, 0, 0)),
             scratch_shapes=[
-                pltpu.VMEM((text, head_size), jnp.bfloat16),
-                pltpu.VMEM((query_sources * padded, text + seq_count * tokens), jnp.bfloat16),
+                pltpu.VMEM((seq_count * padded, head_size), jnp.bfloat16),
+                pltpu.VMEM((all_keys, head_size), jnp.bfloat16),
+                pltpu.VMEM((all_keys, 2 * head_size), jnp.bfloat16),
+                pltpu.VMEM((query_rows, all_keys), jnp.bfloat16),
+                pltpu.VMEM((seq_count * padded, head_size), jnp.bfloat16),
             ],
         ),
         compiler_params=pltpu.CompilerParams(vmem_limit_bytes=40 * 2**20),
@@ -227,16 +209,17 @@
 
     returned = lax.all_to_all(result, "seq", split_axis=0, concat_axis=0, tiled=True)
 
+    finish_steps = 2
     return pl.pallas_call(
         lambda *refs: finish_kernel(per_group, *refs),
         out_shape=jax.ShapeDtypeStruct((tokens, row_width), attn_cache.dtype),
-        grid=(steps,),
+        grid=(finish_steps,),
         in_specs=[
             pl.BlockSpec((groups, padded), lambda i: (0, 0)),
-            pl.BlockSpec((step_heads * groups, padded, head_size), lambda i: (i, 0, 0)),
-            pl.BlockSpec((tokens, width), lambda i: (0, i)),
+            pl.BlockSpec((seq_count // finish_steps, padded, head_size), lambda i: (i, 0, 0)),
+            pl.BlockSpec((tokens, row_width // finish_steps), lambda i: (0, i)),
         ],
-        out_specs=pl.BlockSpec((tokens, width), lambda i: (0, i)),
+        out_specs=pl.BlockSpec((tokens, row_width // finish_steps), lambda i: (0, i)),
         compiler_params=pltpu.CompilerParams(vmem_limit_bytes=32 * 2**20),
         name="finish",
     )(padded_slots, returned, attn_cache)

time: 72.1 us -> 67.7 us (0.939)
  local copies, waits for them, and re-layouts: 6.31 us -> 1.06 us
  Pallas kernels: 9.85 us -> 10.7 us
    unnamed x22 -> x10, local copies, waits for them, and re-layouts: 6.31 us -> 1.06 us
    pallas_call x1, Pallas kernels: 2.54 us -> 4.29 us  [shards(): pl.pallas_call(lambda *refs: prepare_kernel(per_group, padded, *refs), ou...]
where the time goes in v3:
time: 67.7 us; the launch traced here: 67.2 us
  waiting for transfers between devices  39.6 us (58%)
  starting transfers between devices  15.8 us (23%)
  Pallas kernels  10.7 us (16%)
  local copies, waits for them, and re-layouts  1.06 us (2%)
    all_to_all x1, waiting for transfers between devices, shards(): lax.all_to_all(outgoing, 'seq', split_axis=0, concat_axis=0, tiled=True)  28.6 us
    all_to_all x1, waiting for transfers between devices, shards(): lax.all_to_all(result, 'seq', split_axis=0, concat_axis=0, tiled=True)  11.1 us
    all_to_all x1, starting transfers between devices, shards(): lax.all_to_all(result, 'seq', split_axis=0, concat_axis=0, tiled=True)  8.28 us
    all_to_all x1, starting transfers between devices, shards(): lax.all_to_all(outgoing, 'seq', split_axis=0, concat_axis=0, tiled=True)  7.53 us
    pallas_call x1, Pallas kernels, shards(): pl.pallas_call(lambda *refs: attend_kernel(tokens, query_rows, 256, *refs...  5.21 us
    pallas_call x1, Pallas kernels, shards(): pl.pallas_call(lambda *refs: prepare_kernel(per_group, padded, *refs), ou...  4.29 us
  transfers between devices with their start and end apart: 2, of which 2 were waited for; matrix products, arithmetic and copies ran while one was open for 0% of the time, Pallas kernels for 0%

profile of v3, /device:TPU:0, one launch (start us, length us, event | category | flops | bytes accessed | tf_op | source)
XLA Modules:
  0.0 67.2 jit_solution(4984364520901200956)
XLA Ops:
  0.0 4.3 %prepare.1 = bf16[16,336,128]{2,1,0:T(8,128)(2,1)} custom-call(s32[1,76]{1,0:T(1,128)} %bitcast.9, bf16[3,76,2048]{2,1,0:T(8,128)(2,1)} %bitcast.7, bf16[128,2048]{1,0:T(8,128)(2,1)} %refs_2_.3, bf16[128,2048]{1,0:T(8,128)(2,1)} %refs_3_.2, f32[1,128]{1,0:T(1,128)} %bitcast.8, f32[1,128]{1,0:T(1,128)} %bitcast.5), custom_call_target="tpu_custom_call" | custom-call | tf_op jit(solution)/shard_map/prepare/pallas_call | solution.py:165
  4.3 0.0 copy-start
  4.3 0.0 copy-start.1
  4.3 0.0 copy-start.3
  4.3 7.5 %all-to-all-start = ((bf16[16,336,128]{2,1,0:T(8,128)(2,1)}), bf16[16,336,128]{2,1,0:T(8,128)(2,1)S(1)}, u32[]{:S(2)}, u32[]{:S(2)}) async-start(bf16[16,336,128]{2,1,0:T(8,128)(2,1)} %prepare.1), calls=%async_computation | async-start | bytes 2752512 | tf_op jit(solution)/shard_map/all_to_all | solution.py:181
  11.8 28.6 %all-to-all-done.refs_1_ = bf16[16,336,128]{2,1,0:T(8,128)(2,1)S(1)} async-done(((bf16[16,336,128]{2,1,0:T(8,128)(2,1)}), bf16[16,336,128]{2,1,0:T(8,128)(2,1)S(1)}, u32[]{:S(2)}, u32[]{:S(2)}) %all-to-all-start) | async-done | bytes 1376288 | tf_op jit(solution)/shard_map/all_to_all | solution.py:181
  40.4 0.0 copy-done
  40.4 0.0 copy-done.1
  40.4 0.0 copy-done.3
  40.4 0.0 copy-start.4
  40.4 5.2 %attend.1 = bf16[16,80,128]{2,1,0:T(8,128)(2,1)} custom-call(s32[1]{0:T(128)} %bitcast.1.refs_0_, bf16[16,336,128]{2,1,0:T(8,128)(2,1)S(1)} %all-to-all-done.refs_1_, bf16[256,2048]{1,0:T(8,128)(2,1)S(1)} %copy-done, bf16[256,2048]{1,0:T(8,128)(2,1)S(1)} %copy-done.1, f32[1,128]{1,0:T(1,128)S(1)} %bitcast.6), custom_call_target="tpu_custom_call" | custom-call | tf_op jit(solution)/shard_map/attend/pallas_call | solution.py:185
  45.6 8.3 %all-to-all-start.1 = ((bf16[16,80,128]{2,1,0:T(8,128)(2,1)}), bf16[16,80,128]{2,1,0:T(8,128)(2,1)S(1)}, u32[]{:S(2)}, u32[]{:S(2)}) async-start(bf16[16,80,128]{2,1,0:T(8,128)(2,1)} %attend.1), calls=%async_computation.1 | async-start | bytes 655360 | tf_op jit(solution)/shard_map/all_to_all | solution.py:210
  53.9 0.0 copy-done.4
  53.9 11.1 %all-to-all-done.1.refs_1_ = bf16[16,80,128]{2,1,0:T(8,128)(2,1)S(1)} async-done(((bf16[16,80,128]{2,1,0:T(8,128)(2,1)}), bf16[16,80,128]{2,1,0:T(8,128)(2,1)S(1)}, u32[]{:S(2)}, u32[]{:S(2)}) %all-to-all-start.1) | async-done | bytes 327712 | tf_op jit(solution)/shard_map/all_to_all | solution.py:210
  65.0 0.0 copy-start.2
  65.0 1.0 %copy-done.2 = bf16[128,2048]{1,0:T(8,128)(2,1)S(1)} copy-done((bf16[128,2048]{1,0:T(8,128)(2,1)S(1)}, bf16[128,2048]{1,0:T(8,128)(2,1)}, u32[]{:S(2)}) %copy-start.2) | copy-done | bytes 524312
  66.1 1.2 %finish.1 = bf16[128,2048]{1,0:T(8,128)(2,1)} custom-call(s32[1,80]{1,0:T(1,128)S(1)} %pad.4.refs_0_, bf16[16,80,128]{2,1,0:T(8,128)(2,1)S(1)} %all-to-all-done.1.refs_1_, bf16[128,2048]{1,0:T(8,128)(2,1)S(1)} %copy-done.2), custom_call_target="tpu_custom_call" | custom-call | tf_op jit(solution)/shard_map/finish/pallas_call | solution.py:213
  (1 shorter events, 0.0 us)
Async XLA Ops:
  4.3 36.1 %copy-start = (bf16[256,2048]{1,0:T(8,128)(2,1)S(1)}, bf16[256,2048]{1,0:T(8,128)(2,1)}, u32[]{:S(2)}) copy-start(bf16[256,2048]{1,0:T(8,128)(2,1)} %refs_2_.4) | copy-start | bytes 3145732
  4.3 36.1 %copy-start.1 = (bf16[256,2048]{1,0:T(8,128)(2,1)S(1)}, bf16[256,2048]{1,0:T(8,128)(2,1)}, u32[]{:S(2)}) copy-start(bf16[256,2048]{1,0:T(8,128)(2,1)} %refs_3_.3) | copy-start | bytes 3145732
  4.3 36.1 %copy-start.3 = (f32[128]{0:T(128)S(1)}, f32[128]{0:T(128)}, u32[]{:S(2)}) copy-start(f32[128]{0:T(128)} %param.17) | copy-start | bytes 1540
  4.3 36.1 %all-to-all-start = ((bf16[16,336,128]{2,1,0:T(8,128)(2,1)}), bf16[16,336,128]{2,1,0:T(8,128)(2,1)S(1)}, u32[]{:S(2)}, u32[]{:S(2)}) async-start(bf16[16,336,128]{2,1,0:T(8,128)(2,1)} %prepare.1), calls=%async_computation | async-start | bytes 2752512 | tf_op jit(solution)/shard_map/all_to_all | solution.py:181
  40.4 13.5 %copy-start.4 = (s32[76]{0:T(128)S(1)}, s32[76]{0:T(128)}, u32[]{:S(2)}) copy-start(s32[76]{0:T(128)} %param.10) | copy-start | bytes 916
  45.6 19.4 %all-to-all-start.1 = ((bf16[16,80,128]{2,1,0:T(8,128)(2,1)}), bf16[16,80,128]{2,1,0:T(8,128)(2,1)S(1)}, u32[]{:S(2)}, u32[]{:S(2)}) async-start(bf16[16,80,128]{2,1,0:T(8,128)(2,1)} %attend.1), calls=%async_computation.1 | async-start | bytes 655360 | tf_op jit(solution)/shard_map/all_to_all | solution.py:210
  65.0 1.0 %copy-start.2 = (bf16[128,2048]{1,0:T(8,128)(2,1)S(1)}, bf16[128,2048]{1,0:T(8,128)(2,1)}, u32[]{:S(2)}) copy-start(bf16[128,2048]{1,0:T(8,128)(2,1)} %refs_2_.5) | copy-start | bytes 1572868

commit v4 on v2

--- a/solution.py
+++ b/solution.py
@@ -65,12 +65,12 @@
             out_ref[2 * tokens :] = queries_ref[group]
 
 
-def attend_kernel(tokens, query_rows, key_rows, count, me_ref, *rest):
-    del me_ref
+def attend_kernel(tokens, query_rows, key_rows, steps, me_ref, *rest):
+    me = me_ref[0]
+    count = len(steps)
     arrived = rest[:count]
     text_k_ref, text_v_ref, k_gain_ref = rest[count : count + 3]
-    outs = rest[count + 3 : 2 * count + 3]
-    queries_ref, keys_ref, values_ref, weights_ref, result_ref = rest[2 * count + 3 :]
+    out_ref, queries_ref, keys_ref, values_ref, weights_ref, result_ref = rest[count + 3 :]
     head_size = text_k_ref.shape[1]
     padded = arrived[0].shape[0] - 2 * tokens
     factor = head_size ** (-0.5) * LOG2E
@@ -104,31 +104,29 @@
 
     lax.fori_loop(0, queries_ref.shape[0] // query_rows, add_queries, 0)
     for step in range(count):
-        outs[step][...] = result_ref[step * padded : (step + 1) * padded]
-
-
-def finish_kernel(count, me_ref, slots_ref, cache_ref, *rest):
-    returned, out_ref = rest[:count], rest[count]
+        owner = lax.bitwise_xor(me, steps[step])
+        out_ref[owner] = result_ref[step * padded : (step + 1) * padded]
+
+
+def finish_kernel(per_group, slots_ref, returned_ref, cache_ref, out_ref):
     tokens = cache_ref.shape[0]
-    head_size = returned[0].shape[1]
+    head_size = returned_ref.shape[2]
     groups = slots_ref.shape[0]
-    me = me_ref[0]
-    one_hot = []
-    owned = jnp.zeros((tokens, 1), jnp.float32)
-    for low in range(groups):
-        group = lax.bitwise_xor(me % groups, low)
-        mine = place(slots_ref[pl.ds(group, 1)], tokens).astype(jnp.float32)
-        owned = owned + jnp.sum(mine, axis=1, keepdims=True)
-        one_hot.append(mine.astype(jnp.bfloat16))
-    is_fresh = owned > 0.5
-    for high in range(count // groups):
-        head = lax.bitwise_xor(me // groups, high)
-        columns = pl.ds(pl.multiple_of(head * head_size, head_size), head_size)
-        placed = jnp.zeros((tokens, head_size), jnp.float32)
-        for low in range(groups):
-            placed = placed + jnp.dot(
-                one_hot[low], returned[high * groups + low][...], preferred_element_type=jnp.float32
-            )
+    heads = cache_ref.shape[1] // head_size
+    mine = [place(slots_ref[group : group + 1], tokens) for group in range(groups)]
+    count = sum(jnp.sum(m.astype(jnp.float32), axis=1, keepdims=True) for m in mine)
+    is_fresh = count > 0.5
+    one_hot = [m.astype(jnp.bfloat16) for m in mine]
+    for head in range(heads):
+        columns = slice(head * head_size, (head + 1) * head_size)
+        placed = sum(
+            jnp.dot(
+                one_hot[group],
+                returned_ref[head * groups + group],
+                preferred_element_type=jnp.float32,
+            )
+            for group in range(groups)
+        )
         out_ref[:, columns] = jnp.where(
             is_fresh, placed, cache_ref[:, columns].astype(jnp.float32)
         ).astype(out_ref.dtype)
@@ -138,11 +136,24 @@
     return pl.BlockSpec(shape, lambda i, me: (0,) * len(shape))
 
 
-def exchange(blocks):
+def partners(count):
+    half = count // 2
+    order = []
+    for near in reversed(range(half)):
+        order.append(half + near)
+        if near > 0:
+            order.append(near)
+    order[1], order[2] = order[2], order[1]
+    names = sorted(range(count - 1), key=lambda number: str(number) if number else "")
+    return [0] + [order[names.index(number)] for number in range(count - 1)]
+
+
+def exchange(blocks, steps):
     count = len(blocks)
-    arrived = list(blocks)
-    for step in reversed(range(1, count)):
-        arrived[step] = lax.ppermute(blocks[step], "seq", [(a, a ^ step) for a in range(count)])
+    arrived = []
+    for step in steps:
+        pairs = [(a, a ^ step) for a in range(count)]
+        arrived.append(lax.ppermute(blocks[step], "seq", pairs) if step else blocks[0])
     return arrived
 
 
@@ -188,20 +199,21 @@
         name="prepare",
     )(me, slots, qkv, k_cache, v_cache, q_gain, k_gain)
 
-    arrived = exchange(outgoing)
+    steps = partners(seq_count)
+    arrived = exchange(outgoing, steps)
 
     query_rows = 4 * padded
     all_keys = text + seq_count * tokens
     result = pl.pallas_call(
-        lambda *refs: attend_kernel(tokens, query_rows, 256, seq_count, *refs),
-        out_shape=[jax.ShapeDtypeStruct((padded, head_size), jnp.bfloat16)] * seq_count,
+        lambda *refs: attend_kernel(tokens, query_rows, 256, steps, *refs),
+        out_shape=jax.ShapeDtypeStruct((seq_count, padded, head_size), jnp.bfloat16),
         grid_spec=pltpu.PrefetchScalarGridSpec(
             num_scalar_prefetch=1,
             grid=(1,),
             in_specs=[whole((rows, head_size))] * seq_count
             + [pl.BlockSpec((text, head_size), lambda i, me: (0, me[0] // groups))] * 2
             + [whole((1, head_size))],
-            out_specs=[whole((padded, head_size))] * seq_count,
+            out_specs=whole((seq_count, padded, head_size)),
             scratch_shapes=[
                 pltpu.VMEM((seq_count * padded, head_size), jnp.bfloat16),
                 pltpu.VMEM((all_keys, head_size), jnp.bfloat16),
@@ -214,21 +226,22 @@
         name="attend",
     )(me, *arrived, text_k, text_v, k_gain)
 
-    returned = exchange(result)
-
+    returned = lax.all_to_all(result, "seq", split_axis=0, concat_axis=0, tiled=True)
+
+    finish_steps = 1
     return pl.pallas_call(
-        lambda *refs: finish_kernel(seq_count, *refs),
+        lambda *refs: finish_kernel(per_group, *refs),
         out_shape=jax.ShapeDtypeStruct((tokens, row_width), attn_cache.dtype),
-        grid_spec=pltpu.PrefetchScalarGridSpec(
-            num_scalar_prefetch=1,
-            grid=(1,),
-            in_specs=[whole((groups, padded)), whole((tokens, row_width))]
-            + [whole((padded, head_size))] * seq_count,
-            out_specs=whole((tokens, row_width)),
-        ),
+        grid=(finish_steps,),
+        in_specs=[
+            pl.BlockSpec((groups, padded), lambda i: (0, 0)),
+            pl.BlockSpec((seq_count // finish_steps, padded, head_size), lambda i: (i, 0, 0)),
+            pl.BlockSpec((tokens, row_width // finish_steps), lambda i: (0, i)),
+        ],
+        out_specs=pl.BlockSpec((tokens, row_width // finish_steps), lambda i: (0, i)),
         compiler_params=pltpu.CompilerParams(vmem_limit_bytes=32 * 2**20),
         name="finish",
-    )(me, padded_slots, attn_cache, *returned)
+    )(padded_slots, returned, attn_cache)
 
 
 def solution(mesh):

time: 79.8 us -> 65.2 us (0.82)
  starting transfers between devices: 49.3 us -> 27.1 us
  waiting for transfers between devices: 18.8 us -> 25.7 us
    ppermute x30 -> x15, starting transfers between devices: 49.3 us -> 23.5 us  [exchange(): lax.ppermute(blocks[step], 'seq', pairs)]
    all_to_all x0 -> x1, waiting for transfers between devices: none -> 11 us  [shards(): lax.all_to_all(result, 'seq', split_axis=0, concat_axis=0, tiled=True)]
    ppermute x30 -> x15, waiting for transfers between devices: 18.8 us -> 14.7 us  [exchange(): lax.ppermute(blocks[step], 'seq', pairs)]
    all_to_all x0 -> x1, starting transfers between devices: none -> 3.67 us  [shards(): lax.all_to_all(result, 'seq', split_axis=0, concat_axis=0, tiled=True)]
  transfers between devices with their start and end apart: 30 -> 16, of which waited for: 7 -> 7; matrix products, arithmetic and copies ran while one was open for 0% -> 0% of each run, Pallas kernels for 0% -> 0%
where the time goes in v4:
time: 65.2 us; the launch traced here: 64.9 us
  starting transfers between devices  27.1 us (42%)
  waiting for transfers between devices  25.7 us (39%)
  Pallas kernels  9.86 us (15%)
  local copies, waits for them, and re-layouts  2.13 us (3%)
    ppermute x15, starting transfers between devices, exchange(): lax.ppermute(blocks[step], 'seq', pairs)  23.5 us
    ppermute x15, waiting for transfers between devices, exchange(): lax.ppermute(blocks[step], 'seq', pairs)  14.7 us
    all_to_all x1, waiting for transfers between devices, shards(): lax.all_to_all(result, 'seq', split_axis=0, concat_axis=0, tiled=True)  11 us
    pallas_call x1, Pallas kernels, shards(): pl.pallas_call(lambda *refs: attend_kernel(tokens, query_rows, 256, steps...  5.21 us
    all_to_all x1, starting transfers between devices, shards(): lax.all_to_all(result, 'seq', split_axis=0, concat_axis=0, tiled=True)  3.67 us
    pallas_call x1, Pallas kernels, shards(): pl.pallas_call(lambda *refs: prepare_kernel(per_group, padded, *refs), ou...  3.56 us
    unnamed x12, local copies, waits for them, and re-layouts  2.13 us
  transfers between devices with their start and end apart: 16, of which 7 were waited for; matrix products, arithmetic and copies ran while one was open for 0% of the time, Pallas kernels for 0%

profile of v4, /device:TPU:0, one launch (start us, length us, event | category | flops | bytes accessed | tf_op | source)
XLA Modules:
  0.0 64.9 jit_solution(3643011989665060975)
XLA Ops:
  0.0 0.0 copy-start
  0.0 3.6 %prepare.1 = (bf16[336,128]{1,0:T(8,128)(2,1)}, bf16[336,128]{1,0:T(8,128)(2,1)}, bf16[336,128]{1,0:T(8,128)(2,1)}, bf16[336,128]{1,0:T(8,128)(2,1)}, bf16[336,1...) custom-call(s32[1]{0:T(128)} %bitcast.1.refs_0_, ...), custom_call_target="tpu_custom_call" | custom-call | tf_op jit(solution)/shard_map/prepare/pallas_call | solution.py:182
  3.6 5.5 %collective-permute-start = (bf16[336,128]{1,0:T(8,128)(2,1)}, bf16[336,128]{1,0:T(8,128)(2,1)S(1)}, u32[]{:S(2)}, u32[]{:S(2)}) collective-permute-start(bf16[336,128]{1,0:T(8,128)(2,1)} %get-tuple-element.22), channel_id=1, source_target_pairs={{0,15},{1,14},{2,13},{3,12},{4,11},{5,10},{6,9},{7,8},{8,7},{9,6},... | collective-permute-start | bytes 258056 | tf_op jit(solution)/shard_map/ppermute | solution.py:156
  9.0 0.6 collective-permute-start.1
  9.7 0.3 collective-permute-start.10
  10.0 2.3 %collective-permute-start.11 = (bf16[336,128]{1,0:T(8,128)(2,1)}, bf16[336,128]{1,0:T(8,128)(2,1)S(1)}, u32[]{:S(2)}, u32[]{:S(2)}) collective-permute-start(bf16[336,128]{1,0:T(8,128)(2,1)} %get-tuple-element.33), channel_id=1, source_target_pairs={{0,6},{1,7},{2,4},{3,5},{4,2},{5,3},{6,0},{7,1},{8,14},{9,15},{10,... | collective-permute-start | bytes 258056 | tf_op jit(solution)/shard_map/ppermute | solution.py:156
  12.2 3.0 %collective-permute-start.12 = (bf16[336,128]{1,0:T(8,128)(2,1)}, bf16[336,128]{1,0:T(8,128)(2,1)S(1)}, u32[]{:S(2)}, u32[]{:S(2)}) collective-permute-start(bf16[336,128]{1,0:T(8,128)(2,1)} %get-tuple-element.34), channel_id=1, source_target_pairs={{0,13},{1,12},{2,15},{3,14},{4,9},{5,8},{6,11},{7,10},{8,5},{9,4},... | collective-permute-start | bytes 258056 | tf_op jit(solution)/shard_map/ppermute | solution.py:156
  15.2 0.0 collective-permute-done.refs_2_
  15.2 0.0 collective-permute-start.13
  15.2 2.2 %collective-permute-done.1.refs_3_ = bf16[336,128]{1,0:T(8,128)(2,1)S(1)} collective-permute-done((bf16[336,128]{1,0:T(8,128)(2,1)}, bf16[336,128]{1,0:T(8,128)(2,1)S(1)}, u32[]{:S(2)}, u32[]{:S(2)}) %collective-permute-start.1) | collective-permute-done | bytes 86048 | tf_op jit(solution)/shard_map/ppermute | solution.py:156
  17.4 1.0 %collective-permute-start.14 = (bf16[336,128]{1,0:T(8,128)(2,1)}, bf16[336,128]{1,0:T(8,128)(2,1)S(1)}, u32[]{:S(2)}, u32[]{:S(2)}) collective-permute-start(bf16[336,128]{1,0:T(8,128)(2,1)} %get-tuple-element.36), channel_id=1, source_target_pairs={{0,12},{1,13},{2,14},{3,15},{4,8},{5,9},{6,10},{7,11},{8,4},{9,5},... | collective-permute-start | bytes 258056 | tf_op jit(solution)/shard_map/ppermute | solution.py:156
  18.4 0.0 collective-permute-done.10.refs_12_
  18.4 2.6 %collective-permute-start.2 = (bf16[336,128]{1,0:T(8,128)(2,1)}, bf16[336,128]{1,0:T(8,128)(2,1)S(1)}, u32[]{:S(2)}, u32[]{:S(2)}) collective-permute-start(bf16[336,128]{1,0:T(8,128)(2,1)} %get-tuple-element.24), channel_id=1, source_target_pairs={{0,4},{1,5},{2,6},{3,7},{4,0},{5,1},{6,2},{7,3},{8,12},{9,13},{10,... | collective-permute-start | bytes 258056 | tf_op jit(solution)/shard_map/ppermute | solution.py:156
  21.0 0.0 collective-permute-done.11.refs_13_
  21.0 1.2 %collective-permute-start.3 = (bf16[336,128]{1,0:T(8,128)(2,1)}, bf16[336,128]{1,0:T(8,128)(2,1)S(1)}, u32[]{:S(2)}, u32[]{:S(2)}) collective-permute-start(bf16[336,128]{1,0:T(8,128)(2,1)} %get-tuple-element.25), channel_id=1, source_target_pairs={{0,11},{1,10},{2,9},{3,8},{4,15},{5,14},{6,13},{7,12},{8,3},{9,2},... | collective-permute-start | bytes 258056 | tf_op jit(solution)/shard_map/ppermute | solution.py:156
  22.3 0.8 %collective-permute-done.12.refs_14_ = bf16[336,128]{1,0:T(8,128)(2,1)S(1)} collective-permute-done((bf16[336,128]{1,0:T(8,128)(2,1)}, bf16[336,128]{1,0:T(8,128)(2,1)S(1)}, u32[]{:S(2)}, u32[]{:S(2)}) %collective-permute-start.12) | collective-permute-done | bytes 86048 | tf_op jit(solution)/shard_map/ppermute | solution.py:156
  23.1 1.2 %collective-permute-start.4 = (bf16[336,128]{1,0:T(8,128)(2,1)}, bf16[336,128]{1,0:T(8,128)(2,1)S(1)}, u32[]{:S(2)}, u32[]{:S(2)}) collective-permute-start(bf16[336,128]{1,0:T(8,128)(2,1)} %get-tuple-element.26), channel_id=1, source_target_pairs={{0,3},{1,2},{2,1},{3,0},{4,7},{5,6},{6,5},{7,4},{8,11},{9,10},{10,... | collective-permute-start | bytes 258056 | tf_op jit(solution)/shard_map/ppermute | solution.py:156
  24.3 0.0 collective-permute-done.13.refs_15_
  24.3 2.1 %collective-permute-start.5 = (bf16[336,128]{1,0:T(8,128)(2,1)}, bf16[336,128]{1,0:T(8,128)(2,1)S(1)}, u32[]{:S(2)}, u32[]{:S(2)}) collective-permute-start(bf16[336,128]{1,0:T(8,128)(2,1)} %get-tuple-element.27), channel_id=1, source_target_pairs={{0,10},{1,11},{2,8},{3,9},{4,14},{5,15},{6,12},{7,13},{8,2},{9,3},... | collective-permute-start | bytes 258056 | tf_op jit(solution)/shard_map/ppermute | solution.py:156
  26.4 0.9 %collective-permute-done.14.refs_16_ = bf16[336,128]{1,0:T(8,128)(2,1)S(1)} collective-permute-done((bf16[336,128]{1,0:T(8,128)(2,1)}, bf16[336,128]{1,0:T(8,128)(2,1)S(1)}, u32[]{:S(2)}, u32[]{:S(2)}) %collective-permute-start.14) | collective-permute-done | bytes 86048 | tf_op jit(solution)/shard_map/ppermute | solution.py:156
  27.3 1.3 %collective-permute-start.6 = (bf16[336,128]{1,0:T(8,128)(2,1)}, bf16[336,128]{1,0:T(8,128)(2,1)S(1)}, u32[]{:S(2)}, u32[]{:S(2)}) collective-permute-start(bf16[336,128]{1,0:T(8,128)(2,1)} %get-tuple-element.28), channel_id=1, source_target_pairs={{0,2},{1,3},{2,0},{3,1},{4,6},{5,7},{6,4},{7,5},{8,10},{9,11},{10,... | collective-permute-start | bytes 258056 | tf_op jit(solution)/shard_map/ppermute | solution.py:156
  28.6 0.0 collective-permute-done.2.refs_4_
  28.6 0.5 collective-permute-start.7
  29.1 0.7 %collective-permute-done.3.refs_5_ = bf16[336,128]{1,0:T(8,128)(2,1)S(1)} collective-permute-done((bf16[336,128]{1,0:T(8,128)(2,1)}, bf16[336,128]{1,0:T(8,128)(2,1)S(1)}, u32[]{:S(2)}, u32[]{:S(2)}) %collective-permute-start.3) | collective-permute-done | bytes 86048 | tf_op jit(solution)/shard_map/ppermute | solution.py:156
  29.8 0.1 collective-permute-start.8
  29.8 0.0 collective-permute-done.4.refs_6_
  29.8 0.0 copy-start.4
  29.8 1.8 %collective-permute-start.9 = (bf16[336,128]{1,0:T(8,128)(2,1)}, bf16[336,128]{1,0:T(8,128)(2,1)S(1)}, u32[]{:S(2)}, u32[]{:S(2)}) collective-permute-start(bf16[336,128]{1,0:T(8,128)(2,1)} %get-tuple-element.31), channel_id=1, source_target_pairs={{0,8},{1,9},{2,10},{3,11},{4,12},{5,13},{6,14},{7,15},{8,0},{9,1},... | collective-permute-start | bytes 258056 | tf_op jit(solution)/shard_map/ppermute | solution.py:156
  31.6 7.2 %collective-permute-done.5.refs_7_ = bf16[336,128]{1,0:T(8,128)(2,1)S(1)} collective-permute-done((bf16[336,128]{1,0:T(8,128)(2,1)}, bf16[336,128]{1,0:T(8,128)(2,1)S(1)}, u32[]{:S(2)}, u32[]{:S(2)}) %collective-permute-start.5) | collective-permute-done | bytes 86048 | tf_op jit(solution)/shard_map/ppermute | solution.py:156
  38.8 0.0 collective-permute-done.6.refs_8_
  38.8 0.0 collective-permute-done.7.refs_9_
  38.8 0.0 collective-permute-done.8.refs_10_
  38.8 2.9 %collective-permute-done.9.refs_11_ = bf16[336,128]{1,0:T(8,128)(2,1)S(1)} collective-permute-done((bf16[336,128]{1,0:T(8,128)(2,1)}, bf16[336,128]{1,0:T(8,128)(2,1)S(1)}, u32[]{:S(2)}, u32[]{:S(2)}) %collective-permute-start.9) | collective-permute-done | bytes 86048 | tf_op jit(solution)/shard_map/ppermute | solution.py:156
  41.7 0.0 copy-done
  41.7 0.0 copy-done.4
  41.7 0.0 copy-start.1
  41.7 1.2 %copy-done.1 = bf16[256,2048]{1,0:T(8,128)(2,1)S(1)} copy-done((bf16[256,2048]{1,0:T(8,128)(2,1)S(1)}, bf16[256,2048]{1,0:T(8,128)(2,1)}, u32[]{:S(2)}) %copy-start.1) | copy-done | bytes 1048600
  43.0 0.0 copy-start.3
  43.0 0.9 %copy-done.3 = bf16[336,128]{1,0:T(8,128)(2,1)S(1)} copy-done((bf16[336,128]{1,0:T(8,128)(2,1)S(1)}, bf16[336,128]{1,0:T(8,128)(2,1)}, u32[]{:S(2)}) %copy-start.3) | copy-done | bytes 86040
  43.9 5.2 %attend.1 = bf16[16,80,128]{2,1,0:T(8,128)(2,1)} custom-call(s32[1]{0:T(128)} %bitcast.1.refs_0_, bf16[336,128]{1,0:T(8,128)(2,1)S(1)} %copy-done.3, bf16[336,128]{1,0:T(8,128)(2,1)S(1)} %collective-permute-done.refs_2_, bf16[336,128]{1,0:T(8,128)(2,1)S(1)} %collective-permute-done.1.refs_3_, bf16[336,128]{1,0:T(8,128)(2,1)S(1)} %collective-permute-done.2.refs_4_, ...), custom_call_target="tpu_custom_call" | custom-call | tf_op jit(solution)/shard_map/attend/pallas_call | solution.py:207
  49.1 0.0 copy-start.5
  49.1 0.0 copy-start.2
  49.1 3.7 %all-to-all-start = ((bf16[16,80,128]{2,1,0:T(8,128)(2,1)}), bf16[16,80,128]{2,1,0:T(8,128)(2,1)S(1)}, u32[]{:S(2)}, u32[]{:S(2)}) async-start(bf16[16,80,128]{2,1,0:T(8,128)(2,1)} %attend.1), calls=%async_computation | async-start | bytes 655360 | tf_op jit(solution)/shard_map/all_to_all | solution.py:229
  52.8 0.0 copy-done.5
  52.8 11.0 %all-to-all-done.refs_1_ = bf16[16,80,128]{2,1,0:T(8,128)(2,1)S(1)} async-done(((bf16[16,80,128]{2,1,0:T(8,128)(2,1)}), bf16[16,80,128]{2,1,0:T(8,128)(2,1)S(1)}, u32[]{:S(2)}, u32[]{:S(2)}) %all-to-all-start) | async-done | bytes 327712 | tf_op jit(solution)/shard_map/all_to_all | solution.py:229
  63.8 0.0 copy-done.2
  63.8 1.1 %finish.1 = bf16[128,2048]{1,0:T(8,128)(2,1)} custom-call(s32[1,80]{1,0:T(1,128)S(1)} %pad.4.refs_0_, bf16[16,80,128]{2,1,0:T(8,128)(2,1)S(1)} %all-to-all-done.refs_1_, bf16[128,2048]{1,0:T(8,128)(2,1)S(1)} %copy-done.2), custom_call_target="tpu_custom_call" | custom-call | tf_op jit(solution)/shard_map/finish/pallas_call | solution.py:232
  (1 shorter events, 0.0 us)
Async XLA Ops:
  0.0 41.7 %copy-start = (bf16[256,2048]{1,0:T(8,128)(2,1)S(1)}, bf16[256,2048]{1,0:T(8,128)(2,1)}, u32[]{:S(2)}) copy-start(bf16[256,2048]{1,0:T(8,128)(2,1)} %refs_17_.1) | copy-start | bytes 3145732
  3.6 11.7 %collective-permute-start = (bf16[336,128]{1,0:T(8,128)(2,1)}, bf16[336,128]{1,0:T(8,128)(2,1)S(1)}, u32[]{:S(2)}, u32[]{:S(2)}) collective-permute-start(bf16[336,128]{1,0:T(8,128)(2,1)} %get-tuple-element.22), channel_id=1, source_target_pairs={{0,15},{1,14},{2,13},{3,12},{4,11},{5,10},{6,9},{7,8},{8,7},{9,6},... | collective-permute-start | bytes 258056 | tf_op jit(solution)/shard_map/ppermute | solution.py:156
  9.0 8.4 %collective-permute-start.1 = (bf16[336,128]{1,0:T(8,128)(2,1)}, bf16[336,128]{1,0:T(8,128)(2,1)S(1)}, u32[]{:S(2)}, u32[]{:S(2)}) collective-permute-start(bf16[336,128]{1,0:T(8,128)(2,1)} %get-tuple-element.23), channel_id=1, source_target_pairs={{0,14},{1,15},{2,12},{3,13},{4,10},{5,11},{6,8},{7,9},{8,6},{9,7},... | collective-permute-start | bytes 258056 | tf_op jit(solution)/shard_map/ppermute | solution.py:156
  9.7 8.7 %collective-permute-start.10 = (bf16[336,128]{1,0:T(8,128)(2,1)}, bf16[336,128]{1,0:T(8,128)(2,1)S(1)}, u32[]{:S(2)}, u32[]{:S(2)}) collective-permute-start(bf16[336,128]{1,0:T(8,128)(2,1)} %get-tuple-element.32), channel_id=1, source_target_pairs={{0,7},{1,6},{2,5},{3,4},{4,3},{5,2},{6,1},{7,0},{8,15},{9,14},{10,... | collective-permute-start | bytes 258056 | tf_op jit(solution)/shard_map/ppermute | solution.py:156
  10.0 11.1 %collective-permute-start.11 = (bf16[336,128]{1,0:T(8,128)(2,1)}, bf16[336,128]{1,0:T(8,128)(2,1)S(1)}, u32[]{:S(2)}, u32[]{:S(2)}) collective-permute-start(bf16[336,128]{1,0:T(8,128)(2,1)} %get-tuple-element.33), channel_id=1, source_target_pairs={{0,6},{1,7},{2,4},{3,5},{4,2},{5,3},{6,0},{7,1},{8,14},{9,15},{10,... | collective-permute-start | bytes 258056 | tf_op jit(solution)/shard_map/ppermute | solution.py:156
  12.2 10.9 %collective-permute-start.12 = (bf16[336,128]{1,0:T(8,128)(2,1)}, bf16[336,128]{1,0:T(8,128)(2,1)S(1)}, u32[]{:S(2)}, u32[]{:S(2)}) collective-permute-start(bf16[336,128]{1,0:T(8,128)(2,1)} %get-tuple-element.34), channel_id=1, source_target_pairs={{0,13},{1,12},{2,15},{3,14},{4,9},{5,8},{6,11},{7,10},{8,5},{9,4},... | collective-permute-start | bytes 258056 | tf_op jit(solution)/shard_map/ppermute | solution.py:156
  15.2 9.0 %collective-permute-start.13 = (bf16[336,128]{1,0:T(8,128)(2,1)}, bf16[336,128]{1,0:T(8,128)(2,1)S(1)}, u32[]{:S(2)}, u32[]{:S(2)}) collective-permute-start(bf16[336,128]{1,0:T(8,128)(2,1)} %get-tuple-element.35), channel_id=1, source_target_pairs={{0,5},{1,4},{2,7},{3,6},{4,1},{5,0},{6,3},{7,2},{8,13},{9,12},{10,... | collective-permute-start | bytes 258056 | tf_op jit(solution)/shard_map/ppermute | solution.py:156
  17.4 9.9 %collective-permute-start.14 = (bf16[336,128]{1,0:T(8,128)(2,1)}, bf16[336,128]{1,0:T(8,128)(2,1)S(1)}, u32[]{:S(2)}, u32[]{:S(2)}) collective-permute-start(bf16[336,128]{1,0:T(8,128)(2,1)} %get-tuple-element.36), channel_id=1, source_target_pairs={{0,12},{1,13},{2,14},{3,15},{4,8},{5,9},{6,10},{7,11},{8,4},{9,5},... | collective-permute-start | bytes 258056 | tf_op jit(solution)/shard_map/ppermute | solution.py:156
  18.4 10.2 %collective-permute-start.2 = (bf16[336,128]{1,0:T(8,128)(2,1)}, bf16[336,128]{1,0:T(8,128)(2,1)S(1)}, u32[]{:S(2)}, u32[]{:S(2)}) collective-permute-start(bf16[336,128]{1,0:T(8,128)(2,1)} %get-tuple-element.24), channel_id=1, source_target_pairs={{0,4},{1,5},{2,6},{3,7},{4,0},{5,1},{6,2},{7,3},{8,12},{9,13},{10,... | collective-permute-start | bytes 258056 | tf_op jit(solution)/shard_map/ppermute | solution.py:156
  21.0 8.7 %collective-permute-start.3 = (bf16[336,128]{1,0:T(8,128)(2,1)}, bf16[336,128]{1,0:T(8,128)(2,1)S(1)}, u32[]{:S(2)}, u32[]{:S(2)}) collective-permute-start(bf16[336,128]{1,0:T(8,128)(2,1)} %get-tuple-element.25), channel_id=1, source_target_pairs={{0,11},{1,10},{2,9},{3,8},{4,15},{5,14},{6,13},{7,12},{8,3},{9,2},... | collective-permute-start | bytes 258056 | tf_op jit(solution)/shard_map/ppermute | solution.py:156
  23.1 6.7 %collective-permute-start.4 = (bf16[336,128]{1,0:T(8,128)(2,1)}, bf16[336,128]{1,0:T(8,128)(2,1)S(1)}, u32[]{:S(2)}, u32[]{:S(2)}) collective-permute-start(bf16[336,128]{1,0:T(8,128)(2,1)} %get-tuple-element.26), channel_id=1, source_target_pairs={{0,3},{1,2},{2,1},{3,0},{4,7},{5,6},{6,5},{7,4},{8,11},{9,10},{10,... | collective-permute-start | bytes 258056 | tf_op jit(solution)/shard_map/ppermute | solution.py:156
  24.3 14.6 %collective-permute-start.5 = (bf16[336,128]{1,0:T(8,128)(2,1)}, bf16[336,128]{1,0:T(8,128)(2,1)S(1)}, u32[]{:S(2)}, u32[]{:S(2)}) collective-permute-start(bf16[336,128]{1,0:T(8,128)(2,1)} %get-tuple-element.27), channel_id=1, source_target_pairs={{0,10},{1,11},{2,8},{3,9},{4,14},{5,15},{6,12},{7,13},{8,2},{9,3},... | collective-permute-start | bytes 258056 | tf_op jit(solution)/shard_map/ppermute | solution.py:156
  27.3 11.5 %collective-permute-start.6 = (bf16[336,128]{1,0:T(8,128)(2,1)}, bf16[336,128]{1,0:T(8,128)(2,1)S(1)}, u32[]{:S(2)}, u32[]{:S(2)}) collective-permute-start(bf16[336,128]{1,0:T(8,128)(2,1)} %get-tuple-element.28), channel_id=1, source_target_pairs={{0,2},{1,3},{2,0},{3,1},{4,6},{5,7},{6,4},{7,5},{8,10},{9,11},{10,... | collective-permute-start | bytes 258056 | tf_op jit(solution)/shard_map/ppermute | solution.py:156
  28.6 10.2 %collective-permute-start.7 = (bf16[336,128]{1,0:T(8,128)(2,1)}, bf16[336,128]{1,0:T(8,128)(2,1)S(1)}, u32[]{:S(2)}, u32[]{:S(2)}) collective-permute-start(bf16[336,128]{1,0:T(8,128)(2,1)} %get-tuple-element.29), channel_id=1, source_target_pairs={{0,9},{1,8},{2,11},{3,10},{4,13},{5,12},{6,15},{7,14},{8,1},{9,0},... | collective-permute-start | bytes 258056 | tf_op jit(solution)/shard_map/ppermute | solution.py:156
  29.8 9.1 %collective-permute-start.8 = (bf16[336,128]{1,0:T(8,128)(2,1)}, bf16[336,128]{1,0:T(8,128)(2,1)S(1)}, u32[]{:S(2)}, u32[]{:S(2)}) collective-permute-start(bf16[336,128]{1,0:T(8,128)(2,1)} %get-tuple-element.30), channel_id=1, source_target_pairs={{0,1},{1,0},{2,3},{3,2},{4,5},{5,4},{6,7},{7,6},{8,9},{9,8},{10,11... | collective-permute-start | bytes 258056 | tf_op jit(solution)/shard_map/ppermute | solution.py:156
  29.8 11.9 %copy-start.4 = (f32[128]{0:T(128)S(1)}, f32[128]{0:T(128)}, u32[]{:S(2)}) copy-start(f32[128]{0:T(128)} %param.17) | copy-start | bytes 1540
  29.8 11.9 %collective-permute-start.9 = (bf16[336,128]{1,0:T(8,128)(2,1)}, bf16[336,128]{1,0:T(8,128)(2,1)S(1)}, u32[]{:S(2)}, u32[]{:S(2)}) collective-permute-start(bf16[336,128]{1,0:T(8,128)(2,1)} %get-tuple-element.31), channel_id=1, source_target_pairs={{0,8},{1,9},{2,10},{3,11},{4,12},{5,13},{6,14},{7,15},{8,0},{9,1},... | collective-permute-start | bytes 258056 | tf_op jit(solution)/shard_map/ppermute | solution.py:156
  41.7 1.2 %copy-start.1 = (bf16[256,2048]{1,0:T(8,128)(2,1)S(1)}, bf16[256,2048]{1,0:T(8,128)(2,1)}, u32[]{:S(2)}) copy-start(bf16[256,2048]{1,0:T(8,128)(2,1)} %refs_18_.1) | copy-start | bytes 3145732
  43.0 0.9 %copy-start.3 = (bf16[336,128]{1,0:T(8,128)(2,1)S(1)}, bf16[336,128]{1,0:T(8,128)(2,1)}, u32[]{:S(2)}) copy-start(bf16[336,128]{1,0:T(8,128)(2,1)} %get-tuple-element.21.refs_1_) | copy-start | bytes 258052
  49.1 3.7 %copy-start.5 = (s32[76]{0:T(128)S(1)}, s32[76]{0:T(128)}, u32[]{:S(2)}) copy-start(s32[76]{0:T(128)} %param.10) | copy-start | bytes 916
  49.1 14.7 %copy-start.2 = (bf16[128,2048]{1,0:T(8,128)(2,1)S(1)}, bf16[128,2048]{1,0:T(8,128)(2,1)}, u32[]{:S(2)}) copy-start(bf16[128,2048]{1,0:T(8,128)(2,1)} %refs_2_.1) | copy-start | bytes 1572868
  49.1 14.7 %all-to-all-start = ((bf16[16,80,128]{2,1,0:T(8,128)(2,1)}), bf16[16,80,128]{2,1,0:T(8,128)(2,1)S(1)}, u32[]{:S(2)}, u32[]{:S(2)}) async-start(bf16[16,80,128]{2,1,0:T(8,128)(2,1)} %attend.1), calls=%async_computation | async-start | bytes 655360 | tf_op jit(solution)/shard_map/all_to_all | solution.py:229

commit v5 on v4

--- a/solution.py
+++ b/solution.py
@@ -8,6 +8,7 @@
 from jax.sharding import PartitionSpec as P
 
 LOG2E = math.log2(math.e)
+FIRST_HEADS = [15, 14, 13, 1]
 
 
 def round_up(count, step):
@@ -24,33 +25,46 @@
     return owner == slots
 
 
-def prepare_kernel(
-    per_group, padded, me_ref, slots_ref, qkv_ref, k_ref, v_ref, q_gain_ref, k_gain_ref, *rest
-):
-    outs, queries_ref = rest[:-1], rest[-1]
-    tokens = k_ref.shape[0]
+def prepare_kernel(per_group, padded, highs, by_head, me_ref, slots_ref, q_gain_ref, k_gain_ref, *rest):
+    tokens = 0
+    if by_head:
+        groups = slots_ref.shape[1] // per_group
+        loads = [rest[3 * turn : 3 * turn + 3] for turn in range(len(highs))]
+        outs = rest[3 * len(highs) : 3 * len(highs) + groups * len(highs)]
+        queries_ref = rest[-1]
+        tokens = loads[0][1].shape[0]
+    else:
+        groups = slots_ref.shape[1] // per_group
+        qkv_ref, k_ref, v_ref, text_k_ref, text_v_ref = rest[:5]
+        rest = rest[6:]
+        outs = rest[: groups * len(highs)]
+        text_keys_ref, text_values_ref, queries_ref = rest[groups * len(highs) :]
+        tokens = k_ref.shape[0]
     head_size = q_gain_ref.shape[1]
-    groups = qkv_ref.shape[1] // per_group
+    me = me_ref[0]
     mine = place(slots_ref[...], tokens)
     is_fresh = jnp.max(mine.astype(jnp.float32), axis=1, keepdims=True) > 0.5
     one_hot = mine.astype(jnp.bfloat16)
     q_gain = q_gain_ref[...]
     k_gain = k_gain_ref[...]
-    me = me_ref[0]
-
-    for high in range(len(outs) // groups):
-        head = lax.bitwise_xor(me // groups, high)
-        columns = pl.ds(pl.multiple_of(head * head_size, head_size), head_size)
-
-        def merged(part, cache_ref):
-            spread = jnp.dot(
-                one_hot, qkv_ref[part, :, columns], preferred_element_type=jnp.float32
-            )
-            return jnp.where(is_fresh, spread, cache_ref[:, columns].astype(jnp.float32))
-
-        keys = normalize(merged(1, k_ref), k_gain).astype(jnp.bfloat16)
-        values = merged(2, v_ref).astype(jnp.bfloat16)
-        queries = normalize(qkv_ref[0, :, columns].astype(jnp.float32), q_gain)
+
+    def merged(fresh, cache):
+        spread = jnp.dot(one_hot, fresh, preferred_element_type=jnp.float32)
+        return jnp.where(is_fresh, spread, cache.astype(jnp.float32))
+
+    for turn, high in enumerate(highs):
+        if by_head:
+            fresh_ref, cache_k_ref, cache_v_ref = loads[turn]
+            fresh = [fresh_ref[part] for part in range(3)]
+            cache_k, cache_v = cache_k_ref[...], cache_v_ref[...]
+        else:
+            head = lax.bitwise_xor(me // groups, high)
+            columns = pl.ds(pl.multiple_of(head * head_size, head_size), head_size)
+            fresh = [qkv_ref[part, :, columns] for part in range(3)]
+            cache_k, cache_v = k_ref[:, columns], v_ref[:, columns]
+        keys = normalize(merged(fresh[1], cache_k), k_gain).astype(jnp.bfloat16)
+        values = merged(fresh[2], cache_v).astype(jnp.bfloat16)
+        queries = normalize(fresh[0].astype(jnp.float32), q_gain)
         empty = jnp.zeros((padded - per_group, head_size), jnp.float32)
         for group in range(groups):
             share = queries[group * per_group : (group + 1) * per_group]
@@ -58,26 +72,29 @@
                 share = jnp.concatenate([share, empty], axis=0)
             queries_ref[group] = share.astype(jnp.bfloat16)
         for low in range(groups):
-            out_ref = outs[high * groups + low]
+            out_ref = outs[turn * groups + low]
             group = lax.bitwise_xor(me % groups, low)
             out_ref[:tokens] = keys
             out_ref[tokens : 2 * tokens] = values
             out_ref[2 * tokens :] = queries_ref[group]
+    if not by_head:
+        text_keys = normalize(text_k_ref[...].astype(jnp.float32), k_gain)
+        text_keys_ref[...] = text_keys.astype(jnp.bfloat16)
+        text_values_ref[...] = text_v_ref[...]
 
 
 def attend_kernel(tokens, query_rows, key_rows, steps, me_ref, *rest):
     me = me_ref[0]
     count = len(steps)
     arrived = rest[:count]
-    text_k_ref, text_v_ref, k_gain_ref = rest[count : count + 3]
-    out_ref, queries_ref, keys_ref, values_ref, weights_ref, result_ref = rest[count + 3 :]
-    head_size = text_k_ref.shape[1]
+    text_keys_ref, text_values_ref = rest[count : count + 2]
+    out_ref, queries_ref, keys_ref, values_ref, weights_ref, result_ref = rest[count + 2 :]
+    head_size = text_keys_ref.shape[1]
     padded = arrived[0].shape[0] - 2 * tokens
     factor = head_size ** (-0.5) * LOG2E
-    text = text_k_ref.shape[0]
-    text_keys = normalize(text_k_ref[...].astype(jnp.float32), k_gain_ref[...])
-    keys_ref[:text] = text_keys.astype(jnp.bfloat16)
-    values_ref[:text, :head_size] = text_v_ref[...]
+    text = text_keys_ref.shape[0]
+    keys_ref[:text] = text_keys_ref[...]
+    values_ref[:text, :head_size] = text_values_ref[...]
     values_ref[:, head_size:] = jnp.ones((values_ref.shape[0], head_size), jnp.bfloat16)
     for step in range(count):
         first = text + step * tokens
@@ -138,23 +155,20 @@
 
 def partners(count):
     half = count // 2
-    order = []
-    for near in reversed(range(half)):
-        order.append(half + near)
-        if near > 0:
-            order.append(near)
-    order[1], order[2] = order[2], order[1]
+    far = list(reversed(range(half, count)))
+    near = list(reversed(range(1, half)))
+    order = far[:3]
+    for turn in range(max(len(far) - 3, len(near))):
+        order += near[turn : turn + 1] + far[turn + 3 : turn + 4]
     names = sorted(range(count - 1), key=lambda number: str(number) if number else "")
     return [0] + [order[names.index(number)] for number in range(count - 1)]
 
 
-def exchange(blocks, steps):
-    count = len(blocks)
-    arrived = []
-    for step in steps:
-        pairs = [(a, a ^ step) for a in range(count)]
-        arrived.append(lax.ppermute(blocks[step], "seq", pairs) if step else blocks[0])
-    return arrived
+def trade(block, step):
+    if step == 0:
+        return block
+    count = lax.axis_size("seq")
+    return lax.ppermute(block, "seq", [(a, a ^ step) for a in range(count)])
 
 
 def shards(fresh_qkv, slot_rows, k_cache, v_cache, attn_cache, text_k, text_v, q_gain, k_gain):
@@ -179,28 +193,67 @@
         constant_values=tokens,
     )
 
-    outgoing = pl.pallas_call(
-        lambda *refs: prepare_kernel(per_group, padded, *refs),
-        out_shape=[jax.ShapeDtypeStruct((rows, head_size), jnp.bfloat16)] * seq_count,
+    steps = partners(seq_count)
+    block = jax.ShapeDtypeStruct((rows, head_size), jnp.bfloat16)
+    text_block = jax.ShapeDtypeStruct((text, head_size), jnp.bfloat16)
+    scratch = [pltpu.VMEM((groups, padded, head_size), jnp.bfloat16)]
+    common = [whole((1, slot_count)), whole((1, head_size)), whole((1, head_size))]
+    early = FIRST_HEADS
+    late = [high for high in reversed(range(head_count)) if high not in early]
+
+    def head_specs(high):
+        def column(me):
+            return lax.bitwise_xor(me[0] // groups, high)
+
+        return [
+            pl.BlockSpec((3, slot_count, head_size), lambda i, me: (0, 0, column(me))),
+            pl.BlockSpec((tokens, head_size), lambda i, me: (0, column(me))),
+            pl.BlockSpec((tokens, head_size), lambda i, me: (0, column(me))),
+        ]
+
+    first = pl.pallas_call(
+        lambda *refs: prepare_kernel(per_group, padded, early, True, *refs),
+        out_shape=[block] * (groups * len(early)),
         grid_spec=pltpu.PrefetchScalarGridSpec(
             num_scalar_prefetch=1,
             grid=(1,),
-            in_specs=[
-                whole((1, slot_count)),
+            in_specs=common + [spec for high in early for spec in head_specs(high)],
+            out_specs=[whole((rows, head_size))] * (groups * len(early)),
+            scratch_shapes=scratch,
+        ),
+        name="prepare_first",
+    )(me, slots, q_gain, k_gain, *([qkv, k_cache, v_cache] * len(early)))
+    met = {}
+    for turn, made in enumerate(first):
+        step = early[turn // groups] * groups + turn % groups
+        met[step] = trade(made, step)
+    text_spec = pl.BlockSpec((text, head_size), lambda i, me: (0, me[0] // groups))
+    *second, text_keys, text_values = pl.pallas_call(
+        lambda *refs: prepare_kernel(per_group, padded, late, False, *refs),
+        out_shape=[block] * (groups * len(late)) + [text_block] * 2,
+        grid_spec=pltpu.PrefetchScalarGridSpec(
+            num_scalar_prefetch=1,
+            grid=(1,),
+            in_specs=common
+            + [
                 whole((3, slot_count, row_width)),
                 whole((tokens, row_width)),
                 whole((tokens, row_width)),
-                whole((1, head_size)),
-                whole((1, head_size)),
+                text_spec,
+                text_spec,
+                pl.BlockSpec(memory_space=pl.ANY),
             ],
-            out_specs=[whole((rows, head_size))] * seq_count,
-            scratch_shapes=[pltpu.VMEM((groups, padded, head_size), jnp.bfloat16)],
+            out_specs=[whole((rows, head_size))] * (groups * len(late))
+            + [whole((text, head_size))] * 2,
+            scratch_shapes=scratch,
         ),
-        name="prepare",
-    )(me, slots, qkv, k_cache, v_cache, q_gain, k_gain)
-
-    steps = partners(seq_count)
-    arrived = exchange(outgoing, steps)
+        name="prepare_rest",
+    )(me, slots, q_gain, k_gain, qkv, k_cache, v_cache, text_k, text_v, met[groups])
+    arrived = dict(met)
+    for turn, made in enumerate(second):
+        step = late[turn // groups] * groups + turn % groups
+        arrived[step] = trade(made, step)
+    arrived = [arrived[step] for step in steps]
 
     query_rows = 4 * padded
     all_keys = text + seq_count * tokens
@@ -211,8 +264,7 @@
             num_scalar_prefetch=1,
             grid=(1,),
             in_specs=[whole((rows, head_size))] * seq_count
-            + [pl.BlockSpec((text, head_size), lambda i, me: (0, me[0] // groups))] * 2
-            + [whole((1, head_size))],
+            + [whole((text, head_size))] * 2,
             out_specs=whole((seq_count, padded, head_size)),
             scratch_shapes=[
                 pltpu.VMEM((seq_count * padded, head_size), jnp.bfloat16),
@@ -224,7 +276,7 @@
         ),
         compiler_params=pltpu.CompilerParams(vmem_limit_bytes=40 * 2**20),
         name="attend",
-    )(me, *arrived, text_k, text_v, k_gain)
+    )(me, *arrived, text_keys, text_values)
 
     returned = lax.all_to_all(result, "seq", split_axis=0, concat_axis=0, tiled=True)
 

time: 65.2 us -> 64.4 us (0.988)
  waiting for transfers between devices: 25.7 us -> 17.5 us
  starting transfers between devices: 27.1 us -> 30.7 us
  local copies, waits for them, and re-layouts: 2.13 us -> 4.1 us
  Pallas kernels: 9.86 us -> 11.6 us
    ppermute x15, waiting for transfers between devices: 14.7 us -> 6.51 us  [trade(): return lax.ppermute(block, 'seq', [(a, a ^ step) for a in range(count)])]
    ppermute x15, starting transfers between devices: 23.5 us -> 27 us  [trade(): return lax.ppermute(block, 'seq', [(a, a ^ step) for a in range(count)])]
    unnamed x12 -> x14, local copies, waits for them, and re-layouts: 2.13 us -> 4.09 us
    pallas_call x1 -> x2, Pallas kernels: 3.56 us -> 5.34 us  [the longest x1 3.27 us: shards(): pl.pallas_call(lambda *refs: prepare_kernel(per_group, padded, late, Fals...]
  transfers between devices with their start and end apart: 16 -> 16, of which waited for: 7 -> 7; matrix products, arithmetic and copies ran while one was open for 0% -> 0% of each run, Pallas kernels for 0% -> 5%
where the time goes in v5:
time: 64.4 us; the launch traced here: 64 us
  starting transfers between devices  30.7 us (48%)
  waiting for transfers between devices  17.5 us (27%)
  Pallas kernels  11.6 us (18%)
  local copies, waits for them, and re-layouts  4.1 us (6%)
    ppermute x15, starting transfers between devices, trade(): return lax.ppermute(block, 'seq', [(a, a ^ step) for a in range(count)])  27 us
    all_to_all x1, waiting for transfers between devices, shards(): lax.all_to_all(result, 'seq', split_axis=0, concat_axis=0, tiled=True)  11 us
    ppermute x15, waiting for transfers between devices, trade(): return lax.ppermute(block, 'seq', [(a, a ^ step) for a in range(count)])  6.51 us
    pallas_call x1, Pallas kernels, shards(): pl.pallas_call(lambda *refs: attend_kernel(tokens, query_rows, 256, steps...  5.16 us
    unnamed x14, local copies, waits for them, and re-layouts  4.09 us
    all_to_all x1, starting transfers between devices, shards(): lax.all_to_all(result, 'seq', split_axis=0, concat_axis=0, tiled=True)  3.67 us
    pallas_call x1, Pallas kernels, shards(): pl.pallas_call(lambda *refs: prepare_kernel(per_group, padded, late, Fals...  3.27 us
    pallas_call x1, Pallas kernels, shards(): pl.pallas_call(lambda *refs: prepare_kernel(per_group, padded, early, Tru...  2.07 us
  transfers between devices with their start and end apart: 16, of which 7 were waited for; matrix products, arithmetic and copies ran while one was open for 0% of the time, Pallas kernels for 5%

profile of v5, /device:TPU:0, one launch (start us, length us, event | category | flops | bytes accessed | tf_op | source)
XLA Modules:
  0.0 64.0 jit_solution(11376956933953200824)
XLA Ops:
  0.0 2.1 %prepare_first.1 = (bf16[336,128]{1,0:T(8,128)(2,1)}, bf16[336,128]{1,0:T(8,128)(2,1)}, bf16[336,128]{1,0:T(8,128)(2,1)}, bf16[336,128]{1,0:T(8,128)(2,1)}) custom-call(s32[1]{0:T(128)} %bitcast.1.refs_0_, s32[1,76]{1,0:T(1,128)} %bitcast.14, f32[1,128]{1,0:T(1,128)} %bitcast.10, f32[1,128]{1,0:T(1,128)} %bitcast.12, bf16[3,76,2048]{2,1,0:T(8,128)(2,1)} %bitcast.5, ...), custom_call_target="tpu_custom_call" | custom-call | tf_op jit(solution)/shard_map/prepare_first/pallas_call | solution.py:214
  2.1 0.5 collective-permute-start
  2.5 5.7 %collective-permute-start.1 = (bf16[336,128]{1,0:T(8,128)(2,1)}, bf16[336,128]{1,0:T(8,128)(2,1)S(1)}, u32[]{:S(2)}, u32[]{:S(2)}) collective-permute-start(bf16[336,128]{1,0:T(8,128)(2,1)} %get-tuple-element.25), channel_id=1, source_target_pairs={{0,15},{1,14},{2,13},{3,12},{4,11},{5,10},{6,9},{7,8},{8,7},{9,6},... | collective-permute-start | bytes 258056 | tf_op jit(solution)/shard_map/ppermute | solution.py:171
  8.2 0.0 collective-permute-start.10
  8.2 3.4 %collective-permute-start.2 = (bf16[336,128]{1,0:T(8,128)(2,1)}, bf16[336,128]{1,0:T(8,128)(2,1)S(1)}, u32[]{:S(2)}, u32[]{:S(2)}) collective-permute-start(bf16[336,128]{1,0:T(8,128)(2,1)} %get-tuple-element.26), channel_id=1, source_target_pairs={{0,14},{1,15},{2,12},{3,13},{4,10},{5,11},{6,8},{7,9},{8,6},{9,7},... | collective-permute-start | bytes 258056 | tf_op jit(solution)/shard_map/ppermute | solution.py:171
  11.6 0.0 collective-permute-done.refs_9_.refs_11_
  11.6 0.0 copy-start.1
  11.6 0.6 copy-done.1
  12.3 3.3 %prepare_rest.1 = (bf16[336,128]{1,0:T(8,128)(2,1)}, bf16[336,128]{1,0:T(8,128)(2,1)}, bf16[336,128]{1,0:T(8,128)(2,1)}, bf16[336,128]{1,0:T(8,128)(2,1)}, bf16[...) custom-call(s32[1]{0:T(128)} %bitcast.1.refs_0_, ...), custom_call_target="tpu_custom_call" | custom-call | tf_op jit(solution)/shard_map/prepare_rest/pallas_call | solution.py:231
  15.5 0.1 collective-permute-start.11
  15.6 0.4 collective-permute-start.12
  16.1 0.0 collective-permute-done.1.refs_2_
  16.1 2.2 %collective-permute-start.13 = (bf16[336,128]{1,0:T(8,128)(2,1)}, bf16[336,128]{1,0:T(8,128)(2,1)S(1)}, u32[]{:S(2)}, u32[]{:S(2)}) collective-permute-start(bf16[336,128]{1,0:T(8,128)(2,1)} %get-tuple-element.37), channel_id=1, source_target_pairs={{0,6},{1,7},{2,4},{3,5},{4,2},{5,3},{6,0},{7,1},{8,14},{9,15},{10,... | collective-permute-start | bytes 258056 | tf_op jit(solution)/shard_map/ppermute | solution.py:171
  18.3 0.0 collective-permute-done.10.refs_12_
  18.3 1.9 %collective-permute-start.14 = (bf16[336,128]{1,0:T(8,128)(2,1)}, bf16[336,128]{1,0:T(8,128)(2,1)S(1)}, u32[]{:S(2)}, u32[]{:S(2)}) collective-permute-start(bf16[336,128]{1,0:T(8,128)(2,1)} %get-tuple-element.38), channel_id=1, source_target_pairs={{0,11},{1,10},{2,9},{3,8},{4,15},{5,14},{6,13},{7,12},{8,3},{9,2},... | collective-permute-start | bytes 258056 | tf_op jit(solution)/shard_map/ppermute | solution.py:171
  20.2 0.0 collective-permute-done.2.refs_3_
  20.2 2.3 %collective-permute-start.3 = (bf16[336,128]{1,0:T(8,128)(2,1)}, bf16[336,128]{1,0:T(8,128)(2,1)S(1)}, u32[]{:S(2)}, u32[]{:S(2)}) collective-permute-start(bf16[336,128]{1,0:T(8,128)(2,1)} %get-tuple-element.27), channel_id=1, source_target_pairs={{0,5},{1,4},{2,7},{3,6},{4,1},{5,0},{6,3},{7,2},{8,13},{9,12},{10,... | collective-permute-start | bytes 258056 | tf_op jit(solution)/shard_map/ppermute | solution.py:171
  22.5 0.0 collective-permute-done.11.refs_13_
  22.5 0.7 %collective-permute-start.4 = (bf16[336,128]{1,0:T(8,128)(2,1)}, bf16[336,128]{1,0:T(8,128)(2,1)S(1)}, u32[]{:S(2)}, u32[]{:S(2)}) collective-permute-start(bf16[336,128]{1,0:T(8,128)(2,1)} %get-tuple-element.28), channel_id=1, source_target_pairs={{0,10},{1,11},{2,8},{3,9},{4,14},{5,15},{6,12},{7,13},{8,2},{9,3},... | collective-permute-start | bytes 258056 | tf_op jit(solution)/shard_map/ppermute | solution.py:171
  23.2 0.0 collective-permute-done.12.refs_14_
  23.2 2.2 %collective-permute-start.5 = (bf16[336,128]{1,0:T(8,128)(2,1)}, bf16[336,128]{1,0:T(8,128)(2,1)S(1)}, u32[]{:S(2)}, u32[]{:S(2)}) collective-permute-start(bf16[336,128]{1,0:T(8,128)(2,1)} %get-tuple-element.29), channel_id=1, source_target_pairs={{0,4},{1,5},{2,6},{3,7},{4,0},{5,1},{6,2},{7,3},{8,12},{9,13},{10,... | collective-permute-start | bytes 258056 | tf_op jit(solution)/shard_map/ppermute | solution.py:171
  25.4 0.8 %collective-permute-done.13.refs_15_ = bf16[336,128]{1,0:T(8,128)(2,1)S(1)} collective-permute-done((bf16[336,128]{1,0:T(8,128)(2,1)}, bf16[336,128]{1,0:T(8,128)(2,1)S(1)}, u32[]{:S(2)}, u32[]{:S(2)}) %collective-permute-start.13) | collective-permute-done | bytes 86048 | tf_op jit(solution)/shard_map/ppermute | solution.py:171
  26.2 0.6 collective-permute-start.6
  26.8 1.0 %collective-permute-done.14.refs_16_ = bf16[336,128]{1,0:T(8,128)(2,1)S(1)} collective-permute-done((bf16[336,128]{1,0:T(8,128)(2,1)}, bf16[336,128]{1,0:T(8,128)(2,1)S(1)}, u32[]{:S(2)}, u32[]{:S(2)}) %collective-permute-start.14) | collective-permute-done | bytes 86048 | tf_op jit(solution)/shard_map/ppermute | solution.py:171
  27.8 1.7 %collective-permute-start.7 = (bf16[336,128]{1,0:T(8,128)(2,1)}, bf16[336,128]{1,0:T(8,128)(2,1)S(1)}, u32[]{:S(2)}, u32[]{:S(2)}) collective-permute-start(bf16[336,128]{1,0:T(8,128)(2,1)} %get-tuple-element.31), channel_id=1, source_target_pairs={{0,3},{1,2},{2,1},{3,0},{4,7},{5,6},{6,5},{7,4},{8,11},{9,10},{10,... | collective-permute-start | bytes 258056 | tf_op jit(solution)/shard_map/ppermute | solution.py:171
  29.5 0.0 collective-permute-done.3.refs_4_
  29.5 0.5 collective-permute-start.8
  30.1 2.0 %collective-permute-done.4.refs_5_ = bf16[336,128]{1,0:T(8,128)(2,1)S(1)} collective-permute-done((bf16[336,128]{1,0:T(8,128)(2,1)}, bf16[336,128]{1,0:T(8,128)(2,1)S(1)}, u32[]{:S(2)}, u32[]{:S(2)}) %collective-permute-start.4) | collective-permute-done | bytes 86048 | tf_op jit(solution)/shard_map/ppermute | solution.py:171
  32.1 4.8 %collective-permute-start.9 = (bf16[336,128]{1,0:T(8,128)(2,1)}, bf16[336,128]{1,0:T(8,128)(2,1)S(1)}, u32[]{:S(2)}, u32[]{:S(2)}) collective-permute-start(bf16[336,128]{1,0:T(8,128)(2,1)} %get-tuple-element.33), channel_id=1, source_target_pairs={{0,2},{1,3},{2,0},{3,1},{4,6},{5,7},{6,4},{7,5},{8,10},{9,11},{10,... | collective-permute-start | bytes 258056 | tf_op jit(solution)/shard_map/ppermute | solution.py:171
  36.8 0.0 collective-permute-done.5.refs_6_
  36.9 0.1 collective-permute-done.6.refs_7_
  36.9 0.0 collective-permute-done.7.refs_8_
  36.9 2.0 %collective-permute-done.8.refs_9_ = bf16[336,128]{1,0:T(8,128)(2,1)S(1)} collective-permute-done((bf16[336,128]{1,0:T(8,128)(2,1)}, bf16[336,128]{1,0:T(8,128)(2,1)S(1)}, u32[]{:S(2)}, u32[]{:S(2)}) %collective-permute-start.8) | collective-permute-done | bytes 86048 | tf_op jit(solution)/shard_map/ppermute | solution.py:171
  38.9 0.6 collective-permute-done.9.refs_10_
  39.5 0.0 copy-start.2
  39.5 0.9 %copy-done.2 = bf16[336,128]{1,0:T(8,128)(2,1)S(1)} copy-done((bf16[336,128]{1,0:T(8,128)(2,1)S(1)}, bf16[336,128]{1,0:T(8,128)(2,1)}, u32[]{:S(2)}) %copy-start.2) | copy-done | bytes 86040
  40.4 0.0 copy-start.3
  40.4 0.9 %copy-done.3 = bf16[336,128]{1,0:T(8,128)(2,1)S(1)} copy-done((bf16[336,128]{1,0:T(8,128)(2,1)S(1)}, bf16[336,128]{1,0:T(8,128)(2,1)}, u32[]{:S(2)}) %copy-start.3) | copy-done | bytes 86040
  41.3 0.0 copy-start.4
  41.3 0.8 %copy-done.4 = bf16[256,128]{1,0:T(8,128)(2,1)S(1)} copy-done((bf16[256,128]{1,0:T(8,128)(2,1)S(1)}, bf16[256,128]{1,0:T(8,128)(2,1)}, u32[]{:S(2)}) %copy-start.4) | copy-done | bytes 65560
  42.1 0.0 copy-start.5
  42.1 0.8 %copy-done.5 = bf16[256,128]{1,0:T(8,128)(2,1)S(1)} copy-done((bf16[256,128]{1,0:T(8,128)(2,1)S(1)}, bf16[256,128]{1,0:T(8,128)(2,1)}, u32[]{:S(2)}) %copy-start.5) | copy-done | bytes 65560
  43.0 5.2 %attend.1 = bf16[16,80,128]{2,1,0:T(8,128)(2,1)} custom-call(s32[1]{0:T(128)} %bitcast.1.refs_0_, bf16[336,128]{1,0:T(8,128)(2,1)S(1)} %copy-done.3, bf16[336,128]{1,0:T(8,128)(2,1)S(1)} %collective-permute-done.1.refs_2_, bf16[336,128]{1,0:T(8,128)(2,1)S(1)} %collective-permute-done.2.refs_3_, bf16[336,128]{1,0:T(8,128)(2,1)S(1)} %collective-permute-done.3.refs_4_, ...), custom_call_target="tpu_custom_call" | custom-call | tf_op jit(solution)/shard_map/attend/pallas_call | solution.py:260
  48.1 3.7 %all-to-all-start = ((bf16[16,80,128]{2,1,0:T(8,128)(2,1)}), bf16[16,80,128]{2,1,0:T(8,128)(2,1)S(1)}, u32[]{:S(2)}, u32[]{:S(2)}) async-start(bf16[16,80,128]{2,1,0:T(8,128)(2,1)} %attend.1), calls=%async_computation | async-start | bytes 655360 | tf_op jit(solution)/shard_map/all_to_all | solution.py:281
  51.8 0.0 copy-done.6
  51.9 11.0 %all-to-all-done.refs_1_ = bf16[16,80,128]{2,1,0:T(8,128)(2,1)S(1)} async-done(((bf16[16,80,128]{2,1,0:T(8,128)(2,1)}), bf16[16,80,128]{2,1,0:T(8,128)(2,1)S(1)}, u32[]{:S(2)}, u32[]{:S(2)}) %all-to-all-start) | async-done | bytes 327712 | tf_op jit(solution)/shard_map/all_to_all | solution.py:281
  62.9 0.0 copy-done
  62.9 1.1 %finish.1 = bf16[128,2048]{1,0:T(8,128)(2,1)} custom-call(s32[1,80]{1,0:T(1,128)S(1)} %pad.4.refs_0_, bf16[16,80,128]{2,1,0:T(8,128)(2,1)S(1)} %all-to-all-done.refs_1_, bf16[128,2048]{1,0:T(8,128)(2,1)S(1)} %copy-done), custom_call_target="tpu_custom_call" | custom-call | tf_op jit(solution)/shard_map/finish/pallas_call | solution.py:284
  (3 shorter events, 0.0 us)
Async XLA Ops:
  2.1 9.6 %collective-permute-start = (bf16[336,128]{1,0:T(8,128)(2,1)}, bf16[336,128]{1,0:T(8,128)(2,1)S(1)}, u32[]{:S(2)}, u32[]{:S(2)}) collective-permute-start(bf16[336,128]{1,0:T(8,128)(2,1)} %get-tuple-element.23), channel_id=1, source_target_pairs={{0,1},{1,0},{2,3},{3,2},{4,5},{5,4},{6,7},{7,6},{8,9},{9,8},{10,11... | collective-permute-start | bytes 258056 | tf_op jit(solution)/shard_map/ppermute | solution.py:171
  2.5 13.5 %collective-permute-start.1 = (bf16[336,128]{1,0:T(8,128)(2,1)}, bf16[336,128]{1,0:T(8,128)(2,1)S(1)}, u32[]{:S(2)}, u32[]{:S(2)}) collective-permute-start(bf16[336,128]{1,0:T(8,128)(2,1)} %get-tuple-element.25), channel_id=1, source_target_pairs={{0,15},{1,14},{2,13},{3,12},{4,11},{5,10},{6,9},{7,8},{8,7},{9,6},... | collective-permute-start | bytes 258056 | tf_op jit(solution)/shard_map/ppermute | solution.py:171
  8.2 10.1 %collective-permute-start.10 = (bf16[336,128]{1,0:T(8,128)(2,1)}, bf16[336,128]{1,0:T(8,128)(2,1)S(1)}, u32[]{:S(2)}, u32[]{:S(2)}) collective-permute-start(bf16[336,128]{1,0:T(8,128)(2,1)} %get-tuple-element.34), channel_id=1, source_target_pairs={{0,13},{1,12},{2,15},{3,14},{4,9},{5,8},{6,11},{7,10},{8,5},{9,4},... | collective-permute-start | bytes 258056 | tf_op jit(solution)/shard_map/ppermute | solution.py:171
  8.2 12.0 %collective-permute-start.2 = (bf16[336,128]{1,0:T(8,128)(2,1)}, bf16[336,128]{1,0:T(8,128)(2,1)S(1)}, u32[]{:S(2)}, u32[]{:S(2)}) collective-permute-start(bf16[336,128]{1,0:T(8,128)(2,1)} %get-tuple-element.26), channel_id=1, source_target_pairs={{0,14},{1,15},{2,12},{3,13},{4,10},{5,11},{6,8},{7,9},{8,6},{9,7},... | collective-permute-start | bytes 258056 | tf_op jit(solution)/shard_map/ppermute | solution.py:171
  11.6 0.6 copy-start.1
  15.5 6.9 %collective-permute-start.11 = (bf16[336,128]{1,0:T(8,128)(2,1)}, bf16[336,128]{1,0:T(8,128)(2,1)S(1)}, u32[]{:S(2)}, u32[]{:S(2)}) collective-permute-start(bf16[336,128]{1,0:T(8,128)(2,1)} %get-tuple-element.35), channel_id=1, source_target_pairs={{0,7},{1,6},{2,5},{3,4},{4,3},{5,2},{6,1},{7,0},{8,15},{9,14},{10,... | collective-permute-start | bytes 258056 | tf_op jit(solution)/shard_map/ppermute | solution.py:171
  15.6 7.6 %collective-permute-start.12 = (bf16[336,128]{1,0:T(8,128)(2,1)}, bf16[336,128]{1,0:T(8,128)(2,1)S(1)}, u32[]{:S(2)}, u32[]{:S(2)}) collective-permute-start(bf16[336,128]{1,0:T(8,128)(2,1)} %get-tuple-element.36), channel_id=1, source_target_pairs={{0,12},{1,13},{2,14},{3,15},{4,8},{5,9},{6,10},{7,11},{8,4},{9,5},... | collective-permute-start | bytes 258056 | tf_op jit(solution)/shard_map/ppermute | solution.py:171
  16.1 10.2 %collective-permute-start.13 = (bf16[336,128]{1,0:T(8,128)(2,1)}, bf16[336,128]{1,0:T(8,128)(2,1)S(1)}, u32[]{:S(2)}, u32[]{:S(2)}) collective-permute-start(bf16[336,128]{1,0:T(8,128)(2,1)} %get-tuple-element.37), channel_id=1, source_target_pairs={{0,6},{1,7},{2,4},{3,5},{4,2},{5,3},{6,0},{7,1},{8,14},{9,15},{10,... | collective-permute-start | bytes 258056 | tf_op jit(solution)/shard_map/ppermute | solution.py:171
  18.3 9.5 %collective-permute-start.14 = (bf16[336,128]{1,0:T(8,128)(2,1)}, bf16[336,128]{1,0:T(8,128)(2,1)S(1)}, u32[]{:S(2)}, u32[]{:S(2)}) collective-permute-start(bf16[336,128]{1,0:T(8,128)(2,1)} %get-tuple-element.38), channel_id=1, source_target_pairs={{0,11},{1,10},{2,9},{3,8},{4,15},{5,14},{6,13},{7,12},{8,3},{9,2},... | collective-permute-start | bytes 258056 | tf_op jit(solution)/shard_map/ppermute | solution.py:171
  20.2 9.4 %collective-permute-start.3 = (bf16[336,128]{1,0:T(8,128)(2,1)}, bf16[336,128]{1,0:T(8,128)(2,1)S(1)}, u32[]{:S(2)}, u32[]{:S(2)}) collective-permute-start(bf16[336,128]{1,0:T(8,128)(2,1)} %get-tuple-element.27), channel_id=1, source_target_pairs={{0,5},{1,4},{2,7},{3,6},{4,1},{5,0},{6,3},{7,2},{8,13},{9,12},{10,... | collective-permute-start | bytes 258056 | tf_op jit(solution)/shard_map/ppermute | solution.py:171
  22.5 9.6 %collective-permute-start.4 = (bf16[336,128]{1,0:T(8,128)(2,1)}, bf16[336,128]{1,0:T(8,128)(2,1)S(1)}, u32[]{:S(2)}, u32[]{:S(2)}) collective-permute-start(bf16[336,128]{1,0:T(8,128)(2,1)} %get-tuple-element.28), channel_id=1, source_target_pairs={{0,10},{1,11},{2,8},{3,9},{4,14},{5,15},{6,12},{7,13},{8,2},{9,3},... | collective-permute-start | bytes 258056 | tf_op jit(solution)/shard_map/ppermute | solution.py:171
  23.2 13.7 %collective-permute-start.5 = (bf16[336,128]{1,0:T(8,128)(2,1)}, bf16[336,128]{1,0:T(8,128)(2,1)S(1)}, u32[]{:S(2)}, u32[]{:S(2)}) collective-permute-start(bf16[336,128]{1,0:T(8,128)(2,1)} %get-tuple-element.29), channel_id=1, source_target_pairs={{0,4},{1,5},{2,6},{3,7},{4,0},{5,1},{6,2},{7,3},{8,12},{9,13},{10,... | collective-permute-start | bytes 258056 | tf_op jit(solution)/shard_map/ppermute | solution.py:171
  26.2 10.7 %collective-permute-start.6 = (bf16[336,128]{1,0:T(8,128)(2,1)}, bf16[336,128]{1,0:T(8,128)(2,1)S(1)}, u32[]{:S(2)}, u32[]{:S(2)}) collective-permute-start(bf16[336,128]{1,0:T(8,128)(2,1)} %get-tuple-element.30), channel_id=1, source_target_pairs={{0,9},{1,8},{2,11},{3,10},{4,13},{5,12},{6,15},{7,14},{8,1},{9,0},... | collective-permute-start | bytes 258056 | tf_op jit(solution)/shard_map/ppermute | solution.py:171
  27.8 9.1 %collective-permute-start.7 = (bf16[336,128]{1,0:T(8,128)(2,1)}, bf16[336,128]{1,0:T(8,128)(2,1)S(1)}, u32[]{:S(2)}, u32[]{:S(2)}) collective-permute-start(bf16[336,128]{1,0:T(8,128)(2,1)} %get-tuple-element.31), channel_id=1, source_target_pairs={{0,3},{1,2},{2,1},{3,0},{4,7},{5,6},{6,5},{7,4},{8,11},{9,10},{10,... | collective-permute-start | bytes 258056 | tf_op jit(solution)/shard_map/ppermute | solution.py:171
  29.5 9.4 %collective-permute-start.8 = (bf16[336,128]{1,0:T(8,128)(2,1)}, bf16[336,128]{1,0:T(8,128)(2,1)S(1)}, u32[]{:S(2)}, u32[]{:S(2)}) collective-permute-start(bf16[336,128]{1,0:T(8,128)(2,1)} %get-tuple-element.32), channel_id=1, source_target_pairs={{0,8},{1,9},{2,10},{3,11},{4,12},{5,13},{6,14},{7,15},{8,0},{9,1},... | collective-permute-start | bytes 258056 | tf_op jit(solution)/shard_map/ppermute | solution.py:171
  32.1 7.4 %collective-permute-start.9 = (bf16[336,128]{1,0:T(8,128)(2,1)}, bf16[336,128]{1,0:T(8,128)(2,1)S(1)}, u32[]{:S(2)}, u32[]{:S(2)}) collective-permute-start(bf16[336,128]{1,0:T(8,128)(2,1)} %get-tuple-element.33), channel_id=1, source_target_pairs={{0,2},{1,3},{2,0},{3,1},{4,6},{5,7},{6,4},{7,5},{8,10},{9,11},{10,... | collective-permute-start | bytes 258056 | tf_op jit(solution)/shard_map/ppermute | solution.py:171
  39.5 0.9 %copy-start.2 = (bf16[336,128]{1,0:T(8,128)(2,1)S(1)}, bf16[336,128]{1,0:T(8,128)(2,1)}, u32[]{:S(2)}) copy-start(bf16[336,128]{1,0:T(8,128)(2,1)} %copy-done.1) | copy-start | bytes 258052
  40.4 0.9 %copy-start.3 = (bf16[336,128]{1,0:T(8,128)(2,1)S(1)}, bf16[336,128]{1,0:T(8,128)(2,1)}, u32[]{:S(2)}) copy-start(bf16[336,128]{1,0:T(8,128)(2,1)} %get-tuple-element.24.refs_1_) | copy-start | bytes 258052
  41.3 0.8 %copy-start.4 = (bf16[256,128]{1,0:T(8,128)(2,1)S(1)}, bf16[256,128]{1,0:T(8,128)(2,1)}, u32[]{:S(2)}) copy-start(bf16[256,128]{1,0:T(8,128)(2,1)} %get-tuple-element.39.refs_17_) | copy-start | bytes 196612
  42.1 0.8 %copy-start.5 = (bf16[256,128]{1,0:T(8,128)(2,1)S(1)}, bf16[256,128]{1,0:T(8,128)(2,1)}, u32[]{:S(2)}) copy-start(bf16[256,128]{1,0:T(8,128)(2,1)} %get-tuple-element.40.refs_18_) | copy-start | bytes 196612
  48.1 3.7 %copy-start.6 = (s32[76]{0:T(128)S(1)}, s32[76]{0:T(128)}, u32[]{:S(2)}) copy-start(s32[76]{0:T(128)} %param.10) | copy-start | bytes 916
  48.1 14.7 %copy-start = (bf16[128,2048]{1,0:T(8,128)(2,1)S(1)}, bf16[128,2048]{1,0:T(8,128)(2,1)}, u32[]{:S(2)}) copy-start(bf16[128,2048]{1,0:T(8,128)(2,1)} %refs_2_.1) | copy-start | bytes 1572868
  48.1 14.7 %all-to-all-start = ((bf16[16,80,128]{2,1,0:T(8,128)(2,1)}), bf16[16,80,128]{2,1,0:T(8,128)(2,1)S(1)}, u32[]{:S(2)}, u32[]{:S(2)}) async-start(bf16[16,80,128]{2,1,0:T(8,128)(2,1)} %attend.1), calls=%async_computation | async-start | bytes 655360 | tf_op jit(solution)/shard_map/all_to_all | solution.py:281

commit v6 on v0

v6 whole, which is shorter than its diff:
```python
import math

import jax
import jax.numpy as jnp
from jax import lax
from jax.experimental import pallas as pl
from jax.experimental.pallas import tpu as pltpu
from jax.sharding import PartitionSpec as P

LOG2E = math.log2(math.e)
INNER = 2
MIB = 2**20


def round_up(count, step):
    return (count + step - 1) // step * step


def normalize(entries, scales):
    mean_square = jnp.mean(entries * entries, axis=-1, keepdims=True)
    return entries * lax.rsqrt(mean_square + 1e-06) * scales


def place(slots, tokens):
    owner = lax.broadcasted_iota(jnp.int32, (tokens, slots.shape[1]), 0)
    return owner == slots


def prepare_kernel(plan, groups, per_group, padded, with_text, me_ref, *refs):
    slots_hbm, q_gain_hbm, k_gain_hbm, qkv_hbm, k_hbm, v_hbm = refs[:6]
    rest = refs[6:]
    if with_text:
        text_k_hbm, text_v_hbm = rest[:2]
        rest = rest[3:]
    outs = []
    for _, apart in plan:
        taken = 2 if apart else 1
        outs.append(rest[:taken])
        rest = rest[taken:]
    if with_text:
        text_keys_ref, text_values_ref = rest[:2]
        rest = rest[2:]
    slots_ref, q_gain_ref, k_gain_ref, fresh_ref, k_ref, v_ref, text_ref, share_ref = rest[:8]
    small_sems, sems, text_sems = rest[8:]
    tokens, width = k_ref.shape[1:]
    head_size = q_gain_ref.shape[1]
    outer = me_ref[0] // INNER

    def columns(step):
        block = lax.bitwise_xor(outer // groups, step // groups)
        return pl.ds(pl.multiple_of(block * width, width), width)

    small = [
        pltpu.make_async_copy(slots_hbm, slots_ref, small_sems.at[0]),
        pltpu.make_async_copy(q_gain_hbm, q_gain_ref, small_sems.at[1]),
        pltpu.make_async_copy(k_gain_hbm, k_gain_ref, small_sems.at[2]),
    ]
    for copy in small:
        copy.start()
    loads = []
    for turn, (step, _) in enumerate(plan):
        mine = columns(step)
        loads.append(
            [
                pltpu.make_async_copy(
                    qkv_hbm.at[:, :, mine], fresh_ref.at[turn], sems.at[turn, 0]
                ),
                pltpu.make_async_copy(k_hbm.at[:, mine], k_ref.at[turn], sems.at[turn, 1]),
                pltpu.make_async_copy(v_hbm.at[:, mine], v_ref.at[turn], sems.at[turn, 2]),
            ]
        )
        for copy in loads[-1]:
            copy.start()
    if with_text:
        mine = columns(0)
        text_loads = [
            pltpu.make_async_copy(text_k_hbm.at[:, mine], text_ref.at[0], text_sems.at[0]),
            pltpu.make_async_copy(text_v_hbm.at[:, mine], text_ref.at[1], text_sems.at[1]),
        ]
        for copy in text_loads:
            copy.start()
    for copy in small:
        copy.wait()
    belongs = place(slots_ref[...], tokens)
    is_fresh = jnp.max(belongs.astype(jnp.float32), axis=1, keepdims=True) > 0.5
    one_hot = belongs.astype(jnp.bfloat16)
    q_gain = q_gain_ref[...]
    k_gain = k_gain_ref[...]

    def merged(fresh, cache):
        spread = jnp.dot(one_hot, fresh, preferred_element_type=jnp.float32)
        return jnp.where(is_fresh, spread, cache.astype(jnp.float32))

    for turn, (step, apart) in enumerate(plan):
        for copy in loads[turn]:
            copy.wait()
        group = lax.bitwise_xor(outer % groups, step % groups)
        for head in range(width // head_size):
            lanes = slice(head * head_size, (head + 1) * head_size)
            keys = normalize(merged(fresh_ref[turn, 1, :, lanes], k_ref[turn, :, lanes]), k_gain)
            values = merged(fresh_ref[turn, 2, :, lanes], v_ref[turn, :, lanes])
            queries = normalize(fresh_ref[turn, 0, :, lanes].astype(jnp.float32), q_gain)
            for part in range(groups):
                share = queries[part * per_group : (part + 1) * per_group]
                if padded > per_group:
                    empty = jnp.zeros((padded - per_group, head_size), jnp.float32)
                    share = jnp.concatenate([share, empty], axis=0)
                share_ref[part] = share.astype(jnp.bfloat16)
            outs[turn][0][head, :tokens] = keys.astype(jnp.bfloat16)
            outs[turn][0][head, tokens : 2 * tokens] = values.astype(jnp.bfloat16)
            if apart:
                outs[turn][1][head] = share_ref[group]
            else:
                outs[turn][0][head, 2 * tokens :] = share_ref[group]
    if with_text:
        for copy in text_loads:
            copy.wait()
        for head in range(width // head_size):
            lanes = slice(head * head_size, (head + 1) * head_size)
            text_keys = normalize(text_ref[0, :, lanes].astype(jnp.float32), k_gain)
            text_keys_ref[head] = text_keys.astype(jnp.bfloat16)
            text_values_ref[head] = text_ref[1, :, lanes]


def gather_kernel(tokens, extra, count, *refs):
    blocks, refs = refs[:count], refs[count:]
    if extra:
        own, other, text_keys, text_values, own_queries = refs[:5]
        refs = refs[5:]
        kept_ref = refs[2]
        text = text_keys.shape[1]
        for number, block in enumerate([own, other]):
            rows = slice(text + number * tokens, text + (number + 1) * tokens)
            kept_ref[:, 0, rows] = block[:, :tokens]
            kept_ref[:, 1, rows] = block[:, tokens:]
        kept_ref[:, 0, :text] = text_keys[...]
        kept_ref[:, 1, :text] = text_values[...]
        parts = [own_queries[...]]
    else:
        parts = []
    out_ref, queries_ref = refs[:2]
    for number, block in enumerate(blocks):
        rows = slice(number * tokens, (number + 1) * tokens)
        out_ref[:, 0, rows] = block[:, :tokens]
        out_ref[:, 1, rows] = block[:, tokens : 2 * tokens]
        parts.append(block[:, 2 * tokens :])
    padded = parts[0].shape[1]
    for number, part in enumerate(parts):
        queries_ref[:, number * padded : (number + 1) * padded] = part


def add_keys(sums, queries, keys, values):
    factor = queries.shape[1] ** (-0.5) * LOG2E
    scores = lax.dot_general(
        queries, keys, (((1,), (1,)), ((), ())), preferred_element_type=jnp.float32
    )
    weights = jnp.exp2(scores * factor).astype(jnp.bfloat16)
    beside = jnp.concatenate([values, jnp.ones_like(values)], axis=1)
    added = jnp.dot(weights, beside, preferred_element_type=jnp.float32)
    return added if sums is None else sums + added


def add_shared(sums, queries, shared, head, tokens):
    for ref in shared:
        rows = ref.shape[2]
        chunk = next(c * tokens for c in (4, 3, 2, 1) if rows % (c * tokens) == 0)
        for first in range(0, rows, chunk):
            at = slice(first, first + chunk)
            sums = add_keys(sums, queries, ref[head, 0, at], ref[head, 1, at])
    return sums


def row_blocks(ref, padded):
    rows = ref.shape[1]
    return [slice(first, min(first + 5 * padded, rows)) for first in range(0, rows, 5 * padded)]


def attend_early_kernel(tokens, padded, *refs):
    shared, queries_ref, sums_ref = refs[:-2], refs[-2], refs[-1]
    for head in range(queries_ref.shape[0]):
        for rows in row_blocks(queries_ref, padded):
            sums_ref[head, rows] = add_shared(None, queries_ref[head, rows], shared, head, tokens)


def attend_late_kernel(tokens, padded, *refs):
    shared = refs[:-5]
    early_ref, early_sums_ref, late_ref, early_out_ref, late_out_ref = refs[-5:]
    for head in range(early_ref.shape[0]):
        for rows in row_blocks(early_ref, padded):
            early_out_ref[head, rows] = add_shared(
                early_sums_ref[head, rows], early_ref[head, rows], shared[-1:], head, tokens
            )
        for rows in row_blocks(late_ref, padded):
            late_out_ref[head, rows] = add_shared(
                None, late_ref[head, rows], shared, head, tokens
            )


def complete_kernel(tokens, steps, me_ref, shared_ref, *refs):
    outer = me_ref[0] // INNER
    out_ref = refs[-1]
    heads, padded, head_size = out_ref.shape[1:]
    for head in range(heads):
        number = 0
        for queries_ref, sums_ref in (refs[0:2], refs[2:4]):
            for rows in row_blocks(queries_ref, padded):
                sums = add_shared(
                    sums_ref[head, rows], queries_ref[head, rows], [shared_ref], head, tokens
                )
                result = (sums[:, :head_size] / sums[:, head_size:]).astype(jnp.bfloat16)
                for first in range(0, rows.stop - rows.start, padded):
                    owner = lax.bitwise_xor(outer, steps[number])
                    out_ref[owner, head] = result[first : first + padded]
                    number += 1


def finish_kernel(per_group, slots_ref, returned_ref, cache_ref, out_ref):
    tokens = cache_ref.shape[0]
    heads, _, head_size = returned_ref.shape[1:]
    groups = slots_ref.shape[0]
    mine = [place(slots_ref[group : group + 1], tokens) for group in range(groups)]
    count = sum(jnp.sum(m.astype(jnp.float32), axis=1, keepdims=True) for m in mine)
    is_fresh = count > 0.5
    one_hot = [m.astype(jnp.bfloat16) for m in mine]
    for number in range(cache_ref.shape[1] // head_size):
        columns = slice(number * head_size, (number + 1) * head_size)
        placed = sum(
            jnp.dot(
                one_hot[group],
                returned_ref[number // heads * groups + group, number % heads],
                preferred_element_type=jnp.float32,
            )
            for group in range(groups)
        )
        out_ref[:, columns] = jnp.where(
            is_fresh, placed, cache_ref[:, columns].astype(jnp.float32)
        ).astype(out_ref.dtype)


def work(micros):
    return pl.CostEstimate(
        flops=int(micros * 1e9), bytes_accessed=int(micros * 3e6), transcendentals=0
    )


def trade(block, distance):
    count = lax.axis_size("seq")
    return lax.ppermute(block, "seq", [(a, a ^ distance) for a in range(count)])


def shards(fresh_qkv, slot_rows, k_cache, v_cache, attn_cache, text_k, text_v, q_gain, k_gain):
    seq_count = lax.axis_size("seq")
    me = lax.axis_index("seq").reshape(1)
    slot_count = slot_rows.shape[0]
    tokens, row_width = k_cache.shape
    text = text_k.shape[0]
    head_size = q_gain.shape[0]
    outers = seq_count // INNER
    all_heads = row_width // head_size
    heads = max(1, all_heads // outers)
    groups = outers * heads // all_heads
    per_group = slot_count // groups
    padded = round_up(per_group, 16)
    width = heads * head_size
    qkv = jnp.transpose(fresh_qkv, (1, 0, 2))
    q_gain = q_gain.reshape(1, head_size)
    k_gain = k_gain.reshape(1, head_size)
    slots = slot_rows.reshape(1, slot_count)
    padded_slots = jnp.pad(
        slot_rows.reshape(groups, per_group),
        ((0, 0), (0, padded - per_group)),
        constant_values=tokens,
    )

    def shaped(*shape, dtype=jnp.bfloat16):
        return jax.ShapeDtypeStruct(shape, dtype)

    in_hbm = pl.BlockSpec(memory_space=pltpu.HBM)
    in_vmem = pl.BlockSpec(memory_space=pltpu.VMEM)
    in_smem = pl.BlockSpec(memory_space=pltpu.SMEM)

    def prepare(plan, with_text, name, *extra):
        shapes = []
        for _, apart in plan:
            if apart:
                shapes += [shaped(heads, 2 * tokens, head_size), shaped(heads, padded, head_size)]
            else:
                shapes += [shaped(heads, 2 * tokens + padded, head_size)]
        if with_text:
            shapes += [shaped(heads, text, head_size)] * 2
        made = pl.pallas_call(
            lambda *refs: prepare_kernel(plan, groups, per_group, padded, with_text, *refs),
            out_shape=shapes,
            in_specs=[in_smem] + [in_hbm] * 6 + [in_hbm] * (2 * with_text)
            + [pl.BlockSpec(memory_space=pl.ANY)] * with_text,
            out_specs=[in_vmem] * len(shapes),
            scratch_shapes=[
                pltpu.VMEM((1, slot_count), jnp.int32),
                pltpu.VMEM((1, head_size), jnp.float32),
                pltpu.VMEM((1, head_size), jnp.float32),
                pltpu.VMEM((len(plan), 3, slot_count, width), jnp.bfloat16),
                pltpu.VMEM((len(plan), tokens, width), jnp.bfloat16),
                pltpu.VMEM((len(plan), tokens, width), jnp.bfloat16),
                pltpu.VMEM((2, text, width), jnp.bfloat16),
                pltpu.VMEM((groups, padded, head_size), jnp.bfloat16),
                pltpu.SemaphoreType.DMA((3,)),
                pltpu.SemaphoreType.DMA((len(plan), 3)),
                pltpu.SemaphoreType.DMA((2,)),
            ],
            cost_estimate=work(20),
            name=name,
        )(me, slots, q_gain, k_gain, qkv, k_cache, v_cache, *extra)
        return list(made)

    half = outers // 2
    far = list(reversed(range(half, outers)))
    early = far[:1] + list(range(1, half))
    late = far[1:]
    block, own, own_queries = prepare([(far[0], False), (0, True)], False, "prepare_first")
    arrived = {far[0]: trade(block, far[0] * INNER)}
    other = trade(own, 1)

    order = late[:1] + early[1:] + late[1:]
    *made, text_keys, text_values = prepare(
        [(step, False) for step in order], True, "prepare_rest", text_k, text_v, other
    )
    for step, block in zip(order, made):
        arrived[step] = trade(block, step * INNER)

    def gather(steps, name, *extra, after=()):
        count = len(steps) + (1 if extra else 0)
        shapes = [
            shaped(heads, 2, len(steps) * tokens, head_size),
            shaped(heads, count * padded, head_size),
        ]
        if extra:
            shapes.append(shaped(heads, 2, text + 2 * tokens, head_size))
        return pl.pallas_call(
            lambda *refs: gather_kernel(
                tokens, bool(extra), len(steps), *refs[len(after) :]
            ),
            out_shape=shapes,
            in_specs=[pl.BlockSpec(memory_space=pl.ANY)] * len(after)
            + [in_vmem] * (len(steps) + len(extra)),
            out_specs=[in_vmem] * len(shapes),
            compiler_params=pltpu.CompilerParams(vmem_limit_bytes=24 * MIB),
            cost_estimate=work(10),
            name=name,
        )(*after, *[arrived[step] for step in steps], *extra)

    early_keys, early_queries, kept = gather(
        early, "gather_early", own, other, text_keys, text_values, own_queries
    )
    early_other = trade(early_keys, 1)
    sums_shape = shaped(heads, early_queries.shape[1], 2 * head_size, dtype=jnp.float32)
    early_sums = pl.pallas_call(
        lambda *refs: attend_early_kernel(tokens, padded, *refs),
        out_shape=sums_shape,
        in_specs=[in_vmem] * 4,
        out_specs=in_vmem,
        compiler_params=pltpu.CompilerParams(vmem_limit_bytes=24 * MIB),
        cost_estimate=work(10),
        name="attend_early",
    )(kept, early_keys, early_other, early_queries)

    late_keys, late_queries = gather(late, "gather_late", after=(early_sums,))
    late_other = trade(late_keys, 1)
    early_sums, late_sums = pl.pallas_call(
        lambda *refs: attend_late_kernel(tokens, padded, *refs),
        out_shape=[
            sums_shape,
            shaped(heads, late_queries.shape[1], 2 * head_size, dtype=jnp.float32),
        ],
        in_specs=[in_vmem] * 7,
        out_specs=[in_vmem] * 2,
        compiler_params=pltpu.CompilerParams(vmem_limit_bytes=24 * MIB),
        cost_estimate=work(10),
        name="attend_late",
    )(kept, early_keys, early_other, late_keys, early_queries, early_sums, late_queries)
    result = pl.pallas_call(
        lambda *refs: complete_kernel(tokens, [0] + early + late, *refs),
        out_shape=shaped(outers, heads, padded, head_size),
        in_specs=[in_smem] + [in_vmem] * 5,
        out_specs=in_vmem,
        compiler_params=pltpu.CompilerParams(vmem_limit_bytes=24 * MIB),
        name="complete",
    )(me, late_other, early_queries, early_sums, late_queries, late_sums)

    returned = lax.all_to_all(
        result,
        "seq",
        split_axis=0,
        concat_axis=0,
        tiled=True,
        axis_index_groups=[list(range(core, seq_count, INNER)) for core in range(INNER)],
    )

    return pl.pallas_call(
        lambda *refs: finish_kernel(per_group, *refs),
        out_shape=jax.ShapeDtypeStruct((tokens, row_width), attn_cache.dtype),
        in_specs=[in_vmem] * 3,
        out_specs=in_vmem,
        compiler_params=pltpu.CompilerParams(vmem_limit_bytes=24 * MIB),
        name="finish",
    )(padded_slots, returned, attn_cache)


def solution(mesh):
    return jax.shard_map(
        shards,
        mesh=mesh,
        in_specs=(
            P(("parts", "seq"), None, None),
            P(("parts", "seq")),
            P(("parts", "seq"), None),
            P(("parts", "seq"), None),
            P(("parts", "seq"), None),
            P("parts", None),
            P("parts", None),
            P(),
            P(),
        ),
        out_specs=P(("parts", "seq"), None),
        check_vma=False,
    )
```

time: 101 us -> 72.5 us (0.72)
  blocking collectives: 17.5 us -> 0 us
  local copies, waits for them, and re-layouts: 18.7 us -> 4.14 us
  other arithmetic: 14.5 us -> 0 us
  Pallas kernels: 0 us -> 13 us
  matrix products: 12.3 us -> 0 us
  waiting for transfers between devices: 25.4 us -> 37.1 us
  starting transfers between devices: 11.2 us -> 17.8 us
    ppermute x0 -> x10, waiting for transfers between devices: none -> 26 us  [trade(): return lax.ppermute(block, 'seq', [(a, a ^ distance) for a in range(count)])]
    all_to_all x1 -> x0, blocking collectives: 17.5 us -> none  [shards(): lax.all_to_all(result, 'seq', split_axis=1, concat_axis=0, tiled=True)]
    all_to_all x2 -> x1, waiting for transfers between devices: 25.4 us -> 11.1 us  [shards(): lax.all_to_all(result, 'seq', split_axis=0, concat_axis=0, tiled=True, ax...]
    ppermute x0 -> x10, starting transfers between devices: none -> 14.2 us  [trade(): return lax.ppermute(block, 'seq', [(a, a ^ distance) for a in range(count)])]
    pallas_call x0 -> x8, Pallas kernels: none -> 13 us  [the longest x2 6.52 us: prepare(): pl.pallas_call(lambda *refs: prepare_kernel(plan, groups, per_group, padd...]
    dot_general x12 -> x0, matrix products: 12.3 us -> none  [the longest x5 8.14 us: add_block(): lax.dot_general(queries, key_block, (((1,), (1,)), ((), ())), preferred_e...]
    all_to_all x2 -> x1, starting transfers between devices: 11.2 us -> 3.56 us  [shards(): lax.all_to_all(result, 'seq', split_axis=0, concat_axis=0, tiled=True, ax...]
    unnamed x2 -> x0, other arithmetic: 7.34 us -> none
  transfers between devices with their start and end apart: 2 -> 11, of which waited for: 2 -> 7; matrix products, arithmetic and copies ran while one was open for 8% -> 0% of each run, Pallas kernels for 0% -> 11%
where the time goes in v6:
time: 72.5 us; the launch traced here: 72.1 us
  waiting for transfers between devices  37.1 us (51%)
  starting transfers between devices  17.8 us (25%)
  Pallas kernels  13 us (18%)
  local copies, waits for them, and re-layouts  4.14 us (6%)
    ppermute x10, waiting for transfers between devices, trade(): return lax.ppermute(block, 'seq', [(a, a ^ distance) for a in range(count)])  26 us
    ppermute x10, starting transfers between devices, trade(): return lax.ppermute(block, 'seq', [(a, a ^ distance) for a in range(count)])  14.2 us
    all_to_all x1, waiting for transfers between devices, shards(): lax.all_to_all(result, 'seq', split_axis=0, concat_axis=0, tiled=True, ax...  11.1 us
    pallas_call x2, Pallas kernels, prepare(): pl.pallas_call(lambda *refs: prepare_kernel(plan, groups, per_group, padd...  6.52 us
    unnamed x22, local copies, waits for them, and re-layouts  4.13 us
    all_to_all x1, starting transfers between devices, shards(): lax.all_to_all(result, 'seq', split_axis=0, concat_axis=0, tiled=True, ax...  3.56 us
    pallas_call x1, Pallas kernels, shards(): pl.pallas_call(lambda *refs: attend_late_kernel(tokens, padded, *refs), o...  1.87 us
    pallas_call x1, Pallas kernels, shards(): pl.pallas_call(lambda *refs: attend_early_kernel(tokens, padded, *refs),...  1.77 us
  transfers between devices with their start and end apart: 11, of which 7 were waited for; matrix products, arithmetic and copies ran while one was open for 0% of the time, Pallas kernels for 11%

profile of v6, /device:TPU:0, one launch (start us, length us, event | category | flops | bytes accessed | tf_op | source)
XLA Modules:
  0.0 72.1 jit_solution(13437787471597437304)
XLA Ops:
  0.0 2.3 %prepare_first.1 = (bf16[2,336,128]{2,1,0:T(8,128)(2,1)}, bf16[2,256,128]{2,1,0:T(8,128)(2,1)}, bf16[2,80,128]{2,1,0:T(8,128)(2,1)}) custom-call(s32[1]{0:T(128)} %bitcast.1.refs_0_, s32[1,76]{1,0:T(1,128)} %bitcast.11, f32[1,128]{1,0:T(1,128)} %bitcast.7, f32[1,128]{1,0:T(1,128)} %bitcast.9, bf16[3,76,2048]{2,1,0:T(8,128)(2,1)} %bitcast.5, ...), custom_call_target="tpu_custom_call" | custom-call | flops 20000000000 | bytes 60000000 | tf_op jit(solution)/shard_map/prepare_first/pallas_call | solution.py:291
  2.3 0.5 collective-permute-start.1
  2.8 0.0 copy-start.1
  2.8 0.0 copy-start.6
  2.8 5.6 %collective-permute-start = (bf16[2,336,128]{2,1,0:T(8,128)(2,1)}, bf16[2,336,128]{2,1,0:T(8,128)(2,1)S(1)}, u32[]{:S(2)}, u32[]{:S(2)}) collective-permute-start(bf16[2,336,128]{2,1,0:T(8,128)(2,1)} %get-tuple-element.23), channel_id=1, source_target_pairs={{0,14},{1,15},{2,12},{3,13},{4,10},{5,11},{6,8},{7,9},{8,6},{9,7},... | collective-permute-start | bytes 516104 | tf_op jit(solution)/shard_map/ppermute | solution.py:248
  8.4 0.0 collective-permute-done.1.refs_9_.refs_5_
  8.4 0.0 copy-start.2
  8.5 0.6 copy-done.2
  9.1 4.3 %prepare_rest.1 = (bf16[2,336,128]{2,1,0:T(8,128)(2,1)}, bf16[2,336,128]{2,1,0:T(8,128)(2,1)}, bf16[2,336,128]{2,1,0:T(8,128)(2,1)}, bf16[2,336,128]{2,1,0:T(8,1...) custom-call(s32[1]{0:T(128)} %bitcast.1.refs_0_, ...), custom_call_target="tpu_custom_call" | custom-call | flops 20000000000 | bytes 60000000 | tf_op jit(solution)/shard_map/prepare_rest/pallas_call | solution.py:291
  13.4 0.6 collective-permute-start.2
  13.9 0.0 collective-permute-start.3
  13.9 3.0 %collective-permute-start.4 = (bf16[2,336,128]{2,1,0:T(8,128)(2,1)}, bf16[2,336,128]{2,1,0:T(8,128)(2,1)S(1)}, u32[]{:S(2)}, u32[]{:S(2)}) collective-permute-start(bf16[2,336,128]{2,1,0:T(8,128)(2,1)} %get-tuple-element.27), channel_id=1, source_target_pairs={{0,6},{1,7},{2,4},{3,5},{4,2},{5,3},{6,0},{7,1},{8,14},{9,15},{10,... | collective-permute-start | bytes 516104 | tf_op jit(solution)/shard_map/ppermute | solution.py:248
  16.9 0.0 collective-permute-done.refs_0_
  16.9 3.1 %collective-permute-done.2.refs_1_ = bf16[2,336,128]{2,1,0:T(8,128)(2,1)S(1)} collective-permute-done((bf16[2,336,128]{2,1,0:T(8,128)(2,1)}, bf16[2,336,128]{2,1,0:T(8,128)(2,1)S(1)}, u32[]{:S(2)}, u32[]{:S(2)}) %collective-permute-start.2) | collective-permute-done | bytes 172064 | tf_op jit(solution)/shard_map/ppermute | solution.py:248
  20.1 1.3 %collective-permute-done.3.refs_2_ = bf16[2,336,128]{2,1,0:T(8,128)(2,1)S(1)} collective-permute-done((bf16[2,336,128]{2,1,0:T(8,128)(2,1)}, bf16[2,336,128]{2,1,0:T(8,128)(2,1)S(1)}, u32[]{:S(2)}, u32[]{:S(2)}) %collective-permute-start.3) | collective-permute-done | bytes 172064 | tf_op jit(solution)/shard_map/ppermute | solution.py:248
  21.4 3.5 %collective-permute-done.4.refs_3_ = bf16[2,336,128]{2,1,0:T(8,128)(2,1)S(1)} collective-permute-done((bf16[2,336,128]{2,1,0:T(8,128)(2,1)}, bf16[2,336,128]{2,1,0:T(8,128)(2,1)S(1)}, u32[]{:S(2)}, u32[]{:S(2)}) %collective-permute-start.4) | collective-permute-done | bytes 172064 | tf_op jit(solution)/shard_map/ppermute | solution.py:248
  24.9 0.0 copy-done.1
  24.9 0.0 copy-done.6
  24.9 0.0 copy-start.3
  24.9 0.9 %copy-done.3 = bf16[2,256,128]{2,1,0:T(8,128)(2,1)S(1)} copy-done((bf16[2,256,128]{2,1,0:T(8,128)(2,1)S(1)}, bf16[2,256,128]{2,1,0:T(8,128)(2,1)}, u32[]{:S(2)}) %copy-start.3) | copy-done | bytes 131096
  25.8 0.0 copy-start.4
  25.8 0.9 %copy-done.4 = bf16[2,256,128]{2,1,0:T(8,128)(2,1)S(1)} copy-done((bf16[2,256,128]{2,1,0:T(8,128)(2,1)S(1)}, bf16[2,256,128]{2,1,0:T(8,128)(2,1)}, u32[]{:S(2)}) %copy-start.4) | copy-done | bytes 131096
  26.8 0.0 copy-start.5
  26.8 0.9 %copy-done.5 = bf16[2,256,128]{2,1,0:T(8,128)(2,1)S(1)} copy-done((bf16[2,256,128]{2,1,0:T(8,128)(2,1)S(1)}, bf16[2,256,128]{2,1,0:T(8,128)(2,1)}, u32[]{:S(2)}) %copy-start.5) | copy-done | bytes 131096
  27.7 0.0 copy-start.9
  27.7 0.0 copy-start.8
  27.7 0.1 gather_early.1
  27.7 0.1 collective-permute-start.5
  27.8 0.7 %copy-done.9 = bf16[2,336,128]{2,1,0:T(8,128)(2,1)S(1)} copy-done((bf16[2,336,128]{2,1,0:T(8,128)(2,1)S(1)}, bf16[2,336,128]{2,1,0:T(8,128)(2,1)}, u32[]{:S(2)}) %copy-start.9) | copy-done | bytes 172056
  28.6 0.5 collective-permute-start.6
  29.1 0.0 copy-done.8
  29.1 1.3 %collective-permute-start.7 = (bf16[2,336,128]{2,1,0:T(8,128)(2,1)S(1)}, bf16[2,336,128]{2,1,0:T(8,128)(2,1)S(1)}, u32[]{:S(2)}, u32[]{:S(2)}) collective-permute-start(bf16[2,336,128]{2,1,0:T(8,128)(2,1)S(1)} %copy-done.8), channel_id=1, source_target_pairs={{0,10},{1,11},{2,8},{3,9},{4,14},{5,15},{6,12},{7,13},{8,2},{9,3},... | collective-permute-start | bytes 516104 | tf_op jit(solution)/shard_map/ppermute | solution.py:248
  30.4 0.0 copy-done.7
  30.4 2.5 %collective-permute-start.8 = (bf16[2,336,128]{2,1,0:T(8,128)(2,1)S(1)}, bf16[2,336,128]{2,1,0:T(8,128)(2,1)S(1)}, u32[]{:S(2)}, u32[]{:S(2)}) collective-permute-start(bf16[2,336,128]{2,1,0:T(8,128)(2,1)S(1)} %copy-done.7), channel_id=1, source_target_pairs={{0,8},{1,9},{2,10},{3,11},{4,12},{5,13},{6,14},{7,15},{8,0},{9,1},... | collective-permute-start | bytes 516104 | tf_op jit(solution)/shard_map/ppermute | solution.py:248
  33.0 0.0 collective-permute-done.5.refs_2_
  33.0 1.8 %attend_early.1.refs_0_.refs_5_ = f32[2,400,256]{2,1,0:T(8,128)S(1)} custom-call(bf16[2,2,512,128]{3,2,1,0:T(8,128)(2,1)S(1)} %get-tuple-element.31.refs_0_, bf16[2,2,512,128]{3,2,1,0:T(8,128)(2,1)S(1)} %get-tuple-element.32.refs_1_, bf16[2,2,512,128]{3,2,1,0:T(8,128)(2,1)S(1)} %collective-permute-done.5.refs_2_, ...), custom_call_target="tpu_custom_call" | custom-call | flops 10000000000 | bytes 30000000 | tf_op jit(solution)/shard_map/attend_early/pallas_call | solution.py:356
  34.7 3.0 %collective-permute-done.6.refs_1_ = bf16[2,336,128]{2,1,0:T(8,128)(2,1)S(1)} collective-permute-done((bf16[2,336,128]{2,1,0:T(8,128)(2,1)S(1)}, bf16[2,336,128]{2,1,0:T(8,128)(2,1)S(1)}, u32[]{:S(2)}, u32[]{:S(2)}) %collective-permute-start.6) | collective-permute-done | bytes 172064 | tf_op jit(solution)/shard_map/ppermute | solution.py:248
  37.7 12.7 %collective-permute-done.7.refs_2_ = bf16[2,336,128]{2,1,0:T(8,128)(2,1)S(1)} collective-permute-done((bf16[2,336,128]{2,1,0:T(8,128)(2,1)S(1)}, bf16[2,336,128]{2,1,0:T(8,128)(2,1)S(1)}, u32[]{:S(2)}, u32[]{:S(2)}) %collective-permute-start.7) | collective-permute-done | bytes 172064 | tf_op jit(solution)/shard_map/ppermute | solution.py:248
  50.4 2.3 %collective-permute-done.8.refs_3_ = bf16[2,336,128]{2,1,0:T(8,128)(2,1)S(1)} collective-permute-done((bf16[2,336,128]{2,1,0:T(8,128)(2,1)S(1)}, bf16[2,336,128]{2,1,0:T(8,128)(2,1)S(1)}, u32[]{:S(2)}, u32[]{:S(2)}) %collective-permute-start.8) | collective-permute-done | bytes 172064 | tf_op jit(solution)/shard_map/ppermute | solution.py:248
  52.8 0.1 collective-permute-start.9
  52.9 1.9 %attend_late.1 = (f32[2,400,256]{2,1,0:T(8,128)S(1)}, f32[2,240,256]{2,1,0:T(8,128)S(1)}) custom-call(bf16[2,2,512,128]{3,2,1,0:T(8,128)(2,1)S(1)} %get-tuple-element.31.refs_0_, bf16[2,2,512,128]{3,2,1,0:T(8,128)(2,1)S(1)} %get-tuple-element.32.refs_1_, bf16[2,2,512,128]{3,2,1,0:T(8,128)(2,1)S(1)} %collective-permute-done.5.refs_2_, ...), custom_call_target="tpu_custom_call" | custom-call | flops 10000000000 | bytes 30000000 | tf_op jit(solution)/shard_map/attend_late/pallas_call | solution.py:368
  54.8 0.0 collective-permute-done.9.refs_1_
  54.8 1.6 %complete.1 = bf16[8,2,80,128]{3,2,1,0:T(8,128)(2,1)} custom-call(s32[1]{0:T(128)} %bitcast.1.refs_0_, bf16[2,2,384,128]{3,2,1,0:T(8,128)(2,1)S(1)} %collective-permute-done.9.refs_1_, bf16[2,400,128]{2,1,0:T(8,128)(2,1)S(1)} %get-tuple-element.33.refs_3_.refs_4_.refs_2_, f32[2,400,256]{2,1,0:T(8,128)S(1)} %get-tuple-element.39.refs_3_, ...), custom_call_target="tpu_custom_call" | custom-call | tf_op jit(solution)/shard_map/complete/pallas_call | solution.py:380
  56.4 3.6 %all-to-all-start = ((bf16[8,2,80,128]{3,2,1,0:T(8,128)(2,1)}), bf16[8,2,80,128]{3,2,1,0:T(8,128)(2,1)S(1)}, u32[]{:S(2)}, u32[]{:S(2)}) async-start(bf16[8,2,80,128]{3,2,1,0:T(8,128)(2,1)} %complete.1), calls=%async_computation | async-start | bytes 655360 | tf_op jit(solution)/shard_map/all_to_all | solution.py:389
  59.9 0.0 copy-done.10
  60.0 11.1 %all-to-all-done.refs_1_ = bf16[8,2,80,128]{3,2,1,0:T(8,128)(2,1)S(1)} async-done(((bf16[8,2,80,128]{3,2,1,0:T(8,128)(2,1)}), bf16[8,2,80,128]{3,2,1,0:T(8,128)(2,1)S(1)}, u32[]{:S(2)}, u32[]{:S(2)}) %all-to-all-start) | async-done | bytes 327712 | tf_op jit(solution)/shard_map/all_to_all | solution.py:389
  71.1 0.0 copy-done
  71.1 1.1 %finish.1 = bf16[128,2048]{1,0:T(8,128)(2,1)} custom-call(s32[1,80]{1,0:T(1,128)S(1)} %pad.4.refs_0_, bf16[8,2,80,128]{3,2,1,0:T(8,128)(2,1)S(1)} %all-to-all-done.refs_1_, bf16[128,2048]{1,0:T(8,128)(2,1)S(1)} %copy-done), custom_call_target="tpu_custom_call" | custom-call | tf_op jit(solution)/shard_map/finish/pallas_call | solution.py:398
  (5 shorter events, 0.0 us)
Async XLA Ops:
  2.3 6.2 %collective-permute-start.1 = (bf16[2,256,128]{2,1,0:T(8,128)(2,1)}, bf16[2,256,128]{2,1,0:T(8,128)(2,1)S(1)}, u32[]{:S(2)}, u32[]{:S(2)}) collective-permute-start(bf16[2,256,128]{2,1,0:T(8,128)(2,1)} %get-tuple-element.24.refs_4_), channel_id=1, source_target_pairs={{0,1},{1,0},{2,3},{3,2},{4,5},{5,4},{6,7},{7,6},{8,9},{9,8},{10,11... | collective-permute-start | bytes 393224 | tf_op jit(solution)/shard_map/ppermute | solution.py:248
  2.8 22.1 %copy-start.1 = (bf16[2,256,128]{2,1,0:T(8,128)(2,1)S(1)}, bf16[2,256,128]{2,1,0:T(8,128)(2,1)}, u32[]{:S(2)}) copy-start(bf16[2,256,128]{2,1,0:T(8,128)(2,1)} %get-tuple-element.24.refs_4_) | copy-start | bytes 393220
  2.8 22.1 %copy-start.6 = (bf16[2,80,128]{2,1,0:T(8,128)(2,1)S(1)}, bf16[2,80,128]{2,1,0:T(8,128)(2,1)}, u32[]{:S(2)}) copy-start(bf16[2,80,128]{2,1,0:T(8,128)(2,1)} %get-tuple-element.30.refs_8_) | copy-start | bytes 122884
  2.8 14.1 %collective-permute-start = (bf16[2,336,128]{2,1,0:T(8,128)(2,1)}, bf16[2,336,128]{2,1,0:T(8,128)(2,1)S(1)}, u32[]{:S(2)}, u32[]{:S(2)}) collective-permute-start(bf16[2,336,128]{2,1,0:T(8,128)(2,1)} %get-tuple-element.23), channel_id=1, source_target_pairs={{0,14},{1,15},{2,12},{3,13},{4,10},{5,11},{6,8},{7,9},{8,6},{9,7},... | collective-permute-start | bytes 516104 | tf_op jit(solution)/shard_map/ppermute | solution.py:248
  8.4 0.6 copy-start.2
  13.4 6.7 %collective-permute-start.2 = (bf16[2,336,128]{2,1,0:T(8,128)(2,1)}, bf16[2,336,128]{2,1,0:T(8,128)(2,1)S(1)}, u32[]{:S(2)}, u32[]{:S(2)}) collective-permute-start(bf16[2,336,128]{2,1,0:T(8,128)(2,1)} %get-tuple-element.25), channel_id=1, source_target_pairs={{0,2},{1,3},{2,0},{3,1},{4,6},{5,7},{6,4},{7,5},{8,10},{9,11},{10,... | collective-permute-start | bytes 516104 | tf_op jit(solution)/shard_map/ppermute | solution.py:248
  13.9 7.5 %collective-permute-start.3 = (bf16[2,336,128]{2,1,0:T(8,128)(2,1)}, bf16[2,336,128]{2,1,0:T(8,128)(2,1)S(1)}, u32[]{:S(2)}, u32[]{:S(2)}) collective-permute-start(bf16[2,336,128]{2,1,0:T(8,128)(2,1)} %get-tuple-element.26), channel_id=1, source_target_pairs={{0,4},{1,5},{2,6},{3,7},{4,0},{5,1},{6,2},{7,3},{8,12},{9,13},{10,... | collective-permute-start | bytes 516104 | tf_op jit(solution)/shard_map/ppermute | solution.py:248
  13.9 11.0 %collective-permute-start.4 = (bf16[2,336,128]{2,1,0:T(8,128)(2,1)}, bf16[2,336,128]{2,1,0:T(8,128)(2,1)S(1)}, u32[]{:S(2)}, u32[]{:S(2)}) collective-permute-start(bf16[2,336,128]{2,1,0:T(8,128)(2,1)} %get-tuple-element.27), channel_id=1, source_target_pairs={{0,6},{1,7},{2,4},{3,5},{4,2},{5,3},{6,0},{7,1},{8,14},{9,15},{10,... | collective-permute-start | bytes 516104 | tf_op jit(solution)/shard_map/ppermute | solution.py:248
  24.9 0.9 %copy-start.3 = (bf16[2,256,128]{2,1,0:T(8,128)(2,1)S(1)}, bf16[2,256,128]{2,1,0:T(8,128)(2,1)}, u32[]{:S(2)}) copy-start(bf16[2,256,128]{2,1,0:T(8,128)(2,1)} %copy-done.2) | copy-start | bytes 393220
  25.8 0.9 %copy-start.4 = (bf16[2,256,128]{2,1,0:T(8,128)(2,1)S(1)}, bf16[2,256,128]{2,1,0:T(8,128)(2,1)}, u32[]{:S(2)}) copy-start(bf16[2,256,128]{2,1,0:T(8,128)(2,1)} %get-tuple-element.28.refs_6_) | copy-start | bytes 393220
  26.8 0.9 %copy-start.5 = (bf16[2,256,128]{2,1,0:T(8,128)(2,1)S(1)}, bf16[2,256,128]{2,1,0:T(8,128)(2,1)}, u32[]{:S(2)}) copy-start(bf16[2,256,128]{2,1,0:T(8,128)(2,1)} %get-tuple-element.29.refs_7_) | copy-start | bytes 393220
  27.7 0.9 %copy-start.9 = (bf16[2,336,128]{2,1,0:T(8,128)(2,1)S(1)}, bf16[2,336,128]{2,1,0:T(8,128)(2,1)}, u32[]{:S(2)}) copy-start(bf16[2,336,128]{2,1,0:T(8,128)(2,1)} %get-tuple-element.34) | copy-start | bytes 516100
  27.7 1.4 %copy-start.8 = (bf16[2,336,128]{2,1,0:T(8,128)(2,1)S(1)}, bf16[2,336,128]{2,1,0:T(8,128)(2,1)}, u32[]{:S(2)}) copy-start(bf16[2,336,128]{2,1,0:T(8,128)(2,1)} %get-tuple-element.35) | copy-start | bytes 516100
  27.7 2.8 %copy-start.7 = (bf16[2,336,128]{2,1,0:T(8,128)(2,1)S(1)}, bf16[2,336,128]{2,1,0:T(8,128)(2,1)}, u32[]{:S(2)}) copy-start(bf16[2,336,128]{2,1,0:T(8,128)(2,1)} %get-tuple-element.36) | copy-start | bytes 516100
  27.7 5.2 %collective-permute-start.5 = (bf16[2,2,512,128]{3,2,1,0:T(8,128)(2,1)S(1)}, bf16[2,2,512,128]{3,2,1,0:T(8,128)(2,1)S(1)}, u32[]{:S(2)}, u32[]{:S(2)}) collective-permute-start(bf16[2,2,512,128]{3,2,1,0:T(8,128)(2,1)S(1)} %get-tuple-element.32.refs_1_), channel_id=1, source_target_pairs={{0,1},{1,0},{2,3},{3,2},{4,5},{5,4},{6,7},{7,6},{8,9},{9,8},{10,11... | collective-permute-start | bytes 1572872 | tf_op jit(solution)/shard_map/ppermute | solution.py:248
  28.6 9.1 %collective-permute-start.6 = (bf16[2,336,128]{2,1,0:T(8,128)(2,1)S(1)}, bf16[2,336,128]{2,1,0:T(8,128)(2,1)S(1)}, u32[]{:S(2)}, u32[]{:S(2)}) collective-permute-start(bf16[2,336,128]{2,1,0:T(8,128)(2,1)S(1)} %copy-done.9), channel_id=1, source_target_pairs={{0,12},{1,13},{2,14},{3,15},{4,8},{5,9},{6,10},{7,11},{8,4},{9,5},... | collective-permute-start | bytes 516104 | tf_op jit(solution)/shard_map/ppermute | solution.py:248
  29.1 21.3 %collective-permute-start.7 = (bf16[2,336,128]{2,1,0:T(8,128)(2,1)S(1)}, bf16[2,336,128]{2,1,0:T(8,128)(2,1)S(1)}, u32[]{:S(2)}, u32[]{:S(2)}) collective-permute-start(bf16[2,336,128]{2,1,0:T(8,128)(2,1)S(1)} %copy-done.8), channel_id=1, source_target_pairs={{0,10},{1,11},{2,8},{3,9},{4,14},{5,15},{6,12},{7,13},{8,2},{9,3},... | collective-permute-start | bytes 516104 | tf_op jit(solution)/shard_map/ppermute | solution.py:248
  30.4 22.3 %collective-permute-start.8 = (bf16[2,336,128]{2,1,0:T(8,128)(2,1)S(1)}, bf16[2,336,128]{2,1,0:T(8,128)(2,1)S(1)}, u32[]{:S(2)}, u32[]{:S(2)}) collective-permute-start(bf16[2,336,128]{2,1,0:T(8,128)(2,1)S(1)} %copy-done.7), channel_id=1, source_target_pairs={{0,8},{1,9},{2,10},{3,11},{4,12},{5,13},{6,14},{7,15},{8,0},{9,1},... | collective-permute-start | bytes 516104 | tf_op jit(solution)/shard_map/ppermute | solution.py:248
  52.8 2.0 %collective-permute-start.9 = (bf16[2,2,384,128]{3,2,1,0:T(8,128)(2,1)S(1)}, bf16[2,2,384,128]{3,2,1,0:T(8,128)(2,1)S(1)}, u32[]{:S(2)}, u32[]{:S(2)}) collective-permute-start(bf16[2,2,384,128]{3,2,1,0:T(8,128)(2,1)S(1)} %get-tuple-element.37.refs_3_), channel_id=1, source_target_pairs={{0,1},{1,0},{2,3},{3,2},{4,5},{5,4},{6,7},{7,6},{8,9},{9,8},{10,11... | collective-permute-start | bytes 1179656 | tf_op jit(solution)/shard_map/ppermute | solution.py:248
  56.4 3.6 %copy-start.10 = (s32[76]{0:T(128)S(1)}, s32[76]{0:T(128)}, u32[]{:S(2)}) copy-start(s32[76]{0:T(128)} %param.10) | copy-start | bytes 916
  56.4 14.7 %copy-start = (bf16[128,2048]{1,0:T(8,128)(2,1)S(1)}, bf16[128,2048]{1,0:T(8,128)(2,1)}, u32[]{:S(2)}) copy-start(bf16[128,2048]{1,0:T(8,128)(2,1)} %refs_2_.1) | copy-start | bytes 1572868
  56.4 14.7 %all-to-all-start = ((bf16[8,2,80,128]{3,2,1,0:T(8,128)(2,1)}), bf16[8,2,80,128]{3,2,1,0:T(8,128)(2,1)S(1)}, u32[]{:S(2)}, u32[]{:S(2)}) async-start(bf16[8,2,80,128]{3,2,1,0:T(8,128)(2,1)} %complete.1), calls=%async_computation | async-start | bytes 655360 | tf_op jit(solution)/shard_map/all_to_all | solution.py:389

commit v7 on v5

--- a/solution.py
+++ b/solution.py
@@ -247,6 +247,7 @@
             + [whole((text, head_size))] * 2,
             scratch_shapes=scratch,
         ),
+        compiler_params=pltpu.CompilerParams(vmem_limit_bytes=24 * 2**20),
         name="prepare_rest",
     )(me, slots, q_gain, k_gain, qkv, k_cache, v_cache, text_k, text_v, met[groups])
     arrived = dict(met)

time: 64.4 us -> 61 us (0.947)
  local copies, waits for them, and re-layouts: 4.1 us -> 1.26 us
  Pallas kernels: 11.6 us -> 9.33 us
  starting transfers between devices: 30.7 us -> 31.8 us
  waiting for transfers between devices: 17.5 us -> 18.2 us
    unnamed x14 -> x18, local copies, waits for them, and re-layouts: 4.09 us -> 1.25 us
    pallas_call x1, Pallas kernels: 3.27 us -> 0.88 us  [shards(): pl.pallas_call(lambda *refs: prepare_kernel(per_group, padded, late, Fals...]
    ppermute x15, starting transfers between devices: 27 us -> 28.1 us  [trade(): return lax.ppermute(block, 'seq', [(a, a ^ step) for a in range(count)])]
    ppermute x15, waiting for transfers between devices: 6.51 us -> 7.18 us  [trade(): return lax.ppermute(block, 'seq', [(a, a ^ step) for a in range(count)])]
  transfers between devices with their start and end apart: 16 -> 16, of which waited for: 7 -> 3; matrix products, arithmetic and copies ran while one was open for 0% -> 0% of each run, Pallas kernels for 5% -> 1%
where the time goes in v7:
time: 61 us; the launch traced here: 60.8 us
  starting transfers between devices  31.8 us (52%)
  waiting for transfers between devices  18.2 us (30%)
  Pallas kernels  9.33 us (15%)
  local copies, waits for them, and re-layouts  1.26 us (2%)
    ppermute x15, starting transfers between devices, trade(): return lax.ppermute(block, 'seq', [(a, a ^ step) for a in range(count)])  28.1 us
    all_to_all x1, waiting for transfers between devices, shards(): lax.all_to_all(result, 'seq', split_axis=0, concat_axis=0, tiled=True)  11 us
    ppermute x15, waiting for transfers between devices, trade(): return lax.ppermute(block, 'seq', [(a, a ^ step) for a in range(count)])  7.18 us
    pallas_call x1, Pallas kernels, shards(): pl.pallas_call(lambda *refs: attend_kernel(tokens, query_rows, 256, steps...  5.16 us
    all_to_all x1, starting transfers between devices, shards(): lax.all_to_all(result, 'seq', split_axis=0, concat_axis=0, tiled=True)  3.67 us
    pallas_call x1, Pallas kernels, shards(): pl.pallas_call(lambda *refs: prepare_kernel(per_group, padded, early, Tru...  2.21 us
    unnamed x18, local copies, waits for them, and re-layouts  1.25 us
  transfers between devices with their start and end apart: 16, of which 3 were waited for; matrix products, arithmetic and copies ran while one was open for 0% of the time, Pallas kernels for 1%

profile of v7, /device:TPU:0, one launch (start us, length us, event | category | flops | bytes accessed | tf_op | source)
XLA Modules:
  0.0 60.8 jit_solution(9173152876419554669)
XLA Ops:
  0.0 0.0 copy-start
  0.0 0.0 copy-start.1
  0.0 2.2 %prepare_first.1 = (bf16[336,128]{1,0:T(8,128)(2,1)}, bf16[336,128]{1,0:T(8,128)(2,1)}, bf16[336,128]{1,0:T(8,128)(2,1)}, bf16[336,128]{1,0:T(8,128)(2,1)}) custom-call(s32[1]{0:T(128)} %bitcast.1.refs_0_, s32[1,76]{1,0:T(1,128)} %bitcast.14, f32[1,128]{1,0:T(1,128)} %bitcast.10, f32[1,128]{1,0:T(1,128)} %bitcast.12, bf16[3,76,2048]{2,1,0:T(8,128)(2,1)} %bitcast.5, ...), custom_call_target="tpu_custom_call" | custom-call | tf_op jit(solution)/shard_map/prepare_first/pallas_call | solution.py:214
  2.2 0.5 collective-permute-start
  2.7 5.7 %collective-permute-start.1 = (bf16[336,128]{1,0:T(8,128)(2,1)}, bf16[336,128]{1,0:T(8,128)(2,1)S(1)}, u32[]{:S(2)}, u32[]{:S(2)}) collective-permute-start(bf16[336,128]{1,0:T(8,128)(2,1)} %get-tuple-element.25), channel_id=1, source_target_pairs={{0,15},{1,14},{2,13},{3,12},{4,11},{5,10},{6,9},{7,8},{8,7},{9,6},... | collective-permute-start | bytes 258056 | tf_op jit(solution)/shard_map/ppermute | solution.py:171
  8.4 0.0 collective-permute-start.10
  8.4 3.4 %collective-permute-start.2 = (bf16[336,128]{1,0:T(8,128)(2,1)}, bf16[336,128]{1,0:T(8,128)(2,1)S(1)}, u32[]{:S(2)}, u32[]{:S(2)}) collective-permute-start(bf16[336,128]{1,0:T(8,128)(2,1)} %get-tuple-element.26), channel_id=1, source_target_pairs={{0,14},{1,15},{2,12},{3,13},{4,10},{5,11},{6,8},{7,9},{8,6},{9,7},... | collective-permute-start | bytes 258056 | tf_op jit(solution)/shard_map/ppermute | solution.py:171
  11.8 0.0 collective-permute-done.refs_9_.refs_11_
  11.8 0.0 copy-done
  11.8 0.0 copy-done.1
  11.8 0.0 copy-done.2
  11.8 0.0 copy-done.3
  11.8 0.0 copy-done.6
  11.8 0.0 copy-done.7
  11.9 0.0 copy-done.8
  11.9 0.0 copy-start.4
  11.9 1.2 %copy-done.4 = bf16[256,2048]{1,0:T(8,128)(2,1)S(1)} copy-done((bf16[256,2048]{1,0:T(8,128)(2,1)S(1)}, bf16[256,2048]{1,0:T(8,128)(2,1)}, u32[]{:S(2)}) %copy-start.4) | copy-done | bytes 1048600
  13.1 0.9 %prepare_rest.1 = (bf16[336,128]{1,0:T(8,128)(2,1)S(1)}, bf16[336,128]{1,0:T(8,128)(2,1)S(1)}, bf16[336,128]{1,0:T(8,128)(2,1)S(1)}, bf16[336,128]{1,0:T(8,128)(...) custom-call(s32[1]{0:T(128)} %bitcast.1.refs_0_, ...), custom_call_target="tpu_custom_call" | custom-call | tf_op jit(solution)/shard_map/prepare_rest/pallas_call | solution.py:231
  14.0 0.1 collective-permute-start.11
  14.1 0.6 collective-permute-start.12
  14.6 0.0 collective-permute-done.1.refs_2_
  14.6 2.1 %collective-permute-start.13 = (bf16[336,128]{1,0:T(8,128)(2,1)S(1)}, bf16[336,128]{1,0:T(8,128)(2,1)S(1)}, u32[]{:S(2)}, u32[]{:S(2)}) collective-permute-start(bf16[336,128]{1,0:T(8,128)(2,1)S(1)} %get-tuple-element.37), channel_id=1, source_target_pairs={{0,6},{1,7},{2,4},{3,5},{4,2},{5,3},{6,0},{7,1},{8,14},{9,15},{10,... | collective-permute-start | bytes 258056 | tf_op jit(solution)/shard_map/ppermute | solution.py:171
  16.8 0.0 collective-permute-done.10.refs_12_
  16.8 3.2 %collective-permute-start.14 = (bf16[336,128]{1,0:T(8,128)(2,1)S(1)}, bf16[336,128]{1,0:T(8,128)(2,1)S(1)}, u32[]{:S(2)}, u32[]{:S(2)}) collective-permute-start(bf16[336,128]{1,0:T(8,128)(2,1)S(1)} %get-tuple-element.38), channel_id=1, source_target_pairs={{0,11},{1,10},{2,9},{3,8},{4,15},{5,14},{6,13},{7,12},{8,3},{9,2},... | collective-permute-start | bytes 258056 | tf_op jit(solution)/shard_map/ppermute | solution.py:171
  19.9 0.0 collective-permute-done.2.refs_3_
  19.9 1.0 %collective-permute-start.3 = (bf16[336,128]{1,0:T(8,128)(2,1)S(1)}, bf16[336,128]{1,0:T(8,128)(2,1)S(1)}, u32[]{:S(2)}, u32[]{:S(2)}) collective-permute-start(bf16[336,128]{1,0:T(8,128)(2,1)S(1)} %get-tuple-element.27), channel_id=1, source_target_pairs={{0,5},{1,4},{2,7},{3,6},{4,1},{5,0},{6,3},{7,2},{8,13},{9,12},{10,... | collective-permute-start | bytes 258056 | tf_op jit(solution)/shard_map/ppermute | solution.py:171
  20.9 0.0 collective-permute-done.11.refs_13_
  20.9 6.9 %collective-permute-start.4 = (bf16[336,128]{1,0:T(8,128)(2,1)S(1)}, bf16[336,128]{1,0:T(8,128)(2,1)S(1)}, u32[]{:S(2)}, u32[]{:S(2)}) collective-permute-start(bf16[336,128]{1,0:T(8,128)(2,1)S(1)} %get-tuple-element.28), channel_id=1, source_target_pairs={{0,10},{1,11},{2,8},{3,9},{4,14},{5,15},{6,12},{7,13},{8,2},{9,3},... | collective-permute-start | bytes 258056 | tf_op jit(solution)/shard_map/ppermute | solution.py:171
  27.8 0.0 collective-permute-done.12.refs_14_
  27.8 0.0 collective-permute-start.5
  27.8 0.0 collective-permute-done.13.refs_15_
  27.9 0.1 collective-permute-start.6
  27.9 0.0 collective-permute-done.14.refs_16_
  27.9 0.4 collective-permute-start.7
  28.3 0.0 collective-permute-done.3.refs_4_
  28.3 3.7 %collective-permute-start.8 = (bf16[336,128]{1,0:T(8,128)(2,1)S(1)}, bf16[336,128]{1,0:T(8,128)(2,1)S(1)}, u32[]{:S(2)}, u32[]{:S(2)}) collective-permute-start(bf16[336,128]{1,0:T(8,128)(2,1)S(1)} %get-tuple-element.32), channel_id=1, source_target_pairs={{0,8},{1,9},{2,10},{3,11},{4,12},{5,13},{6,14},{7,15},{8,0},{9,1},... | collective-permute-start | bytes 258056 | tf_op jit(solution)/shard_map/ppermute | solution.py:171
  32.0 0.0 collective-permute-done.4.refs_5_
  32.0 0.6 collective-permute-start.9
  32.6 1.6 %collective-permute-done.5.refs_6_ = bf16[336,128]{1,0:T(8,128)(2,1)S(1)} collective-permute-done((bf16[336,128]{1,0:T(8,128)(2,1)S(1)}, bf16[336,128]{1,0:T(8,128)(2,1)S(1)}, u32[]{:S(2)}, u32[]{:S(2)}) %collective-permute-start.5) | collective-permute-done | bytes 86048 | tf_op jit(solution)/shard_map/ppermute | solution.py:171
  34.2 0.0 collective-permute-done.6.refs_7_
  34.2 0.0 collective-permute-done.7.refs_8_
  34.2 5.6 %collective-permute-done.8.refs_9_ = bf16[336,128]{1,0:T(8,128)(2,1)S(1)} collective-permute-done((bf16[336,128]{1,0:T(8,128)(2,1)S(1)}, bf16[336,128]{1,0:T(8,128)(2,1)S(1)}, u32[]{:S(2)}, u32[]{:S(2)}) %collective-permute-start.8) | collective-permute-done | bytes 86048 | tf_op jit(solution)/shard_map/ppermute | solution.py:171
  39.8 0.0 collective-permute-done.9.refs_10_
  39.8 5.2 %attend.1 = bf16[16,80,128]{2,1,0:T(8,128)(2,1)} custom-call(s32[1]{0:T(128)} %bitcast.1.refs_0_, bf16[336,128]{1,0:T(8,128)(2,1)S(1)} %get-tuple-element.24.refs_1_, bf16[336,128]{1,0:T(8,128)(2,1)S(1)} %collective-permute-done.1.refs_2_, bf16[336,128]{1,0:T(8,128)(2,1)S(1)} %collective-permute-done.2.refs_3_, ...), custom_call_target="tpu_custom_call" | custom-call | tf_op jit(solution)/shard_map/attend/pallas_call | solution.py:261
  44.9 3.7 %all-to-all-start = ((bf16[16,80,128]{2,1,0:T(8,128)(2,1)}), bf16[16,80,128]{2,1,0:T(8,128)(2,1)S(1)}, u32[]{:S(2)}, u32[]{:S(2)}) async-start(bf16[16,80,128]{2,1,0:T(8,128)(2,1)} %attend.1), calls=%async_computation | async-start | bytes 655360 | tf_op jit(solution)/shard_map/all_to_all | solution.py:282
  48.6 11.0 %all-to-all-done.refs_1_ = bf16[16,80,128]{2,1,0:T(8,128)(2,1)S(1)} async-done(((bf16[16,80,128]{2,1,0:T(8,128)(2,1)}), bf16[16,80,128]{2,1,0:T(8,128)(2,1)S(1)}, u32[]{:S(2)}, u32[]{:S(2)}) %all-to-all-start) | async-done | bytes 327712 | tf_op jit(solution)/shard_map/all_to_all | solution.py:282
  59.7 0.0 copy-done.5
  59.7 1.1 %finish.1 = bf16[128,2048]{1,0:T(8,128)(2,1)} custom-call(s32[1,80]{1,0:T(1,128)S(1)} %pad.4.refs_0_, bf16[16,80,128]{2,1,0:T(8,128)(2,1)S(1)} %all-to-all-done.refs_1_, bf16[128,2048]{1,0:T(8,128)(2,1)S(1)} %copy-done.5), custom_call_target="tpu_custom_call" | custom-call | tf_op jit(solution)/shard_map/finish/pallas_call | solution.py:285
  (7 shorter events, 0.0 us)
Async XLA Ops:
  0.0 11.8 %copy-start = (bf16[76,3,2048]{2,0,1:T(8,128)(2,1)S(1)}, bf16[76,3,2048]{2,0,1:T(8,128)(2,1)}, u32[]{:S(2)}) copy-start(bf16[76,3,2048]{2,0,1:T(8,128)(2,1)} %param.9) | copy-start | bytes 2801668
  0.0 11.8 %copy-start.1 = (bf16[128,2048]{1,0:T(8,128)(2,1)S(1)}, bf16[128,2048]{1,0:T(8,128)(2,1)}, u32[]{:S(2)}) copy-start(bf16[128,2048]{1,0:T(8,128)(2,1)} %refs_5_.3) | copy-start | bytes 1572868
  0.0 11.8 %copy-start.2 = (bf16[128,2048]{1,0:T(8,128)(2,1)S(1)}, bf16[128,2048]{1,0:T(8,128)(2,1)}, u32[]{:S(2)}) copy-start(bf16[128,2048]{1,0:T(8,128)(2,1)} %refs_6_.3) | copy-start | bytes 1572868
  0.0 11.8 %copy-start.3 = (bf16[256,2048]{1,0:T(8,128)(2,1)S(1)}, bf16[256,2048]{1,0:T(8,128)(2,1)}, u32[]{:S(2)}) copy-start(bf16[256,2048]{1,0:T(8,128)(2,1)} %refs_7_.1) | copy-start | bytes 3145732
  2.2 9.6 %collective-permute-start = (bf16[336,128]{1,0:T(8,128)(2,1)}, bf16[336,128]{1,0:T(8,128)(2,1)S(1)}, u32[]{:S(2)}, u32[]{:S(2)}) collective-permute-start(bf16[336,128]{1,0:T(8,128)(2,1)} %get-tuple-element.23), channel_id=1, source_target_pairs={{0,1},{1,0},{2,3},{3,2},{4,5},{5,4},{6,7},{7,6},{8,9},{9,8},{10,11... | collective-permute-start | bytes 258056 | tf_op jit(solution)/shard_map/ppermute | solution.py:171
  2.7 11.9 %collective-permute-start.1 = (bf16[336,128]{1,0:T(8,128)(2,1)}, bf16[336,128]{1,0:T(8,128)(2,1)S(1)}, u32[]{:S(2)}, u32[]{:S(2)}) collective-permute-start(bf16[336,128]{1,0:T(8,128)(2,1)} %get-tuple-element.25), channel_id=1, source_target_pairs={{0,15},{1,14},{2,13},{3,12},{4,11},{5,10},{6,9},{7,8},{8,7},{9,6},... | collective-permute-start | bytes 258056 | tf_op jit(solution)/shard_map/ppermute | solution.py:171
  8.4 3.5 %copy-start.6 = (f32[128]{0:T(128)S(1)}, f32[128]{0:T(128)}, u32[]{:S(2)}) copy-start(f32[128]{0:T(128)} %param.16) | copy-start | bytes 1540
  8.4 3.5 %copy-start.7 = (f32[128]{0:T(128)S(1)}, f32[128]{0:T(128)}, u32[]{:S(2)}) copy-start(f32[128]{0:T(128)} %param.17) | copy-start | bytes 1540
  8.4 3.5 %copy-start.8 = (s32[76]{0:T(128)S(1)}, s32[76]{0:T(128)}, u32[]{:S(2)}) copy-start(s32[76]{0:T(128)} %param.10) | copy-start | bytes 916
  8.4 8.4 %collective-permute-start.10 = (bf16[336,128]{1,0:T(8,128)(2,1)}, bf16[336,128]{1,0:T(8,128)(2,1)S(1)}, u32[]{:S(2)}, u32[]{:S(2)}) collective-permute-start(bf16[336,128]{1,0:T(8,128)(2,1)} %get-tuple-element.34), channel_id=1, source_target_pairs={{0,13},{1,12},{2,15},{3,14},{4,9},{5,8},{6,11},{7,10},{8,5},{9,4},... | collective-permute-start | bytes 258056 | tf_op jit(solution)/shard_map/ppermute | solution.py:171
  8.4 11.6 %collective-permute-start.2 = (bf16[336,128]{1,0:T(8,128)(2,1)}, bf16[336,128]{1,0:T(8,128)(2,1)S(1)}, u32[]{:S(2)}, u32[]{:S(2)}) collective-permute-start(bf16[336,128]{1,0:T(8,128)(2,1)} %get-tuple-element.26), channel_id=1, source_target_pairs={{0,14},{1,15},{2,12},{3,13},{4,10},{5,11},{6,8},{7,9},{8,6},{9,7},... | collective-permute-start | bytes 258056 | tf_op jit(solution)/shard_map/ppermute | solution.py:171
  11.9 1.2 %copy-start.4 = (bf16[256,2048]{1,0:T(8,128)(2,1)S(1)}, bf16[256,2048]{1,0:T(8,128)(2,1)}, u32[]{:S(2)}) copy-start(bf16[256,2048]{1,0:T(8,128)(2,1)} %refs_8_.3) | copy-start | bytes 3145732
  14.0 6.9 %collective-permute-start.11 = (bf16[336,128]{1,0:T(8,128)(2,1)S(1)}, bf16[336,128]{1,0:T(8,128)(2,1)S(1)}, u32[]{:S(2)}, u32[]{:S(2)}) collective-permute-start(bf16[336,128]{1,0:T(8,128)(2,1)S(1)} %get-tuple-element.35), channel_id=1, source_target_pairs={{0,7},{1,6},{2,5},{3,4},{4,3},{5,2},{6,1},{7,0},{8,15},{9,14},{10,... | collective-permute-start | bytes 258056 | tf_op jit(solution)/shard_map/ppermute | solution.py:171
  14.1 13.8 %collective-permute-start.12 = (bf16[336,128]{1,0:T(8,128)(2,1)S(1)}, bf16[336,128]{1,0:T(8,128)(2,1)S(1)}, u32[]{:S(2)}, u32[]{:S(2)}) collective-permute-start(bf16[336,128]{1,0:T(8,128)(2,1)S(1)} %get-tuple-element.36), channel_id=1, source_target_pairs={{0,12},{1,13},{2,14},{3,15},{4,8},{5,9},{6,10},{7,11},{8,4},{9,5},... | collective-permute-start | bytes 258056 | tf_op jit(solution)/shard_map/ppermute | solution.py:171
  14.6 13.2 %collective-permute-start.13 = (bf16[336,128]{1,0:T(8,128)(2,1)S(1)}, bf16[336,128]{1,0:T(8,128)(2,1)S(1)}, u32[]{:S(2)}, u32[]{:S(2)}) collective-permute-start(bf16[336,128]{1,0:T(8,128)(2,1)S(1)} %get-tuple-element.37), channel_id=1, source_target_pairs={{0,6},{1,7},{2,4},{3,5},{4,2},{5,3},{6,0},{7,1},{8,14},{9,15},{10,... | collective-permute-start | bytes 258056 | tf_op jit(solution)/shard_map/ppermute | solution.py:171
  16.8 11.2 %collective-permute-start.14 = (bf16[336,128]{1,0:T(8,128)(2,1)S(1)}, bf16[336,128]{1,0:T(8,128)(2,1)S(1)}, u32[]{:S(2)}, u32[]{:S(2)}) collective-permute-start(bf16[336,128]{1,0:T(8,128)(2,1)S(1)} %get-tuple-element.38), channel_id=1, source_target_pairs={{0,11},{1,10},{2,9},{3,8},{4,15},{5,14},{6,13},{7,12},{8,3},{9,2},... | collective-permute-start | bytes 258056 | tf_op jit(solution)/shard_map/ppermute | solution.py:171
  19.9 8.4 %collective-permute-start.3 = (bf16[336,128]{1,0:T(8,128)(2,1)S(1)}, bf16[336,128]{1,0:T(8,128)(2,1)S(1)}, u32[]{:S(2)}, u32[]{:S(2)}) collective-permute-start(bf16[336,128]{1,0:T(8,128)(2,1)S(1)} %get-tuple-element.27), channel_id=1, source_target_pairs={{0,5},{1,4},{2,7},{3,6},{4,1},{5,0},{6,3},{7,2},{8,13},{9,12},{10,... | collective-permute-start | bytes 258056 | tf_op jit(solution)/shard_map/ppermute | solution.py:171
  20.9 11.1 %collective-permute-start.4 = (bf16[336,128]{1,0:T(8,128)(2,1)S(1)}, bf16[336,128]{1,0:T(8,128)(2,1)S(1)}, u32[]{:S(2)}, u32[]{:S(2)}) collective-permute-start(bf16[336,128]{1,0:T(8,128)(2,1)S(1)} %get-tuple-element.28), channel_id=1, source_target_pairs={{0,10},{1,11},{2,8},{3,9},{4,14},{5,15},{6,12},{7,13},{8,2},{9,3},... | collective-permute-start | bytes 258056 | tf_op jit(solution)/shard_map/ppermute | solution.py:171
  27.8 6.3 %collective-permute-start.5 = (bf16[336,128]{1,0:T(8,128)(2,1)S(1)}, bf16[336,128]{1,0:T(8,128)(2,1)S(1)}, u32[]{:S(2)}, u32[]{:S(2)}) collective-permute-start(bf16[336,128]{1,0:T(8,128)(2,1)S(1)} %get-tuple-element.29), channel_id=1, source_target_pairs={{0,4},{1,5},{2,6},{3,7},{4,0},{5,1},{6,2},{7,3},{8,12},{9,13},{10,... | collective-permute-start | bytes 258056 | tf_op jit(solution)/shard_map/ppermute | solution.py:171
  27.9 6.3 %collective-permute-start.6 = (bf16[336,128]{1,0:T(8,128)(2,1)S(1)}, bf16[336,128]{1,0:T(8,128)(2,1)S(1)}, u32[]{:S(2)}, u32[]{:S(2)}) collective-permute-start(bf16[336,128]{1,0:T(8,128)(2,1)S(1)} %get-tuple-element.30), channel_id=1, source_target_pairs={{0,9},{1,8},{2,11},{3,10},{4,13},{5,12},{6,15},{7,14},{8,1},{9,0},... | collective-permute-start | bytes 258056 | tf_op jit(solution)/shard_map/ppermute | solution.py:171
  27.9 6.2 %collective-permute-start.7 = (bf16[336,128]{1,0:T(8,128)(2,1)S(1)}, bf16[336,128]{1,0:T(8,128)(2,1)S(1)}, u32[]{:S(2)}, u32[]{:S(2)}) collective-permute-start(bf16[336,128]{1,0:T(8,128)(2,1)S(1)} %get-tuple-element.31), channel_id=1, source_target_pairs={{0,3},{1,2},{2,1},{3,0},{4,7},{5,6},{6,5},{7,4},{8,11},{9,10},{10,... | collective-permute-start | bytes 258056 | tf_op jit(solution)/shard_map/ppermute | solution.py:171
  28.3 11.4 %collective-permute-start.8 = (bf16[336,128]{1,0:T(8,128)(2,1)S(1)}, bf16[336,128]{1,0:T(8,128)(2,1)S(1)}, u32[]{:S(2)}, u32[]{:S(2)}) collective-permute-start(bf16[336,128]{1,0:T(8,128)(2,1)S(1)} %get-tuple-element.32), channel_id=1, source_target_pairs={{0,8},{1,9},{2,10},{3,11},{4,12},{5,13},{6,14},{7,15},{8,0},{9,1},... | collective-permute-start | bytes 258056 | tf_op jit(solution)/shard_map/ppermute | solution.py:171
  32.0 7.7 %collective-permute-start.9 = (bf16[336,128]{1,0:T(8,128)(2,1)S(1)}, bf16[336,128]{1,0:T(8,128)(2,1)S(1)}, u32[]{:S(2)}, u32[]{:S(2)}) collective-permute-start(bf16[336,128]{1,0:T(8,128)(2,1)S(1)} %get-tuple-element.33), channel_id=1, source_target_pairs={{0,2},{1,3},{2,0},{3,1},{4,6},{5,7},{6,4},{7,5},{8,10},{9,11},{10,... | collective-permute-start | bytes 258056 | tf_op jit(solution)/shard_map/ppermute | solution.py:171
  44.9 14.7 %copy-start.5 = (bf16[128,2048]{1,0:T(8,128)(2,1)S(1)}, bf16[128,2048]{1,0:T(8,128)(2,1)}, u32[]{:S(2)}) copy-start(bf16[128,2048]{1,0:T(8,128)(2,1)} %refs_2_.1) | copy-start | bytes 1572868
  44.9 14.7 %all-to-all-start = ((bf16[16,80,128]{2,1,0:T(8,128)(2,1)}), bf16[16,80,128]{2,1,0:T(8,128)(2,1)S(1)}, u32[]{:S(2)}, u32[]{:S(2)}) async-start(bf16[16,80,128]{2,1,0:T(8,128)(2,1)} %attend.1), calls=%async_computation | async-start | bytes 655360 | tf_op jit(solution)/shard_map/all_to_all | solution.py:282

commit v8 on v6

--- a/solution.py
+++ b/solution.py
@@ -172,69 +172,57 @@
 
 def row_blocks(ref, padded):
     rows = ref.shape[1]
-    return [slice(first, min(first + 5 * padded, rows)) for first in range(0, rows, 5 * padded)]
-
-
-def attend_early_kernel(tokens, padded, *refs):
+    return [slice(first, min(first + 4 * padded, rows)) for first in range(0, rows, 4 * padded)]
+
+
+def attend_kernel(tokens, padded, *refs):
     shared, queries_ref, sums_ref = refs[:-2], refs[-2], refs[-1]
     for head in range(queries_ref.shape[0]):
         for rows in row_blocks(queries_ref, padded):
             sums_ref[head, rows] = add_shared(None, queries_ref[head, rows], shared, head, tokens)
 
 
-def attend_late_kernel(tokens, padded, *refs):
-    shared = refs[:-5]
-    early_ref, early_sums_ref, late_ref, early_out_ref, late_out_ref = refs[-5:]
-    for head in range(early_ref.shape[0]):
-        for rows in row_blocks(early_ref, padded):
-            early_out_ref[head, rows] = add_shared(
-                early_sums_ref[head, rows], early_ref[head, rows], shared[-1:], head, tokens
+def complete_kernel(tokens, first, shared_ref, queries_ref, sums_ref, *outs):
+    heads, padded, head_size = outs[0].shape
+    for head in range(heads):
+        for number in range(0, len(outs), 4):
+            mine = outs[number : number + 4]
+            at = (first + number) * padded
+            rows = slice(at, at + len(mine) * padded)
+            sums = add_shared(
+                sums_ref[head, rows], queries_ref[head, rows], [shared_ref], head, tokens
             )
-        for rows in row_blocks(late_ref, padded):
-            late_out_ref[head, rows] = add_shared(
-                None, late_ref[head, rows], shared, head, tokens
-            )
-
-
-def complete_kernel(tokens, steps, me_ref, shared_ref, *refs):
+            result = (sums[:, :head_size] / sums[:, head_size:]).astype(jnp.bfloat16)
+            for turn, out_ref in enumerate(mine):
+                out_ref[head] = result[turn * padded : (turn + 1) * padded]
+
+
+def finish_kernel(heads, steps, me_ref, slots_ref, cache_ref, *rest):
+    returned, out_ref = rest[:-1], rest[-1]
+    tokens = cache_ref.shape[0]
+    head_size = returned[0].shape[2]
+    groups = slots_ref.shape[0]
     outer = me_ref[0] // INNER
-    out_ref = refs[-1]
-    heads, padded, head_size = out_ref.shape[1:]
-    for head in range(heads):
-        number = 0
-        for queries_ref, sums_ref in (refs[0:2], refs[2:4]):
-            for rows in row_blocks(queries_ref, padded):
-                sums = add_shared(
-                    sums_ref[head, rows], queries_ref[head, rows], [shared_ref], head, tokens
-                )
-                result = (sums[:, :head_size] / sums[:, head_size:]).astype(jnp.bfloat16)
-                for first in range(0, rows.stop - rows.start, padded):
-                    owner = lax.bitwise_xor(outer, steps[number])
-                    out_ref[owner, head] = result[first : first + padded]
-                    number += 1
-
-
-def finish_kernel(per_group, slots_ref, returned_ref, cache_ref, out_ref):
-    tokens = cache_ref.shape[0]
-    heads, _, head_size = returned_ref.shape[1:]
-    groups = slots_ref.shape[0]
-    mine = [place(slots_ref[group : group + 1], tokens) for group in range(groups)]
-    count = sum(jnp.sum(m.astype(jnp.float32), axis=1, keepdims=True) for m in mine)
-    is_fresh = count > 0.5
-    one_hot = [m.astype(jnp.bfloat16) for m in mine]
-    for number in range(cache_ref.shape[1] // head_size):
-        columns = slice(number * head_size, (number + 1) * head_size)
-        placed = sum(
-            jnp.dot(
-                one_hot[group],
-                returned_ref[number // heads * groups + group, number % heads],
-                preferred_element_type=jnp.float32,
-            )
-            for group in range(groups)
-        )
-        out_ref[:, columns] = jnp.where(
-            is_fresh, placed, cache_ref[:, columns].astype(jnp.float32)
-        ).astype(out_ref.dtype)
+    one_hot = []
+    owned = jnp.zeros((tokens, 1), jnp.float32)
+    for low in range(groups):
+        group = lax.bitwise_xor(outer % groups, low)
+        mine = place(slots_ref[pl.ds(group, 1)], tokens).astype(jnp.float32)
+        owned = owned + jnp.sum(mine, axis=1, keepdims=True)
+        one_hot.append(mine.astype(jnp.bfloat16))
+    is_fresh = owned > 0.5
+    for high in range(len(steps) // groups):
+        block = lax.bitwise_xor(outer // groups, high)
+        for head in range(heads):
+            at = (block * heads + head) * head_size
+            columns = pl.ds(pl.multiple_of(at, head_size), head_size)
+            placed = jnp.zeros((tokens, head_size), jnp.float32)
+            for low in range(groups):
+                made = returned[steps.index(high * groups + low)][head]
+                placed = placed + jnp.dot(one_hot[low], made, preferred_element_type=jnp.float32)
+            out_ref[:, columns] = jnp.where(
+                is_fresh, placed, cache_ref[:, columns].astype(jnp.float32)
+            ).astype(out_ref.dtype)
 
 
 def work(micros):
@@ -279,7 +267,7 @@
     in_vmem = pl.BlockSpec(memory_space=pltpu.VMEM)
     in_smem = pl.BlockSpec(memory_space=pltpu.SMEM)
 
-    def prepare(plan, with_text, name, *extra):
+    def prepare(plan, with_text, name, params, *extra):
         shapes = []
         for _, apart in plan:
             if apart:
@@ -307,102 +295,82 @@
                 pltpu.SemaphoreType.DMA((len(plan), 3)),
                 pltpu.SemaphoreType.DMA((2,)),
             ],
-            cost_estimate=work(20),
+            compiler_params=params,
             name=name,
         )(me, slots, q_gain, k_gain, qkv, k_cache, v_cache, *extra)
         return list(made)
 
     half = outers // 2
     far = list(reversed(range(half, outers)))
-    early = far[:1] + list(range(1, half))
-    late = far[1:]
-    block, own, own_queries = prepare([(far[0], False), (0, True)], False, "prepare_first")
+    near = list(range(1, half))
+    small = pltpu.CompilerParams(vmem_limit_bytes=24 * MIB)
+    block, own, own_queries = prepare(
+        [(far[0], False), (0, True)], False, "prepare_first", pltpu.CompilerParams()
+    )
     arrived = {far[0]: trade(block, far[0] * INNER)}
     other = trade(own, 1)
 
-    order = late[:1] + early[1:] + late[1:]
+    late = far[1:2]
+    for turn in range(half):
+        late += near[turn : turn + 1] + far[turn + 2 : turn + 3]
     *made, text_keys, text_values = prepare(
-        [(step, False) for step in order], True, "prepare_rest", text_k, text_v, other
-    )
-    for step, block in zip(order, made):
+        [(step, False) for step in late], True, "prepare_rest", small, text_k, text_v, other
+    )
+    for step, block in zip(late, made):
         arrived[step] = trade(block, step * INNER)
 
-    def gather(steps, name, *extra, after=()):
-        count = len(steps) + (1 if extra else 0)
-        shapes = [
+    steps = [far[0]] + late
+    count = len(steps) + 1
+    keys, queries, kept = pl.pallas_call(
+        lambda *refs: gather_kernel(tokens, True, len(steps), *refs),
+        out_shape=[
             shaped(heads, 2, len(steps) * tokens, head_size),
             shaped(heads, count * padded, head_size),
-        ]
-        if extra:
-            shapes.append(shaped(heads, 2, text + 2 * tokens, head_size))
-        return pl.pallas_call(
-            lambda *refs: gather_kernel(
-                tokens, bool(extra), len(steps), *refs[len(after) :]
-            ),
-            out_shape=shapes,
-            in_specs=[pl.BlockSpec(memory_space=pl.ANY)] * len(after)
-            + [in_vmem] * (len(steps) + len(extra)),
-            out_specs=[in_vmem] * len(shapes),
-            compiler_params=pltpu.CompilerParams(vmem_limit_bytes=24 * MIB),
-            cost_estimate=work(10),
-            name=name,
-        )(*after, *[arrived[step] for step in steps], *extra)
-
-    early_keys, early_queries, kept = gather(
-        early, "gather_early", own, other, text_keys, text_values, own_queries
-    )
-    early_other = trade(early_keys, 1)
-    sums_shape = shaped(heads, early_queries.shape[1], 2 * head_size, dtype=jnp.float32)
-    early_sums = pl.pallas_call(
-        lambda *refs: attend_early_kernel(tokens, padded, *refs),
-        out_shape=sums_shape,
-        in_specs=[in_vmem] * 4,
-        out_specs=in_vmem,
-        compiler_params=pltpu.CompilerParams(vmem_limit_bytes=24 * MIB),
-        cost_estimate=work(10),
-        name="attend_early",
-    )(kept, early_keys, early_other, early_queries)
-
-    late_keys, late_queries = gather(late, "gather_late", after=(early_sums,))
-    late_other = trade(late_keys, 1)
-    early_sums, late_sums = pl.pallas_call(
-        lambda *refs: attend_late_kernel(tokens, padded, *refs),
-        out_shape=[
-            sums_shape,
-            shaped(heads, late_queries.shape[1], 2 * head_size, dtype=jnp.float32),
+            shaped(heads, 2, text + 2 * tokens, head_size),
         ],
-        in_specs=[in_vmem] * 7,
-        out_specs=[in_vmem] * 2,
-        compiler_params=pltpu.CompilerParams(vmem_limit_bytes=24 * MIB),
-        cost_estimate=work(10),
-        name="attend_late",
-    )(kept, early_keys, early_other, late_keys, early_queries, early_sums, late_queries)
-    result = pl.pallas_call(
-        lambda *refs: complete_kernel(tokens, [0] + early + late, *refs),
-        out_shape=shaped(outers, heads, padded, head_size),
-        in_specs=[in_smem] + [in_vmem] * 5,
-        out_specs=in_vmem,
-        compiler_params=pltpu.CompilerParams(vmem_limit_bytes=24 * MIB),
-        name="complete",
-    )(me, late_other, early_queries, early_sums, late_queries, late_sums)
-
-    returned = lax.all_to_all(
-        result,
-        "seq",
-        split_axis=0,
-        concat_axis=0,
-        tiled=True,
-        axis_index_groups=[list(range(core, seq_count, INNER)) for core in range(INNER)],
-    )
-
-    return pl.pallas_call(
-        lambda *refs: finish_kernel(per_group, *refs),
-        out_shape=jax.ShapeDtypeStruct((tokens, row_width), attn_cache.dtype),
+        in_specs=[in_vmem] * (len(steps) + 5),
+        out_specs=[in_vmem] * 3,
+        compiler_params=small,
+        name="gather",
+    )(*[arrived[step] for step in steps], own, other, text_keys, text_values, own_queries)
+    other_keys = trade(keys, 1)
+    sums = pl.pallas_call(
+        lambda *refs: attend_kernel(tokens, padded, *refs),
+        out_shape=shaped(heads, count * padded, 2 * head_size, dtype=jnp.float32),
         in_specs=[in_vmem] * 3,
         out_specs=in_vmem,
-        compiler_params=pltpu.CompilerParams(vmem_limit_bytes=24 * MIB),
+        compiler_params=small,
+        cost_estimate=work(5),
+        name="attend",
+    )(kept, keys, queries)
+
+    sources = [0] + steps
+
+    def complete(first, last, name):
+        return pl.pallas_call(
+            lambda *refs: complete_kernel(tokens, first, *refs),
+            out_shape=[shaped(heads, padded, head_size)] * (last - first),
+            in_specs=[in_vmem] * 3,
+            out_specs=[in_vmem] * (last - first),
+            compiler_params=small,
+            name=name,
+        )(other_keys, queries, sums)
+
+    results = dict(zip(sources, complete(0, count, "complete")))
+    order = near[-1:] + far + near[:-1]
+    returned = {0: results[0]}
+    for step in order:
+        returned[step] = trade(results[step], step * INNER)
+    order = order + [0]
+
+    return pl.pallas_call(
+        lambda *refs: finish_kernel(heads, order, *refs),
+        out_shape=jax.ShapeDtypeStruct((tokens, row_width), attn_cache.dtype),
+        in_specs=[in_smem] + [in_vmem] * (2 + len(order)),
+        out_specs=in_vmem,
+        compiler_params=small,
         name="finish",
-    )(padded_slots, returned, attn_cache)
+    )(me, padded_slots, attn_cache, *[returned[step] for step in order])
 
 
 def solution(mesh):

time: 72.5 us -> 62.9 us (0.87)
  waiting for transfers between devices: 37.1 us -> 18.4 us
  starting transfers between devices: 17.8 us -> 29.6 us
  local copies, waits for them, and re-layouts: 4.14 us -> 2.49 us
  Pallas kernels: 13 us -> 12 us
    ppermute x10 -> x16, starting transfers between devices: 14.2 us -> 29.6 us  [trade(): return lax.ppermute(block, 'seq', [(a, a ^ distance) for a in range(count)])]
    all_to_all x1 -> x0, waiting for transfers between devices: 11.1 us -> none  [shards(): lax.all_to_all(result, 'seq', split_axis=0, concat_axis=0, tiled=True, ax...]
    ppermute x10 -> x16, waiting for transfers between devices: 26 us -> 18.4 us  [trade(): return lax.ppermute(block, 'seq', [(a, a ^ distance) for a in range(count)])]
    all_to_all x1 -> x0, starting transfers between devices: 3.56 us -> none  [shards(): lax.all_to_all(result, 'seq', split_axis=0, concat_axis=0, tiled=True, ax...]
    pallas_call x2, Pallas kernels: 6.52 us -> 4.74 us  [prepare(): pl.pallas_call(lambda *refs: prepare_kernel(plan, groups, per_group, padd...]
    unnamed x22, local copies, waits for them, and re-layouts: 4.13 us -> 2.48 us
    pallas_call x6 -> x4, Pallas kernels: 6.44 us -> 7.29 us  [the longest x1 3.37 us: shards(): pl.pallas_call(lambda *refs: attend_kernel(tokens, padded, *refs), out_sh...]
  transfers between devices with their start and end apart: 11 -> 16, of which waited for: 7 -> 7; matrix products, arithmetic and copies ran while one was open for 0% -> 0% of each run, Pallas kernels for 11% -> 9%
where the time goes in v8:
time: 62.9 us; the launch traced here: 62.7 us
  starting transfers between devices  29.6 us (47%)
  waiting for transfers between devices  18.4 us (29%)
  Pallas kernels  12 us (19%)
  local copies, waits for them, and re-layouts  2.49 us (4%)
    ppermute x16, starting transfers between devices, trade(): return lax.ppermute(block, 'seq', [(a, a ^ distance) for a in range(count)])  29.6 us
    ppermute x16, waiting for transfers between devices, trade(): return lax.ppermute(block, 'seq', [(a, a ^ distance) for a in range(count)])  18.4 us
    pallas_call x2, Pallas kernels, prepare(): pl.pallas_call(lambda *refs: prepare_kernel(plan, groups, per_group, padd...  4.74 us
    pallas_call x1, Pallas kernels, shards(): pl.pallas_call(lambda *refs: attend_kernel(tokens, padded, *refs), out_sh...  3.37 us
    pallas_call x1, Pallas kernels, complete(): pl.pallas_call(lambda *refs: complete_kernel(tokens, first, *refs), out_s...  2.68 us
    unnamed x22, local copies, waits for them, and re-layouts  2.48 us
  transfers between devices with their start and end apart: 16, of which 7 were waited for; matrix products, arithmetic and copies ran while one was open for 0% of the time, Pallas kernels for 9%

profile of v8, /device:TPU:0, one launch (start us, length us, event | category | flops | bytes accessed | tf_op | source)
XLA Modules:
  0.0 62.7 jit_solution(6336803847533091563)
XLA Ops:
  0.0 0.0 copy-start.2
  0.0 2.4 %prepare_first.1 = (bf16[2,336,128]{2,1,0:T(8,128)(2,1)}, bf16[2,256,128]{2,1,0:T(8,128)(2,1)}, bf16[2,80,128]{2,1,0:T(8,128)(2,1)}) custom-call(s32[1]{0:T(128)} %bitcast.refs_0_, s32[1,76]{1,0:T(1,128)} %bitcast.11, f32[1,128]{1,0:T(1,128)} %bitcast.7, f32[1,128]{1,0:T(1,128)} %bitcast.9, bf16[3,76,2048]{2,1,0:T(8,128)(2,1)} %bitcast.5, ...), custom_call_target="tpu_custom_call" | custom-call | tf_op jit(solution)/shard_map/prepare_first/pallas_call | solution.py:279
  2.4 0.5 collective-permute-start.1
  3.0 5.6 %collective-permute-start = (bf16[2,336,128]{2,1,0:T(8,128)(2,1)}, bf16[2,336,128]{2,1,0:T(8,128)(2,1)S(1)}, u32[]{:S(2)}, u32[]{:S(2)}) collective-permute-start(bf16[2,336,128]{2,1,0:T(8,128)(2,1)} %get-tuple-element.27), channel_id=1, source_target_pairs={{0,14},{1,15},{2,12},{3,13},{4,10},{5,11},{6,8},{7,9},{8,6},{9,7},... | collective-permute-start | bytes 516104 | tf_op jit(solution)/shard_map/ppermute | solution.py:236
  8.6 0.0 collective-permute-done.1.refs_9_.refs_8_
  8.6 0.0 copy-done.10
  8.6 0.0 copy-done.8
  8.6 0.0 copy-done.9
  8.7 0.0 copy-start.3
  8.7 1.2 %copy-done.3 = bf16[256,2048]{1,0:T(8,128)(2,1)S(1)} copy-done((bf16[256,2048]{1,0:T(8,128)(2,1)S(1)}, bf16[256,2048]{1,0:T(8,128)(2,1)}, u32[]{:S(2)}) %copy-start.3) | copy-done | bytes 1048600
  9.9 1.2 %copy-done.4 = bf16[256,2048]{1,0:T(8,128)(2,1)S(1)} copy-done((bf16[256,2048]{1,0:T(8,128)(2,1)S(1)}, bf16[256,2048]{1,0:T(8,128)(2,1)}, u32[]{:S(2)}) %copy-start.4) | copy-done | bytes 1048600
  11.1 2.3 %prepare_rest.1 = (bf16[2,336,128]{2,1,0:T(8,128)(2,1)S(1)}, bf16[2,336,128]{2,1,0:T(8,128)(2,1)S(1)}, bf16[2,336,128]{2,1,0:T(8,128)(2,1)S(1)}, bf16[2,336,128]...) custom-call(s32[1]{0:T(128)} %bitcast.refs_0_, ...), custom_call_target="tpu_custom_call" | custom-call | tf_op jit(solution)/shard_map/prepare_rest/pallas_call | solution.py:279
  13.5 0.6 collective-permute-start.2
  14.0 1.5 %collective-permute-start.3 = (bf16[2,336,128]{2,1,0:T(8,128)(2,1)S(1)}, bf16[2,336,128]{2,1,0:T(8,128)(2,1)S(1)}, u32[]{:S(2)}, u32[]{:S(2)}) collective-permute-start(bf16[2,336,128]{2,1,0:T(8,128)(2,1)S(1)} %get-tuple-element.30), channel_id=1, source_target_pairs={{0,2},{1,3},{2,0},{3,1},{4,6},{5,7},{6,4},{7,5},{8,10},{9,11},{10,... | collective-permute-start | bytes 516104 | tf_op jit(solution)/shard_map/ppermute | solution.py:236
  15.6 0.4 collective-permute-start.4
  16.0 3.4 %collective-permute-start.5 = (bf16[2,336,128]{2,1,0:T(8,128)(2,1)S(1)}, bf16[2,336,128]{2,1,0:T(8,128)(2,1)S(1)}, u32[]{:S(2)}, u32[]{:S(2)}) collective-permute-start(bf16[2,336,128]{2,1,0:T(8,128)(2,1)S(1)} %get-tuple-element.32), channel_id=1, source_target_pairs={{0,4},{1,5},{2,6},{3,7},{4,0},{5,1},{6,2},{7,3},{8,12},{9,13},{10,... | collective-permute-start | bytes 516104 | tf_op jit(solution)/shard_map/ppermute | solution.py:236
  19.4 0.0 collective-permute-done.refs_0_
  19.4 0.0 collective-permute-start.6
  19.4 3.3 %collective-permute-done.2.refs_1_ = bf16[2,336,128]{2,1,0:T(8,128)(2,1)S(1)} collective-permute-done((bf16[2,336,128]{2,1,0:T(8,128)(2,1)S(1)}, bf16[2,336,128]{2,1,0:T(8,128)(2,1)S(1)}, u32[]{:S(2)}, u32[]{:S(2)}) %collective-permute-start.2) | collective-permute-done | bytes 172064 | tf_op jit(solution)/shard_map/ppermute | solution.py:236
  22.6 6.0 %collective-permute-start.7 = (bf16[2,336,128]{2,1,0:T(8,128)(2,1)S(1)}, bf16[2,336,128]{2,1,0:T(8,128)(2,1)S(1)}, u32[]{:S(2)}, u32[]{:S(2)}) collective-permute-start(bf16[2,336,128]{2,1,0:T(8,128)(2,1)S(1)} %get-tuple-element.34), channel_id=1, source_target_pairs={{0,6},{1,7},{2,4},{3,5},{4,2},{5,3},{6,0},{7,1},{8,14},{9,15},{10,... | collective-permute-start | bytes 516104 | tf_op jit(solution)/shard_map/ppermute | solution.py:236
  28.7 0.0 collective-permute-done.3.refs_2_
  28.7 6.9 %collective-permute-done.4.refs_3_ = bf16[2,336,128]{2,1,0:T(8,128)(2,1)S(1)} collective-permute-done((bf16[2,336,128]{2,1,0:T(8,128)(2,1)S(1)}, bf16[2,336,128]{2,1,0:T(8,128)(2,1)S(1)}, u32[]{:S(2)}, u32[]{:S(2)}) %collective-permute-start.4) | collective-permute-done | bytes 172064 | tf_op jit(solution)/shard_map/ppermute | solution.py:236
  35.6 0.0 collective-permute-done.5.refs_4_
  35.6 3.3 %collective-permute-done.6.refs_5_ = bf16[2,336,128]{2,1,0:T(8,128)(2,1)S(1)} collective-permute-done((bf16[2,336,128]{2,1,0:T(8,128)(2,1)S(1)}, bf16[2,336,128]{2,1,0:T(8,128)(2,1)S(1)}, u32[]{:S(2)}, u32[]{:S(2)}) %collective-permute-start.6) | collective-permute-done | bytes 172064 | tf_op jit(solution)/shard_map/ppermute | solution.py:236
  38.9 0.0 collective-permute-done.7.refs_6_
  38.9 0.0 copy-done.7
  38.9 0.1 gather.1
  39.0 0.1 collective-permute-start.8
  39.1 3.4 %attend.1.refs_2_ = f32[2,640,256]{2,1,0:T(8,128)S(1)} custom-call(bf16[2,2,512,128]{3,2,1,0:T(8,128)(2,1)S(1)} %get-tuple-element.40.refs_0_, bf16[2,2,896,128]{3,2,1,0:T(8,128)(2,1)S(1)} %get-tuple-element.38.refs_1_, bf16[2,640,128]{2,1,0:T(8,128)(2,1)S(1)} %get-tuple-element.39.refs_2_.refs_1_), custom_call_target="tpu_custom_call" | custom-call | flops 5000000000 | bytes 15000000 | tf_op jit(solution)/shard_map/attend/pallas_call | solution.py:337
  42.5 0.0 copy-start.5
  42.5 0.0 collective-permute-done.8.refs_0_
  42.5 2.7 %complete.1 = (bf16[2,80,128]{2,1,0:T(8,128)(2,1)S(1)}, bf16[2,80,128]{2,1,0:T(8,128)(2,1)S(1)}, bf16[2,80,128]{2,1,0:T(8,128)(2,1)S(1)}, bf16[2,80,128]{2,1,0:T...) custom-call(bf16[2,2,896,128]{3,2,1,0:T(8,128)(2,1)S(1)} %collective, ...), custom_call_target="tpu_custom_call" | custom-call | tf_op jit(solution)/shard_map/complete/pallas_call | solution.py:350
  45.2 5.2 %collective-permute-start.10 = (bf16[2,80,128]{2,1,0:T(8,128)(2,1)S(1)}, bf16[2,80,128]{2,1,0:T(8,128)(2,1)S(1)}, u32[]{:S(2)}, u32[]{:S(2)}) collective-permute-start(bf16[2,80,128]{2,1,0:T(8,128)(2,1)S(1)} %get-tuple-element.42), channel_id=1, source_target_pairs={{0,14},{1,15},{2,12},{3,13},{4,10},{5,11},{6,8},{7,9},{8,6},{9,7},... | collective-permute-start | bytes 122888 | tf_op jit(solution)/shard_map/ppermute | solution.py:236
  50.4 0.8 %collective-permute-start.11 = (bf16[2,80,128]{2,1,0:T(8,128)(2,1)S(1)}, bf16[2,80,128]{2,1,0:T(8,128)(2,1)S(1)}, u32[]{:S(2)}, u32[]{:S(2)}) collective-permute-start(bf16[2,80,128]{2,1,0:T(8,128)(2,1)S(1)} %get-tuple-element.43), channel_id=1, source_target_pairs={{0,12},{1,13},{2,14},{3,15},{4,8},{5,9},{6,10},{7,11},{8,4},{9,5},... | collective-permute-start | bytes 122888 | tf_op jit(solution)/shard_map/ppermute | solution.py:236
  51.2 0.0 collective-permute-start.12
  51.2 2.2 %collective-permute-start.13 = (bf16[2,80,128]{2,1,0:T(8,128)(2,1)S(1)}, bf16[2,80,128]{2,1,0:T(8,128)(2,1)S(1)}, u32[]{:S(2)}, u32[]{:S(2)}) collective-permute-start(bf16[2,80,128]{2,1,0:T(8,128)(2,1)S(1)} %get-tuple-element.45), channel_id=1, source_target_pairs={{0,8},{1,9},{2,10},{3,11},{4,12},{5,13},{6,14},{7,15},{8,0},{9,1},... | collective-permute-start | bytes 122888 | tf_op jit(solution)/shard_map/ppermute | solution.py:236
  53.4 2.2 %collective-permute-start.14 = (bf16[2,80,128]{2,1,0:T(8,128)(2,1)S(1)}, bf16[2,80,128]{2,1,0:T(8,128)(2,1)S(1)}, u32[]{:S(2)}, u32[]{:S(2)}) collective-permute-start(bf16[2,80,128]{2,1,0:T(8,128)(2,1)S(1)} %get-tuple-element.46), channel_id=1, source_target_pairs={{0,2},{1,3},{2,0},{3,1},{4,6},{5,7},{6,4},{7,5},{8,10},{9,11},{10,... | collective-permute-start | bytes 122888 | tf_op jit(solution)/shard_map/ppermute | solution.py:236
  55.6 0.0 collective-permute-done.10.refs_4_
  55.6 0.7 %collective-permute-start.15 = (bf16[2,80,128]{2,1,0:T(8,128)(2,1)S(1)}, bf16[2,80,128]{2,1,0:T(8,128)(2,1)S(1)}, u32[]{:S(2)}, u32[]{:S(2)}) collective-permute-start(bf16[2,80,128]{2,1,0:T(8,128)(2,1)S(1)} %get-tuple-element.47), channel_id=1, source_target_pairs={{0,4},{1,5},{2,6},{3,7},{4,0},{5,1},{6,2},{7,3},{8,12},{9,13},{10,... | collective-permute-start | bytes 122888 | tf_op jit(solution)/shard_map/ppermute | solution.py:236
  56.3 0.4 collective-permute-done.11.refs_5_
  56.7 0.4 collective-permute-start.9
  57.1 0.0 collective-permute-done.12.refs_6_
  57.1 1.5 %collective-permute-done.13.refs_7_ = bf16[2,80,128]{2,1,0:T(8,128)(2,1)S(1)} collective-permute-done((bf16[2,80,128]{2,1,0:T(8,128)(2,1)S(1)}, bf16[2,80,128]{2,1,0:T(8,128)(2,1)S(1)}, u32[]{:S(2)}, u32[]{:S(2)}) %collective-permute-start.13) | collective-permute-done | bytes 40992 | tf_op jit(solution)/shard_map/ppermute | solution.py:236
  58.6 0.0 collective-permute-done.14.refs_8_
  58.6 1.0 %collective-permute-done.15.refs_9_ = bf16[2,80,128]{2,1,0:T(8,128)(2,1)S(1)} collective-permute-done((bf16[2,80,128]{2,1,0:T(8,128)(2,1)S(1)}, bf16[2,80,128]{2,1,0:T(8,128)(2,1)S(1)}, u32[]{:S(2)}, u32[]{:S(2)}) %collective-permute-start.15) | collective-permute-done | bytes 40992 | tf_op jit(solution)/shard_map/ppermute | solution.py:236
  59.6 2.0 %collective-permute-done.9.refs_3_ = bf16[2,80,128]{2,1,0:T(8,128)(2,1)S(1)} collective-permute-done((bf16[2,80,128]{2,1,0:T(8,128)(2,1)S(1)}, bf16[2,80,128]{2,1,0:T(8,128)(2,1)S(1)}, u32[]{:S(2)}, u32[]{:S(2)}) %collective-permute-start.9) | collective-permute-done | bytes 40992 | tf_op jit(solution)/shard_map/ppermute | solution.py:236
  61.6 0.0 copy-done.5
  61.6 1.1 %finish.1 = bf16[128,2048]{1,0:T(8,128)(2,1)} custom-call(s32[1]{0:T(128)} %bitcast.refs_0_, s32[1,80]{1,0:T(1,128)S(1)} %pad.4.refs_1_, bf16[128,2048]{1,0:T(8,128)(2,1)S(1)} %copy-done.5, bf16[2,80,128]{2,1,0:T(8,128)(2,1)S(1)} %collective-permute-done.9.refs_3_, bf16[2,80,128]{2,1,0:T(8,128)(2,1)S(1)} %collective-permute-done.10.refs_4_, ...), custom_call_target="tpu_custom_call" | custom-call | tf_op jit(solution)/shard_map/finish/pallas_call | solution.py:366
  (13 shorter events, 0.0 us)
Async XLA Ops:
  0.0 8.6 %copy-start.10 = (s32[76]{0:T(128)S(1)}, s32[76]{0:T(128)}, u32[]{:S(2)}) copy-start(s32[76]{0:T(128)} %param.10) | copy-start | bytes 916
  0.0 8.6 %copy-start.8 = (f32[128]{0:T(128)S(1)}, f32[128]{0:T(128)}, u32[]{:S(2)}) copy-start(f32[128]{0:T(128)} %param.16) | copy-start | bytes 1540
  0.0 8.6 %copy-start.9 = (f32[128]{0:T(128)S(1)}, f32[128]{0:T(128)}, u32[]{:S(2)}) copy-start(f32[128]{0:T(128)} %param.17) | copy-start | bytes 1540
  0.0 8.6 %copy-start = (bf16[76,3,2048]{2,0,1:T(8,128)(2,1)S(1)}, bf16[76,3,2048]{2,0,1:T(8,128)(2,1)}, u32[]{:S(2)}) copy-start(bf16[76,3,2048]{2,0,1:T(8,128)(2,1)} %param.9) | copy-start | bytes 2801668
  0.0 8.6 %copy-start.1 = (bf16[128,2048]{1,0:T(8,128)(2,1)S(1)}, bf16[128,2048]{1,0:T(8,128)(2,1)}, u32[]{:S(2)}) copy-start(bf16[128,2048]{1,0:T(8,128)(2,1)} %refs_5_.3) | copy-start | bytes 1572868
  0.0 8.6 %copy-start.2 = (bf16[128,2048]{1,0:T(8,128)(2,1)S(1)}, bf16[128,2048]{1,0:T(8,128)(2,1)}, u32[]{:S(2)}) copy-start(bf16[128,2048]{1,0:T(8,128)(2,1)} %refs_6_.3) | copy-start | bytes 1572868
  2.4 6.2 %collective-permute-start.1 = (bf16[2,256,128]{2,1,0:T(8,128)(2,1)}, bf16[2,256,128]{2,1,0:T(8,128)(2,1)S(1)}, u32[]{:S(2)}, u32[]{:S(2)}) collective-permute-start(bf16[2,256,128]{2,1,0:T(8,128)(2,1)} %get-tuple-element.28.refs_7_), channel_id=1, source_target_pairs={{0,1},{1,0},{2,3},{3,2},{4,5},{5,4},{6,7},{7,6},{8,9},{9,8},{10,11... | collective-permute-start | bytes 393224 | tf_op jit(solution)/shard_map/ppermute | solution.py:236
  3.0 16.4 %collective-permute-start = (bf16[2,336,128]{2,1,0:T(8,128)(2,1)}, bf16[2,336,128]{2,1,0:T(8,128)(2,1)S(1)}, u32[]{:S(2)}, u32[]{:S(2)}) collective-permute-start(bf16[2,336,128]{2,1,0:T(8,128)(2,1)} %get-tuple-element.27), channel_id=1, source_target_pairs={{0,14},{1,15},{2,12},{3,13},{4,10},{5,11},{6,8},{7,9},{8,6},{9,7},... | collective-permute-start | bytes 516104 | tf_op jit(solution)/shard_map/ppermute | solution.py:236
  8.7 1.2 %copy-start.3 = (bf16[256,2048]{1,0:T(8,128)(2,1)S(1)}, bf16[256,2048]{1,0:T(8,128)(2,1)}, u32[]{:S(2)}) copy-start(bf16[256,2048]{1,0:T(8,128)(2,1)} %refs_7_.1) | copy-start | bytes 3145732
  9.9 1.2 %copy-start.4 = (bf16[256,2048]{1,0:T(8,128)(2,1)S(1)}, bf16[256,2048]{1,0:T(8,128)(2,1)}, u32[]{:S(2)}) copy-start(bf16[256,2048]{1,0:T(8,128)(2,1)} %refs_8_.1) | copy-start | bytes 3145732
  11.1 27.8 %copy-start.6 = (bf16[2,256,128]{2,1,0:T(8,128)(2,1)S(1)}, bf16[2,256,128]{2,1,0:T(8,128)(2,1)}, u32[]{:S(2)}) copy-start(bf16[2,256,128]{2,1,0:T(8,128)(2,1)} %get-tuple-element.28.refs_7_) | copy-start | bytes 393220
  11.1 27.8 %copy-start.7 = (bf16[2,80,128]{2,1,0:T(8,128)(2,1)S(1)}, bf16[2,80,128]{2,1,0:T(8,128)(2,1)}, u32[]{:S(2)}) copy-start(bf16[2,80,128]{2,1,0:T(8,128)(2,1)} %get-tuple-element.37.refs_11_) | copy-start | bytes 122884
  13.5 9.2 %collective-permute-start.2 = (bf16[2,336,128]{2,1,0:T(8,128)(2,1)S(1)}, bf16[2,336,128]{2,1,0:T(8,128)(2,1)S(1)}, u32[]{:S(2)}, u32[]{:S(2)}) collective-permute-start(bf16[2,336,128]{2,1,0:T(8,128)(2,1)S(1)} %get-tuple-element.29), channel_id=1, source_target_pairs={{0,12},{1,13},{2,14},{3,15},{4,8},{5,9},{6,10},{7,11},{8,4},{9,5},... | collective-permute-start | bytes 516104 | tf_op jit(solution)/shard_map/ppermute | solution.py:236
  14.0 14.6 %collective-permute-start.3 = (bf16[2,336,128]{2,1,0:T(8,128)(2,1)S(1)}, bf16[2,336,128]{2,1,0:T(8,128)(2,1)S(1)}, u32[]{:S(2)}, u32[]{:S(2)}) collective-permute-start(bf16[2,336,128]{2,1,0:T(8,128)(2,1)S(1)} %get-tuple-element.30), channel_id=1, source_target_pairs={{0,2},{1,3},{2,0},{3,1},{4,6},{5,7},{6,4},{7,5},{8,10},{9,11},{10,... | collective-permute-start | bytes 516104 | tf_op jit(solution)/shard_map/ppermute | solution.py:236
  15.6 20.0 %collective-permute-start.4 = (bf16[2,336,128]{2,1,0:T(8,128)(2,1)S(1)}, bf16[2,336,128]{2,1,0:T(8,128)(2,1)S(1)}, u32[]{:S(2)}, u32[]{:S(2)}) collective-permute-start(bf16[2,336,128]{2,1,0:T(8,128)(2,1)S(1)} %get-tuple-element.31), channel_id=1, source_target_pairs={{0,10},{1,11},{2,8},{3,9},{4,14},{5,15},{6,12},{7,13},{8,2},{9,3},... | collective-permute-start | bytes 516104 | tf_op jit(solution)/shard_map/ppermute | solution.py:236
  16.0 19.6 %collective-permute-start.5 = (bf16[2,336,128]{2,1,0:T(8,128)(2,1)S(1)}, bf16[2,336,128]{2,1,0:T(8,128)(2,1)S(1)}, u32[]{:S(2)}, u32[]{:S(2)}) collective-permute-start(bf16[2,336,128]{2,1,0:T(8,128)(2,1)S(1)} %get-tuple-element.32), channel_id=1, source_target_pairs={{0,4},{1,5},{2,6},{3,7},{4,0},{5,1},{6,2},{7,3},{8,12},{9,13},{10,... | collective-permute-start | bytes 516104 | tf_op jit(solution)/shard_map/ppermute | solution.py:236
  19.4 19.5 %collective-permute-start.6 = (bf16[2,336,128]{2,1,0:T(8,128)(2,1)S(1)}, bf16[2,336,128]{2,1,0:T(8,128)(2,1)S(1)}, u32[]{:S(2)}, u32[]{:S(2)}) collective-permute-start(bf16[2,336,128]{2,1,0:T(8,128)(2,1)S(1)} %get-tuple-element.33), channel_id=1, source_target_pairs={{0,8},{1,9},{2,10},{3,11},{4,12},{5,13},{6,14},{7,15},{8,0},{9,1},... | collective-permute-start | bytes 516104 | tf_op jit(solution)/shard_map/ppermute | solution.py:236
  22.6 16.2 %collective-permute-start.7 = (bf16[2,336,128]{2,1,0:T(8,128)(2,1)S(1)}, bf16[2,336,128]{2,1,0:T(8,128)(2,1)S(1)}, u32[]{:S(2)}, u32[]{:S(2)}) collective-permute-start(bf16[2,336,128]{2,1,0:T(8,128)(2,1)S(1)} %get-tuple-element.34), channel_id=1, source_target_pairs={{0,6},{1,7},{2,4},{3,5},{4,2},{5,3},{6,0},{7,1},{8,14},{9,15},{10,... | collective-permute-start | bytes 516104 | tf_op jit(solution)/shard_map/ppermute | solution.py:236
  39.0 3.5 %collective-permute-start.8 = (bf16[2,2,896,128]{3,2,1,0:T(8,128)(2,1)S(1)}, bf16[2,2,896,128]{3,2,1,0:T(8,128)(2,1)S(1)}, u32[]{:S(2)}, u32[]{:S(2)}) collective-permute-start(bf16[2,2,896,128]{3,2,1,0:T(8,128)(2,1)S(1)} %get-tuple-element.38.refs_1_), channel_id=1, source_target_pairs={{0,1},{1,0},{2,3},{3,2},{4,5},{5,4},{6,7},{7,6},{8,9},{9,8},{10,11... | collective-permute-start | bytes 2752520 | tf_op jit(solution)/shard_map/ppermute | solution.py:236
  42.5 19.1 %copy-start.5 = (bf16[128,2048]{1,0:T(8,128)(2,1)S(1)}, bf16[128,2048]{1,0:T(8,128)(2,1)}, u32[]{:S(2)}) copy-start(bf16[128,2048]{1,0:T(8,128)(2,1)} %refs_2_.1) | copy-start | bytes 1572868
  45.2 10.4 %collective-permute-start.10 = (bf16[2,80,128]{2,1,0:T(8,128)(2,1)S(1)}, bf16[2,80,128]{2,1,0:T(8,128)(2,1)S(1)}, u32[]{:S(2)}, u32[]{:S(2)}) collective-permute-start(bf16[2,80,128]{2,1,0:T(8,128)(2,1)S(1)} %get-tuple-element.42), channel_id=1, source_target_pairs={{0,14},{1,15},{2,12},{3,13},{4,10},{5,11},{6,8},{7,9},{8,6},{9,7},... | collective-permute-start | bytes 122888 | tf_op jit(solution)/shard_map/ppermute | solution.py:236
  50.4 6.3 %collective-permute-start.11 = (bf16[2,80,128]{2,1,0:T(8,128)(2,1)S(1)}, bf16[2,80,128]{2,1,0:T(8,128)(2,1)S(1)}, u32[]{:S(2)}, u32[]{:S(2)}) collective-permute-start(bf16[2,80,128]{2,1,0:T(8,128)(2,1)S(1)} %get-tuple-element.43), channel_id=1, source_target_pairs={{0,12},{1,13},{2,14},{3,15},{4,8},{5,9},{6,10},{7,11},{8,4},{9,5},... | collective-permute-start | bytes 122888 | tf_op jit(solution)/shard_map/ppermute | solution.py:236
  51.2 5.9 %collective-permute-start.12 = (bf16[2,80,128]{2,1,0:T(8,128)(2,1)S(1)}, bf16[2,80,128]{2,1,0:T(8,128)(2,1)S(1)}, u32[]{:S(2)}, u32[]{:S(2)}) collective-permute-start(bf16[2,80,128]{2,1,0:T(8,128)(2,1)S(1)} %get-tuple-element.44), channel_id=1, source_target_pairs={{0,10},{1,11},{2,8},{3,9},{4,14},{5,15},{6,12},{7,13},{8,2},{9,3},... | collective-permute-start | bytes 122888 | tf_op jit(solution)/shard_map/ppermute | solution.py:236
  51.2 7.4 %collective-permute-start.13 = (bf16[2,80,128]{2,1,0:T(8,128)(2,1)S(1)}, bf16[2,80,128]{2,1,0:T(8,128)(2,1)S(1)}, u32[]{:S(2)}, u32[]{:S(2)}) collective-permute-start(bf16[2,80,128]{2,1,0:T(8,128)(2,1)S(1)} %get-tuple-element.45), channel_id=1, source_target_pairs={{0,8},{1,9},{2,10},{3,11},{4,12},{5,13},{6,14},{7,15},{8,0},{9,1},... | collective-permute-start | bytes 122888 | tf_op jit(solution)/shard_map/ppermute | solution.py:236
  53.4 5.2 %collective-permute-start.14 = (bf16[2,80,128]{2,1,0:T(8,128)(2,1)S(1)}, bf16[2,80,128]{2,1,0:T(8,128)(2,1)S(1)}, u32[]{:S(2)}, u32[]{:S(2)}) collective-permute-start(bf16[2,80,128]{2,1,0:T(8,128)(2,1)S(1)} %get-tuple-element.46), channel_id=1, source_target_pairs={{0,2},{1,3},{2,0},{3,1},{4,6},{5,7},{6,4},{7,5},{8,10},{9,11},{10,... | collective-permute-start | bytes 122888 | tf_op jit(solution)/shard_map/ppermute | solution.py:236
  55.6 4.0 %collective-permute-start.15 = (bf16[2,80,128]{2,1,0:T(8,128)(2,1)S(1)}, bf16[2,80,128]{2,1,0:T(8,128)(2,1)S(1)}, u32[]{:S(2)}, u32[]{:S(2)}) collective-permute-start(bf16[2,80,128]{2,1,0:T(8,128)(2,1)S(1)} %get-tuple-element.47), channel_id=1, source_target_pairs={{0,4},{1,5},{2,6},{3,7},{4,0},{5,1},{6,2},{7,3},{8,12},{9,13},{10,... | collective-permute-start | bytes 122888 | tf_op jit(solution)/shard_map/ppermute | solution.py:236
  56.7 4.9 %collective-permute-start.9 = (bf16[2,80,128]{2,1,0:T(8,128)(2,1)S(1)}, bf16[2,80,128]{2,1,0:T(8,128)(2,1)S(1)}, u32[]{:S(2)}, u32[]{:S(2)}) collective-permute-start(bf16[2,80,128]{2,1,0:T(8,128)(2,1)S(1)} %get-tuple-element.41), channel_id=1, source_target_pairs={{0,6},{1,7},{2,4},{3,5},{4,2},{5,3},{6,0},{7,1},{8,14},{9,15},{10,... | collective-permute-start | bytes 122888 | tf_op jit(solution)/shard_map/ppermute | solution.py:236

commit v9 on v7

--- a/solution.py
+++ b/solution.py
@@ -88,23 +88,24 @@
     count = len(steps)
     arrived = rest[:count]
     text_keys_ref, text_values_ref = rest[count : count + 2]
-    out_ref, queries_ref, keys_ref, values_ref, weights_ref, result_ref = rest[count + 2 :]
+    out_ref, queries_ref, keys_ref, values_ref, result_ref = rest[count + 2 :]
     head_size = text_keys_ref.shape[1]
     padded = arrived[0].shape[0] - 2 * tokens
     factor = head_size ** (-0.5) * LOG2E
     text = text_keys_ref.shape[0]
     keys_ref[:text] = text_keys_ref[...]
-    values_ref[:text, :head_size] = text_values_ref[...]
-    values_ref[:, head_size:] = jnp.ones((values_ref.shape[0], head_size), jnp.bfloat16)
+    values_ref[:text] = text_values_ref[...]
     for step in range(count):
         first = text + step * tokens
         keys_ref[first : first + tokens] = arrived[step][:tokens]
-        values_ref[first : first + tokens, :head_size] = arrived[step][tokens : 2 * tokens]
+        values_ref[first : first + tokens] = arrived[step][tokens : 2 * tokens]
         queries_ref[step * padded : (step + 1) * padded] = arrived[step][2 * tokens :]
 
     def add_queries(step, carry):
-        mine = pl.ds(pl.multiple_of(step * query_rows, 16), query_rows)
+        first_row = step * query_rows
+        mine = pl.ds(first_row if isinstance(step, int) else pl.multiple_of(first_row, 16), query_rows)
         queries = queries_ref[mine]
+        sums = None
         for first in range(0, keys_ref.shape[0], key_rows):
             scores = lax.dot_general(
                 queries,
@@ -112,14 +113,20 @@
                 (((1,), (1,)), ((), ())),
                 preferred_element_type=jnp.float32,
             )
-            weights_ref[:, first : first + key_rows] = jnp.exp2(scores * factor).astype(
-                jnp.bfloat16
-            )
-        sums = jnp.dot(weights_ref[...], values_ref[...], preferred_element_type=jnp.float32)
+            weights = jnp.exp2(scores * factor).astype(jnp.bfloat16)
+            values = values_ref[first : first + key_rows]
+            beside = jnp.concatenate([values, jnp.ones_like(values)], axis=1)
+            added = jnp.dot(weights, beside, preferred_element_type=jnp.float32)
+            sums = added if sums is None else sums + added
         result_ref[mine] = (sums[:, :head_size] / sums[:, head_size:]).astype(jnp.bfloat16)
         return carry
 
-    lax.fori_loop(0, queries_ref.shape[0] // query_rows, add_queries, 0)
+    turns = queries_ref.shape[0] // query_rows
+    if turns <= 4:
+        for step in range(turns):
+            add_queries(step, 0)
+    else:
+        lax.fori_loop(0, turns, add_queries, 0)
     for step in range(count):
         owner = lax.bitwise_xor(me, steps[step])
         out_ref[owner] = result_ref[step * padded : (step + 1) * padded]
@@ -157,9 +164,7 @@
     half = count // 2
     far = list(reversed(range(half, count)))
     near = list(reversed(range(1, half)))
-    order = far[:3]
-    for turn in range(max(len(far) - 3, len(near))):
-        order += near[turn : turn + 1] + far[turn + 3 : turn + 4]
+    order = far + near
     names = sorted(range(count - 1), key=lambda number: str(number) if number else "")
     return [0] + [order[names.index(number)] for number in range(count - 1)]
 
@@ -259,7 +264,7 @@
     query_rows = 4 * padded
     all_keys = text + seq_count * tokens
     result = pl.pallas_call(
-        lambda *refs: attend_kernel(tokens, query_rows, 256, steps, *refs),
+        lambda *refs: attend_kernel(tokens, query_rows, 768, steps, *refs),
         out_shape=jax.ShapeDtypeStruct((seq_count, padded, head_size), jnp.bfloat16),
         grid_spec=pltpu.PrefetchScalarGridSpec(
             num_scalar_prefetch=1,
@@ -270,8 +275,7 @@
             scratch_shapes=[
                 pltpu.VMEM((seq_count * padded, head_size), jnp.bfloat16),
                 pltpu.VMEM((all_keys, head_size), jnp.bfloat16),
-                pltpu.VMEM((all_keys, 2 * head_size), jnp.bfloat16),
-                pltpu.VMEM((query_rows, all_keys), jnp.bfloat16),
+                pltpu.VMEM((all_keys, head_size), jnp.bfloat16),
                 pltpu.VMEM((seq_count * padded, head_size), jnp.bfloat16),
             ],
         ),

time: 61 us -> 67.6 us (1.11)
  waiting for transfers between devices: 18.2 us -> 23.7 us
  starting transfers between devices: 31.8 us -> 33.6 us
    ppermute x15, waiting for transfers between devices: 7.18 us -> 12.6 us  [trade(): return lax.ppermute(block, 'seq', [(a, a ^ step) for a in range(count)])]
    all_to_all x1, starting transfers between devices: 3.67 us -> 4.88 us  [shards(): lax.all_to_all(result, 'seq', split_axis=0, concat_axis=0, tiled=True)]
  transfers between devices with their start and end apart: 16 -> 16, of which waited for: 3 -> 8; matrix products, arithmetic and copies ran while one was open for 0% -> 0% of each run, Pallas kernels for 1% -> 1%
where the time goes in v9:
time: 67.6 us; the launch traced here: 67.4 us
  starting transfers between devices  33.6 us (50%)
  waiting for transfers between devices  23.7 us (35%)
  Pallas kernels  8.69 us (13%)
  local copies, waits for them, and re-layouts  1.26 us (2%)
    ppermute x15, starting transfers between devices, trade(): return lax.ppermute(block, 'seq', [(a, a ^ step) for a in range(count)])  28.8 us
    ppermute x15, waiting for transfers between devices, trade(): return lax.ppermute(block, 'seq', [(a, a ^ step) for a in range(count)])  12.6 us
    all_to_all x1, waiting for transfers between devices, shards(): lax.all_to_all(result, 'seq', split_axis=0, concat_axis=0, tiled=True)  11.1 us
    all_to_all x1, starting transfers between devices, shards(): lax.all_to_all(result, 'seq', split_axis=0, concat_axis=0, tiled=True)  4.88 us
    pallas_call x1, Pallas kernels, shards(): pl.pallas_call(lambda *refs: attend_kernel(tokens, query_rows, 768, steps...  4.5 us
    pallas_call x1, Pallas kernels, shards(): pl.pallas_call(lambda *refs: prepare_kernel(per_group, padded, early, Tru...  2.21 us
  transfers between devices with their start and end apart: 16, of which 8 were waited for; matrix products, arithmetic and copies ran while one was open for 0% of the time, Pallas kernels for 1%

profile of v9, /device:TPU:0, one launch (start us, length us, event | category | flops | bytes accessed | tf_op | source)
XLA Modules:
  0.0 67.4 jit_solution(6565919059293284482)
XLA Ops:
  0.0 0.0 copy-start
  0.0 0.0 copy-start.1
  0.0 2.2 %prepare_first.1 = (bf16[336,128]{1,0:T(8,128)(2,1)}, bf16[336,128]{1,0:T(8,128)(2,1)}, bf16[336,128]{1,0:T(8,128)(2,1)}, bf16[336,128]{1,0:T(8,128)(2,1)}) custom-call(s32[1]{0:T(128)} %bitcast.1.refs_0_, s32[1,76]{1,0:T(1,128)} %bitcast.14, f32[1,128]{1,0:T(1,128)} %bitcast.10, f32[1,128]{1,0:T(1,128)} %bitcast.12, bf16[3,76,2048]{2,1,0:T(8,128)(2,1)} %bitcast.5, ...), custom_call_target="tpu_custom_call" | custom-call | tf_op jit(solution)/shard_map/prepare_first/pallas_call | solution.py:219
  2.2 0.5 collective-permute-start
  2.7 5.7 %collective-permute-start.1 = (bf16[336,128]{1,0:T(8,128)(2,1)}, bf16[336,128]{1,0:T(8,128)(2,1)S(1)}, u32[]{:S(2)}, u32[]{:S(2)}) collective-permute-start(bf16[336,128]{1,0:T(8,128)(2,1)} %get-tuple-element.25), channel_id=1, source_target_pairs={{0,15},{1,14},{2,13},{3,12},{4,11},{5,10},{6,9},{7,8},{8,7},{9,6},... | collective-permute-start | bytes 258056 | tf_op jit(solution)/shard_map/ppermute | solution.py:176
  8.4 0.0 collective-permute-start.10
  8.4 3.4 %collective-permute-start.2 = (bf16[336,128]{1,0:T(8,128)(2,1)}, bf16[336,128]{1,0:T(8,128)(2,1)S(1)}, u32[]{:S(2)}, u32[]{:S(2)}) collective-permute-start(bf16[336,128]{1,0:T(8,128)(2,1)} %get-tuple-element.26), channel_id=1, source_target_pairs={{0,14},{1,15},{2,12},{3,13},{4,10},{5,11},{6,8},{7,9},{8,6},{9,7},... | collective-permute-start | bytes 258056 | tf_op jit(solution)/shard_map/ppermute | solution.py:176
  11.8 0.0 collective-permute-done.refs_9_.refs_11_
  11.8 0.0 copy-done
  11.8 0.0 copy-done.1
  11.8 0.0 copy-done.2
  11.8 0.0 copy-done.3
  11.8 0.0 copy-done.6
  11.8 0.0 copy-done.7
  11.9 0.0 copy-done.8
  11.9 0.0 copy-start.4
  11.9 1.2 %copy-done.4 = bf16[256,2048]{1,0:T(8,128)(2,1)S(1)} copy-done((bf16[256,2048]{1,0:T(8,128)(2,1)S(1)}, bf16[256,2048]{1,0:T(8,128)(2,1)}, u32[]{:S(2)}) %copy-start.4) | copy-done | bytes 1048600
  13.1 0.9 %prepare_rest.1 = (bf16[336,128]{1,0:T(8,128)(2,1)S(1)}, bf16[336,128]{1,0:T(8,128)(2,1)S(1)}, bf16[336,128]{1,0:T(8,128)(2,1)S(1)}, bf16[336,128]{1,0:T(8,128)(...) custom-call(s32[1]{0:T(128)} %bitcast.1.refs_0_, ...), custom_call_target="tpu_custom_call" | custom-call | tf_op jit(solution)/shard_map/prepare_rest/pallas_call | solution.py:236
  14.0 0.5 collective-permute-start.11
  14.5 0.0 collective-permute-start.12
  14.5 0.0 collective-permute-done.1.refs_2_
  14.5 3.2 %collective-permute-start.13 = (bf16[336,128]{1,0:T(8,128)(2,1)S(1)}, bf16[336,128]{1,0:T(8,128)(2,1)S(1)}, u32[]{:S(2)}, u32[]{:S(2)}) collective-permute-start(bf16[336,128]{1,0:T(8,128)(2,1)S(1)} %get-tuple-element.37), channel_id=1, source_target_pairs={{0,10},{1,11},{2,8},{3,9},{4,14},{5,15},{6,12},{7,13},{8,2},{9,3},... | collective-permute-start | bytes 258056 | tf_op jit(solution)/shard_map/ppermute | solution.py:176
  17.7 0.0 collective-permute-done.10.refs_12_
  17.7 6.7 %collective-permute-start.14 = (bf16[336,128]{1,0:T(8,128)(2,1)S(1)}, bf16[336,128]{1,0:T(8,128)(2,1)S(1)}, u32[]{:S(2)}, u32[]{:S(2)}) collective-permute-start(bf16[336,128]{1,0:T(8,128)(2,1)S(1)} %get-tuple-element.38), channel_id=1, source_target_pairs={{0,9},{1,8},{2,11},{3,10},{4,13},{5,12},{6,15},{7,14},{8,1},{9,0},... | collective-permute-start | bytes 258056 | tf_op jit(solution)/shard_map/ppermute | solution.py:176
  24.4 0.0 collective-permute-done.2.refs_3_
  24.4 4.1 %collective-permute-start.3 = (bf16[336,128]{1,0:T(8,128)(2,1)S(1)}, bf16[336,128]{1,0:T(8,128)(2,1)S(1)}, u32[]{:S(2)}, u32[]{:S(2)}) collective-permute-start(bf16[336,128]{1,0:T(8,128)(2,1)S(1)} %get-tuple-element.27), channel_id=1, source_target_pairs={{0,8},{1,9},{2,10},{3,11},{4,12},{5,13},{6,14},{7,15},{8,0},{9,1},... | collective-permute-start | bytes 258056 | tf_op jit(solution)/shard_map/ppermute | solution.py:176
  28.5 0.0 collective-permute-done.11.refs_13_
  28.5 0.3 collective-permute-start.4
  28.9 2.5 %collective-permute-done.12.refs_14_ = bf16[336,128]{1,0:T(8,128)(2,1)S(1)} collective-permute-done((bf16[336,128]{1,0:T(8,128)(2,1)S(1)}, bf16[336,128]{1,0:T(8,128)(2,1)S(1)}, u32[]{:S(2)}, u32[]{:S(2)}) %collective-permute-start.12) | collective-permute-done | bytes 86048 | tf_op jit(solution)/shard_map/ppermute | solution.py:176
  31.3 0.9 %collective-permute-start.5 = (bf16[336,128]{1,0:T(8,128)(2,1)S(1)}, bf16[336,128]{1,0:T(8,128)(2,1)S(1)}, u32[]{:S(2)}, u32[]{:S(2)}) collective-permute-start(bf16[336,128]{1,0:T(8,128)(2,1)S(1)} %get-tuple-element.29), channel_id=1, source_target_pairs={{0,6},{1,7},{2,4},{3,5},{4,2},{5,3},{6,0},{7,1},{8,14},{9,15},{10,... | collective-permute-start | bytes 258056 | tf_op jit(solution)/shard_map/ppermute | solution.py:176
  32.2 3.1 %collective-permute-done.13.refs_15_ = bf16[336,128]{1,0:T(8,128)(2,1)S(1)} collective-permute-done((bf16[336,128]{1,0:T(8,128)(2,1)S(1)}, bf16[336,128]{1,0:T(8,128)(2,1)S(1)}, u32[]{:S(2)}, u32[]{:S(2)}) %collective-permute-start.13) | collective-permute-done | bytes 86048 | tf_op jit(solution)/shard_map/ppermute | solution.py:176
  35.4 0.3 collective-permute-start.6
  35.6 0.5 collective-permute-done.14.refs_16_
  36.1 0.7 %collective-permute-start.7 = (bf16[336,128]{1,0:T(8,128)(2,1)S(1)}, bf16[336,128]{1,0:T(8,128)(2,1)S(1)}, u32[]{:S(2)}, u32[]{:S(2)}) collective-permute-start(bf16[336,128]{1,0:T(8,128)(2,1)S(1)} %get-tuple-element.31), channel_id=1, source_target_pairs={{0,4},{1,5},{2,6},{3,7},{4,0},{5,1},{6,2},{7,3},{8,12},{9,13},{10,... | collective-permute-start | bytes 258056 | tf_op jit(solution)/shard_map/ppermute | solution.py:176
  36.8 1.7 %collective-permute-done.3.refs_4_ = bf16[336,128]{1,0:T(8,128)(2,1)S(1)} collective-permute-done((bf16[336,128]{1,0:T(8,128)(2,1)S(1)}, bf16[336,128]{1,0:T(8,128)(2,1)S(1)}, u32[]{:S(2)}, u32[]{:S(2)}) %collective-permute-start.3) | collective-permute-done | bytes 86048 | tf_op jit(solution)/shard_map/ppermute | solution.py:176
  38.5 0.0 collective-permute-start.8
  38.5 0.7 %collective-permute-done.4.refs_5_ = bf16[336,128]{1,0:T(8,128)(2,1)S(1)} collective-permute-done((bf16[336,128]{1,0:T(8,128)(2,1)S(1)}, bf16[336,128]{1,0:T(8,128)(2,1)S(1)}, u32[]{:S(2)}, u32[]{:S(2)}) %collective-permute-start.4) | collective-permute-done | bytes 86048 | tf_op jit(solution)/shard_map/ppermute | solution.py:176
  39.3 2.4 %collective-permute-start.9 = (bf16[336,128]{1,0:T(8,128)(2,1)S(1)}, bf16[336,128]{1,0:T(8,128)(2,1)S(1)}, u32[]{:S(2)}, u32[]{:S(2)}) collective-permute-start(bf16[336,128]{1,0:T(8,128)(2,1)S(1)} %get-tuple-element.33), channel_id=1, source_target_pairs={{0,2},{1,3},{2,0},{3,1},{4,6},{5,7},{6,4},{7,5},{8,10},{9,11},{10,... | collective-permute-start | bytes 258056 | tf_op jit(solution)/shard_map/ppermute | solution.py:176
  41.7 0.0 collective-permute-done.5.refs_6_
  41.7 2.2 %collective-permute-done.6.refs_7_ = bf16[336,128]{1,0:T(8,128)(2,1)S(1)} collective-permute-done((bf16[336,128]{1,0:T(8,128)(2,1)S(1)}, bf16[336,128]{1,0:T(8,128)(2,1)S(1)}, u32[]{:S(2)}, u32[]{:S(2)}) %collective-permute-start.6) | collective-permute-done | bytes 86048 | tf_op jit(solution)/shard_map/ppermute | solution.py:176
  43.9 1.9 %collective-permute-done.7.refs_8_ = bf16[336,128]{1,0:T(8,128)(2,1)S(1)} collective-permute-done((bf16[336,128]{1,0:T(8,128)(2,1)S(1)}, bf16[336,128]{1,0:T(8,128)(2,1)S(1)}, u32[]{:S(2)}, u32[]{:S(2)}) %collective-permute-start.7) | collective-permute-done | bytes 86048 | tf_op jit(solution)/shard_map/ppermute | solution.py:176
  45.8 0.0 collective-permute-done.8.refs_9_
  45.8 0.0 collective-permute-done.9.refs_10_
  45.8 4.5 %attend.1 = bf16[16,80,128]{2,1,0:T(8,128)(2,1)} custom-call(s32[1]{0:T(128)} %bitcast.1.refs_0_, bf16[336,128]{1,0:T(8,128)(2,1)S(1)} %get-tuple-element.24.refs_1_, bf16[336,128]{1,0:T(8,128)(2,1)S(1)} %collective-permute-done.1.refs_2_, bf16[336,128]{1,0:T(8,128)(2,1)S(1)} %collective-permute-done.2.refs_3_, ...), custom_call_target="tpu_custom_call" | custom-call | tf_op jit(solution)/shard_map/attend/pallas_call | solution.py:266
  50.3 4.9 %all-to-all-start = ((bf16[16,80,128]{2,1,0:T(8,128)(2,1)}), bf16[16,80,128]{2,1,0:T(8,128)(2,1)S(1)}, u32[]{:S(2)}, u32[]{:S(2)}) async-start(bf16[16,80,128]{2,1,0:T(8,128)(2,1)} %attend.1), calls=%async_computation | async-start | bytes 655360 | tf_op jit(solution)/shard_map/all_to_all | solution.py:286
  55.2 11.1 %all-to-all-done.refs_1_ = bf16[16,80,128]{2,1,0:T(8,128)(2,1)S(1)} async-done(((bf16[16,80,128]{2,1,0:T(8,128)(2,1)}), bf16[16,80,128]{2,1,0:T(8,128)(2,1)S(1)}, u32[]{:S(2)}, u32[]{:S(2)}) %all-to-all-start) | async-done | bytes 327712 | tf_op jit(solution)/shard_map/all_to_all | solution.py:286
  66.3 0.0 copy-done.5
  66.3 1.1 %finish.1 = bf16[128,2048]{1,0:T(8,128)(2,1)} custom-call(s32[1,80]{1,0:T(1,128)S(1)} %pad.4.refs_0_, bf16[16,80,128]{2,1,0:T(8,128)(2,1)S(1)} %all-to-all-done.refs_1_, bf16[128,2048]{1,0:T(8,128)(2,1)S(1)} %copy-done.5), custom_call_target="tpu_custom_call" | custom-call | tf_op jit(solution)/shard_map/finish/pallas_call | solution.py:289
  (7 shorter events, 0.0 us)
Async XLA Ops:
  0.0 11.8 %copy-start = (bf16[76,3,2048]{2,0,1:T(8,128)(2,1)S(1)}, bf16[76,3,2048]{2,0,1:T(8,128)(2,1)}, u32[]{:S(2)}) copy-start(bf16[76,3,2048]{2,0,1:T(8,128)(2,1)} %param.9) | copy-start | bytes 2801668
  0.0 11.8 %copy-start.1 = (bf16[128,2048]{1,0:T(8,128)(2,1)S(1)}, bf16[128,2048]{1,0:T(8,128)(2,1)}, u32[]{:S(2)}) copy-start(bf16[128,2048]{1,0:T(8,128)(2,1)} %refs_5_.3) | copy-start | bytes 1572868
  0.0 11.8 %copy-start.2 = (bf16[128,2048]{1,0:T(8,128)(2,1)S(1)}, bf16[128,2048]{1,0:T(8,128)(2,1)}, u32[]{:S(2)}) copy-start(bf16[128,2048]{1,0:T(8,128)(2,1)} %refs_6_.3) | copy-start | bytes 1572868
  0.0 11.8 %copy-start.3 = (bf16[256,2048]{1,0:T(8,128)(2,1)S(1)}, bf16[256,2048]{1,0:T(8,128)(2,1)}, u32[]{:S(2)}) copy-start(bf16[256,2048]{1,0:T(8,128)(2,1)} %refs_7_.1) | copy-start | bytes 3145732
  2.2 9.6 %collective-permute-start = (bf16[336,128]{1,0:T(8,128)(2,1)}, bf16[336,128]{1,0:T(8,128)(2,1)S(1)}, u32[]{:S(2)}, u32[]{:S(2)}) collective-permute-start(bf16[336,128]{1,0:T(8,128)(2,1)} %get-tuple-element.23), channel_id=1, source_target_pairs={{0,1},{1,0},{2,3},{3,2},{4,5},{5,4},{6,7},{7,6},{8,9},{9,8},{10,11... | collective-permute-start | bytes 258056 | tf_op jit(solution)/shard_map/ppermute | solution.py:176
  2.7 11.9 %collective-permute-start.1 = (bf16[336,128]{1,0:T(8,128)(2,1)}, bf16[336,128]{1,0:T(8,128)(2,1)S(1)}, u32[]{:S(2)}, u32[]{:S(2)}) collective-permute-start(bf16[336,128]{1,0:T(8,128)(2,1)} %get-tuple-element.25), channel_id=1, source_target_pairs={{0,15},{1,14},{2,13},{3,12},{4,11},{5,10},{6,9},{7,8},{8,7},{9,6},... | collective-permute-start | bytes 258056 | tf_op jit(solution)/shard_map/ppermute | solution.py:176
  8.4 3.5 %copy-start.6 = (f32[128]{0:T(128)S(1)}, f32[128]{0:T(128)}, u32[]{:S(2)}) copy-start(f32[128]{0:T(128)} %param.16) | copy-start | bytes 1540
  8.4 3.5 %copy-start.7 = (f32[128]{0:T(128)S(1)}, f32[128]{0:T(128)}, u32[]{:S(2)}) copy-start(f32[128]{0:T(128)} %param.17) | copy-start | bytes 1540
  8.4 3.5 %copy-start.8 = (s32[76]{0:T(128)S(1)}, s32[76]{0:T(128)}, u32[]{:S(2)}) copy-start(s32[76]{0:T(128)} %param.10) | copy-start | bytes 916
  8.4 9.4 %collective-permute-start.10 = (bf16[336,128]{1,0:T(8,128)(2,1)}, bf16[336,128]{1,0:T(8,128)(2,1)S(1)}, u32[]{:S(2)}, u32[]{:S(2)}) collective-permute-start(bf16[336,128]{1,0:T(8,128)(2,1)} %get-tuple-element.34), channel_id=1, source_target_pairs={{0,13},{1,12},{2,15},{3,14},{4,9},{5,8},{6,11},{7,10},{8,5},{9,4},... | collective-permute-start | bytes 258056 | tf_op jit(solution)/shard_map/ppermute | solution.py:176
  8.4 16.0 %collective-permute-start.2 = (bf16[336,128]{1,0:T(8,128)(2,1)}, bf16[336,128]{1,0:T(8,128)(2,1)S(1)}, u32[]{:S(2)}, u32[]{:S(2)}) collective-permute-start(bf16[336,128]{1,0:T(8,128)(2,1)} %get-tuple-element.26), channel_id=1, source_target_pairs={{0,14},{1,15},{2,12},{3,13},{4,10},{5,11},{6,8},{7,9},{8,6},{9,7},... | collective-permute-start | bytes 258056 | tf_op jit(solution)/shard_map/ppermute | solution.py:176
  11.9 1.2 %copy-start.4 = (bf16[256,2048]{1,0:T(8,128)(2,1)S(1)}, bf16[256,2048]{1,0:T(8,128)(2,1)}, u32[]{:S(2)}) copy-start(bf16[256,2048]{1,0:T(8,128)(2,1)} %refs_8_.3) | copy-start | bytes 3145732
  14.0 14.5 %collective-permute-start.11 = (bf16[336,128]{1,0:T(8,128)(2,1)S(1)}, bf16[336,128]{1,0:T(8,128)(2,1)S(1)}, u32[]{:S(2)}, u32[]{:S(2)}) collective-permute-start(bf16[336,128]{1,0:T(8,128)(2,1)S(1)} %get-tuple-element.35), channel_id=1, source_target_pairs={{0,12},{1,13},{2,14},{3,15},{4,8},{5,9},{6,10},{7,11},{8,4},{9,5},... | collective-permute-start | bytes 258056 | tf_op jit(solution)/shard_map/ppermute | solution.py:176
  14.5 16.8 %collective-permute-start.12 = (bf16[336,128]{1,0:T(8,128)(2,1)S(1)}, bf16[336,128]{1,0:T(8,128)(2,1)S(1)}, u32[]{:S(2)}, u32[]{:S(2)}) collective-permute-start(bf16[336,128]{1,0:T(8,128)(2,1)S(1)} %get-tuple-element.36), channel_id=1, source_target_pairs={{0,11},{1,10},{2,9},{3,8},{4,15},{5,14},{6,13},{7,12},{8,3},{9,2},... | collective-permute-start | bytes 258056 | tf_op jit(solution)/shard_map/ppermute | solution.py:176
  14.5 20.8 %collective-permute-start.13 = (bf16[336,128]{1,0:T(8,128)(2,1)S(1)}, bf16[336,128]{1,0:T(8,128)(2,1)S(1)}, u32[]{:S(2)}, u32[]{:S(2)}) collective-permute-start(bf16[336,128]{1,0:T(8,128)(2,1)S(1)} %get-tuple-element.37), channel_id=1, source_target_pairs={{0,10},{1,11},{2,8},{3,9},{4,14},{5,15},{6,12},{7,13},{8,2},{9,3},... | collective-permute-start | bytes 258056 | tf_op jit(solution)/shard_map/ppermute | solution.py:176
  17.7 18.4 %collective-permute-start.14 = (bf16[336,128]{1,0:T(8,128)(2,1)S(1)}, bf16[336,128]{1,0:T(8,128)(2,1)S(1)}, u32[]{:S(2)}, u32[]{:S(2)}) collective-permute-start(bf16[336,128]{1,0:T(8,128)(2,1)S(1)} %get-tuple-element.38), channel_id=1, source_target_pairs={{0,9},{1,8},{2,11},{3,10},{4,13},{5,12},{6,15},{7,14},{8,1},{9,0},... | collective-permute-start | bytes 258056 | tf_op jit(solution)/shard_map/ppermute | solution.py:176
  24.4 14.1 %collective-permute-start.3 = (bf16[336,128]{1,0:T(8,128)(2,1)S(1)}, bf16[336,128]{1,0:T(8,128)(2,1)S(1)}, u32[]{:S(2)}, u32[]{:S(2)}) collective-permute-start(bf16[336,128]{1,0:T(8,128)(2,1)S(1)} %get-tuple-element.27), channel_id=1, source_target_pairs={{0,8},{1,9},{2,10},{3,11},{4,12},{5,13},{6,14},{7,15},{8,0},{9,1},... | collective-permute-start | bytes 258056 | tf_op jit(solution)/shard_map/ppermute | solution.py:176
  28.5 10.7 %collective-permute-start.4 = (bf16[336,128]{1,0:T(8,128)(2,1)S(1)}, bf16[336,128]{1,0:T(8,128)(2,1)S(1)}, u32[]{:S(2)}, u32[]{:S(2)}) collective-permute-start(bf16[336,128]{1,0:T(8,128)(2,1)S(1)} %get-tuple-element.28), channel_id=1, source_target_pairs={{0,7},{1,6},{2,5},{3,4},{4,3},{5,2},{6,1},{7,0},{8,15},{9,14},{10,... | collective-permute-start | bytes 258056 | tf_op jit(solution)/shard_map/ppermute | solution.py:176
  31.3 10.4 %collective-permute-start.5 = (bf16[336,128]{1,0:T(8,128)(2,1)S(1)}, bf16[336,128]{1,0:T(8,128)(2,1)S(1)}, u32[]{:S(2)}, u32[]{:S(2)}) collective-permute-start(bf16[336,128]{1,0:T(8,128)(2,1)S(1)} %get-tuple-element.29), channel_id=1, source_target_pairs={{0,6},{1,7},{2,4},{3,5},{4,2},{5,3},{6,0},{7,1},{8,14},{9,15},{10,... | collective-permute-start | bytes 258056 | tf_op jit(solution)/shard_map/ppermute | solution.py:176
  35.4 8.5 %collective-permute-start.6 = (bf16[336,128]{1,0:T(8,128)(2,1)S(1)}, bf16[336,128]{1,0:T(8,128)(2,1)S(1)}, u32[]{:S(2)}, u32[]{:S(2)}) collective-permute-start(bf16[336,128]{1,0:T(8,128)(2,1)S(1)} %get-tuple-element.30), channel_id=1, source_target_pairs={{0,5},{1,4},{2,7},{3,6},{4,1},{5,0},{6,3},{7,2},{8,13},{9,12},{10,... | collective-permute-start | bytes 258056 | tf_op jit(solution)/shard_map/ppermute | solution.py:176
  36.1 9.7 %collective-permute-start.7 = (bf16[336,128]{1,0:T(8,128)(2,1)S(1)}, bf16[336,128]{1,0:T(8,128)(2,1)S(1)}, u32[]{:S(2)}, u32[]{:S(2)}) collective-permute-start(bf16[336,128]{1,0:T(8,128)(2,1)S(1)} %get-tuple-element.31), channel_id=1, source_target_pairs={{0,4},{1,5},{2,6},{3,7},{4,0},{5,1},{6,2},{7,3},{8,12},{9,13},{10,... | collective-permute-start | bytes 258056 | tf_op jit(solution)/shard_map/ppermute | solution.py:176
  38.5 7.3 %collective-permute-start.8 = (bf16[336,128]{1,0:T(8,128)(2,1)S(1)}, bf16[336,128]{1,0:T(8,128)(2,1)S(1)}, u32[]{:S(2)}, u32[]{:S(2)}) collective-permute-start(bf16[336,128]{1,0:T(8,128)(2,1)S(1)} %get-tuple-element.32), channel_id=1, source_target_pairs={{0,3},{1,2},{2,1},{3,0},{4,7},{5,6},{6,5},{7,4},{8,11},{9,10},{10,... | collective-permute-start | bytes 258056 | tf_op jit(solution)/shard_map/ppermute | solution.py:176
  39.3 6.5 %collective-permute-start.9 = (bf16[336,128]{1,0:T(8,128)(2,1)S(1)}, bf16[336,128]{1,0:T(8,128)(2,1)S(1)}, u32[]{:S(2)}, u32[]{:S(2)}) collective-permute-start(bf16[336,128]{1,0:T(8,128)(2,1)S(1)} %get-tuple-element.33), channel_id=1, source_target_pairs={{0,2},{1,3},{2,0},{3,1},{4,6},{5,7},{6,4},{7,5},{8,10},{9,11},{10,... | collective-permute-start | bytes 258056 | tf_op jit(solution)/shard_map/ppermute | solution.py:176
  50.3 16.0 %copy-start.5 = (bf16[128,2048]{1,0:T(8,128)(2,1)S(1)}, bf16[128,2048]{1,0:T(8,128)(2,1)}, u32[]{:S(2)}) copy-start(bf16[128,2048]{1,0:T(8,128)(2,1)} %refs_2_.1) | copy-start | bytes 1572868
  50.3 16.0 %all-to-all-start = ((bf16[16,80,128]{2,1,0:T(8,128)(2,1)}), bf16[16,80,128]{2,1,0:T(8,128)(2,1)S(1)}, u32[]{:S(2)}, u32[]{:S(2)}) async-start(bf16[16,80,128]{2,1,0:T(8,128)(2,1)} %attend.1), calls=%async_computation | async-start | bytes 655360 | tf_op jit(solution)/shard_map/all_to_all | solution.py:286

commit v10 on v9

--- a/solution.py
+++ b/solution.py
@@ -103,7 +103,9 @@
 
     def add_queries(step, carry):
         first_row = step * query_rows
-        mine = pl.ds(first_row if isinstance(step, int) else pl.multiple_of(first_row, 16), query_rows)
+        if not isinstance(step, int):
+            first_row = pl.multiple_of(first_row, 16)
+        mine = pl.ds(first_row, query_rows)
         queries = queries_ref[mine]
         sums = None
         for first in range(0, keys_ref.shape[0], key_rows):
@@ -164,7 +166,9 @@
     half = count // 2
     far = list(reversed(range(half, count)))
     near = list(reversed(range(1, half)))
-    order = far + near
+    order = far[:3]
+    for turn in range(max(len(far) - 3, len(near))):
+        order += far[turn + 3 : turn + 4] + near[turn : turn + 1]
     names = sorted(range(count - 1), key=lambda number: str(number) if number else "")
     return [0] + [order[names.index(number)] for number in range(count - 1)]
 

time: 67.6 us -> 60.6 us (0.90)
  waiting for transfers between devices: 23.7 us -> 14.6 us
  starting transfers between devices: 33.6 us -> 35.7 us
    ppermute x15, waiting for transfers between devices: 12.6 us -> 3.54 us  [trade(): return lax.ppermute(block, 'seq', [(a, a ^ step) for a in range(count)])]
    ppermute x15, starting transfers between devices: 28.8 us -> 31.2 us  [trade(): return lax.ppermute(block, 'seq', [(a, a ^ step) for a in range(count)])]
  transfers between devices with their start and end apart: 16 -> 16, of which waited for: 8 -> 5; matrix products, arithmetic and copies ran while one was open for 0% -> 0% of each run, Pallas kernels for 1% -> 1%
where the time goes in v10:
time: 60.6 us; the launch traced here: 60.4 us
  starting transfers between devices  35.7 us (59%)
  waiting for transfers between devices  14.6 us (24%)
  Pallas kernels  8.68 us (14%)
  local copies, waits for them, and re-layouts  1.26 us (2%)
    ppermute x15, starting transfers between devices, trade(): return lax.ppermute(block, 'seq', [(a, a ^ step) for a in range(count)])  31.2 us
    all_to_all x1, waiting for transfers between devices, shards(): lax.all_to_all(result, 'seq', split_axis=0, concat_axis=0, tiled=True)  11.1 us
    pallas_call x1, Pallas kernels, shards(): pl.pallas_call(lambda *refs: attend_kernel(tokens, query_rows, 768, steps...  4.5 us
    all_to_all x1, starting transfers between devices, shards(): lax.all_to_all(result, 'seq', split_axis=0, concat_axis=0, tiled=True)  4.48 us
    ppermute x15, waiting for transfers between devices, trade(): return lax.ppermute(block, 'seq', [(a, a ^ step) for a in range(count)])  3.54 us
    pallas_call x1, Pallas kernels, shards(): pl.pallas_call(lambda *refs: prepare_kernel(per_group, padded, early, Tru...  2.21 us
    unnamed x18, local copies, waits for them, and re-layouts  1.25 us
  transfers between devices with their start and end apart: 16, of which 5 were waited for; matrix products, arithmetic and copies ran while one was open for 0% of the time, Pallas kernels for 1%

profile of v10, /device:TPU:0, one launch (start us, length us, event | category | flops | bytes accessed | tf_op | source)
XLA Modules:
  0.0 60.4 jit_solution(11182303244220800946)
XLA Ops:
  0.0 0.0 copy-start
  0.0 0.0 copy-start.1
  0.0 2.2 %prepare_first.1 = (bf16[336,128]{1,0:T(8,128)(2,1)}, bf16[336,128]{1,0:T(8,128)(2,1)}, bf16[336,128]{1,0:T(8,128)(2,1)}, bf16[336,128]{1,0:T(8,128)(2,1)}) custom-call(s32[1]{0:T(128)} %bitcast.1.refs_0_, s32[1,76]{1,0:T(1,128)} %bitcast.14, f32[1,128]{1,0:T(1,128)} %bitcast.10, f32[1,128]{1,0:T(1,128)} %bitcast.12, bf16[3,76,2048]{2,1,0:T(8,128)(2,1)} %bitcast.5, ...), custom_call_target="tpu_custom_call" | custom-call | tf_op jit(solution)/shard_map/prepare_first/pallas_call | solution.py:223
  2.2 0.5 collective-permute-start
  2.7 5.7 %collective-permute-start.1 = (bf16[336,128]{1,0:T(8,128)(2,1)}, bf16[336,128]{1,0:T(8,128)(2,1)S(1)}, u32[]{:S(2)}, u32[]{:S(2)}) collective-permute-start(bf16[336,128]{1,0:T(8,128)(2,1)} %get-tuple-element.25), channel_id=1, source_target_pairs={{0,15},{1,14},{2,13},{3,12},{4,11},{5,10},{6,9},{7,8},{8,7},{9,6},... | collective-permute-start | bytes 258056 | tf_op jit(solution)/shard_map/ppermute | solution.py:180
  8.4 0.0 collective-permute-start.10
  8.4 3.4 %collective-permute-start.2 = (bf16[336,128]{1,0:T(8,128)(2,1)}, bf16[336,128]{1,0:T(8,128)(2,1)S(1)}, u32[]{:S(2)}, u32[]{:S(2)}) collective-permute-start(bf16[336,128]{1,0:T(8,128)(2,1)} %get-tuple-element.26), channel_id=1, source_target_pairs={{0,14},{1,15},{2,12},{3,13},{4,10},{5,11},{6,8},{7,9},{8,6},{9,7},... | collective-permute-start | bytes 258056 | tf_op jit(solution)/shard_map/ppermute | solution.py:180
  11.8 0.0 collective-permute-done.refs_9_.refs_11_
  11.8 0.0 copy-done
  11.8 0.0 copy-done.1
  11.8 0.0 copy-done.2
  11.8 0.0 copy-done.3
  11.8 0.0 copy-done.6
  11.8 0.0 copy-done.7
  11.9 0.0 copy-done.8
  11.9 0.0 copy-start.4
  11.9 1.2 %copy-done.4 = bf16[256,2048]{1,0:T(8,128)(2,1)S(1)} copy-done((bf16[256,2048]{1,0:T(8,128)(2,1)S(1)}, bf16[256,2048]{1,0:T(8,128)(2,1)}, u32[]{:S(2)}) %copy-start.4) | copy-done | bytes 1048600
  13.1 0.9 %prepare_rest.1 = (bf16[336,128]{1,0:T(8,128)(2,1)S(1)}, bf16[336,128]{1,0:T(8,128)(2,1)S(1)}, bf16[336,128]{1,0:T(8,128)(2,1)S(1)}, bf16[336,128]{1,0:T(8,128)(...) custom-call(s32[1]{0:T(128)} %bitcast.1.refs_0_, ...), custom_call_target="tpu_custom_call" | custom-call | tf_op jit(solution)/shard_map/prepare_rest/pallas_call | solution.py:240
  14.0 0.6 collective-permute-start.11
  14.5 0.0 collective-permute-start.12
  14.5 0.0 collective-permute-done.1.refs_2_
  14.5 5.5 %collective-permute-start.13 = (bf16[336,128]{1,0:T(8,128)(2,1)S(1)}, bf16[336,128]{1,0:T(8,128)(2,1)S(1)}, u32[]{:S(2)}, u32[]{:S(2)}) collective-permute-start(bf16[336,128]{1,0:T(8,128)(2,1)S(1)} %get-tuple-element.37), channel_id=1, source_target_pairs={{0,11},{1,10},{2,9},{3,8},{4,15},{5,14},{6,13},{7,12},{8,3},{9,2},... | collective-permute-start | bytes 258056 | tf_op jit(solution)/shard_map/ppermute | solution.py:180
  20.0 0.0 collective-permute-done.10.refs_12_
  20.1 0.1 collective-permute-start.14
  20.1 0.0 collective-permute-done.2.refs_3_
  20.1 8.2 %collective-permute-start.3 = (bf16[336,128]{1,0:T(8,128)(2,1)S(1)}, bf16[336,128]{1,0:T(8,128)(2,1)S(1)}, u32[]{:S(2)}, u32[]{:S(2)}) collective-permute-start(bf16[336,128]{1,0:T(8,128)(2,1)S(1)} %get-tuple-element.27), channel_id=1, source_target_pairs={{0,10},{1,11},{2,8},{3,9},{4,14},{5,15},{6,12},{7,13},{8,2},{9,3},... | collective-permute-start | bytes 258056 | tf_op jit(solution)/shard_map/ppermute | solution.py:180
  28.3 0.0 collective-permute-done.11.refs_13_
  28.3 0.0 collective-permute-start.4
  28.3 0.0 collective-permute-done.12.refs_14_
  28.3 1.5 %collective-permute-start.5 = (bf16[336,128]{1,0:T(8,128)(2,1)S(1)}, bf16[336,128]{1,0:T(8,128)(2,1)S(1)}, u32[]{:S(2)}, u32[]{:S(2)}) collective-permute-start(bf16[336,128]{1,0:T(8,128)(2,1)S(1)} %get-tuple-element.29), channel_id=1, source_target_pairs={{0,9},{1,8},{2,11},{3,10},{4,13},{5,12},{6,15},{7,14},{8,1},{9,0},... | collective-permute-start | bytes 258056 | tf_op jit(solution)/shard_map/ppermute | solution.py:180
  29.9 0.0 collective-permute-done.13.refs_15_
  29.9 0.2 collective-permute-start.6
  30.1 0.0 collective-permute-done.14.refs_16_
  30.1 2.9 %collective-permute-start.7 = (bf16[336,128]{1,0:T(8,128)(2,1)S(1)}, bf16[336,128]{1,0:T(8,128)(2,1)S(1)}, u32[]{:S(2)}, u32[]{:S(2)}) collective-permute-start(bf16[336,128]{1,0:T(8,128)(2,1)S(1)} %get-tuple-element.31), channel_id=1, source_target_pairs={{0,8},{1,9},{2,10},{3,11},{4,12},{5,13},{6,14},{7,15},{8,0},{9,1},... | collective-permute-start | bytes 258056 | tf_op jit(solution)/shard_map/ppermute | solution.py:180
  33.0 0.0 collective-permute-done.3.refs_4_
  33.0 0.0 collective-permute-start.8
  33.0 0.1 collective-permute-done.4.refs_5_
  33.1 2.6 %collective-permute-start.9 = (bf16[336,128]{1,0:T(8,128)(2,1)S(1)}, bf16[336,128]{1,0:T(8,128)(2,1)S(1)}, u32[]{:S(2)}, u32[]{:S(2)}) collective-permute-start(bf16[336,128]{1,0:T(8,128)(2,1)S(1)} %get-tuple-element.33), channel_id=1, source_target_pairs={{0,2},{1,3},{2,0},{3,1},{4,6},{5,7},{6,4},{7,5},{8,10},{9,11},{10,... | collective-permute-start | bytes 258056 | tf_op jit(solution)/shard_map/ppermute | solution.py:180
  35.7 0.2 collective-permute-done.5.refs_6_
  35.9 0.8 %collective-permute-done.6.refs_7_ = bf16[336,128]{1,0:T(8,128)(2,1)S(1)} collective-permute-done((bf16[336,128]{1,0:T(8,128)(2,1)S(1)}, bf16[336,128]{1,0:T(8,128)(2,1)S(1)}, u32[]{:S(2)}, u32[]{:S(2)}) %collective-permute-start.6) | collective-permute-done | bytes 86048 | tf_op jit(solution)/shard_map/ppermute | solution.py:180
  36.8 2.4 %collective-permute-done.7.refs_8_ = bf16[336,128]{1,0:T(8,128)(2,1)S(1)} collective-permute-done((bf16[336,128]{1,0:T(8,128)(2,1)S(1)}, bf16[336,128]{1,0:T(8,128)(2,1)S(1)}, u32[]{:S(2)}, u32[]{:S(2)}) %collective-permute-start.7) | collective-permute-done | bytes 86048 | tf_op jit(solution)/shard_map/ppermute | solution.py:180
  39.2 0.0 collective-permute-done.8.refs_9_
  39.2 0.0 collective-permute-done.9.refs_10_
  39.2 4.5 %attend.1 = bf16[16,80,128]{2,1,0:T(8,128)(2,1)} custom-call(s32[1]{0:T(128)} %bitcast.1.refs_0_, bf16[336,128]{1,0:T(8,128)(2,1)S(1)} %get-tuple-element.24.refs_1_, bf16[336,128]{1,0:T(8,128)(2,1)S(1)} %collective-permute-done.1.refs_2_, bf16[336,128]{1,0:T(8,128)(2,1)S(1)} %collective-permute-done.2.refs_3_, ...), custom_call_target="tpu_custom_call" | custom-call | tf_op jit(solution)/shard_map/attend/pallas_call | solution.py:270
  43.7 4.5 %all-to-all-start = ((bf16[16,80,128]{2,1,0:T(8,128)(2,1)}), bf16[16,80,128]{2,1,0:T(8,128)(2,1)S(1)}, u32[]{:S(2)}, u32[]{:S(2)}) async-start(bf16[16,80,128]{2,1,0:T(8,128)(2,1)} %attend.1), calls=%async_computation | async-start | bytes 655360 | tf_op jit(solution)/shard_map/all_to_all | solution.py:290
  48.2 11.1 %all-to-all-done.refs_1_ = bf16[16,80,128]{2,1,0:T(8,128)(2,1)S(1)} async-done(((bf16[16,80,128]{2,1,0:T(8,128)(2,1)}), bf16[16,80,128]{2,1,0:T(8,128)(2,1)S(1)}, u32[]{:S(2)}, u32[]{:S(2)}) %all-to-all-start) | async-done | bytes 327712 | tf_op jit(solution)/shard_map/all_to_all | solution.py:290
  59.3 0.0 copy-done.5
  59.3 1.1 %finish.1 = bf16[128,2048]{1,0:T(8,128)(2,1)} custom-call(s32[1,80]{1,0:T(1,128)S(1)} %pad.4.refs_0_, bf16[16,80,128]{2,1,0:T(8,128)(2,1)S(1)} %all-to-all-done.refs_1_, bf16[128,2048]{1,0:T(8,128)(2,1)S(1)} %copy-done.5), custom_call_target="tpu_custom_call" | custom-call | tf_op jit(solution)/shard_map/finish/pallas_call | solution.py:293
  (7 shorter events, 0.0 us)
Async XLA Ops:
  0.0 11.8 %copy-start = (bf16[76,3,2048]{2,0,1:T(8,128)(2,1)S(1)}, bf16[76,3,2048]{2,0,1:T(8,128)(2,1)}, u32[]{:S(2)}) copy-start(bf16[76,3,2048]{2,0,1:T(8,128)(2,1)} %param.9) | copy-start | bytes 2801668
  0.0 11.8 %copy-start.1 = (bf16[128,2048]{1,0:T(8,128)(2,1)S(1)}, bf16[128,2048]{1,0:T(8,128)(2,1)}, u32[]{:S(2)}) copy-start(bf16[128,2048]{1,0:T(8,128)(2,1)} %refs_5_.3) | copy-start | bytes 1572868
  0.0 11.8 %copy-start.2 = (bf16[128,2048]{1,0:T(8,128)(2,1)S(1)}, bf16[128,2048]{1,0:T(8,128)(2,1)}, u32[]{:S(2)}) copy-start(bf16[128,2048]{1,0:T(8,128)(2,1)} %refs_6_.3) | copy-start | bytes 1572868
  0.0 11.8 %copy-start.3 = (bf16[256,2048]{1,0:T(8,128)(2,1)S(1)}, bf16[256,2048]{1,0:T(8,128)(2,1)}, u32[]{:S(2)}) copy-start(bf16[256,2048]{1,0:T(8,128)(2,1)} %refs_7_.1) | copy-start | bytes 3145732
  2.2 9.6 %collective-permute-start = (bf16[336,128]{1,0:T(8,128)(2,1)}, bf16[336,128]{1,0:T(8,128)(2,1)S(1)}, u32[]{:S(2)}, u32[]{:S(2)}) collective-permute-start(bf16[336,128]{1,0:T(8,128)(2,1)} %get-tuple-element.23), channel_id=1, source_target_pairs={{0,1},{1,0},{2,3},{3,2},{4,5},{5,4},{6,7},{7,6},{8,9},{9,8},{10,11... | collective-permute-start | bytes 258056 | tf_op jit(solution)/shard_map/ppermute | solution.py:180
  2.7 11.9 %collective-permute-start.1 = (bf16[336,128]{1,0:T(8,128)(2,1)}, bf16[336,128]{1,0:T(8,128)(2,1)S(1)}, u32[]{:S(2)}, u32[]{:S(2)}) collective-permute-start(bf16[336,128]{1,0:T(8,128)(2,1)} %get-tuple-element.25), channel_id=1, source_target_pairs={{0,15},{1,14},{2,13},{3,12},{4,11},{5,10},{6,9},{7,8},{8,7},{9,6},... | collective-permute-start | bytes 258056 | tf_op jit(solution)/shard_map/ppermute | solution.py:180
  8.4 3.5 %copy-start.6 = (f32[128]{0:T(128)S(1)}, f32[128]{0:T(128)}, u32[]{:S(2)}) copy-start(f32[128]{0:T(128)} %param.16) | copy-start | bytes 1540
  8.4 3.5 %copy-start.7 = (f32[128]{0:T(128)S(1)}, f32[128]{0:T(128)}, u32[]{:S(2)}) copy-start(f32[128]{0:T(128)} %param.17) | copy-start | bytes 1540
  8.4 3.5 %copy-start.8 = (s32[76]{0:T(128)S(1)}, s32[76]{0:T(128)}, u32[]{:S(2)}) copy-start(s32[76]{0:T(128)} %param.10) | copy-start | bytes 916
  8.4 11.7 %collective-permute-start.10 = (bf16[336,128]{1,0:T(8,128)(2,1)}, bf16[336,128]{1,0:T(8,128)(2,1)S(1)}, u32[]{:S(2)}, u32[]{:S(2)}) collective-permute-start(bf16[336,128]{1,0:T(8,128)(2,1)} %get-tuple-element.34), channel_id=1, source_target_pairs={{0,13},{1,12},{2,15},{3,14},{4,9},{5,8},{6,11},{7,10},{8,5},{9,4},... | collective-permute-start | bytes 258056 | tf_op jit(solution)/shard_map/ppermute | solution.py:180
  8.4 11.7 %collective-permute-start.2 = (bf16[336,128]{1,0:T(8,128)(2,1)}, bf16[336,128]{1,0:T(8,128)(2,1)S(1)}, u32[]{:S(2)}, u32[]{:S(2)}) collective-permute-start(bf16[336,128]{1,0:T(8,128)(2,1)} %get-tuple-element.26), channel_id=1, source_target_pairs={{0,14},{1,15},{2,12},{3,13},{4,10},{5,11},{6,8},{7,9},{8,6},{9,7},... | collective-permute-start | bytes 258056 | tf_op jit(solution)/shard_map/ppermute | solution.py:180
  11.9 1.2 %copy-start.4 = (bf16[256,2048]{1,0:T(8,128)(2,1)S(1)}, bf16[256,2048]{1,0:T(8,128)(2,1)}, u32[]{:S(2)}) copy-start(bf16[256,2048]{1,0:T(8,128)(2,1)} %refs_8_.3) | copy-start | bytes 3145732
  14.0 14.3 %collective-permute-start.11 = (bf16[336,128]{1,0:T(8,128)(2,1)S(1)}, bf16[336,128]{1,0:T(8,128)(2,1)S(1)}, u32[]{:S(2)}, u32[]{:S(2)}) collective-permute-start(bf16[336,128]{1,0:T(8,128)(2,1)S(1)} %get-tuple-element.35), channel_id=1, source_target_pairs={{0,12},{1,13},{2,14},{3,15},{4,8},{5,9},{6,10},{7,11},{8,4},{9,5},... | collective-permute-start | bytes 258056 | tf_op jit(solution)/shard_map/ppermute | solution.py:180
  14.5 13.8 %collective-permute-start.12 = (bf16[336,128]{1,0:T(8,128)(2,1)S(1)}, bf16[336,128]{1,0:T(8,128)(2,1)S(1)}, u32[]{:S(2)}, u32[]{:S(2)}) collective-permute-start(bf16[336,128]{1,0:T(8,128)(2,1)S(1)} %get-tuple-element.36), channel_id=1, source_target_pairs={{0,7},{1,6},{2,5},{3,4},{4,3},{5,2},{6,1},{7,0},{8,15},{9,14},{10,... | collective-permute-start | bytes 258056 | tf_op jit(solution)/shard_map/ppermute | solution.py:180
  14.5 15.3 %collective-permute-start.13 = (bf16[336,128]{1,0:T(8,128)(2,1)S(1)}, bf16[336,128]{1,0:T(8,128)(2,1)S(1)}, u32[]{:S(2)}, u32[]{:S(2)}) collective-permute-start(bf16[336,128]{1,0:T(8,128)(2,1)S(1)} %get-tuple-element.37), channel_id=1, source_target_pairs={{0,11},{1,10},{2,9},{3,8},{4,15},{5,14},{6,13},{7,12},{8,3},{9,2},... | collective-permute-start | bytes 258056 | tf_op jit(solution)/shard_map/ppermute | solution.py:180
  20.1 10.0 %collective-permute-start.14 = (bf16[336,128]{1,0:T(8,128)(2,1)S(1)}, bf16[336,128]{1,0:T(8,128)(2,1)S(1)}, u32[]{:S(2)}, u32[]{:S(2)}) collective-permute-start(bf16[336,128]{1,0:T(8,128)(2,1)S(1)} %get-tuple-element.38), channel_id=1, source_target_pairs={{0,6},{1,7},{2,4},{3,5},{4,2},{5,3},{6,0},{7,1},{8,14},{9,15},{10,... | collective-permute-start | bytes 258056 | tf_op jit(solution)/shard_map/ppermute | solution.py:180
  20.1 12.9 %collective-permute-start.3 = (bf16[336,128]{1,0:T(8,128)(2,1)S(1)}, bf16[336,128]{1,0:T(8,128)(2,1)S(1)}, u32[]{:S(2)}, u32[]{:S(2)}) collective-permute-start(bf16[336,128]{1,0:T(8,128)(2,1)S(1)} %get-tuple-element.27), channel_id=1, source_target_pairs={{0,10},{1,11},{2,8},{3,9},{4,14},{5,15},{6,12},{7,13},{8,2},{9,3},... | collective-permute-start | bytes 258056 | tf_op jit(solution)/shard_map/ppermute | solution.py:180
  28.3 4.8 %collective-permute-start.4 = (bf16[336,128]{1,0:T(8,128)(2,1)S(1)}, bf16[336,128]{1,0:T(8,128)(2,1)S(1)}, u32[]{:S(2)}, u32[]{:S(2)}) collective-permute-start(bf16[336,128]{1,0:T(8,128)(2,1)S(1)} %get-tuple-element.28), channel_id=1, source_target_pairs={{0,5},{1,4},{2,7},{3,6},{4,1},{5,0},{6,3},{7,2},{8,13},{9,12},{10,... | collective-permute-start | bytes 258056 | tf_op jit(solution)/shard_map/ppermute | solution.py:180
  28.3 7.6 %collective-permute-start.5 = (bf16[336,128]{1,0:T(8,128)(2,1)S(1)}, bf16[336,128]{1,0:T(8,128)(2,1)S(1)}, u32[]{:S(2)}, u32[]{:S(2)}) collective-permute-start(bf16[336,128]{1,0:T(8,128)(2,1)S(1)} %get-tuple-element.29), channel_id=1, source_target_pairs={{0,9},{1,8},{2,11},{3,10},{4,13},{5,12},{6,15},{7,14},{8,1},{9,0},... | collective-permute-start | bytes 258056 | tf_op jit(solution)/shard_map/ppermute | solution.py:180
  29.9 6.9 %collective-permute-start.6 = (bf16[336,128]{1,0:T(8,128)(2,1)S(1)}, bf16[336,128]{1,0:T(8,128)(2,1)S(1)}, u32[]{:S(2)}, u32[]{:S(2)}) collective-permute-start(bf16[336,128]{1,0:T(8,128)(2,1)S(1)} %get-tuple-element.30), channel_id=1, source_target_pairs={{0,4},{1,5},{2,6},{3,7},{4,0},{5,1},{6,2},{7,3},{8,12},{9,13},{10,... | collective-permute-start | bytes 258056 | tf_op jit(solution)/shard_map/ppermute | solution.py:180
  30.1 9.1 %collective-permute-start.7 = (bf16[336,128]{1,0:T(8,128)(2,1)S(1)}, bf16[336,128]{1,0:T(8,128)(2,1)S(1)}, u32[]{:S(2)}, u32[]{:S(2)}) collective-permute-start(bf16[336,128]{1,0:T(8,128)(2,1)S(1)} %get-tuple-element.31), channel_id=1, source_target_pairs={{0,8},{1,9},{2,10},{3,11},{4,12},{5,13},{6,14},{7,15},{8,0},{9,1},... | collective-permute-start | bytes 258056 | tf_op jit(solution)/shard_map/ppermute | solution.py:180
  33.0 6.2 %collective-permute-start.8 = (bf16[336,128]{1,0:T(8,128)(2,1)S(1)}, bf16[336,128]{1,0:T(8,128)(2,1)S(1)}, u32[]{:S(2)}, u32[]{:S(2)}) collective-permute-start(bf16[336,128]{1,0:T(8,128)(2,1)S(1)} %get-tuple-element.32), channel_id=1, source_target_pairs={{0,3},{1,2},{2,1},{3,0},{4,7},{5,6},{6,5},{7,4},{8,11},{9,10},{10,... | collective-permute-start | bytes 258056 | tf_op jit(solution)/shard_map/ppermute | solution.py:180
  33.1 6.1 %collective-permute-start.9 = (bf16[336,128]{1,0:T(8,128)(2,1)S(1)}, bf16[336,128]{1,0:T(8,128)(2,1)S(1)}, u32[]{:S(2)}, u32[]{:S(2)}) collective-permute-start(bf16[336,128]{1,0:T(8,128)(2,1)S(1)} %get-tuple-element.33), channel_id=1, source_target_pairs={{0,2},{1,3},{2,0},{3,1},{4,6},{5,7},{6,4},{7,5},{8,10},{9,11},{10,... | collective-permute-start | bytes 258056 | tf_op jit(solution)/shard_map/ppermute | solution.py:180
  43.7 15.6 %copy-start.5 = (bf16[128,2048]{1,0:T(8,128)(2,1)S(1)}, bf16[128,2048]{1,0:T(8,128)(2,1)}, u32[]{:S(2)}) copy-start(bf16[128,2048]{1,0:T(8,128)(2,1)} %refs_2_.1) | copy-start | bytes 1572868
  43.7 15.6 %all-to-all-start = ((bf16[16,80,128]{2,1,0:T(8,128)(2,1)}), bf16[16,80,128]{2,1,0:T(8,128)(2,1)S(1)}, u32[]{:S(2)}, u32[]{:S(2)}) async-start(bf16[16,80,128]{2,1,0:T(8,128)(2,1)} %attend.1), calls=%async_computation | async-start | bytes 655360 | tf_op jit(solution)/shard_map/all_to_all | solution.py:290

commit v11 on v10

--- a/solution.py
+++ b/solution.py
@@ -8,7 +8,7 @@
 from jax.sharding import PartitionSpec as P
 
 LOG2E = math.log2(math.e)
-FIRST_HEADS = [15, 14, 13, 1]
+FIRST_HEADS = [15, 14, 1]
 
 
 def round_up(count, step):
@@ -48,6 +48,12 @@
     q_gain = q_gain_ref[...]
     k_gain = k_gain_ref[...]
 
+    spare = []
+    for group in range(groups):
+        held = slots_ref[:, group * per_group : (group + 1) * per_group] < tokens
+        fresh_count = jnp.sum(held.astype(jnp.float32), axis=1, keepdims=True)
+        spare.append(jnp.broadcast_to(fresh_count, (padded - per_group, head_size)))
+
     def merged(fresh, cache):
         spread = jnp.dot(one_hot, fresh, preferred_element_type=jnp.float32)
         return jnp.where(is_fresh, spread, cache.astype(jnp.float32))
@@ -65,11 +71,9 @@
         keys = normalize(merged(fresh[1], cache_k), k_gain).astype(jnp.bfloat16)
         values = merged(fresh[2], cache_v).astype(jnp.bfloat16)
         queries = normalize(fresh[0].astype(jnp.float32), q_gain)
-        empty = jnp.zeros((padded - per_group, head_size), jnp.float32)
         for group in range(groups):
             share = queries[group * per_group : (group + 1) * per_group]
-            if padded > per_group:
-                share = jnp.concatenate([share, empty], axis=0)
+            share = jnp.concatenate([share, spare[group]], axis=0)
             queries_ref[group] = share.astype(jnp.bfloat16)
         for low in range(groups):
             out_ref = outs[turn * groups + low]
@@ -83,7 +87,7 @@
         text_values_ref[...] = text_v_ref[...]
 
 
-def attend_kernel(tokens, query_rows, key_rows, steps, me_ref, *rest):
+def attend_kernel(tokens, per_group, query_rows, key_rows, turns, steps, me_ref, *rest):
     me = me_ref[0]
     count = len(steps)
     arrived = rest[:count]
@@ -99,14 +103,26 @@
         first = text + step * tokens
         keys_ref[first : first + tokens] = arrived[step][:tokens]
         values_ref[first : first + tokens] = arrived[step][tokens : 2 * tokens]
-        queries_ref[step * padded : (step + 1) * padded] = arrived[step][2 * tokens :]
+
+    last_rows = slice(2 * tokens + padded - 16, 2 * tokens + padded)
+    count_row = per_group - (padded - 16)
+    firsts = [0]
+    for step in range(count):
+        spare = arrived[step][last_rows].astype(jnp.float32)[count_row : count_row + 1]
+        firsts.append(firsts[-1] + jnp.max(spare).astype(jnp.int32))
+    result_ref[...] = jnp.zeros_like(result_ref)
+    for step in range(count):
+        rows = arrived[step][2 * tokens :].astype(jnp.float32)
+        queries_ref[pl.ds(firsts[step], padded)] = rows
+    after = query_rows + padded
+    queries_ref[pl.ds(firsts[count], after)] = jnp.zeros((after, head_size), jnp.float32)
 
     def add_queries(step, carry):
         first_row = step * query_rows
         if not isinstance(step, int):
             first_row = pl.multiple_of(first_row, 16)
         mine = pl.ds(first_row, query_rows)
-        queries = queries_ref[mine]
+        queries = queries_ref[mine].astype(jnp.bfloat16)
         sums = None
         for first in range(0, keys_ref.shape[0], key_rows):
             scores = lax.dot_general(
@@ -120,18 +136,17 @@
             beside = jnp.concatenate([values, jnp.ones_like(values)], axis=1)
             added = jnp.dot(weights, beside, preferred_element_type=jnp.float32)
             sums = added if sums is None else sums + added
-        result_ref[mine] = (sums[:, :head_size] / sums[:, head_size:]).astype(jnp.bfloat16)
+        result_ref[mine] = sums[:, :head_size] / sums[:, head_size:]
         return carry
 
-    turns = queries_ref.shape[0] // query_rows
-    if turns <= 4:
+    if turns is not None:
         for step in range(turns):
             add_queries(step, 0)
     else:
-        lax.fori_loop(0, turns, add_queries, 0)
+        lax.fori_loop(0, (firsts[count] + query_rows - 1) // query_rows, add_queries, 0)
     for step in range(count):
         owner = lax.bitwise_xor(me, steps[step])
-        out_ref[owner] = result_ref[step * padded : (step + 1) * padded]
+        out_ref[owner] = result_ref[pl.ds(firsts[step], padded)].astype(jnp.bfloat16)
 
 
 def finish_kernel(per_group, slots_ref, returned_ref, cache_ref, out_ref):
@@ -190,7 +205,7 @@
     head_count = row_width // head_size
     groups = seq_count // head_count
     per_group = slot_count // groups
-    padded = round_up(per_group, 16)
+    padded = round_up(per_group + 1, 16)
     rows = 2 * tokens + padded
     q_gain = q_gain.reshape(1, head_size)
     k_gain = k_gain.reshape(1, head_size)
@@ -265,10 +280,15 @@
         arrived[step] = trade(made, step)
     arrived = [arrived[step] for step in steps]
 
-    query_rows = 4 * padded
+    all_fresh = seq_count * slot_count // 2
+    query_rows = 4 * slot_count
+    turns = -(-all_fresh // query_rows) if groups == 1 else None
+    packed_rows = seq_count * padded + query_rows + padded
     all_keys = text + seq_count * tokens
     result = pl.pallas_call(
-        lambda *refs: attend_kernel(tokens, query_rows, 768, steps, *refs),
+        lambda *refs: attend_kernel(
+            tokens, per_group, query_rows, 768, turns, steps, *refs
+        ),
         out_shape=jax.ShapeDtypeStruct((seq_count, padded, head_size), jnp.bfloat16),
         grid_spec=pltpu.PrefetchScalarGridSpec(
             num_scalar_prefetch=1,
@@ -277,10 +297,10 @@
             + [whole((text, head_size))] * 2,
             out_specs=whole((seq_count, padded, head_size)),
             scratch_shapes=[
-                pltpu.VMEM((seq_count * padded, head_size), jnp.bfloat16),
+                pltpu.VMEM((packed_rows, head_size), jnp.float32),
                 pltpu.VMEM((all_keys, head_size), jnp.bfloat16),
                 pltpu.VMEM((all_keys, head_size), jnp.bfloat16),
-                pltpu.VMEM((seq_count * padded, head_size), jnp.bfloat16),
+                pltpu.VMEM((packed_rows, head_size), jnp.float32),
             ],
         ),
         compiler_params=pltpu.CompilerParams(vmem_limit_bytes=40 * 2**20),

time: 60.6 us -> 59.4 us (0.980)
  waiting for transfers between devices: 14.6 us -> 17.5 us
  starting transfers between devices: 35.7 us -> 33.3 us
  Pallas kernels: 8.68 us -> 7.03 us
    ppermute x15, waiting for transfers between devices: 3.54 us -> 6.4 us  [trade(): return lax.ppermute(block, 'seq', [(a, a ^ step) for a in range(count)])]
    ppermute x15, starting transfers between devices: 31.2 us -> 28.5 us  [trade(): return lax.ppermute(block, 'seq', [(a, a ^ step) for a in range(count)])]
    pallas_call x1, Pallas kernels: 4.5 us -> 2.95 us  [shards(): pl.pallas_call(lambda *refs: attend_kernel(tokens, per_group, query_rows,...]
  transfers between devices with their start and end apart: 16 -> 16, of which waited for: 5 -> 6; matrix products, arithmetic and copies ran while one was open for 0% -> 0% of each run, Pallas kernels for 1% -> 2%
where the time goes in v11:
time: 59.4 us; the launch traced here: 59.1 us
  starting transfers between devices  33.3 us (56%)
  waiting for transfers between devices  17.5 us (29%)
  Pallas kernels  7.03 us (12%)
  local copies, waits for them, and re-layouts  1.26 us (2%)
    ppermute x15, starting transfers between devices, trade(): return lax.ppermute(block, 'seq', [(a, a ^ step) for a in range(count)])  28.5 us
    all_to_all x1, waiting for transfers between devices, shards(): lax.all_to_all(result, 'seq', split_axis=0, concat_axis=0, tiled=True)  11.1 us
    ppermute x15, waiting for transfers between devices, trade(): return lax.ppermute(block, 'seq', [(a, a ^ step) for a in range(count)])  6.4 us
    all_to_all x1, starting transfers between devices, shards(): lax.all_to_all(result, 'seq', split_axis=0, concat_axis=0, tiled=True)  4.75 us
    pallas_call x1, Pallas kernels, shards(): pl.pallas_call(lambda *refs: attend_kernel(tokens, per_group, query_rows,...  2.95 us
    pallas_call x1, Pallas kernels, shards(): pl.pallas_call(lambda *refs: prepare_kernel(per_group, padded, early, Tru...  2.06 us
    unnamed x18, local copies, waits for them, and re-layouts  1.25 us
  transfers between devices with their start and end apart: 16, of which 6 were waited for; matrix products, arithmetic and copies ran while one was open for 0% of the time, Pallas kernels for 2%

profile of v11, /device:TPU:0, one launch (start us, length us, event | category | flops | bytes accessed | tf_op | source)
XLA Modules:
  0.0 59.1 jit_solution(13380739481750544000)
XLA Ops:
  0.0 0.0 copy-start
  0.0 0.0 copy-start.1
  0.0 2.1 %prepare_first.1 = (bf16[336,128]{1,0:T(8,128)(2,1)}, bf16[336,128]{1,0:T(8,128)(2,1)}, bf16[336,128]{1,0:T(8,128)(2,1)}) custom-call(s32[1]{0:T(128)} %bitcast.1.refs_0_, s32[1,76]{1,0:T(1,128)} %bitcast.13, f32[1,128]{1,0:T(1,128)} %bitcast.9, f32[1,128]{1,0:T(1,128)} %bitcast.11, bf16[3,76,2048]{2,1,0:T(8,128)(2,1)} %bitcast.5, ...), custom_call_target="tpu_custom_call" | custom-call | tf_op jit(solution)/shard_map/prepare_first/pallas_call | solution.py:238
  2.1 0.5 collective-permute-start
  2.5 5.7 %collective-permute-start.1 = (bf16[336,128]{1,0:T(8,128)(2,1)}, bf16[336,128]{1,0:T(8,128)(2,1)S(1)}, u32[]{:S(2)}, u32[]{:S(2)}) collective-permute-start(bf16[336,128]{1,0:T(8,128)(2,1)} %get-tuple-element.25), channel_id=1, source_target_pairs={{0,15},{1,14},{2,13},{3,12},{4,11},{5,10},{6,9},{7,8},{8,7},{9,6},... | collective-permute-start | bytes 258056 | tf_op jit(solution)/shard_map/ppermute | solution.py:195
  8.2 0.0 collective-permute-start.2
  8.3 0.0 collective-permute-done.refs_9_.refs_11_
  8.3 0.0 copy-done
  8.3 0.0 copy-done.1
  8.3 0.0 copy-done.2
  8.3 0.0 copy-done.3
  8.3 0.0 copy-done.6
  8.3 0.0 copy-done.7
  8.3 0.0 copy-done.8
  8.3 0.0 copy-start.4
  8.3 1.2 %copy-done.4 = bf16[256,2048]{1,0:T(8,128)(2,1)S(1)} copy-done((bf16[256,2048]{1,0:T(8,128)(2,1)S(1)}, bf16[256,2048]{1,0:T(8,128)(2,1)}, u32[]{:S(2)}) %copy-start.4) | copy-done | bytes 1048600
  9.6 0.9 %prepare_rest.1 = (bf16[336,128]{1,0:T(8,128)(2,1)S(1)}, bf16[336,128]{1,0:T(8,128)(2,1)S(1)}, bf16[336,128]{1,0:T(8,128)(2,1)S(1)}, bf16[336,128]{1,0:T(8,128)(...) custom-call(s32[1]{0:T(128)} %bitcast.1.refs_0_, ...), custom_call_target="tpu_custom_call" | custom-call | tf_op jit(solution)/shard_map/prepare_rest/pallas_call | solution.py:255
  10.5 3.2 %collective-permute-start.10 = (bf16[336,128]{1,0:T(8,128)(2,1)S(1)}, bf16[336,128]{1,0:T(8,128)(2,1)S(1)}, u32[]{:S(2)}, u32[]{:S(2)}) collective-permute-start(bf16[336,128]{1,0:T(8,128)(2,1)S(1)} %get-tuple-element.34), channel_id=1, source_target_pairs={{0,13},{1,12},{2,15},{3,14},{4,9},{5,8},{6,11},{7,10},{8,5},{9,4},... | collective-permute-start | bytes 258056 | tf_op jit(solution)/shard_map/ppermute | solution.py:195
  13.7 0.7 %collective-permute-start.11 = (bf16[336,128]{1,0:T(8,128)(2,1)S(1)}, bf16[336,128]{1,0:T(8,128)(2,1)S(1)}, u32[]{:S(2)}, u32[]{:S(2)}) collective-permute-start(bf16[336,128]{1,0:T(8,128)(2,1)S(1)} %get-tuple-element.35), channel_id=1, source_target_pairs={{0,12},{1,13},{2,14},{3,15},{4,8},{5,9},{6,10},{7,11},{8,4},{9,5},... | collective-permute-start | bytes 258056 | tf_op jit(solution)/shard_map/ppermute | solution.py:195
  14.4 0.0 collective-permute-start.12
  14.4 0.0 collective-permute-done.1.refs_2_
  14.4 4.3 %collective-permute-start.13 = (bf16[336,128]{1,0:T(8,128)(2,1)S(1)}, bf16[336,128]{1,0:T(8,128)(2,1)S(1)}, u32[]{:S(2)}, u32[]{:S(2)}) collective-permute-start(bf16[336,128]{1,0:T(8,128)(2,1)S(1)} %get-tuple-element.37), channel_id=1, source_target_pairs={{0,11},{1,10},{2,9},{3,8},{4,15},{5,14},{6,13},{7,12},{8,3},{9,2},... | collective-permute-start | bytes 258056 | tf_op jit(solution)/shard_map/ppermute | solution.py:195
  18.7 0.0 collective-permute-done.2.refs_3_
  18.7 1.3 %collective-permute-start.14 = (bf16[336,128]{1,0:T(8,128)(2,1)S(1)}, bf16[336,128]{1,0:T(8,128)(2,1)S(1)}, u32[]{:S(2)}, u32[]{:S(2)}) collective-permute-start(bf16[336,128]{1,0:T(8,128)(2,1)S(1)} %get-tuple-element.38), channel_id=1, source_target_pairs={{0,6},{1,7},{2,4},{3,5},{4,2},{5,3},{6,0},{7,1},{8,14},{9,15},{10,... | collective-permute-start | bytes 258056 | tf_op jit(solution)/shard_map/ppermute | solution.py:195
  20.0 0.0 collective-permute-done.10.refs_12_
  20.0 2.9 %collective-permute-start.3 = (bf16[336,128]{1,0:T(8,128)(2,1)S(1)}, bf16[336,128]{1,0:T(8,128)(2,1)S(1)}, u32[]{:S(2)}, u32[]{:S(2)}) collective-permute-start(bf16[336,128]{1,0:T(8,128)(2,1)S(1)} %get-tuple-element.27), channel_id=1, source_target_pairs={{0,10},{1,11},{2,8},{3,9},{4,14},{5,15},{6,12},{7,13},{8,2},{9,3},... | collective-permute-start | bytes 258056 | tf_op jit(solution)/shard_map/ppermute | solution.py:195
  22.9 0.0 collective-permute-done.11.refs_13_
  22.9 2.2 %collective-permute-start.4 = (bf16[336,128]{1,0:T(8,128)(2,1)S(1)}, bf16[336,128]{1,0:T(8,128)(2,1)S(1)}, u32[]{:S(2)}, u32[]{:S(2)}) collective-permute-start(bf16[336,128]{1,0:T(8,128)(2,1)S(1)} %get-tuple-element.28), channel_id=1, source_target_pairs={{0,5},{1,4},{2,7},{3,6},{4,1},{5,0},{6,3},{7,2},{8,13},{9,12},{10,... | collective-permute-start | bytes 258056 | tf_op jit(solution)/shard_map/ppermute | solution.py:195
  25.1 0.0 collective-permute-done.12.refs_14_
  25.1 1.0 %collective-permute-start.5 = (bf16[336,128]{1,0:T(8,128)(2,1)S(1)}, bf16[336,128]{1,0:T(8,128)(2,1)S(1)}, u32[]{:S(2)}, u32[]{:S(2)}) collective-permute-start(bf16[336,128]{1,0:T(8,128)(2,1)S(1)} %get-tuple-element.29), channel_id=1, source_target_pairs={{0,9},{1,8},{2,11},{3,10},{4,13},{5,12},{6,15},{7,14},{8,1},{9,0},... | collective-permute-start | bytes 258056 | tf_op jit(solution)/shard_map/ppermute | solution.py:195
  26.1 0.7 %collective-permute-done.13.refs_15_ = bf16[336,128]{1,0:T(8,128)(2,1)S(1)} collective-permute-done((bf16[336,128]{1,0:T(8,128)(2,1)S(1)}, bf16[336,128]{1,0:T(8,128)(2,1)S(1)}, u32[]{:S(2)}, u32[]{:S(2)}) %collective-permute-start.13) | collective-permute-done | bytes 86048 | tf_op jit(solution)/shard_map/ppermute | solution.py:195
  26.8 2.9 %collective-permute-start.6 = (bf16[336,128]{1,0:T(8,128)(2,1)S(1)}, bf16[336,128]{1,0:T(8,128)(2,1)S(1)}, u32[]{:S(2)}, u32[]{:S(2)}) collective-permute-start(bf16[336,128]{1,0:T(8,128)(2,1)S(1)} %get-tuple-element.30), channel_id=1, source_target_pairs={{0,4},{1,5},{2,6},{3,7},{4,0},{5,1},{6,2},{7,3},{8,12},{9,13},{10,... | collective-permute-start | bytes 258056 | tf_op jit(solution)/shard_map/ppermute | solution.py:195
  29.7 0.0 collective-permute-done.14.refs_16_
  29.7 0.1 collective-permute-start.7
  29.8 1.4 %collective-permute-done.3.refs_4_ = bf16[336,128]{1,0:T(8,128)(2,1)S(1)} collective-permute-done((bf16[336,128]{1,0:T(8,128)(2,1)S(1)}, bf16[336,128]{1,0:T(8,128)(2,1)S(1)}, u32[]{:S(2)}, u32[]{:S(2)}) %collective-permute-start.3) | collective-permute-done | bytes 86048 | tf_op jit(solution)/shard_map/ppermute | solution.py:195
  31.2 2.7 %collective-permute-start.8 = (bf16[336,128]{1,0:T(8,128)(2,1)S(1)}, bf16[336,128]{1,0:T(8,128)(2,1)S(1)}, u32[]{:S(2)}, u32[]{:S(2)}) collective-permute-start(bf16[336,128]{1,0:T(8,128)(2,1)S(1)} %get-tuple-element.32), channel_id=1, source_target_pairs={{0,3},{1,2},{2,1},{3,0},{4,7},{5,6},{6,5},{7,4},{8,11},{9,10},{10,... | collective-permute-start | bytes 258056 | tf_op jit(solution)/shard_map/ppermute | solution.py:195
  33.9 0.0 collective-permute-done.4.refs_5_
  33.9 1.0 %collective-permute-start.9 = (bf16[336,128]{1,0:T(8,128)(2,1)S(1)}, bf16[336,128]{1,0:T(8,128)(2,1)S(1)}, u32[]{:S(2)}, u32[]{:S(2)}) collective-permute-start(bf16[336,128]{1,0:T(8,128)(2,1)S(1)} %get-tuple-element.33), channel_id=1, source_target_pairs={{0,2},{1,3},{2,0},{3,1},{4,6},{5,7},{6,4},{7,5},{8,10},{9,11},{10,... | collective-permute-start | bytes 258056 | tf_op jit(solution)/shard_map/ppermute | solution.py:195
  34.9 0.0 collective-permute-done.5.refs_6_
  34.9 0.8 %collective-permute-done.6.refs_7_ = bf16[336,128]{1,0:T(8,128)(2,1)S(1)} collective-permute-done((bf16[336,128]{1,0:T(8,128)(2,1)S(1)}, bf16[336,128]{1,0:T(8,128)(2,1)S(1)}, u32[]{:S(2)}, u32[]{:S(2)}) %collective-permute-start.6) | collective-permute-done | bytes 86048 | tf_op jit(solution)/shard_map/ppermute | solution.py:195
  35.7 2.7 %collective-permute-done.7.refs_8_ = bf16[336,128]{1,0:T(8,128)(2,1)S(1)} collective-permute-done((bf16[336,128]{1,0:T(8,128)(2,1)S(1)}, bf16[336,128]{1,0:T(8,128)(2,1)S(1)}, u32[]{:S(2)}, u32[]{:S(2)}) %collective-permute-start.7) | collective-permute-done | bytes 86048 | tf_op jit(solution)/shard_map/ppermute | solution.py:195
  38.3 0.0 collective-permute-done.8.refs_9_
  38.3 0.9 %collective-permute-done.9.refs_10_ = bf16[336,128]{1,0:T(8,128)(2,1)S(1)} collective-permute-done((bf16[336,128]{1,0:T(8,128)(2,1)S(1)}, bf16[336,128]{1,0:T(8,128)(2,1)S(1)}, u32[]{:S(2)}, u32[]{:S(2)}) %collective-permute-start.9) | collective-permute-done | bytes 86048 | tf_op jit(solution)/shard_map/ppermute | solution.py:195
  39.2 2.9 %attend.1 = bf16[16,80,128]{2,1,0:T(8,128)(2,1)} custom-call(s32[1]{0:T(128)} %bitcast.1.refs_0_, bf16[336,128]{1,0:T(8,128)(2,1)S(1)} %get-tuple-element.24.refs_1_, bf16[336,128]{1,0:T(8,128)(2,1)S(1)} %collective-permute-done.1.refs_2_, bf16[336,128]{1,0:T(8,128)(2,1)S(1)} %collective-permute-done.2.refs_3_, ...), custom_call_target="tpu_custom_call" | custom-call | tf_op jit(solution)/shard_map/attend/pallas_call | solution.py:288
  42.2 4.8 %all-to-all-start = ((bf16[16,80,128]{2,1,0:T(8,128)(2,1)}), bf16[16,80,128]{2,1,0:T(8,128)(2,1)S(1)}, u32[]{:S(2)}, u32[]{:S(2)}) async-start(bf16[16,80,128]{2,1,0:T(8,128)(2,1)} %attend.1), calls=%async_computation | async-start | bytes 655360 | tf_op jit(solution)/shard_map/all_to_all | solution.py:310
  47.0 11.1 %all-to-all-done.refs_1_ = bf16[16,80,128]{2,1,0:T(8,128)(2,1)S(1)} async-done(((bf16[16,80,128]{2,1,0:T(8,128)(2,1)}), bf16[16,80,128]{2,1,0:T(8,128)(2,1)S(1)}, u32[]{:S(2)}, u32[]{:S(2)}) %all-to-all-start) | async-done | bytes 327712 | tf_op jit(solution)/shard_map/all_to_all | solution.py:310
  58.0 0.0 copy-done.5
  58.0 1.1 %finish.1 = bf16[128,2048]{1,0:T(8,128)(2,1)} custom-call(s32[1,80]{1,0:T(1,128)S(1)} %pad.4.refs_0_, bf16[16,80,128]{2,1,0:T(8,128)(2,1)S(1)} %all-to-all-done.refs_1_, bf16[128,2048]{1,0:T(8,128)(2,1)S(1)} %copy-done.5), custom_call_target="tpu_custom_call" | custom-call | tf_op jit(solution)/shard_map/finish/pallas_call | solution.py:313
  (7 shorter events, 0.0 us)
Async XLA Ops:
  0.0 8.3 %copy-start = (bf16[76,3,2048]{2,0,1:T(8,128)(2,1)S(1)}, bf16[76,3,2048]{2,0,1:T(8,128)(2,1)}, u32[]{:S(2)}) copy-start(bf16[76,3,2048]{2,0,1:T(8,128)(2,1)} %param.9) | copy-start | bytes 2801668
  0.0 8.3 %copy-start.1 = (bf16[128,2048]{1,0:T(8,128)(2,1)S(1)}, bf16[128,2048]{1,0:T(8,128)(2,1)}, u32[]{:S(2)}) copy-start(bf16[128,2048]{1,0:T(8,128)(2,1)} %refs_5_.3) | copy-start | bytes 1572868
  0.0 8.3 %copy-start.2 = (bf16[128,2048]{1,0:T(8,128)(2,1)S(1)}, bf16[128,2048]{1,0:T(8,128)(2,1)}, u32[]{:S(2)}) copy-start(bf16[128,2048]{1,0:T(8,128)(2,1)} %refs_6_.3) | copy-start | bytes 1572868
  0.0 8.3 %copy-start.3 = (bf16[256,2048]{1,0:T(8,128)(2,1)S(1)}, bf16[256,2048]{1,0:T(8,128)(2,1)}, u32[]{:S(2)}) copy-start(bf16[256,2048]{1,0:T(8,128)(2,1)} %refs_7_.1) | copy-start | bytes 3145732
  2.1 6.2 %collective-permute-start = (bf16[336,128]{1,0:T(8,128)(2,1)}, bf16[336,128]{1,0:T(8,128)(2,1)S(1)}, u32[]{:S(2)}, u32[]{:S(2)}) collective-permute-start(bf16[336,128]{1,0:T(8,128)(2,1)} %get-tuple-element.23), channel_id=1, source_target_pairs={{0,1},{1,0},{2,3},{3,2},{4,5},{5,4},{6,7},{7,6},{8,9},{9,8},{10,11... | collective-permute-start | bytes 258056 | tf_op jit(solution)/shard_map/ppermute | solution.py:195
  2.5 5.8 %copy-start.6 = (f32[128]{0:T(128)S(1)}, f32[128]{0:T(128)}, u32[]{:S(2)}) copy-start(f32[128]{0:T(128)} %param.16) | copy-start | bytes 1540
  2.5 5.8 %copy-start.7 = (f32[128]{0:T(128)S(1)}, f32[128]{0:T(128)}, u32[]{:S(2)}) copy-start(f32[128]{0:T(128)} %param.17) | copy-start | bytes 1540
  2.5 5.8 %copy-start.8 = (s32[76]{0:T(128)S(1)}, s32[76]{0:T(128)}, u32[]{:S(2)}) copy-start(s32[76]{0:T(128)} %param.10) | copy-start | bytes 916
  2.5 11.8 %collective-permute-start.1 = (bf16[336,128]{1,0:T(8,128)(2,1)}, bf16[336,128]{1,0:T(8,128)(2,1)S(1)}, u32[]{:S(2)}, u32[]{:S(2)}) collective-permute-start(bf16[336,128]{1,0:T(8,128)(2,1)} %get-tuple-element.25), channel_id=1, source_target_pairs={{0,15},{1,14},{2,13},{3,12},{4,11},{5,10},{6,9},{7,8},{8,7},{9,6},... | collective-permute-start | bytes 258056 | tf_op jit(solution)/shard_map/ppermute | solution.py:195
  8.2 10.5 %collective-permute-start.2 = (bf16[336,128]{1,0:T(8,128)(2,1)}, bf16[336,128]{1,0:T(8,128)(2,1)S(1)}, u32[]{:S(2)}, u32[]{:S(2)}) collective-permute-start(bf16[336,128]{1,0:T(8,128)(2,1)} %get-tuple-element.26), channel_id=1, source_target_pairs={{0,14},{1,15},{2,12},{3,13},{4,10},{5,11},{6,8},{7,9},{8,6},{9,7},... | collective-permute-start | bytes 258056 | tf_op jit(solution)/shard_map/ppermute | solution.py:195
  8.3 1.2 %copy-start.4 = (bf16[256,2048]{1,0:T(8,128)(2,1)S(1)}, bf16[256,2048]{1,0:T(8,128)(2,1)}, u32[]{:S(2)}) copy-start(bf16[256,2048]{1,0:T(8,128)(2,1)} %refs_8_.3) | copy-start | bytes 3145732
  10.5 9.5 %collective-permute-start.10 = (bf16[336,128]{1,0:T(8,128)(2,1)S(1)}, bf16[336,128]{1,0:T(8,128)(2,1)S(1)}, u32[]{:S(2)}, u32[]{:S(2)}) collective-permute-start(bf16[336,128]{1,0:T(8,128)(2,1)S(1)} %get-tuple-element.34), channel_id=1, source_target_pairs={{0,13},{1,12},{2,15},{3,14},{4,9},{5,8},{6,11},{7,10},{8,5},{9,4},... | collective-permute-start | bytes 258056 | tf_op jit(solution)/shard_map/ppermute | solution.py:195
  13.7 9.2 %collective-permute-start.11 = (bf16[336,128]{1,0:T(8,128)(2,1)S(1)}, bf16[336,128]{1,0:T(8,128)(2,1)S(1)}, u32[]{:S(2)}, u32[]{:S(2)}) collective-permute-start(bf16[336,128]{1,0:T(8,128)(2,1)S(1)} %get-tuple-element.35), channel_id=1, source_target_pairs={{0,12},{1,13},{2,14},{3,15},{4,8},{5,9},{6,10},{7,11},{8,4},{9,5},... | collective-permute-start | bytes 258056 | tf_op jit(solution)/shard_map/ppermute | solution.py:195
  14.4 10.7 %collective-permute-start.12 = (bf16[336,128]{1,0:T(8,128)(2,1)S(1)}, bf16[336,128]{1,0:T(8,128)(2,1)S(1)}, u32[]{:S(2)}, u32[]{:S(2)}) collective-permute-start(bf16[336,128]{1,0:T(8,128)(2,1)S(1)} %get-tuple-element.36), channel_id=1, source_target_pairs={{0,7},{1,6},{2,5},{3,4},{4,3},{5,2},{6,1},{7,0},{8,15},{9,14},{10,... | collective-permute-start | bytes 258056 | tf_op jit(solution)/shard_map/ppermute | solution.py:195
  14.4 12.4 %collective-permute-start.13 = (bf16[336,128]{1,0:T(8,128)(2,1)S(1)}, bf16[336,128]{1,0:T(8,128)(2,1)S(1)}, u32[]{:S(2)}, u32[]{:S(2)}) collective-permute-start(bf16[336,128]{1,0:T(8,128)(2,1)S(1)} %get-tuple-element.37), channel_id=1, source_target_pairs={{0,11},{1,10},{2,9},{3,8},{4,15},{5,14},{6,13},{7,12},{8,3},{9,2},... | collective-permute-start | bytes 258056 | tf_op jit(solution)/shard_map/ppermute | solution.py:195
  18.7 11.0 %collective-permute-start.14 = (bf16[336,128]{1,0:T(8,128)(2,1)S(1)}, bf16[336,128]{1,0:T(8,128)(2,1)S(1)}, u32[]{:S(2)}, u32[]{:S(2)}) collective-permute-start(bf16[336,128]{1,0:T(8,128)(2,1)S(1)} %get-tuple-element.38), channel_id=1, source_target_pairs={{0,6},{1,7},{2,4},{3,5},{4,2},{5,3},{6,0},{7,1},{8,14},{9,15},{10,... | collective-permute-start | bytes 258056 | tf_op jit(solution)/shard_map/ppermute | solution.py:195
  20.0 11.2 %collective-permute-start.3 = (bf16[336,128]{1,0:T(8,128)(2,1)S(1)}, bf16[336,128]{1,0:T(8,128)(2,1)S(1)}, u32[]{:S(2)}, u32[]{:S(2)}) collective-permute-start(bf16[336,128]{1,0:T(8,128)(2,1)S(1)} %get-tuple-element.27), channel_id=1, source_target_pairs={{0,10},{1,11},{2,8},{3,9},{4,14},{5,15},{6,12},{7,13},{8,2},{9,3},... | collective-permute-start | bytes 258056 | tf_op jit(solution)/shard_map/ppermute | solution.py:195
  22.9 11.0 %collective-permute-start.4 = (bf16[336,128]{1,0:T(8,128)(2,1)S(1)}, bf16[336,128]{1,0:T(8,128)(2,1)S(1)}, u32[]{:S(2)}, u32[]{:S(2)}) collective-permute-start(bf16[336,128]{1,0:T(8,128)(2,1)S(1)} %get-tuple-element.28), channel_id=1, source_target_pairs={{0,5},{1,4},{2,7},{3,6},{4,1},{5,0},{6,3},{7,2},{8,13},{9,12},{10,... | collective-permute-start | bytes 258056 | tf_op jit(solution)/shard_map/ppermute | solution.py:195
  25.1 9.8 %collective-permute-start.5 = (bf16[336,128]{1,0:T(8,128)(2,1)S(1)}, bf16[336,128]{1,0:T(8,128)(2,1)S(1)}, u32[]{:S(2)}, u32[]{:S(2)}) collective-permute-start(bf16[336,128]{1,0:T(8,128)(2,1)S(1)} %get-tuple-element.29), channel_id=1, source_target_pairs={{0,9},{1,8},{2,11},{3,10},{4,13},{5,12},{6,15},{7,14},{8,1},{9,0},... | collective-permute-start | bytes 258056 | tf_op jit(solution)/shard_map/ppermute | solution.py:195
  26.8 8.8 %collective-permute-start.6 = (bf16[336,128]{1,0:T(8,128)(2,1)S(1)}, bf16[336,128]{1,0:T(8,128)(2,1)S(1)}, u32[]{:S(2)}, u32[]{:S(2)}) collective-permute-start(bf16[336,128]{1,0:T(8,128)(2,1)S(1)} %get-tuple-element.30), channel_id=1, source_target_pairs={{0,4},{1,5},{2,6},{3,7},{4,0},{5,1},{6,2},{7,3},{8,12},{9,13},{10,... | collective-permute-start | bytes 258056 | tf_op jit(solution)/shard_map/ppermute | solution.py:195
  29.7 8.6 %collective-permute-start.7 = (bf16[336,128]{1,0:T(8,128)(2,1)S(1)}, bf16[336,128]{1,0:T(8,128)(2,1)S(1)}, u32[]{:S(2)}, u32[]{:S(2)}) collective-permute-start(bf16[336,128]{1,0:T(8,128)(2,1)S(1)} %get-tuple-element.31), channel_id=1, source_target_pairs={{0,8},{1,9},{2,10},{3,11},{4,12},{5,13},{6,14},{7,15},{8,0},{9,1},... | collective-permute-start | bytes 258056 | tf_op jit(solution)/shard_map/ppermute | solution.py:195
  31.2 7.1 %collective-permute-start.8 = (bf16[336,128]{1,0:T(8,128)(2,1)S(1)}, bf16[336,128]{1,0:T(8,128)(2,1)S(1)}, u32[]{:S(2)}, u32[]{:S(2)}) collective-permute-start(bf16[336,128]{1,0:T(8,128)(2,1)S(1)} %get-tuple-element.32), channel_id=1, source_target_pairs={{0,3},{1,2},{2,1},{3,0},{4,7},{5,6},{6,5},{7,4},{8,11},{9,10},{10,... | collective-permute-start | bytes 258056 | tf_op jit(solution)/shard_map/ppermute | solution.py:195
  33.9 5.3 %collective-permute-start.9 = (bf16[336,128]{1,0:T(8,128)(2,1)S(1)}, bf16[336,128]{1,0:T(8,128)(2,1)S(1)}, u32[]{:S(2)}, u32[]{:S(2)}) collective-permute-start(bf16[336,128]{1,0:T(8,128)(2,1)S(1)} %get-tuple-element.33), channel_id=1, source_target_pairs={{0,2},{1,3},{2,0},{3,1},{4,6},{5,7},{6,4},{7,5},{8,10},{9,11},{10,... | collective-permute-start | bytes 258056 | tf_op jit(solution)/shard_map/ppermute | solution.py:195
  42.2 15.9 %copy-start.5 = (bf16[128,2048]{1,0:T(8,128)(2,1)S(1)}, bf16[128,2048]{1,0:T(8,128)(2,1)}, u32[]{:S(2)}) copy-start(bf16[128,2048]{1,0:T(8,128)(2,1)} %refs_2_.1) | copy-start | bytes 1572868
  42.2 15.9 %all-to-all-start = ((bf16[16,80,128]{2,1,0:T(8,128)(2,1)}), bf16[16,80,128]{2,1,0:T(8,128)(2,1)S(1)}, u32[]{:S(2)}, u32[]{:S(2)}) async-start(bf16[16,80,128]{2,1,0:T(8,128)(2,1)} %attend.1), calls=%async_computation | async-start | bytes 655360 | tf_op jit(solution)/shard_map/all_to_all | solution.py:310

commit v12 on v8

v12 whole, which is shorter than its diff:
```python
import math

import jax
import jax.numpy as jnp
from jax import lax
from jax.experimental import pallas as pl
from jax.experimental.pallas import tpu as pltpu
from jax.sharding import PartitionSpec as P

LOG2E = math.log2(math.e)
INNER = 4
CORE, NEXT = 1, 2
MIB = 2**20


def round_up(count, step):
    return (count + step - 1) // step * step


def normalize(entries, scales):
    mean_square = jnp.mean(entries * entries, axis=-1, keepdims=True)
    return entries * lax.rsqrt(mean_square + 1e-06) * scales


def place(slots, tokens):
    owner = lax.broadcasted_iota(jnp.int32, (tokens, slots.shape[1]), 0)
    return owner == slots


def prepare_kernel(plan, padded, me_ref, *refs):
    with_text = any(share for _, _, share in plan)
    slots_hbm, q_gain_hbm, k_gain_hbm, qkv_hbm, k_hbm, v_hbm = refs[:6]
    rest = refs[6:]
    if with_text:
        text_k_hbm, text_v_hbm = rest[:2]
        rest = rest[2:]
    outs = []
    for _, pair, share in plan:
        outs.append((rest[0] if pair else None, rest[pair] if share else None))
        rest = rest[pair + share :]
    if with_text:
        text_out_ref, rest = rest[0], rest[1:]
    slots_ref, q_gain_ref, k_gain_ref, fresh_ref, k_ref, v_ref, text_ref = rest[:7]
    small_sems, sems, text_sems = rest[7:]
    slot_count = slots_ref.shape[1]
    tokens, width = k_ref.shape[1:]
    head_size = q_gain_ref.shape[1]
    outer = me_ref[0] // INNER

    def columns(step):
        return pl.ds(pl.multiple_of(lax.bitwise_xor(outer, step) * width, width), width)

    small = [
        pltpu.make_async_copy(slots_hbm, slots_ref, small_sems.at[0]),
        pltpu.make_async_copy(q_gain_hbm, q_gain_ref, small_sems.at[1]),
        pltpu.make_async_copy(k_gain_hbm, k_gain_ref, small_sems.at[2]),
    ]
    for copy in small:
        copy.start()
    loads = []
    for turn, (step, pair, _) in enumerate(plan):
        mine = columns(step)
        copies = [
            pltpu.make_async_copy(qkv_hbm.at[:, :, mine], fresh_ref.at[turn], sems.at[turn, 0])
        ]
        if pair:
            copies += [
                pltpu.make_async_copy(k_hbm.at[:, mine], k_ref.at[turn], sems.at[turn, 1]),
                pltpu.make_async_copy(v_hbm.at[:, mine], v_ref.at[turn], sems.at[turn, 2]),
            ]
        for copy in copies:
            copy.start()
        loads.append(copies)
    if with_text:
        mine = columns(0)
        text_loads = [
            pltpu.make_async_copy(text_k_hbm.at[:, mine], text_ref.at[0], text_sems.at[0]),
            pltpu.make_async_copy(text_v_hbm.at[:, mine], text_ref.at[1], text_sems.at[1]),
        ]
        for copy in text_loads:
            copy.start()
    for copy in small:
        copy.wait()
    belongs = place(slots_ref[...], tokens)
    is_fresh = jnp.max(belongs.astype(jnp.float32), axis=1, keepdims=True) > 0.5
    one_hot = belongs.astype(jnp.bfloat16)
    q_gain = q_gain_ref[...]
    k_gain = k_gain_ref[...]
    empty = jnp.zeros((padded - slot_count, head_size), jnp.float32)

    def merged(fresh, cache):
        spread = jnp.dot(one_hot, fresh, preferred_element_type=jnp.float32)
        return jnp.where(is_fresh, spread, cache.astype(jnp.float32))

    for turn, (pair_ref, share_ref) in enumerate(outs):
        for copy in loads[turn]:
            copy.wait()
        for head in range(width // head_size):
            lanes = slice(head * head_size, (head + 1) * head_size)
            if pair_ref is not None:
                keys = merged(fresh_ref[turn, 1, :, lanes], k_ref[turn, :, lanes])
                values = merged(fresh_ref[turn, 2, :, lanes], v_ref[turn, :, lanes])
                pair_ref[0, head] = normalize(keys, k_gain).astype(jnp.bfloat16)
                pair_ref[1, head] = values.astype(jnp.bfloat16)
            if share_ref is not None:
                queries = normalize(fresh_ref[turn, 0, :, lanes].astype(jnp.float32), q_gain)
                if padded > slot_count:
                    queries = jnp.concatenate([queries, empty], axis=0)
                share_ref[head] = queries.astype(jnp.bfloat16)
    if with_text:
        for copy in text_loads:
            copy.wait()
        for head in range(width // head_size):
            lanes = slice(head * head_size, (head + 1) * head_size)
            text_keys = normalize(text_ref[0, :, lanes].astype(jnp.float32), k_gain)
            text_out_ref[0, head] = text_keys.astype(jnp.bfloat16)
            text_out_ref[1, head] = text_ref[1, :, lanes]


def stack_kernel(*refs):
    out_ref = refs[-1]
    for number, ref in enumerate(refs[:-1]):
        out_ref[number] = ref[...]


def add_keys(sums, queries, keys, values):
    factor = queries.shape[1] ** (-0.5) * LOG2E
    scores = lax.dot_general(
        queries, keys, (((1,), (1,)), ((), ())), preferred_element_type=jnp.float32
    )
    weights = jnp.exp2(scores * factor).astype(jnp.bfloat16)
    beside = jnp.concatenate([values, jnp.ones_like(values)], axis=1)
    added = jnp.dot(weights, beside, preferred_element_type=jnp.float32)
    return added if sums is None else sums + added


def add_pairs(sums, queries, refs, head):
    pairs = []
    for ref in refs:
        if len(ref.shape) == 4:
            pairs.append(lambda part, ref=ref: ref[part, head])
        else:
            for number in range(ref.shape[0]):
                pairs.append(lambda part, ref=ref, number=number: ref[number, part, head])
    for first in range(0, len(pairs), 6):
        some = pairs[first : first + 6]
        keys = jnp.concatenate([pair(0) for pair in some], axis=0)
        values = jnp.concatenate([pair(1) for pair in some], axis=0)
        sums = add_keys(sums, queries, keys, values)
    return sums


def query_blocks(queries, head):
    for first in range(0, len(queries), 4):
        yield first, jnp.concatenate([ref[head] for ref in queries[first : first + 4]], axis=0)


def attend_kernel(count, *refs):
    queries, pairs, sums_ref = refs[:count], refs[count:-1], refs[-1]
    for head in range(queries[0].shape[0]):
        for first, block in query_blocks(queries, head):
            sums_ref[head, first // 4] = add_pairs(None, block, pairs, head)


def complete_kernel(count, *refs):
    queries, rest = refs[:count], refs[count:]
    pairs, sums_ref, outs = rest[:2], rest[2], rest[3:]
    heads, padded, head_size = queries[0].shape
    for head in range(heads):
        for first, block in query_blocks(queries, head):
            sums = add_pairs(sums_ref[head, first // 4], block, pairs, head)
            result = (sums[:, :head_size] / sums[:, head_size:]).astype(jnp.bfloat16)
            for turn in range(block.shape[0] // padded):
                outs[first + turn][head] = result[turn * padded : (turn + 1) * padded]


def finish_kernel(heads, steps, me_ref, slots_ref, cache_ref, *rest):
    returned, out_ref = rest[:-1], rest[-1]
    tokens = cache_ref.shape[0]
    head_size = returned[0].shape[2]
    groups = slots_ref.shape[0]
    outer = me_ref[0] // INNER
    one_hot = []
    owned = jnp.zeros((tokens, 1), jnp.float32)
    for low in range(groups):
        group = lax.bitwise_xor(outer % groups, low)
        mine = place(slots_ref[pl.ds(group, 1)], tokens).astype(jnp.float32)
        owned = owned + jnp.sum(mine, axis=1, keepdims=True)
        one_hot.append(mine.astype(jnp.bfloat16))
    is_fresh = owned > 0.5
    for high in range(len(steps) // groups):
        block = lax.bitwise_xor(outer // groups, high)
        for head in range(heads):
            at = (block * heads + head) * head_size
            columns = pl.ds(pl.multiple_of(at, head_size), head_size)
            placed = jnp.zeros((tokens, head_size), jnp.float32)
            for low in range(groups):
                made = returned[steps.index(high * groups + low)][head]
                placed = placed + jnp.dot(one_hot[low], made, preferred_element_type=jnp.float32)
            out_ref[:, columns] = jnp.where(
                is_fresh, placed, cache_ref[:, columns].astype(jnp.float32)
            ).astype(out_ref.dtype)


def trade(block, distance):
    count = lax.axis_size("seq")
    return lax.ppermute(block, "seq", [(a, a ^ distance) for a in range(count)])


def shards(fresh_qkv, slot_rows, k_cache, v_cache, attn_cache, text_k, text_v, q_gain, k_gain):
    seq_count = lax.axis_size("seq")
    me = lax.axis_index("seq").reshape(1)
    slot_count = slot_rows.shape[0]
    tokens, row_width = k_cache.shape
    text = text_k.shape[0]
    head_size = q_gain.shape[0]
    outers = seq_count // INNER
    width = row_width // outers
    heads = width // head_size
    padded = round_up(slot_count, 16)
    qkv = jnp.transpose(fresh_qkv, (1, 0, 2))
    q_gain = q_gain.reshape(1, head_size)
    k_gain = k_gain.reshape(1, head_size)
    slots = slot_rows.reshape(1, slot_count)
    padded_slots = jnp.pad(
        slots, ((0, 0), (0, padded - slot_count)), constant_values=tokens
    )

    def shaped(*shape, dtype=jnp.bfloat16):
        return jax.ShapeDtypeStruct(shape, dtype)

    in_hbm = pl.BlockSpec(memory_space=pltpu.HBM)
    in_vmem = pl.BlockSpec(memory_space=pltpu.VMEM)
    in_smem = pl.BlockSpec(memory_space=pltpu.SMEM)
    small = pltpu.CompilerParams(vmem_limit_bytes=24 * MIB)

    def prepare(plan, name, params, *extra):
        with_text = len(extra) > 0
        shapes = []
        for _, pair, share in plan:
            shapes += [shaped(2, heads, tokens, head_size)] * pair
            shapes += [shaped(heads, padded, head_size)] * share
        if with_text:
            shapes.append(shaped(2, heads, text, head_size))
        made = pl.pallas_call(
            lambda *refs: prepare_kernel(plan, padded, *refs),
            out_shape=shapes,
            in_specs=[in_smem] + [in_hbm] * 6 + [in_hbm] * (2 * with_text),
            out_specs=[in_vmem] * len(shapes),
            scratch_shapes=[
                pltpu.VMEM((1, slot_count), jnp.int32),
                pltpu.VMEM((1, head_size), jnp.float32),
                pltpu.VMEM((1, head_size), jnp.float32),
                pltpu.VMEM((len(plan), 3, slot_count, width), jnp.bfloat16),
                pltpu.VMEM((len(plan), tokens, width), jnp.bfloat16),
                pltpu.VMEM((len(plan), tokens, width), jnp.bfloat16),
                pltpu.VMEM((2, text, width), jnp.bfloat16),
                pltpu.SemaphoreType.DMA((3,)),
                pltpu.SemaphoreType.DMA((len(plan), 3)),
                pltpu.SemaphoreType.DMA((2,)),
            ],
            compiler_params=params,
            name=name,
        )(me, slots, q_gain, k_gain, qkv, k_cache, v_cache, *extra)
        return list(made)

    def stack(blocks, after, name):
        return pl.pallas_call(
            lambda *refs: stack_kernel(*refs[len(after) :]),
            out_shape=shaped(len(blocks), *blocks[0].shape),
            in_specs=[pl.BlockSpec(memory_space=pl.ANY)] * len(after) + [in_vmem] * len(blocks),
            out_specs=in_vmem,
            compiler_params=small,
            name=name,
        )(*after, *blocks)

    half = outers // 2
    near = list(range(1, half))
    far = list(reversed(range(half + 1, outers)))
    order = far[:1] + near + [half] + far[1:] + [0]
    made = prepare(
        [(step, True, True) for step in order], "prepare", pltpu.CompilerParams(), text_k, text_v
    )
    text_pair = made.pop()
    own = made[-2]
    own_other = trade(own, CORE)
    pairs, shares = {}, {0: made[-1]}
    for number, step in enumerate(order[:-1]):
        pairs[step] = trade(made[2 * number], step * INNER)
        shares[step] = trade(made[2 * number + 1], step * INNER)

    own_next = trade(own, NEXT)
    early = [own_next]
    for step in near:
        early += [pairs[step], trade(pairs[step], NEXT)]
    early = stack(early, [shares[step] for step in near], "stack_near")
    middle = []
    for step in far:
        middle += [pairs[step], trade(pairs[step], NEXT)]
    middle = stack(middle, [shares[step] for step in far], "stack_far")
    late = stack([pairs[half], trade(pairs[half], NEXT)], [shares[half]], "stack_last")

    sources = far + [half] + near + [0]
    queries = [shares[step] for step in sources]
    known = [own, own_other, early, trade(early, CORE), middle, trade(middle, CORE)]
    blocks = -(-outers // 4)
    sums = pl.pallas_call(
        lambda *refs: attend_kernel(outers, *refs),
        out_shape=shaped(heads, blocks, 4 * padded, 2 * head_size, dtype=jnp.float32),
        in_specs=[in_vmem] * (outers + 1 + len(known)),
        out_specs=in_vmem,
        compiler_params=small,
        name="attend",
    )(*queries, text_pair, *known)
    results = pl.pallas_call(
        lambda *refs: complete_kernel(outers, *refs),
        out_shape=[shaped(heads, padded, head_size)] * outers,
        in_specs=[in_vmem] * (outers + 3),
        out_specs=[in_vmem] * outers,
        compiler_params=small,
        name="complete",
    )(*queries, late, trade(late, CORE), sums)

    returned = [
        trade(result, step * INNER) if step else result
        for step, result in zip(sources, results)
    ]
    return pl.pallas_call(
        lambda *refs: finish_kernel(heads, sources, *refs),
        out_shape=jax.ShapeDtypeStruct((tokens, row_width), attn_cache.dtype),
        in_specs=[in_smem] + [in_vmem] * (2 + outers),
        out_specs=in_vmem,
        compiler_params=small,
        name="finish",
    )(me, padded_slots, attn_cache, *returned)


def solution(mesh):
    return jax.shard_map(
        shards,
        mesh=mesh,
        in_specs=(
            P(("parts", "seq"), None, None),
            P(("parts", "seq")),
            P(("parts", "seq"), None),
            P(("parts", "seq"), None),
            P(("parts", "seq"), None),
            P("parts", None),
            P("parts", None),
            P(),
            P(),
        ),
        out_specs=P(("parts", "seq"), None),
        check_vma=False,
    )
```

time: 62.9 us -> 61.4 us (0.976)
  waiting for transfers between devices: 18.4 us -> 24.8 us
  Pallas kernels: 12 us -> 9.29 us
  starting transfers between devices: 29.6 us -> 26.9 us
  local copies, waits for them, and re-layouts: 2.49 us -> 0.04 us
    ppermute x16 -> x17, waiting for transfers between devices: 18.4 us -> 24.8 us  [trade(): return lax.ppermute(block, 'seq', [(a, a ^ distance) for a in range(count)])]
    pallas_call x6 -> x7, Pallas kernels: 12 us -> 9.29 us  [the longest x1 4.18 us: prepare(): pl.pallas_call(lambda *refs: prepare_kernel(plan, padded, *refs), out_sha...]
    ppermute x16 -> x17, starting transfers between devices: 29.6 us -> 26.9 us  [trade(): return lax.ppermute(block, 'seq', [(a, a ^ distance) for a in range(count)])]
    unnamed x22 -> x14, local copies, waits for them, and re-layouts: 2.48 us -> 0.04 us
  transfers between devices with their start and end apart: 16 -> 17, of which waited for: 7 -> 8; matrix products, arithmetic and copies ran while one was open for 0% -> 0% of each run, Pallas kernels for 9% -> 5%
where the time goes in v12:
time: 61.4 us; the launch traced here: 61.2 us
  starting transfers between devices  26.9 us (44%)
  waiting for transfers between devices  24.8 us (40%)
  Pallas kernels  9.29 us (15%)
    ppermute x17, starting transfers between devices, trade(): return lax.ppermute(block, 'seq', [(a, a ^ distance) for a in range(count)])  26.9 us
    ppermute x17, waiting for transfers between devices, trade(): return lax.ppermute(block, 'seq', [(a, a ^ distance) for a in range(count)])  24.8 us
    pallas_call x1, Pallas kernels, prepare(): pl.pallas_call(lambda *refs: prepare_kernel(plan, padded, *refs), out_sha...  4.18 us
    pallas_call x1, Pallas kernels, shards(): pl.pallas_call(lambda *refs: attend_kernel(outers, *refs), out_shape=shap...  2.91 us
  transfers between devices with their start and end apart: 17, of which 8 were waited for; matrix products, arithmetic and copies ran while one was open for 0% of the time, Pallas kernels for 5%

profile of v12, /device:TPU:0, one launch (start us, length us, event | category | flops | bytes accessed | tf_op | source)
XLA Modules:
  0.0 61.2 jit_solution(18353032103026185144)
XLA Ops:
  0.0 4.2 %prepare.1 = (bf16[2,4,128,128]{3,2,1,0:T(8,128)(2,1)}, bf16[4,80,128]{2,1,0:T(8,128)(2,1)}, bf16[2,4,128,128]{3,2,1,0:T(8,128)(2,1)}, bf16[4,80,128]{2,1,0:T(8,...) custom-call(s32[1]{0:T(128)} %bitcast.refs_0_, ...), custom_call_target="tpu_custom_call" | custom-call | tf_op jit(solution)/shard_map/prepare/pallas_call | solution.py:245
  4.2 0.0 copy-start.6
  4.2 0.0 copy-start.5
  4.2 3.1 %collective-permute-start.8 = (bf16[2,4,128,128]{3,2,1,0:T(8,128)(2,1)}, bf16[2,4,128,128]{3,2,1,0:T(8,128)(2,1)S(1)}, u32[]{:S(2)}, u32[]{:S(2)}) collective-permute-start(bf16[2,4,128,128]{3,2,1,0:T(8,128)(2,1)} %get-tuple-element.25), channel_id=1, source_target_pairs={{0,4},{1,5},{2,6},{3,7},{4,0},{5,1},{6,2},{7,3},{8,12},{9,13},{10,... | collective-permute-start | bytes 786440 | tf_op jit(solution)/shard_map/ppermute | solution.py:207
  7.3 2.5 %collective-permute-start.11 = (bf16[2,4,128,128]{3,2,1,0:T(8,128)(2,1)}, bf16[2,4,128,128]{3,2,1,0:T(8,128)(2,1)S(1)}, u32[]{:S(2)}, u32[]{:S(2)}) collective-permute-start(bf16[2,4,128,128]{3,2,1,0:T(8,128)(2,1)} %get-tuple-element.26), channel_id=1, source_target_pairs={{0,12},{1,13},{2,14},{3,15},{4,8},{5,9},{6,10},{7,11},{8,4},{9,5},... | collective-permute-start | bytes 786440 | tf_op jit(solution)/shard_map/ppermute | solution.py:207
  9.8 1.5 %collective-permute-start.7 = (bf16[2,4,128,128]{3,2,1,0:T(8,128)(2,1)}, bf16[2,4,128,128]{3,2,1,0:T(8,128)(2,1)S(1)}, u32[]{:S(2)}, u32[]{:S(2)}) collective-permute-start(bf16[2,4,128,128]{3,2,1,0:T(8,128)(2,1)} %get-tuple-element.24.refs_5_), channel_id=1, source_target_pairs={{0,2},{1,3},{2,0},{3,1},{4,6},{5,7},{6,4},{7,5},{8,10},{9,11},{10,... | collective-permute-start | bytes 786440 | tf_op jit(solution)/shard_map/ppermute | solution.py:207
  11.3 3.0 %collective-permute-done.8.refs_2_ = bf16[2,4,128,128]{3,2,1,0:T(8,128)(2,1)S(1)} collective-permute-done((bf16[2,4,128,128]{3,2,1,0:T(8,128)(2,1)}, bf16[2,4,128,128]{3,2,1,0:T(8,128)(2,1)S(1)}, u32[]{:S(2)}, u32[]{:S(2)}) %collective-permute-start.8) | collective-permute-done | bytes 262176 | tf_op jit(solution)/shard_map/ppermute | solution.py:207
  14.3 1.5 %collective-permute-start.9 = (bf16[2,4,128,128]{3,2,1,0:T(8,128)(2,1)S(1)}, bf16[2,4,128,128]{3,2,1,0:T(8,128)(2,1)S(1)}, u32[]{:S(2)}, u32[]{:S(2)}) collective-permute-start(bf16[2,4,128,128]{3,2,1,0:T(8,128)(2,1)S(1)} %collective-permute-done.8.refs_2_), channel_id=1, source_target_pairs={{0,2},{1,3},{2,0},{3,1},{4,6},{5,7},{6,4},{7,5},{8,10},{9,11},{10,... | collective-permute-start | bytes 786440 | tf_op jit(solution)/shard_map/ppermute | solution.py:207
  15.9 3.4 %collective-permute-start.3 = (bf16[2,4,128,128]{3,2,1,0:T(8,128)(2,1)}, bf16[2,4,128,128]{3,2,1,0:T(8,128)(2,1)S(1)}, u32[]{:S(2)}, u32[]{:S(2)}) collective-permute-start(bf16[2,4,128,128]{3,2,1,0:T(8,128)(2,1)} %get-tuple-element.22), channel_id=1, source_target_pairs={{0,8},{1,9},{2,10},{3,11},{4,12},{5,13},{6,14},{7,15},{8,0},{9,1},... | collective-permute-start | bytes 786440 | tf_op jit(solution)/shard_map/ppermute | solution.py:207
  19.2 5.0 %collective-permute-start.2 = (bf16[4,80,128]{2,1,0:T(8,128)(2,1)}, bf16[4,80,128]{2,1,0:T(8,128)(2,1)S(1)}, u32[]{:S(2)}, u32[]{:S(2)}) collective-permute-start(bf16[4,80,128]{2,1,0:T(8,128)(2,1)} %get-tuple-element.20), channel_id=1, source_target_pairs={{0,4},{1,5},{2,6},{3,7},{4,0},{5,1},{6,2},{7,3},{8,12},{9,13},{10,... | collective-permute-start | bytes 245768 | tf_op jit(solution)/shard_map/ppermute | solution.py:207
  24.3 0.0 collective-permute-done.11.refs_1_
  24.3 0.5 collective-permute-start.12
  24.8 2.1 %collective-permute-done.2.refs_0_.refs_2_ = bf16[4,80,128]{2,1,0:T(8,128)(2,1)S(1)} collective-permute-done((bf16[4,80,128]{2,1,0:T(8,128)(2,1)}, bf16[4,80,128]{2,1,0:T(8,128)(2,1)S(1)}, u32[]{:S(2)}, u32[]{:S(2)}) %collective-permute-start.2) | collective-permute-done | bytes 81952 | tf_op jit(solution)/shard_map/ppermute | solution.py:207
  26.9 0.0 collective-permute-done.7.refs_1_
  26.9 0.0 collective-permute-done.9.refs_3_
  26.9 0.1 stack_near.1.refs_7_
  27.0 0.0 copy-start.3
  27.0 0.0 copy-start.1
  27.0 0.0 copy-start.2
  27.0 0.1 collective-permute-start.10
  27.1 5.8 %collective-permute-done.3.refs_1_ = bf16[2,4,128,128]{3,2,1,0:T(8,128)(2,1)S(1)} collective-permute-done((bf16[2,4,128,128]{3,2,1,0:T(8,128)(2,1)}, bf16[2,4,128,128]{3,2,1,0:T(8,128)(2,1)S(1)}, u32[]{:S(2)}, u32[]{:S(2)}) %collective-permute-start.3) | collective-permute-done | bytes 262176 | tf_op jit(solution)/shard_map/ppermute | solution.py:207
  32.9 1.6 %collective-permute-start.4 = (bf16[2,4,128,128]{3,2,1,0:T(8,128)(2,1)S(1)}, bf16[2,4,128,128]{3,2,1,0:T(8,128)(2,1)S(1)}, u32[]{:S(2)}, u32[]{:S(2)}) collective-permute-start(bf16[2,4,128,128]{3,2,1,0:T(8,128)(2,1)S(1)} %collective-permute-done.3.refs_1_), channel_id=1, source_target_pairs={{0,2},{1,3},{2,0},{3,1},{4,6},{5,7},{6,4},{7,5},{8,10},{9,11},{10,... | collective-permute-start | bytes 786440 | tf_op jit(solution)/shard_map/ppermute | solution.py:207
  34.5 0.0 copy-done.6
  34.5 2.6 %collective-permute-start = (bf16[4,80,128]{2,1,0:T(8,128)(2,1)S(1)}, bf16[4,80,128]{2,1,0:T(8,128)(2,1)S(1)}, u32[]{:S(2)}, u32[]{:S(2)}) collective-permute-start(bf16[4,80,128]{2,1,0:T(8,128)(2,1)S(1)} %copy-done.6), channel_id=1, source_target_pairs={{0,12},{1,13},{2,14},{3,15},{4,8},{5,9},{6,10},{7,11},{8,4},{9,5},... | collective-permute-start | bytes 245768 | tf_op jit(solution)/shard_map/ppermute | solution.py:207
  37.1 0.0 collective-permute-start.1
  37.1 4.2 %collective-permute-done.refs_0_ = bf16[4,80,128]{2,1,0:T(8,128)(2,1)S(1)} collective-permute-done((bf16[4,80,128]{2,1,0:T(8,128)(2,1)S(1)}, bf16[4,80,128]{2,1,0:T(8,128)(2,1)S(1)}, u32[]{:S(2)}, u32[]{:S(2)}) %collective-permute-start) | collective-permute-done | bytes 81952 | tf_op jit(solution)/shard_map/ppermute | solution.py:207
  41.4 0.0 collective-permute-done.12.refs_2_
  41.4 0.1 collective-permute-start.13
  41.5 2.4 %collective-permute-done.1.refs_0_.refs_1_ = bf16[4,80,128]{2,1,0:T(8,128)(2,1)S(1)} collective-permute-done((bf16[4,80,128]{2,1,0:T(8,128)(2,1)S(1)}, bf16[4,80,128]{2,1,0:T(8,128)(2,1)S(1)}, u32[]{:S(2)}, u32[]{:S(2)}) %collective-permute-start.1) | collective-permute-done | bytes 81952 | tf_op jit(solution)/shard_map/ppermute | solution.py:207
  43.9 0.0 collective-permute-done.4.refs_2_
  43.9 0.1 collective-permute-start.5
  44.0 0.5 collective-permute-start.6
  44.5 1.8 %collective-permute-done.6.refs_6_ = bf16[2,4,128,128]{3,2,1,0:T(8,128)(2,1)S(1)} collective-permute-done((bf16[2,4,128,128]{3,2,1,0:T(8,128)(2,1)S(1)}, bf16[2,4,128,128]{3,2,1,0:T(8,128)(2,1)S(1)}, u32[]{:S(2)}, u32[]{:S(2)}) %collective-permute-start.6) | collective-permute-done | bytes 262176 | tf_op jit(solution)/shard_map/ppermute | solution.py:207
  46.3 0.0 collective-permute-done.13.refs_10_
  46.3 0.0 collective-permute-done.10.refs_8_
  46.3 2.9 %attend.1.refs_6_ = f32[4,1,320,256]{3,2,1,0:T(8,128)S(1)} custom-call(bf16[4,80,128]{2,1,0:T(8,128)(2,1)S(1)} %collective-permute-done.refs_0_, bf16[4,80,128]{2,1,0:T(8,128)(2,1)S(1)} %collective-permute-done.1.refs_0_.refs_1_, bf16[4,80,128]{2,1,0:T(8,128)(2,1)S(1)} %collective-permute-done.2.refs_0_.refs_2_, bf16[4,80,128]{2,1,0:T(8,128)(2,1)S(1)} %copy-done.2, ...), custom_call_target="tpu_custom_call" | custom-call | tf_op jit(solution)/shard_map/attend/pallas_call | solution.py:307
  49.2 0.0 copy-start.4
  49.2 0.0 copy-start
  49.3 0.0 collective-permute-done.5.refs_5_
  49.3 1.0 %complete.1 = (bf16[4,80,128]{2,1,0:T(8,128)(2,1)S(1)}, bf16[4,80,128]{2,1,0:T(8,128)(2,1)S(1)}, bf16[4,80,128]{2,1,0:T(8,128)(2,1)S(1)}, bf16[4,80,128]{2,1,0:T(8,128)(2,1)S(1)}) custom-call(bf16[4,80,128]{2,1,0:T(8,128)(2,1)S(1)} %collective-permute-done.refs_0_, bf16[4,80,128]{2,1,0:T(8,128)(2,1)S(1)} %collective-permute-done.1.refs_0_.refs_1_, ...), custom_call_target="tpu_custom_call" | custom-call | tf_op jit(solution)/shard_map/complete/pallas_call | solution.py:315
  50.2 1.5 %collective-permute-start.14 = (bf16[4,80,128]{2,1,0:T(8,128)(2,1)S(1)}, bf16[4,80,128]{2,1,0:T(8,128)(2,1)S(1)}, u32[]{:S(2)}, u32[]{:S(2)}) collective-permute-start(bf16[4,80,128]{2,1,0:T(8,128)(2,1)S(1)} %get-tuple-element.27), channel_id=1, source_target_pairs={{0,12},{1,13},{2,14},{3,15},{4,8},{5,9},{6,10},{7,11},{8,4},{9,5},... | collective-permute-start | bytes 245768 | tf_op jit(solution)/shard_map/ppermute | solution.py:207
  51.8 0.0 collective-permute-start.15
  51.8 2.9 %collective-permute-start.16 = (bf16[4,80,128]{2,1,0:T(8,128)(2,1)S(1)}, bf16[4,80,128]{2,1,0:T(8,128)(2,1)S(1)}, u32[]{:S(2)}, u32[]{:S(2)}) collective-permute-start(bf16[4,80,128]{2,1,0:T(8,128)(2,1)S(1)} %get-tuple-element.29), channel_id=1, source_target_pairs={{0,4},{1,5},{2,6},{3,7},{4,0},{5,1},{6,2},{7,3},{8,12},{9,13},{10,... | collective-permute-start | bytes 245768 | tf_op jit(solution)/shard_map/ppermute | solution.py:207
  54.7 2.8 %collective-permute-done.14.refs_3_ = bf16[4,80,128]{2,1,0:T(8,128)(2,1)S(1)} collective-permute-done((bf16[4,80,128]{2,1,0:T(8,128)(2,1)S(1)}, bf16[4,80,128]{2,1,0:T(8,128)(2,1)S(1)}, u32[]{:S(2)}, u32[]{:S(2)}) %collective-permute-start.14) | collective-permute-done | bytes 81952 | tf_op jit(solution)/shard_map/ppermute | solution.py:207
  57.5 2.6 %collective-permute-done.15.refs_4_ = bf16[4,80,128]{2,1,0:T(8,128)(2,1)S(1)} collective-permute-done((bf16[4,80,128]{2,1,0:T(8,128)(2,1)S(1)}, bf16[4,80,128]{2,1,0:T(8,128)(2,1)S(1)}, u32[]{:S(2)}, u32[]{:S(2)}) %collective-permute-start.15) | collective-permute-done | bytes 81952 | tf_op jit(solution)/shard_map/ppermute | solution.py:207
  60.1 0.0 collective-permute-done.16.refs_5_
  60.1 0.0 copy-done
  60.1 1.1 %finish.1 = bf16[128,2048]{1,0:T(8,128)(2,1)} custom-call(s32[1]{0:T(128)} %bitcast.refs_0_, s32[1,80]{1,0:T(1,128)S(1)} %pad.4.refs_1_, bf16[128,2048]{1,0:T(8,128)(2,1)S(1)} %copy-done, bf16[4,80,128]{2,1,0:T(8,128)(2,1)S(1)} %collective-permute-done.14.refs_3_, bf16[4,80,128]{2,1,0:T(8,128)(2,1)S(1)} %collective-permute-done.15.refs_4_, ...), custom_call_target="tpu_custom_call" | custom-call | tf_op jit(solution)/shard_map/finish/pallas_call | solution.py:328
  (8 shorter events, 0.1 us)
Async XLA Ops:
  4.2 30.3 %copy-start.6 = (bf16[4,80,128]{2,1,0:T(8,128)(2,1)S(1)}, bf16[4,80,128]{2,1,0:T(8,128)(2,1)}, u32[]{:S(2)}) copy-start(bf16[4,80,128]{2,1,0:T(8,128)(2,1)} %get-tuple-element.18) | copy-start | bytes 245764
  4.2 32.9 %copy-start.5 = (bf16[4,80,128]{2,1,0:T(8,128)(2,1)S(1)}, bf16[4,80,128]{2,1,0:T(8,128)(2,1)}, u32[]{:S(2)}) copy-start(bf16[4,80,128]{2,1,0:T(8,128)(2,1)} %get-tuple-element.19) | copy-start | bytes 245764
  4.2 10.1 %collective-permute-start.8 = (bf16[2,4,128,128]{3,2,1,0:T(8,128)(2,1)}, bf16[2,4,128,128]{3,2,1,0:T(8,128)(2,1)S(1)}, u32[]{:S(2)}, u32[]{:S(2)}) collective-permute-start(bf16[2,4,128,128]{3,2,1,0:T(8,128)(2,1)} %get-tuple-element.25), channel_id=1, source_target_pairs={{0,4},{1,5},{2,6},{3,7},{4,0},{5,1},{6,2},{7,3},{8,12},{9,13},{10,... | collective-permute-start | bytes 786440 | tf_op jit(solution)/shard_map/ppermute | solution.py:207
  7.3 17.0 %collective-permute-start.11 = (bf16[2,4,128,128]{3,2,1,0:T(8,128)(2,1)}, bf16[2,4,128,128]{3,2,1,0:T(8,128)(2,1)S(1)}, u32[]{:S(2)}, u32[]{:S(2)}) collective-permute-start(bf16[2,4,128,128]{3,2,1,0:T(8,128)(2,1)} %get-tuple-element.26), channel_id=1, source_target_pairs={{0,12},{1,13},{2,14},{3,15},{4,8},{5,9},{6,10},{7,11},{8,4},{9,5},... | collective-permute-start | bytes 786440 | tf_op jit(solution)/shard_map/ppermute | solution.py:207
  9.8 17.1 %collective-permute-start.7 = (bf16[2,4,128,128]{3,2,1,0:T(8,128)(2,1)}, bf16[2,4,128,128]{3,2,1,0:T(8,128)(2,1)S(1)}, u32[]{:S(2)}, u32[]{:S(2)}) collective-permute-start(bf16[2,4,128,128]{3,2,1,0:T(8,128)(2,1)} %get-tuple-element.24.refs_5_), channel_id=1, source_target_pairs={{0,2},{1,3},{2,0},{3,1},{4,6},{5,7},{6,4},{7,5},{8,10},{9,11},{10,... | collective-permute-start | bytes 786440 | tf_op jit(solution)/shard_map/ppermute | solution.py:207
  14.3 12.6 %collective-permute-start.9 = (bf16[2,4,128,128]{3,2,1,0:T(8,128)(2,1)S(1)}, bf16[2,4,128,128]{3,2,1,0:T(8,128)(2,1)S(1)}, u32[]{:S(2)}, u32[]{:S(2)}) collective-permute-start(bf16[2,4,128,128]{3,2,1,0:T(8,128)(2,1)S(1)} %collective-permute-done.8.refs_2_), channel_id=1, source_target_pairs={{0,2},{1,3},{2,0},{3,1},{4,6},{5,7},{6,4},{7,5},{8,10},{9,11},{10,... | collective-permute-start | bytes 786440 | tf_op jit(solution)/shard_map/ppermute | solution.py:207
  15.9 17.1 %collective-permute-start.3 = (bf16[2,4,128,128]{3,2,1,0:T(8,128)(2,1)}, bf16[2,4,128,128]{3,2,1,0:T(8,128)(2,1)S(1)}, u32[]{:S(2)}, u32[]{:S(2)}) collective-permute-start(bf16[2,4,128,128]{3,2,1,0:T(8,128)(2,1)} %get-tuple-element.22), channel_id=1, source_target_pairs={{0,8},{1,9},{2,10},{3,11},{4,12},{5,13},{6,14},{7,15},{8,0},{9,1},... | collective-permute-start | bytes 786440 | tf_op jit(solution)/shard_map/ppermute | solution.py:207
  19.2 7.7 %collective-permute-start.2 = (bf16[4,80,128]{2,1,0:T(8,128)(2,1)}, bf16[4,80,128]{2,1,0:T(8,128)(2,1)S(1)}, u32[]{:S(2)}, u32[]{:S(2)}) collective-permute-start(bf16[4,80,128]{2,1,0:T(8,128)(2,1)} %get-tuple-element.20), channel_id=1, source_target_pairs={{0,4},{1,5},{2,6},{3,7},{4,0},{5,1},{6,2},{7,3},{8,12},{9,13},{10,... | collective-permute-start | bytes 245768 | tf_op jit(solution)/shard_map/ppermute | solution.py:207
  24.3 17.1 %collective-permute-start.12 = (bf16[2,4,128,128]{3,2,1,0:T(8,128)(2,1)S(1)}, bf16[2,4,128,128]{3,2,1,0:T(8,128)(2,1)S(1)}, u32[]{:S(2)}, u32[]{:S(2)}) collective-permute-start(bf16[2,4,128,128]{3,2,1,0:T(8,128)(2,1)S(1)} %collective-permute-done.11.refs_1_), channel_id=1, source_target_pairs={{0,2},{1,3},{2,0},{3,1},{4,6},{5,7},{6,4},{7,5},{8,10},{9,11},{10,... | collective-permute-start | bytes 786440 | tf_op jit(solution)/shard_map/ppermute | solution.py:207
  27.0 17.1 %copy-start.3 = (bf16[2,4,128,128]{3,2,1,0:T(8,128)(2,1)S(1)}, bf16[2,4,128,128]{3,2,1,0:T(8,128)(2,1)}, u32[]{:S(2)}) copy-start(bf16[2,4,128,128]{3,2,1,0:T(8,128)(2,1)} %get-tuple-element.24.refs_5_) | copy-start | bytes 786436
  27.0 19.3 %copy-start.1 = (bf16[2,4,256,128]{3,2,1,0:T(8,128)(2,1)S(1)}, bf16[2,4,256,128]{3,2,1,0:T(8,128)(2,1)}, u32[]{:S(2)}) copy-start(bf16[2,4,256,128]{3,2,1,0:T(8,128)(2,1)} %get-tuple-element.23.refs_4_) | copy-start | bytes 1572868
  27.0 19.3 %copy-start.2 = (bf16[4,80,128]{2,1,0:T(8,128)(2,1)S(1)}, bf16[4,80,128]{2,1,0:T(8,128)(2,1)}, u32[]{:S(2)}) copy-start(bf16[4,80,128]{2,1,0:T(8,128)(2,1)} %get-tuple-element.21.refs_3_) | copy-start | bytes 245764
  27.0 19.3 %collective-permute-start.10 = (bf16[3,2,4,128,128]{4,3,2,1,0:T(8,128)(2,1)S(1)}, bf16[3,2,4,128,128]{4,3,2,1,0:T(8,128)(2,1)S(1)}, u32[]{:S(2)}, u32[]{:S(2)}) collective-permute-start(bf16[3,2,4,128,128]{4,3,2,1,0:T(8,128)(2,1)S(1)} %stack_near.1.refs_7_), channel_id=1, source_target_pairs={{0,1},{1,0},{2,3},{3,2},{4,5},{5,4},{6,7},{7,6},{8,9},{9,8},{10,11... | collective-permute-start | bytes 2359304 | tf_op jit(solution)/shard_map/ppermute | solution.py:207
  32.9 11.0 %collective-permute-start.4 = (bf16[2,4,128,128]{3,2,1,0:T(8,128)(2,1)S(1)}, bf16[2,4,128,128]{3,2,1,0:T(8,128)(2,1)S(1)}, u32[]{:S(2)}, u32[]{:S(2)}) collective-permute-start(bf16[2,4,128,128]{3,2,1,0:T(8,128)(2,1)S(1)} %collective-permute-done.3.refs_1_), channel_id=1, source_target_pairs={{0,2},{1,3},{2,0},{3,1},{4,6},{5,7},{6,4},{7,5},{8,10},{9,11},{10,... | collective-permute-start | bytes 786440 | tf_op jit(solution)/shard_map/ppermute | solution.py:207
  34.5 6.8 %collective-permute-start = (bf16[4,80,128]{2,1,0:T(8,128)(2,1)S(1)}, bf16[4,80,128]{2,1,0:T(8,128)(2,1)S(1)}, u32[]{:S(2)}, u32[]{:S(2)}) collective-permute-start(bf16[4,80,128]{2,1,0:T(8,128)(2,1)S(1)} %copy-done.6), channel_id=1, source_target_pairs={{0,12},{1,13},{2,14},{3,15},{4,8},{5,9},{6,10},{7,11},{8,4},{9,5},... | collective-permute-start | bytes 245768 | tf_op jit(solution)/shard_map/ppermute | solution.py:207
  37.1 6.8 %collective-permute-start.1 = (bf16[4,80,128]{2,1,0:T(8,128)(2,1)S(1)}, bf16[4,80,128]{2,1,0:T(8,128)(2,1)S(1)}, u32[]{:S(2)}, u32[]{:S(2)}) collective-permute-start(bf16[4,80,128]{2,1,0:T(8,128)(2,1)S(1)} %copy-done.5), channel_id=1, source_target_pairs={{0,8},{1,9},{2,10},{3,11},{4,12},{5,13},{6,14},{7,15},{8,0},{9,1},... | collective-permute-start | bytes 245768 | tf_op jit(solution)/shard_map/ppermute | solution.py:207
  41.4 4.9 %collective-permute-start.13 = (bf16[2,2,4,128,128]{4,3,2,1,0:T(8,128)(2,1)S(1)}, bf16[2,2,4,128,128]{4,3,2,1,0:T(8,128)(2,1)S(1)}, u32[]{:S(2)}, u32[]{:S(2)}) collective-permute-start(bf16[2,2,4,128,128]{4,3,2,1,0:T(8,128)(2,1)S(1)} %stack_far.1.refs_9_), channel_id=1, source_target_pairs={{0,1},{1,0},{2,3},{3,2},{4,5},{5,4},{6,7},{7,6},{8,9},{9,8},{10,11... | collective-permute-start | bytes 1572872 | tf_op jit(solution)/shard_map/ppermute | solution.py:207
  43.9 5.3 %collective-permute-start.5 = (bf16[2,2,4,128,128]{4,3,2,1,0:T(8,128)(2,1)S(1)}, bf16[2,2,4,128,128]{4,3,2,1,0:T(8,128)(2,1)S(1)}, u32[]{:S(2)}, u32[]{:S(2)}) collective-permute-start(bf16[2,2,4,128,128]{4,3,2,1,0:T(8,128)(2,1)S(1)} %stack_last.1.refs_4_), channel_id=1, source_target_pairs={{0,1},{1,0},{2,3},{3,2},{4,5},{5,4},{6,7},{7,6},{8,9},{9,8},{10,11... | collective-permute-start | bytes 1572872 | tf_op jit(solution)/shard_map/ppermute | solution.py:207
  44.0 2.3 %collective-permute-start.6 = (bf16[2,4,128,128]{3,2,1,0:T(8,128)(2,1)S(1)}, bf16[2,4,128,128]{3,2,1,0:T(8,128)(2,1)S(1)}, u32[]{:S(2)}, u32[]{:S(2)}) collective-permute-start(bf16[2,4,128,128]{3,2,1,0:T(8,128)(2,1)S(1)} %copy-done.3), channel_id=1, source_target_pairs={{0,1},{1,0},{2,3},{3,2},{4,5},{5,4},{6,7},{7,6},{8,9},{9,8},{10,11... | collective-permute-start | bytes 786440 | tf_op jit(solution)/shard_map/ppermute | solution.py:207
  49.2 5.5 %copy-start.4 = (s32[76]{0:T(128)S(1)}, s32[76]{0:T(128)}, u32[]{:S(2)}) copy-start(s32[76]{0:T(128)} %param.10) | copy-start | bytes 916
  49.2 10.9 %copy-start = (bf16[128,2048]{1,0:T(8,128)(2,1)S(1)}, bf16[128,2048]{1,0:T(8,128)(2,1)}, u32[]{:S(2)}) copy-start(bf16[128,2048]{1,0:T(8,128)(2,1)} %refs_2_.1) | copy-start | bytes 1572868
  50.2 7.2 %collective-permute-start.14 = (bf16[4,80,128]{2,1,0:T(8,128)(2,1)S(1)}, bf16[4,80,128]{2,1,0:T(8,128)(2,1)S(1)}, u32[]{:S(2)}, u32[]{:S(2)}) collective-permute-start(bf16[4,80,128]{2,1,0:T(8,128)(2,1)S(1)} %get-tuple-element.27), channel_id=1, source_target_pairs={{0,12},{1,13},{2,14},{3,15},{4,8},{5,9},{6,10},{7,11},{8,4},{9,5},... | collective-permute-start | bytes 245768 | tf_op jit(solution)/shard_map/ppermute | solution.py:207
  51.8 8.3 %collective-permute-start.15 = (bf16[4,80,128]{2,1,0:T(8,128)(2,1)S(1)}, bf16[4,80,128]{2,1,0:T(8,128)(2,1)S(1)}, u32[]{:S(2)}, u32[]{:S(2)}) collective-permute-start(bf16[4,80,128]{2,1,0:T(8,128)(2,1)S(1)} %get-tuple-element.28), channel_id=1, source_target_pairs={{0,8},{1,9},{2,10},{3,11},{4,12},{5,13},{6,14},{7,15},{8,0},{9,1},... | collective-permute-start | bytes 245768 | tf_op jit(solution)/shard_map/ppermute | solution.py:207
  51.8 8.3 %collective-permute-start.16 = (bf16[4,80,128]{2,1,0:T(8,128)(2,1)S(1)}, bf16[4,80,128]{2,1,0:T(8,128)(2,1)S(1)}, u32[]{:S(2)}, u32[]{:S(2)}) collective-permute-start(bf16[4,80,128]{2,1,0:T(8,128)(2,1)S(1)} %get-tuple-element.29), channel_id=1, source_target_pairs={{0,4},{1,5},{2,6},{3,7},{4,0},{5,1},{6,2},{7,3},{8,12},{9,13},{10,... | collective-permute-start | bytes 245768 | tf_op jit(solution)/shard_map/ppermute | solution.py:207

commit v13 on v12

--- a/solution.py
+++ b/solution.py
@@ -28,20 +28,14 @@
 
 
 def prepare_kernel(plan, padded, me_ref, *refs):
-    with_text = any(share for _, _, share in plan)
     slots_hbm, q_gain_hbm, k_gain_hbm, qkv_hbm, k_hbm, v_hbm = refs[:6]
     rest = refs[6:]
-    if with_text:
-        text_k_hbm, text_v_hbm = rest[:2]
-        rest = rest[2:]
     outs = []
     for _, pair, share in plan:
         outs.append((rest[0] if pair else None, rest[pair] if share else None))
         rest = rest[pair + share :]
-    if with_text:
-        text_out_ref, rest = rest[0], rest[1:]
-    slots_ref, q_gain_ref, k_gain_ref, fresh_ref, k_ref, v_ref, text_ref = rest[:7]
-    small_sems, sems, text_sems = rest[7:]
+    slots_ref, q_gain_ref, k_gain_ref, fresh_ref, k_ref, v_ref = rest[:6]
+    small_sems, sems = rest[6:]
     slot_count = slots_ref.shape[1]
     tokens, width = k_ref.shape[1:]
     head_size = q_gain_ref.shape[1]
@@ -71,14 +65,6 @@
         for copy in copies:
             copy.start()
         loads.append(copies)
-    if with_text:
-        mine = columns(0)
-        text_loads = [
-            pltpu.make_async_copy(text_k_hbm.at[:, mine], text_ref.at[0], text_sems.at[0]),
-            pltpu.make_async_copy(text_v_hbm.at[:, mine], text_ref.at[1], text_sems.at[1]),
-        ]
-        for copy in text_loads:
-            copy.start()
     for copy in small:
         copy.wait()
     belongs = place(slots_ref[...], tokens)
@@ -107,14 +93,28 @@
                 if padded > slot_count:
                     queries = jnp.concatenate([queries, empty], axis=0)
                 share_ref[head] = queries.astype(jnp.bfloat16)
-    if with_text:
-        for copy in text_loads:
-            copy.wait()
-        for head in range(width // head_size):
-            lanes = slice(head * head_size, (head + 1) * head_size)
-            text_keys = normalize(text_ref[0, :, lanes].astype(jnp.float32), k_gain)
-            text_out_ref[0, head] = text_keys.astype(jnp.bfloat16)
-            text_out_ref[1, head] = text_ref[1, :, lanes]
+
+
+def text_kernel(me_ref, text_k_hbm, text_v_hbm, k_gain_ref, *refs):
+    blocks, out_ref, pair_ref, text_ref, sems = refs[:-4], *refs[-4:]
+    heads, text, head_size = pair_ref.shape[1:]
+    width = heads * head_size
+    mine = pl.ds(pl.multiple_of(me_ref[0] // INNER * width, width), width)
+    loads = [
+        pltpu.make_async_copy(text_k_hbm.at[:, mine], text_ref.at[0], sems.at[0]),
+        pltpu.make_async_copy(text_v_hbm.at[:, mine], text_ref.at[1], sems.at[1]),
+    ]
+    for copy in loads:
+        copy.start()
+    for number, ref in enumerate(blocks):
+        out_ref[number] = ref[...]
+    for copy in loads:
+        copy.wait()
+    for head in range(heads):
+        lanes = slice(head * head_size, (head + 1) * head_size)
+        keys = normalize(text_ref[0, :, lanes].astype(jnp.float32), k_gain_ref[...])
+        pair_ref[0, head] = keys.astype(jnp.bfloat16)
+        pair_ref[1, head] = text_ref[1, :, lanes]
 
 
 def stack_kernel(*refs):
@@ -234,18 +234,15 @@
     in_smem = pl.BlockSpec(memory_space=pltpu.SMEM)
     small = pltpu.CompilerParams(vmem_limit_bytes=24 * MIB)
 
-    def prepare(plan, name, params, *extra):
-        with_text = len(extra) > 0
+    def prepare(plan, name, params):
         shapes = []
         for _, pair, share in plan:
             shapes += [shaped(2, heads, tokens, head_size)] * pair
             shapes += [shaped(heads, padded, head_size)] * share
-        if with_text:
-            shapes.append(shaped(2, heads, text, head_size))
         made = pl.pallas_call(
             lambda *refs: prepare_kernel(plan, padded, *refs),
             out_shape=shapes,
-            in_specs=[in_smem] + [in_hbm] * 6 + [in_hbm] * (2 * with_text),
+            in_specs=[in_smem] + [in_hbm] * 6,
             out_specs=[in_vmem] * len(shapes),
             scratch_shapes=[
                 pltpu.VMEM((1, slot_count), jnp.int32),
@@ -254,14 +251,12 @@
                 pltpu.VMEM((len(plan), 3, slot_count, width), jnp.bfloat16),
                 pltpu.VMEM((len(plan), tokens, width), jnp.bfloat16),
                 pltpu.VMEM((len(plan), tokens, width), jnp.bfloat16),
-                pltpu.VMEM((2, text, width), jnp.bfloat16),
                 pltpu.SemaphoreType.DMA((3,)),
                 pltpu.SemaphoreType.DMA((len(plan), 3)),
-                pltpu.SemaphoreType.DMA((2,)),
             ],
             compiler_params=params,
             name=name,
-        )(me, slots, q_gain, k_gain, qkv, k_cache, v_cache, *extra)
+        )(me, slots, q_gain, k_gain, qkv, k_cache, v_cache)
         return list(made)
 
     def stack(blocks, after, name):
@@ -278,10 +273,7 @@
     near = list(range(1, half))
     far = list(reversed(range(half + 1, outers)))
     order = far[:1] + near + [half] + far[1:] + [0]
-    made = prepare(
-        [(step, True, True) for step in order], "prepare", pltpu.CompilerParams(), text_k, text_v
-    )
-    text_pair = made.pop()
+    made = prepare([(step, True, True) for step in order], "prepare", pltpu.CompilerParams())
     own = made[-2]
     own_other = trade(own, CORE)
     pairs, shares = {}, {0: made[-1]}
@@ -293,11 +285,28 @@
     early = [own_next]
     for step in near:
         early += [pairs[step], trade(pairs[step], NEXT)]
-    early = stack(early, [shares[step] for step in near], "stack_near")
+    after = [shares[step] for step in near + far] + [own_other]
+    early, text_pair = pl.pallas_call(
+        lambda *refs: text_kernel(*refs[len(after) :]),
+        out_shape=[
+            shaped(len(early), 2, heads, tokens, head_size),
+            shaped(2, heads, text, head_size),
+        ],
+        in_specs=[pl.BlockSpec(memory_space=pl.ANY)] * len(after)
+        + [in_smem, in_hbm, in_hbm, in_vmem]
+        + [in_vmem] * len(early),
+        out_specs=[in_vmem] * 2,
+        scratch_shapes=[
+            pltpu.VMEM((2, text, width), jnp.bfloat16),
+            pltpu.SemaphoreType.DMA((2,)),
+        ],
+        compiler_params=small,
+        name="stack_near",
+    )(*after, me, text_k, text_v, k_gain, *early)
     middle = []
     for step in far:
         middle += [pairs[step], trade(pairs[step], NEXT)]
-    middle = stack(middle, [shares[step] for step in far], "stack_far")
+    middle = stack(middle, [], "stack_far")
     late = stack([pairs[half], trade(pairs[half], NEXT)], [shares[half]], "stack_last")
 
     sources = far + [half] + near + [0]

time: 61.4 us -> 61.9 us (level)
  starting transfers between devices: 26.9 us -> 17.1 us
  waiting for transfers between devices: 24.8 us -> 34.1 us
  local copies, waits for them, and re-layouts: 0.04 us -> 1.26 us
    ppermute x17, starting transfers between devices: 26.9 us -> 17.1 us  [trade(): return lax.ppermute(block, 'seq', [(a, a ^ distance) for a in range(count)])]
    ppermute x17, waiting for transfers between devices: 24.8 us -> 34.1 us  [trade(): return lax.ppermute(block, 'seq', [(a, a ^ distance) for a in range(count)])]
    unnamed x14 -> x16, local copies, waits for them, and re-layouts: 0.04 us -> 1.26 us
  transfers between devices with their start and end apart: 17 -> 17, of which waited for: 8 -> 9; matrix products, arithmetic and copies ran while one was open for 0% -> 0% of each run, Pallas kernels for 5% -> 5%
where the time goes in v13:
time: 61.9 us; the launch traced here: 61.7 us
  waiting for transfers between devices  34.1 us (55%)
  starting transfers between devices  17.1 us (28%)
  Pallas kernels  9.13 us (15%)
  local copies, waits for them, and re-layouts  1.26 us (2%)
    ppermute x17, waiting for transfers between devices, trade(): return lax.ppermute(block, 'seq', [(a, a ^ distance) for a in range(count)])  34.1 us
    ppermute x17, starting transfers between devices, trade(): return lax.ppermute(block, 'seq', [(a, a ^ distance) for a in range(count)])  17.1 us
    pallas_call x1, Pallas kernels, prepare(): pl.pallas_call(lambda *refs: prepare_kernel(plan, padded, *refs), out_sha...  3.68 us
    pallas_call x1, Pallas kernels, shards(): pl.pallas_call(lambda *refs: attend_kernel(outers, *refs), out_shape=shap...  2.91 us
    unnamed x16, local copies, waits for them, and re-layouts  1.26 us
  transfers between devices with their start and end apart: 17, of which 9 were waited for; matrix products, arithmetic and copies ran while one was open for 0% of the time, Pallas kernels for 5%

profile of v13, /device:TPU:0, one launch (start us, length us, event | category | flops | bytes accessed | tf_op | source)
XLA Modules:
  0.0 61.7 jit_solution(9737437416373540558)
XLA Ops:
  0.0 3.7 %prepare.1 = (bf16[2,4,128,128]{3,2,1,0:T(8,128)(2,1)}, bf16[4,80,128]{2,1,0:T(8,128)(2,1)}, bf16[2,4,128,128]{3,2,1,0:T(8,128)(2,1)}, bf16[4,80,128]{2,1,0:T(8,...) custom-call(s32[1]{0:T(128)} %bitcast.refs_0_.refs_3_, ...), custom_call_target="tpu_custom_call" | custom-call | tf_op jit(solution)/shard_map/prepare/pallas_call | solution.py:242
  3.7 3.1 %collective-permute-start.8 = (bf16[2,4,128,128]{3,2,1,0:T(8,128)(2,1)}, bf16[2,4,128,128]{3,2,1,0:T(8,128)(2,1)S(1)}, u32[]{:S(2)}, u32[]{:S(2)}) collective-permute-start(bf16[2,4,128,128]{3,2,1,0:T(8,128)(2,1)} %get-tuple-element.25), channel_id=1, source_target_pairs={{0,4},{1,5},{2,6},{3,7},{4,0},{5,1},{6,2},{7,3},{8,12},{9,13},{10,... | collective-permute-start | bytes 786440 | tf_op jit(solution)/shard_map/ppermute | solution.py:207
  6.8 2.5 %collective-permute-start = (bf16[4,80,128]{2,1,0:T(8,128)(2,1)}, bf16[4,80,128]{2,1,0:T(8,128)(2,1)S(1)}, u32[]{:S(2)}, u32[]{:S(2)}) collective-permute-start(bf16[4,80,128]{2,1,0:T(8,128)(2,1)} %get-tuple-element.19), channel_id=1, source_target_pairs={{0,12},{1,13},{2,14},{3,15},{4,8},{5,9},{6,10},{7,11},{8,4},{9,5},... | collective-permute-start | bytes 245768 | tf_op jit(solution)/shard_map/ppermute | solution.py:207
  9.3 0.7 %collective-permute-start.2 = (bf16[4,80,128]{2,1,0:T(8,128)(2,1)}, bf16[4,80,128]{2,1,0:T(8,128)(2,1)S(1)}, u32[]{:S(2)}, u32[]{:S(2)}) collective-permute-start(bf16[4,80,128]{2,1,0:T(8,128)(2,1)} %get-tuple-element.21), channel_id=1, source_target_pairs={{0,4},{1,5},{2,6},{3,7},{4,0},{5,1},{6,2},{7,3},{8,12},{9,13},{10,... | collective-permute-start | bytes 245768 | tf_op jit(solution)/shard_map/ppermute | solution.py:207
  9.9 0.0 collective-permute-start.6
  9.9 0.9 %collective-permute-start.11 = (bf16[2,4,128,128]{3,2,1,0:T(8,128)(2,1)}, bf16[2,4,128,128]{3,2,1,0:T(8,128)(2,1)S(1)}, u32[]{:S(2)}, u32[]{:S(2)}) collective-permute-start(bf16[2,4,128,128]{3,2,1,0:T(8,128)(2,1)} %get-tuple-element.28), channel_id=1, source_target_pairs={{0,12},{1,13},{2,14},{3,15},{4,8},{5,9},{6,10},{7,11},{8,4},{9,5},... | collective-permute-start | bytes 786440 | tf_op jit(solution)/shard_map/ppermute | solution.py:207
  10.8 7.7 %collective-permute-done.refs_1_.refs_0_ = bf16[4,80,128]{2,1,0:T(8,128)(2,1)S(1)} collective-permute-done((bf16[4,80,128]{2,1,0:T(8,128)(2,1)}, bf16[4,80,128]{2,1,0:T(8,128)(2,1)S(1)}, u32[]{:S(2)}, u32[]{:S(2)}) %collective-permute-start) | collective-permute-done | bytes 81952 | tf_op jit(solution)/shard_map/ppermute | solution.py:207
  18.5 1.5 %collective-permute-start.7 = (bf16[2,4,128,128]{3,2,1,0:T(8,128)(2,1)}, bf16[2,4,128,128]{3,2,1,0:T(8,128)(2,1)S(1)}, u32[]{:S(2)}, u32[]{:S(2)}) collective-permute-start(bf16[2,4,128,128]{3,2,1,0:T(8,128)(2,1)} %get-tuple-element.24.refs_5_), channel_id=1, source_target_pairs={{0,2},{1,3},{2,0},{3,1},{4,6},{5,7},{6,4},{7,5},{8,10},{9,11},{10,... | collective-permute-start | bytes 786440 | tf_op jit(solution)/shard_map/ppermute | solution.py:207
  20.0 0.0 collective-permute-done.8.refs_8_
  20.0 0.5 collective-permute-start.9
  20.5 0.0 collective-permute-done.2.refs_0_.refs_2_
  20.5 0.2 collective-permute-start.3
  20.7 5.1 %collective-permute-done.11.refs_0_ = bf16[2,4,128,128]{3,2,1,0:T(8,128)(2,1)S(1)} collective-permute-done((bf16[2,4,128,128]{3,2,1,0:T(8,128)(2,1)}, bf16[2,4,128,128]{3,2,1,0:T(8,128)(2,1)S(1)}, u32[]{:S(2)}, u32[]{:S(2)}) %collective-permute-start.11) | collective-permute-done | bytes 262176 | tf_op jit(solution)/shard_map/ppermute | solution.py:207
  25.8 1.5 %collective-permute-start.12 = (bf16[2,4,128,128]{3,2,1,0:T(8,128)(2,1)S(1)}, bf16[2,4,128,128]{3,2,1,0:T(8,128)(2,1)S(1)}, u32[]{:S(2)}, u32[]{:S(2)}) collective-permute-start(bf16[2,4,128,128]{3,2,1,0:T(8,128)(2,1)S(1)} %collective-permute-done.11.refs_0_), channel_id=1, source_target_pairs={{0,2},{1,3},{2,0},{3,1},{4,6},{5,7},{6,4},{7,5},{8,10},{9,11},{10,... | collective-permute-start | bytes 786440 | tf_op jit(solution)/shard_map/ppermute | solution.py:207
  27.3 0.0 collective-permute-done.6.refs_2_.refs_6_
  27.3 0.6 collective-permute-done.7.refs_7_
  28.0 4.8 %collective-permute-done.9.refs_9_ = bf16[2,4,128,128]{3,2,1,0:T(8,128)(2,1)S(1)} collective-permute-done((bf16[2,4,128,128]{3,2,1,0:T(8,128)(2,1)S(1)}, bf16[2,4,128,128]{3,2,1,0:T(8,128)(2,1)S(1)}, u32[]{:S(2)}, u32[]{:S(2)}) %collective-permute-start.9) | collective-permute-done | bytes 262176 | tf_op jit(solution)/shard_map/ppermute | solution.py:207
  32.8 0.0 copy-done.5
  32.8 0.0 copy-done
  32.8 1.2 %copy-done.1 = bf16[256,2048]{1,0:T(8,128)(2,1)S(1)} copy-done((bf16[256,2048]{1,0:T(8,128)(2,1)S(1)}, bf16[256,2048]{1,0:T(8,128)(2,1)}, u32[]{:S(2)}) %copy-start.1) | copy-done | bytes 1048600
  34.0 0.4 stack_near.1
  34.4 0.0 copy-start.3
  34.4 0.0 copy-start.4
  34.4 0.1 collective-permute-start.10
  34.5 3.8 %collective-permute-done.3.refs_1_ = bf16[2,4,128,128]{3,2,1,0:T(8,128)(2,1)S(1)} collective-permute-done((bf16[2,4,128,128]{3,2,1,0:T(8,128)(2,1)}, bf16[2,4,128,128]{3,2,1,0:T(8,128)(2,1)S(1)}, u32[]{:S(2)}, u32[]{:S(2)}) %collective-permute-start.3) | collective-permute-done | bytes 262176 | tf_op jit(solution)/shard_map/ppermute | solution.py:207
  38.3 1.5 %collective-permute-start.4 = (bf16[2,4,128,128]{3,2,1,0:T(8,128)(2,1)S(1)}, bf16[2,4,128,128]{3,2,1,0:T(8,128)(2,1)S(1)}, u32[]{:S(2)}, u32[]{:S(2)}) collective-permute-start(bf16[2,4,128,128]{3,2,1,0:T(8,128)(2,1)S(1)} %collective-permute-done.3.refs_1_), channel_id=1, source_target_pairs={{0,2},{1,3},{2,0},{3,1},{4,6},{5,7},{6,4},{7,5},{8,10},{9,11},{10,... | collective-permute-start | bytes 786440 | tf_op jit(solution)/shard_map/ppermute | solution.py:207
  39.8 0.0 copy-done.7
  39.8 0.0 collective-permute-start.1
  39.8 0.0 collective-permute-done.12.refs_1_
  39.8 0.1 collective-permute-start.13
  39.9 5.4 %collective-permute-done.1.refs_0_.refs_1_ = bf16[4,80,128]{2,1,0:T(8,128)(2,1)S(1)} collective-permute-done((bf16[4,80,128]{2,1,0:T(8,128)(2,1)S(1)}, bf16[4,80,128]{2,1,0:T(8,128)(2,1)S(1)}, u32[]{:S(2)}, u32[]{:S(2)}) %collective-permute-start.1) | collective-permute-done | bytes 81952 | tf_op jit(solution)/shard_map/ppermute | solution.py:207
  45.3 1.0 %collective-permute-done.4.refs_2_ = bf16[2,4,128,128]{3,2,1,0:T(8,128)(2,1)S(1)} collective-permute-done((bf16[2,4,128,128]{3,2,1,0:T(8,128)(2,1)S(1)}, bf16[2,4,128,128]{3,2,1,0:T(8,128)(2,1)S(1)}, u32[]{:S(2)}, u32[]{:S(2)}) %collective-permute-start.4) | collective-permute-done | bytes 262176 | tf_op jit(solution)/shard_map/ppermute | solution.py:207
  46.3 0.1 collective-permute-start.5
  46.4 0.0 collective-permute-done.13.refs_10_
  46.4 0.0 collective-permute-done.10.refs_8_
  46.4 0.0 copy-done.3
  46.4 2.9 %attend.1.refs_6_ = f32[4,1,320,256]{3,2,1,0:T(8,128)S(1)} custom-call(bf16[4,80,128]{2,1,0:T(8,128)(2,1)S(1)} %collective-permute-done.refs_1_.refs_0_, bf16[4,80,128]{2,1,0:T(8,128)(2,1)S(1)} %collective-permute-done.1.refs_0_.refs_1_, bf16[4,80,128]{2,1,0:T(8,128)(2,1)S(1)} %collective-permute-done.2.refs_0_.refs_2_, bf16[4,80,128]{2,1,0:T(8,128)(2,1)S(1)} %copy-done.3, ...), custom_call_target="tpu_custom_call" | custom-call | tf_op jit(solution)/shard_map/attend/pallas_call | solution.py:316
  49.4 0.0 copy-start.6
  49.4 0.0 copy-start.2
  49.4 0.0 collective-permute-done.5.refs_5_
  49.4 1.0 %complete.1 = (bf16[4,80,128]{2,1,0:T(8,128)(2,1)S(1)}, bf16[4,80,128]{2,1,0:T(8,128)(2,1)S(1)}, bf16[4,80,128]{2,1,0:T(8,128)(2,1)S(1)}, bf16[4,80,128]{2,1,0:T(8,128)(2,1)S(1)}) custom-call(bf16[4,80,128]{2,1,0:T(8,128)(2,1)S(1)} %collective-permute-done.refs_1_.refs_0_, bf16[4,80,128]{2,1,0:T(8,128)(2,1)S(1)} %collective-permute-done.1.refs_0_.refs_1_, ...), custom_call_target="tpu_custom_call" | custom-call | tf_op jit(solution)/shard_map/complete/pallas_call | solution.py:324
  50.4 1.4 %collective-permute-start.14 = (bf16[4,80,128]{2,1,0:T(8,128)(2,1)S(1)}, bf16[4,80,128]{2,1,0:T(8,128)(2,1)S(1)}, u32[]{:S(2)}, u32[]{:S(2)}) collective-permute-start(bf16[4,80,128]{2,1,0:T(8,128)(2,1)S(1)} %get-tuple-element.29), channel_id=1, source_target_pairs={{0,12},{1,13},{2,14},{3,15},{4,8},{5,9},{6,10},{7,11},{8,4},{9,5},... | collective-permute-start | bytes 245768 | tf_op jit(solution)/shard_map/ppermute | solution.py:207
  51.8 0.7 %collective-permute-start.15 = (bf16[4,80,128]{2,1,0:T(8,128)(2,1)S(1)}, bf16[4,80,128]{2,1,0:T(8,128)(2,1)S(1)}, u32[]{:S(2)}, u32[]{:S(2)}) collective-permute-start(bf16[4,80,128]{2,1,0:T(8,128)(2,1)S(1)} %get-tuple-element.30), channel_id=1, source_target_pairs={{0,8},{1,9},{2,10},{3,11},{4,12},{5,13},{6,14},{7,15},{8,0},{9,1},... | collective-permute-start | bytes 245768 | tf_op jit(solution)/shard_map/ppermute | solution.py:207
  52.5 2.4 %collective-permute-start.16 = (bf16[4,80,128]{2,1,0:T(8,128)(2,1)S(1)}, bf16[4,80,128]{2,1,0:T(8,128)(2,1)S(1)}, u32[]{:S(2)}, u32[]{:S(2)}) collective-permute-start(bf16[4,80,128]{2,1,0:T(8,128)(2,1)S(1)} %get-tuple-element.31), channel_id=1, source_target_pairs={{0,4},{1,5},{2,6},{3,7},{4,0},{5,1},{6,2},{7,3},{8,12},{9,13},{10,... | collective-permute-start | bytes 245768 | tf_op jit(solution)/shard_map/ppermute | solution.py:207
  54.8 2.7 %collective-permute-done.14.refs_3_ = bf16[4,80,128]{2,1,0:T(8,128)(2,1)S(1)} collective-permute-done((bf16[4,80,128]{2,1,0:T(8,128)(2,1)S(1)}, bf16[4,80,128]{2,1,0:T(8,128)(2,1)S(1)}, u32[]{:S(2)}, u32[]{:S(2)}) %collective-permute-start.14) | collective-permute-done | bytes 81952 | tf_op jit(solution)/shard_map/ppermute | solution.py:207
  57.6 3.0 %collective-permute-done.15.refs_4_ = bf16[4,80,128]{2,1,0:T(8,128)(2,1)S(1)} collective-permute-done((bf16[4,80,128]{2,1,0:T(8,128)(2,1)S(1)}, bf16[4,80,128]{2,1,0:T(8,128)(2,1)S(1)}, u32[]{:S(2)}, u32[]{:S(2)}) %collective-permute-start.15) | collective-permute-done | bytes 81952 | tf_op jit(solution)/shard_map/ppermute | solution.py:207
  60.6 0.0 collective-permute-done.16.refs_5_
  60.6 1.1 %finish.1 = bf16[128,2048]{1,0:T(8,128)(2,1)} custom-call(s32[1]{0:T(128)} %bitcast.refs_0_.refs_3_, s32[1,80]{1,0:T(1,128)S(1)} %pad.4.refs_1_, bf16[128,2048]{1,0:T(8,128)(2,1)S(1)} %copy-done.2, bf16[4,80,128]{2,1,0:T(8,128)(2,1)S(1)} %collective-permute-done.14.refs_3_, bf16[4,80,128]{2,1,0:T(8,128)(2,1)S(1)} %collective-permute-done.15.refs_4_, ...), custom_call_target="tpu_custom_call" | custom-call | tf_op jit(solution)/shard_map/finish/pallas_call | solution.py:337
  (10 shorter events, 0.1 us)
Async XLA Ops:
  0.0 32.8 %copy-start.5 = (f32[128]{0:T(128)S(1)}, f32[128]{0:T(128)}, u32[]{:S(2)}) copy-start(f32[128]{0:T(128)} %param.17) | copy-start | bytes 1540
  0.0 32.8 %copy-start = (bf16[256,2048]{1,0:T(8,128)(2,1)S(1)}, bf16[256,2048]{1,0:T(8,128)(2,1)}, u32[]{:S(2)}) copy-start(bf16[256,2048]{1,0:T(8,128)(2,1)} %refs_4_.1) | copy-start | bytes 3145732
  3.7 16.3 %collective-permute-start.8 = (bf16[2,4,128,128]{3,2,1,0:T(8,128)(2,1)}, bf16[2,4,128,128]{3,2,1,0:T(8,128)(2,1)S(1)}, u32[]{:S(2)}, u32[]{:S(2)}) collective-permute-start(bf16[2,4,128,128]{3,2,1,0:T(8,128)(2,1)} %get-tuple-element.25), channel_id=1, source_target_pairs={{0,4},{1,5},{2,6},{3,7},{4,0},{5,1},{6,2},{7,3},{8,12},{9,13},{10,... | collective-permute-start | bytes 786440 | tf_op jit(solution)/shard_map/ppermute | solution.py:207
  6.8 11.7 %collective-permute-start = (bf16[4,80,128]{2,1,0:T(8,128)(2,1)}, bf16[4,80,128]{2,1,0:T(8,128)(2,1)S(1)}, u32[]{:S(2)}, u32[]{:S(2)}) collective-permute-start(bf16[4,80,128]{2,1,0:T(8,128)(2,1)} %get-tuple-element.19), channel_id=1, source_target_pairs={{0,12},{1,13},{2,14},{3,15},{4,8},{5,9},{6,10},{7,11},{8,4},{9,5},... | collective-permute-start | bytes 245768 | tf_op jit(solution)/shard_map/ppermute | solution.py:207
  9.3 11.3 %collective-permute-start.2 = (bf16[4,80,128]{2,1,0:T(8,128)(2,1)}, bf16[4,80,128]{2,1,0:T(8,128)(2,1)S(1)}, u32[]{:S(2)}, u32[]{:S(2)}) collective-permute-start(bf16[4,80,128]{2,1,0:T(8,128)(2,1)} %get-tuple-element.21), channel_id=1, source_target_pairs={{0,4},{1,5},{2,6},{3,7},{4,0},{5,1},{6,2},{7,3},{8,12},{9,13},{10,... | collective-permute-start | bytes 245768 | tf_op jit(solution)/shard_map/ppermute | solution.py:207
  9.9 17.4 %collective-permute-start.6 = (bf16[2,4,128,128]{3,2,1,0:T(8,128)(2,1)}, bf16[2,4,128,128]{3,2,1,0:T(8,128)(2,1)S(1)}, u32[]{:S(2)}, u32[]{:S(2)}) collective-permute-start(bf16[2,4,128,128]{3,2,1,0:T(8,128)(2,1)} %get-tuple-element.24.refs_5_), channel_id=1, source_target_pairs={{0,1},{1,0},{2,3},{3,2},{4,5},{5,4},{6,7},{7,6},{8,9},{9,8},{10,11... | collective-permute-start | bytes 786440 | tf_op jit(solution)/shard_map/ppermute | solution.py:207
  9.9 15.9 %collective-permute-start.11 = (bf16[2,4,128,128]{3,2,1,0:T(8,128)(2,1)}, bf16[2,4,128,128]{3,2,1,0:T(8,128)(2,1)S(1)}, u32[]{:S(2)}, u32[]{:S(2)}) collective-permute-start(bf16[2,4,128,128]{3,2,1,0:T(8,128)(2,1)} %get-tuple-element.28), channel_id=1, source_target_pairs={{0,12},{1,13},{2,14},{3,15},{4,8},{5,9},{6,10},{7,11},{8,4},{9,5},... | collective-permute-start | bytes 786440 | tf_op jit(solution)/shard_map/ppermute | solution.py:207
  18.5 9.5 %collective-permute-start.7 = (bf16[2,4,128,128]{3,2,1,0:T(8,128)(2,1)}, bf16[2,4,128,128]{3,2,1,0:T(8,128)(2,1)S(1)}, u32[]{:S(2)}, u32[]{:S(2)}) collective-permute-start(bf16[2,4,128,128]{3,2,1,0:T(8,128)(2,1)} %get-tuple-element.24.refs_5_), channel_id=1, source_target_pairs={{0,2},{1,3},{2,0},{3,1},{4,6},{5,7},{6,4},{7,5},{8,10},{9,11},{10,... | collective-permute-start | bytes 786440 | tf_op jit(solution)/shard_map/ppermute | solution.py:207
  20.0 12.7 %collective-permute-start.9 = (bf16[2,4,128,128]{3,2,1,0:T(8,128)(2,1)S(1)}, bf16[2,4,128,128]{3,2,1,0:T(8,128)(2,1)S(1)}, u32[]{:S(2)}, u32[]{:S(2)}) collective-permute-start(bf16[2,4,128,128]{3,2,1,0:T(8,128)(2,1)S(1)} %collective-permute-done.8.refs_8_), channel_id=1, source_target_pairs={{0,2},{1,3},{2,0},{3,1},{4,6},{5,7},{6,4},{7,5},{8,10},{9,11},{10,... | collective-permute-start | bytes 786440 | tf_op jit(solution)/shard_map/ppermute | solution.py:207
  20.5 17.7 %collective-permute-start.3 = (bf16[2,4,128,128]{3,2,1,0:T(8,128)(2,1)}, bf16[2,4,128,128]{3,2,1,0:T(8,128)(2,1)S(1)}, u32[]{:S(2)}, u32[]{:S(2)}) collective-permute-start(bf16[2,4,128,128]{3,2,1,0:T(8,128)(2,1)} %get-tuple-element.23), channel_id=1, source_target_pairs={{0,8},{1,9},{2,10},{3,11},{4,12},{5,13},{6,14},{7,15},{8,0},{9,1},... | collective-permute-start | bytes 786440 | tf_op jit(solution)/shard_map/ppermute | solution.py:207
  25.8 14.0 %collective-permute-start.12 = (bf16[2,4,128,128]{3,2,1,0:T(8,128)(2,1)S(1)}, bf16[2,4,128,128]{3,2,1,0:T(8,128)(2,1)S(1)}, u32[]{:S(2)}, u32[]{:S(2)}) collective-permute-start(bf16[2,4,128,128]{3,2,1,0:T(8,128)(2,1)S(1)} %collective-permute-done.11.refs_0_), channel_id=1, source_target_pairs={{0,2},{1,3},{2,0},{3,1},{4,6},{5,7},{6,4},{7,5},{8,10},{9,11},{10,... | collective-permute-start | bytes 786440 | tf_op jit(solution)/shard_map/ppermute | solution.py:207
  32.8 1.2 %copy-start.1 = (bf16[256,2048]{1,0:T(8,128)(2,1)S(1)}, bf16[256,2048]{1,0:T(8,128)(2,1)}, u32[]{:S(2)}) copy-start(bf16[256,2048]{1,0:T(8,128)(2,1)} %refs_5_.3) | copy-start | bytes 3145732
  34.0 5.8 %copy-start.7 = (bf16[4,80,128]{2,1,0:T(8,128)(2,1)S(1)}, bf16[4,80,128]{2,1,0:T(8,128)(2,1)}, u32[]{:S(2)}) copy-start(bf16[4,80,128]{2,1,0:T(8,128)(2,1)} %get-tuple-element.20) | copy-start | bytes 245764
  34.4 12.0 %copy-start.3 = (bf16[4,80,128]{2,1,0:T(8,128)(2,1)S(1)}, bf16[4,80,128]{2,1,0:T(8,128)(2,1)}, u32[]{:S(2)}) copy-start(bf16[4,80,128]{2,1,0:T(8,128)(2,1)} %get-tuple-element.22.refs_3_) | copy-start | bytes 245764
  34.4 12.0 %copy-start.4 = (bf16[2,4,128,128]{3,2,1,0:T(8,128)(2,1)S(1)}, bf16[2,4,128,128]{3,2,1,0:T(8,128)(2,1)}, u32[]{:S(2)}) copy-start(bf16[2,4,128,128]{3,2,1,0:T(8,128)(2,1)} %get-tuple-element.24.refs_5_) | copy-start | bytes 786436
  34.4 12.0 %collective-permute-start.10 = (bf16[3,2,4,128,128]{4,3,2,1,0:T(8,128)(2,1)S(1)}, bf16[3,2,4,128,128]{4,3,2,1,0:T(8,128)(2,1)S(1)}, u32[]{:S(2)}, u32[]{:S(2)}) collective-permute-start(bf16[3,2,4,128,128]{4,3,2,1,0:T(8,128)(2,1)S(1)} %get-tuple-element.27.refs_7_), channel_id=1, source_target_pairs={{0,1},{1,0},{2,3},{3,2},{4,5},{5,4},{6,7},{7,6},{8,9},{9,8},{10,11... | collective-permute-start | bytes 2359304 | tf_op jit(solution)/shard_map/ppermute | solution.py:207
  38.3 8.0 %collective-permute-start.4 = (bf16[2,4,128,128]{3,2,1,0:T(8,128)(2,1)S(1)}, bf16[2,4,128,128]{3,2,1,0:T(8,128)(2,1)S(1)}, u32[]{:S(2)}, u32[]{:S(2)}) collective-permute-start(bf16[2,4,128,128]{3,2,1,0:T(8,128)(2,1)S(1)} %collective-permute-done.3.refs_1_), channel_id=1, source_target_pairs={{0,2},{1,3},{2,0},{3,1},{4,6},{5,7},{6,4},{7,5},{8,10},{9,11},{10,... | collective-permute-start | bytes 786440 | tf_op jit(solution)/shard_map/ppermute | solution.py:207
  39.8 5.5 %collective-permute-start.1 = (bf16[4,80,128]{2,1,0:T(8,128)(2,1)S(1)}, bf16[4,80,128]{2,1,0:T(8,128)(2,1)S(1)}, u32[]{:S(2)}, u32[]{:S(2)}) collective-permute-start(bf16[4,80,128]{2,1,0:T(8,128)(2,1)S(1)} %copy-done.7), channel_id=1, source_target_pairs={{0,8},{1,9},{2,10},{3,11},{4,12},{5,13},{6,14},{7,15},{8,0},{9,1},... | collective-permute-start | bytes 245768 | tf_op jit(solution)/shard_map/ppermute | solution.py:207
  39.8 6.6 %collective-permute-start.13 = (bf16[2,2,4,128,128]{4,3,2,1,0:T(8,128)(2,1)S(1)}, bf16[2,2,4,128,128]{4,3,2,1,0:T(8,128)(2,1)S(1)}, u32[]{:S(2)}, u32[]{:S(2)}) collective-permute-start(bf16[2,2,4,128,128]{4,3,2,1,0:T(8,128)(2,1)S(1)} %stack_far.1.refs_9_), channel_id=1, source_target_pairs={{0,1},{1,0},{2,3},{3,2},{4,5},{5,4},{6,7},{7,6},{8,9},{9,8},{10,11... | collective-permute-start | bytes 1572872 | tf_op jit(solution)/shard_map/ppermute | solution.py:207
  46.3 3.1 %collective-permute-start.5 = (bf16[2,2,4,128,128]{4,3,2,1,0:T(8,128)(2,1)S(1)}, bf16[2,2,4,128,128]{4,3,2,1,0:T(8,128)(2,1)S(1)}, u32[]{:S(2)}, u32[]{:S(2)}) collective-permute-start(bf16[2,2,4,128,128]{4,3,2,1,0:T(8,128)(2,1)S(1)} %stack_last.1.refs_4_), channel_id=1, source_target_pairs={{0,1},{1,0},{2,3},{3,2},{4,5},{5,4},{6,7},{7,6},{8,9},{9,8},{10,11... | collective-permute-start | bytes 1572872 | tf_op jit(solution)/shard_map/ppermute | solution.py:207
  49.4 5.5 %copy-start.6 = (s32[76]{0:T(128)S(1)}, s32[76]{0:T(128)}, u32[]{:S(2)}) copy-start(s32[76]{0:T(128)} %param.10) | copy-start | bytes 916
  49.4 11.2 %copy-start.2 = (bf16[128,2048]{1,0:T(8,128)(2,1)S(1)}, bf16[128,2048]{1,0:T(8,128)(2,1)}, u32[]{:S(2)}) copy-start(bf16[128,2048]{1,0:T(8,128)(2,1)} %refs_2_.1) | copy-start | bytes 1572868
  50.4 7.2 %collective-permute-start.14 = (bf16[4,80,128]{2,1,0:T(8,128)(2,1)S(1)}, bf16[4,80,128]{2,1,0:T(8,128)(2,1)S(1)}, u32[]{:S(2)}, u32[]{:S(2)}) collective-permute-start(bf16[4,80,128]{2,1,0:T(8,128)(2,1)S(1)} %get-tuple-element.29), channel_id=1, source_target_pairs={{0,12},{1,13},{2,14},{3,15},{4,8},{5,9},{6,10},{7,11},{8,4},{9,5},... | collective-permute-start | bytes 245768 | tf_op jit(solution)/shard_map/ppermute | solution.py:207
  51.8 8.8 %collective-permute-start.15 = (bf16[4,80,128]{2,1,0:T(8,128)(2,1)S(1)}, bf16[4,80,128]{2,1,0:T(8,128)(2,1)S(1)}, u32[]{:S(2)}, u32[]{:S(2)}) collective-permute-start(bf16[4,80,128]{2,1,0:T(8,128)(2,1)S(1)} %get-tuple-element.30), channel_id=1, source_target_pairs={{0,8},{1,9},{2,10},{3,11},{4,12},{5,13},{6,14},{7,15},{8,0},{9,1},... | collective-permute-start | bytes 245768 | tf_op jit(solution)/shard_map/ppermute | solution.py:207
  52.5 8.1 %collective-permute-start.16 = (bf16[4,80,128]{2,1,0:T(8,128)(2,1)S(1)}, bf16[4,80,128]{2,1,0:T(8,128)(2,1)S(1)}, u32[]{:S(2)}, u32[]{:S(2)}) collective-permute-start(bf16[4,80,128]{2,1,0:T(8,128)(2,1)S(1)} %get-tuple-element.31), channel_id=1, source_target_pairs={{0,4},{1,5},{2,6},{3,7},{4,0},{5,1},{6,2},{7,3},{8,12},{9,13},{10,... | collective-permute-start | bytes 245768 | tf_op jit(solution)/shard_map/ppermute | solution.py:207

commit v14 on v13

--- a/solution.py
+++ b/solution.py
@@ -285,7 +285,11 @@
     early = [own_next]
     for step in near:
         early += [pairs[step], trade(pairs[step], NEXT)]
-    after = [shares[step] for step in near + far] + [own_other]
+    middle = []
+    for step in far:
+        middle += [pairs[step], trade(pairs[step], NEXT)]
+    middle = stack(middle, [shares[step] for step in far], "stack_far")
+    after = [shares[step] for step in near] + [own_other, middle]
     early, text_pair = pl.pallas_call(
         lambda *refs: text_kernel(*refs[len(after) :]),
         out_shape=[
@@ -303,10 +307,6 @@
         compiler_params=small,
         name="stack_near",
     )(*after, me, text_k, text_v, k_gain, *early)
-    middle = []
-    for step in far:
-        middle += [pairs[step], trade(pairs[step], NEXT)]
-    middle = stack(middle, [], "stack_far")
     late = stack([pairs[half], trade(pairs[half], NEXT)], [shares[half]], "stack_last")
 
     sources = far + [half] + near + [0]

time: 61.9 us -> 63.5 us (1.026)
  starting transfers between devices: 17.1 us -> 25.2 us
  waiting for transfers between devices: 34.1 us -> 28.8 us
  local copies, waits for them, and re-layouts: 1.26 us -> 0.04 us
    ppermute x17, starting transfers between devices: 17.1 us -> 25.2 us  [trade(): return lax.ppermute(block, 'seq', [(a, a ^ distance) for a in range(count)])]
    ppermute x17, waiting for transfers between devices: 34.1 us -> 28.8 us  [trade(): return lax.ppermute(block, 'seq', [(a, a ^ distance) for a in range(count)])]
    unnamed x16, local copies, waits for them, and re-layouts: 1.26 us -> 0.04 us
  transfers between devices with their start and end apart: 17 -> 17, of which waited for: 9 -> 8; matrix products, arithmetic and copies ran while one was open for 0% -> 0% of each run, Pallas kernels for 5% -> 5%
where the time goes in v14:
time: 63.5 us; the launch traced here: 63.4 us
  waiting for transfers between devices  28.8 us (45%)
  starting transfers between devices  25.2 us (40%)
  Pallas kernels  9.2 us (14%)
    ppermute x17, waiting for transfers between devices, trade(): return lax.ppermute(block, 'seq', [(a, a ^ distance) for a in range(count)])  28.8 us
    ppermute x17, starting transfers between devices, trade(): return lax.ppermute(block, 'seq', [(a, a ^ distance) for a in range(count)])  25.2 us
    pallas_call x1, Pallas kernels, prepare(): pl.pallas_call(lambda *refs: prepare_kernel(plan, padded, *refs), out_sha...  3.74 us
    pallas_call x1, Pallas kernels, shards(): pl.pallas_call(lambda *refs: attend_kernel(outers, *refs), out_shape=shap...  2.91 us
  transfers between devices with their start and end apart: 17, of which 8 were waited for; matrix products, arithmetic and copies ran while one was open for 0% of the time, Pallas kernels for 5%

profile of v14, /device:TPU:0, one launch (start us, length us, event | category | flops | bytes accessed | tf_op | source)
XLA Modules:
  0.0 63.4 jit_solution(7132891004636231488)
XLA Ops:
  0.0 3.7 %prepare.1 = (bf16[2,4,128,128]{3,2,1,0:T(8,128)(2,1)}, bf16[4,80,128]{2,1,0:T(8,128)(2,1)}, bf16[2,4,128,128]{3,2,1,0:T(8,128)(2,1)}, bf16[4,80,128]{2,1,0:T(8,...) custom-call(s32[1]{0:T(128)} %bitcast.refs_0_.refs_3_, ...), custom_call_target="tpu_custom_call" | custom-call | tf_op jit(solution)/shard_map/prepare/pallas_call | solution.py:242
  3.8 5.1 %collective-permute-start.7 = (bf16[2,4,128,128]{3,2,1,0:T(8,128)(2,1)}, bf16[2,4,128,128]{3,2,1,0:T(8,128)(2,1)S(1)}, u32[]{:S(2)}, u32[]{:S(2)}) collective-permute-start(bf16[2,4,128,128]{3,2,1,0:T(8,128)(2,1)} %get-tuple-element.25), channel_id=1, source_target_pairs={{0,12},{1,13},{2,14},{3,15},{4,8},{5,9},{6,10},{7,11},{8,4},{9,5},... | collective-permute-start | bytes 786440 | tf_op jit(solution)/shard_map/ppermute | solution.py:207
  8.9 0.0 collective-permute-start.10
  8.9 7.4 %collective-permute-done.7.refs_1_ = bf16[2,4,128,128]{3,2,1,0:T(8,128)(2,1)S(1)} collective-permute-done((bf16[2,4,128,128]{3,2,1,0:T(8,128)(2,1)}, bf16[2,4,128,128]{3,2,1,0:T(8,128)(2,1)S(1)}, u32[]{:S(2)}, u32[]{:S(2)}) %collective-permute-start.7) | collective-permute-done | bytes 262176 | tf_op jit(solution)/shard_map/ppermute | solution.py:207
  16.3 1.7 %collective-permute-start.8 = (bf16[2,4,128,128]{3,2,1,0:T(8,128)(2,1)S(1)}, bf16[2,4,128,128]{3,2,1,0:T(8,128)(2,1)S(1)}, u32[]{:S(2)}, u32[]{:S(2)}) collective-permute-start(bf16[2,4,128,128]{3,2,1,0:T(8,128)(2,1)S(1)} %collective-permute-done.7.refs_1_), channel_id=1, source_target_pairs={{0,2},{1,3},{2,0},{3,1},{4,6},{5,7},{6,4},{7,5},{8,10},{9,11},{10,... | collective-permute-start | bytes 786440 | tf_op jit(solution)/shard_map/ppermute | solution.py:207
  18.0 3.6 %collective-permute-start = (bf16[4,80,128]{2,1,0:T(8,128)(2,1)}, bf16[4,80,128]{2,1,0:T(8,128)(2,1)S(1)}, u32[]{:S(2)}, u32[]{:S(2)}) collective-permute-start(bf16[4,80,128]{2,1,0:T(8,128)(2,1)} %get-tuple-element.19), channel_id=1, source_target_pairs={{0,12},{1,13},{2,14},{3,15},{4,8},{5,9},{6,10},{7,11},{8,4},{9,5},... | collective-permute-start | bytes 245768 | tf_op jit(solution)/shard_map/ppermute | solution.py:207
  21.6 0.0 collective-permute-start.6
  21.6 0.5 collective-permute-start.9
  22.1 0.0 collective-permute-done.10.refs_8_
  22.1 1.5 %collective-permute-start.11 = (bf16[2,4,128,128]{3,2,1,0:T(8,128)(2,1)S(1)}, bf16[2,4,128,128]{3,2,1,0:T(8,128)(2,1)S(1)}, u32[]{:S(2)}, u32[]{:S(2)}) collective-permute-start(bf16[2,4,128,128]{3,2,1,0:T(8,128)(2,1)S(1)} %collective-permute-done.10.refs_8_), channel_id=1, source_target_pairs={{0,2},{1,3},{2,0},{3,1},{4,6},{5,7},{6,4},{7,5},{8,10},{9,11},{10,... | collective-permute-start | bytes 786440 | tf_op jit(solution)/shard_map/ppermute | solution.py:207
  23.6 0.9 %collective-permute-done.refs_0_ = bf16[4,80,128]{2,1,0:T(8,128)(2,1)S(1)} collective-permute-done((bf16[4,80,128]{2,1,0:T(8,128)(2,1)}, bf16[4,80,128]{2,1,0:T(8,128)(2,1)S(1)}, u32[]{:S(2)}, u32[]{:S(2)}) %collective-permute-start) | collective-permute-done | bytes 81952 | tf_op jit(solution)/shard_map/ppermute | solution.py:207
  24.6 3.4 %collective-permute-start.3 = (bf16[2,4,128,128]{3,2,1,0:T(8,128)(2,1)}, bf16[2,4,128,128]{3,2,1,0:T(8,128)(2,1)S(1)}, u32[]{:S(2)}, u32[]{:S(2)}) collective-permute-start(bf16[2,4,128,128]{3,2,1,0:T(8,128)(2,1)} %get-tuple-element.23), channel_id=1, source_target_pairs={{0,8},{1,9},{2,10},{3,11},{4,12},{5,13},{6,14},{7,15},{8,0},{9,1},... | collective-permute-start | bytes 786440 | tf_op jit(solution)/shard_map/ppermute | solution.py:207
  28.0 0.0 collective-permute-done.8.refs_2_
  28.0 1.0 %collective-permute-start.2 = (bf16[4,80,128]{2,1,0:T(8,128)(2,1)}, bf16[4,80,128]{2,1,0:T(8,128)(2,1)S(1)}, u32[]{:S(2)}, u32[]{:S(2)}) collective-permute-start(bf16[4,80,128]{2,1,0:T(8,128)(2,1)} %get-tuple-element.21), channel_id=1, source_target_pairs={{0,4},{1,5},{2,6},{3,7},{4,0},{5,1},{6,2},{7,3},{8,12},{9,13},{10,... | collective-permute-start | bytes 245768 | tf_op jit(solution)/shard_map/ppermute | solution.py:207
  29.1 0.0 copy-start.7
  29.1 0.0 copy-start.3
  29.1 4.6 %collective-permute-done.2.refs_0_.refs_2_ = bf16[4,80,128]{2,1,0:T(8,128)(2,1)S(1)} collective-permute-done((bf16[4,80,128]{2,1,0:T(8,128)(2,1)}, bf16[4,80,128]{2,1,0:T(8,128)(2,1)S(1)}, u32[]{:S(2)}, u32[]{:S(2)}) %collective-permute-start.2) | collective-permute-done | bytes 81952 | tf_op jit(solution)/shard_map/ppermute | solution.py:207
  33.6 0.0 collective-permute-done.6.refs_1_.refs_6_
  33.6 0.0 collective-permute-done.9.refs_7_
  33.6 2.5 %collective-permute-done.11.refs_9_ = bf16[2,4,128,128]{3,2,1,0:T(8,128)(2,1)S(1)} collective-permute-done((bf16[2,4,128,128]{3,2,1,0:T(8,128)(2,1)S(1)}, bf16[2,4,128,128]{3,2,1,0:T(8,128)(2,1)S(1)}, u32[]{:S(2)}, u32[]{:S(2)}) %collective-permute-start.11) | collective-permute-done | bytes 262176 | tf_op jit(solution)/shard_map/ppermute | solution.py:207
  36.2 0.0 copy-done
  36.2 0.0 copy-done.1
  36.2 0.0 copy-done.5
  36.2 0.4 stack_near.1
  36.6 0.0 copy-start.4
  36.6 0.1 collective-permute-start.12
  36.7 1.9 %collective-permute-done.3.refs_1_ = bf16[2,4,128,128]{3,2,1,0:T(8,128)(2,1)S(1)} collective-permute-done((bf16[2,4,128,128]{3,2,1,0:T(8,128)(2,1)}, bf16[2,4,128,128]{3,2,1,0:T(8,128)(2,1)S(1)}, u32[]{:S(2)}, u32[]{:S(2)}) %collective-permute-start.3) | collective-permute-done | bytes 262176 | tf_op jit(solution)/shard_map/ppermute | solution.py:207
  38.5 0.5 collective-permute-start.4
  39.0 0.0 copy-done.7
  39.0 3.2 %collective-permute-start.1 = (bf16[4,80,128]{2,1,0:T(8,128)(2,1)S(1)}, bf16[4,80,128]{2,1,0:T(8,128)(2,1)S(1)}, u32[]{:S(2)}, u32[]{:S(2)}) collective-permute-start(bf16[4,80,128]{2,1,0:T(8,128)(2,1)S(1)} %copy-done.7), channel_id=1, source_target_pairs={{0,8},{1,9},{2,10},{3,11},{4,12},{5,13},{6,14},{7,15},{8,0},{9,1},... | collective-permute-start | bytes 245768 | tf_op jit(solution)/shard_map/ppermute | solution.py:207
  42.3 0.0 collective-permute-start.13
  42.3 4.5 %collective-permute-done.1.refs_0_.refs_1_ = bf16[4,80,128]{2,1,0:T(8,128)(2,1)S(1)} collective-permute-done((bf16[4,80,128]{2,1,0:T(8,128)(2,1)S(1)}, bf16[4,80,128]{2,1,0:T(8,128)(2,1)S(1)}, u32[]{:S(2)}, u32[]{:S(2)}) %collective-permute-start.1) | collective-permute-done | bytes 81952 | tf_op jit(solution)/shard_map/ppermute | solution.py:207
  46.8 0.0 collective-permute-done.4.refs_2_
  46.8 0.1 collective-permute-start.5
  46.9 0.0 collective-permute-done.13.refs_10_
  46.9 0.0 collective-permute-done.12.refs_8_
  46.9 2.9 %attend.1.refs_6_ = f32[4,1,320,256]{3,2,1,0:T(8,128)S(1)} custom-call(bf16[4,80,128]{2,1,0:T(8,128)(2,1)S(1)} %collective-permute-done.refs_0_, bf16[4,80,128]{2,1,0:T(8,128)(2,1)S(1)} %collective-permute-done.1.refs_0_.refs_1_, bf16[4,80,128]{2,1,0:T(8,128)(2,1)S(1)} %collective-permute-done.2.refs_0_.refs_2_, bf16[4,80,128]{2,1,0:T(8,128)(2,1)S(1)} %copy-done.3, ...), custom_call_target="tpu_custom_call" | custom-call | tf_op jit(solution)/shard_map/attend/pallas_call | solution.py:316
  49.9 0.0 copy-start.6
  49.9 0.0 copy-start.2
  49.9 0.0 collective-permute-done.5.refs_5_
  49.9 1.0 %complete.1 = (bf16[4,80,128]{2,1,0:T(8,128)(2,1)S(1)}, bf16[4,80,128]{2,1,0:T(8,128)(2,1)S(1)}, bf16[4,80,128]{2,1,0:T(8,128)(2,1)S(1)}, bf16[4,80,128]{2,1,0:T(8,128)(2,1)S(1)}) custom-call(bf16[4,80,128]{2,1,0:T(8,128)(2,1)S(1)} %collective-permute-done.refs_0_, bf16[4,80,128]{2,1,0:T(8,128)(2,1)S(1)} %collective-permute-done.1.refs_0_.refs_1_, ...), custom_call_target="tpu_custom_call" | custom-call | tf_op jit(solution)/shard_map/complete/pallas_call | solution.py:324
  50.9 0.8 %collective-permute-start.14 = (bf16[4,80,128]{2,1,0:T(8,128)(2,1)S(1)}, bf16[4,80,128]{2,1,0:T(8,128)(2,1)S(1)}, u32[]{:S(2)}, u32[]{:S(2)}) collective-permute-start(bf16[4,80,128]{2,1,0:T(8,128)(2,1)S(1)} %get-tuple-element.29), channel_id=1, source_target_pairs={{0,12},{1,13},{2,14},{3,15},{4,8},{5,9},{6,10},{7,11},{8,4},{9,5},... | collective-permute-start | bytes 245768 | tf_op jit(solution)/shard_map/ppermute | solution.py:207
  51.6 2.5 %collective-permute-start.15 = (bf16[4,80,128]{2,1,0:T(8,128)(2,1)S(1)}, bf16[4,80,128]{2,1,0:T(8,128)(2,1)S(1)}, u32[]{:S(2)}, u32[]{:S(2)}) collective-permute-start(bf16[4,80,128]{2,1,0:T(8,128)(2,1)S(1)} %get-tuple-element.30), channel_id=1, source_target_pairs={{0,8},{1,9},{2,10},{3,11},{4,12},{5,13},{6,14},{7,15},{8,0},{9,1},... | collective-permute-start | bytes 245768 | tf_op jit(solution)/shard_map/ppermute | solution.py:207
  54.2 1.2 %collective-permute-start.16 = (bf16[4,80,128]{2,1,0:T(8,128)(2,1)S(1)}, bf16[4,80,128]{2,1,0:T(8,128)(2,1)S(1)}, u32[]{:S(2)}, u32[]{:S(2)}) collective-permute-start(bf16[4,80,128]{2,1,0:T(8,128)(2,1)S(1)} %get-tuple-element.31), channel_id=1, source_target_pairs={{0,4},{1,5},{2,6},{3,7},{4,0},{5,1},{6,2},{7,3},{8,12},{9,13},{10,... | collective-permute-start | bytes 245768 | tf_op jit(solution)/shard_map/ppermute | solution.py:207
  55.3 2.7 %collective-permute-done.14.refs_3_ = bf16[4,80,128]{2,1,0:T(8,128)(2,1)S(1)} collective-permute-done((bf16[4,80,128]{2,1,0:T(8,128)(2,1)S(1)}, bf16[4,80,128]{2,1,0:T(8,128)(2,1)S(1)}, u32[]{:S(2)}, u32[]{:S(2)}) %collective-permute-start.14) | collective-permute-done | bytes 81952 | tf_op jit(solution)/shard_map/ppermute | solution.py:207
  58.0 4.2 %collective-permute-done.15.refs_4_ = bf16[4,80,128]{2,1,0:T(8,128)(2,1)S(1)} collective-permute-done((bf16[4,80,128]{2,1,0:T(8,128)(2,1)S(1)}, bf16[4,80,128]{2,1,0:T(8,128)(2,1)S(1)}, u32[]{:S(2)}, u32[]{:S(2)}) %collective-permute-start.15) | collective-permute-done | bytes 81952 | tf_op jit(solution)/shard_map/ppermute | solution.py:207
  62.2 0.0 collective-permute-done.16.refs_5_
  62.2 1.1 %finish.1 = bf16[128,2048]{1,0:T(8,128)(2,1)} custom-call(s32[1]{0:T(128)} %bitcast.refs_0_.refs_3_, s32[1,80]{1,0:T(1,128)S(1)} %pad.4.refs_1_, bf16[128,2048]{1,0:T(8,128)(2,1)S(1)} %copy-done.2, bf16[4,80,128]{2,1,0:T(8,128)(2,1)S(1)} %collective-permute-done.14.refs_3_, bf16[4,80,128]{2,1,0:T(8,128)(2,1)S(1)} %collective-permute-done.15.refs_4_, ...), custom_call_target="tpu_custom_call" | custom-call | tf_op jit(solution)/shard_map/finish/pallas_call | solution.py:337
  (10 shorter events, 0.1 us)
Async XLA Ops:
  0.0 36.2 %copy-start = (bf16[256,2048]{1,0:T(8,128)(2,1)S(1)}, bf16[256,2048]{1,0:T(8,128)(2,1)}, u32[]{:S(2)}) copy-start(bf16[256,2048]{1,0:T(8,128)(2,1)} %refs_4_.1) | copy-start | bytes 3145732
  0.0 36.2 %copy-start.1 = (bf16[256,2048]{1,0:T(8,128)(2,1)S(1)}, bf16[256,2048]{1,0:T(8,128)(2,1)}, u32[]{:S(2)}) copy-start(bf16[256,2048]{1,0:T(8,128)(2,1)} %refs_5_.3) | copy-start | bytes 3145732
  0.0 36.2 %copy-start.5 = (f32[128]{0:T(128)S(1)}, f32[128]{0:T(128)}, u32[]{:S(2)}) copy-start(f32[128]{0:T(128)} %param.17) | copy-start | bytes 1540
  3.8 12.6 %collective-permute-start.7 = (bf16[2,4,128,128]{3,2,1,0:T(8,128)(2,1)}, bf16[2,4,128,128]{3,2,1,0:T(8,128)(2,1)S(1)}, u32[]{:S(2)}, u32[]{:S(2)}) collective-permute-start(bf16[2,4,128,128]{3,2,1,0:T(8,128)(2,1)} %get-tuple-element.25), channel_id=1, source_target_pairs={{0,12},{1,13},{2,14},{3,15},{4,8},{5,9},{6,10},{7,11},{8,4},{9,5},... | collective-permute-start | bytes 786440 | tf_op jit(solution)/shard_map/ppermute | solution.py:207
  8.9 13.2 %collective-permute-start.10 = (bf16[2,4,128,128]{3,2,1,0:T(8,128)(2,1)}, bf16[2,4,128,128]{3,2,1,0:T(8,128)(2,1)S(1)}, u32[]{:S(2)}, u32[]{:S(2)}) collective-permute-start(bf16[2,4,128,128]{3,2,1,0:T(8,128)(2,1)} %get-tuple-element.26), channel_id=1, source_target_pairs={{0,4},{1,5},{2,6},{3,7},{4,0},{5,1},{6,2},{7,3},{8,12},{9,13},{10,... | collective-permute-start | bytes 786440 | tf_op jit(solution)/shard_map/ppermute | solution.py:207
  16.3 11.7 %collective-permute-start.8 = (bf16[2,4,128,128]{3,2,1,0:T(8,128)(2,1)S(1)}, bf16[2,4,128,128]{3,2,1,0:T(8,128)(2,1)S(1)}, u32[]{:S(2)}, u32[]{:S(2)}) collective-permute-start(bf16[2,4,128,128]{3,2,1,0:T(8,128)(2,1)S(1)} %collective-permute-done.7.refs_1_), channel_id=1, source_target_pairs={{0,2},{1,3},{2,0},{3,1},{4,6},{5,7},{6,4},{7,5},{8,10},{9,11},{10,... | collective-permute-start | bytes 786440 | tf_op jit(solution)/shard_map/ppermute | solution.py:207
  18.0 6.6 %collective-permute-start = (bf16[4,80,128]{2,1,0:T(8,128)(2,1)}, bf16[4,80,128]{2,1,0:T(8,128)(2,1)S(1)}, u32[]{:S(2)}, u32[]{:S(2)}) collective-permute-start(bf16[4,80,128]{2,1,0:T(8,128)(2,1)} %get-tuple-element.19), channel_id=1, source_target_pairs={{0,12},{1,13},{2,14},{3,15},{4,8},{5,9},{6,10},{7,11},{8,4},{9,5},... | collective-permute-start | bytes 245768 | tf_op jit(solution)/shard_map/ppermute | solution.py:207
  21.6 12.0 %collective-permute-start.6 = (bf16[2,4,128,128]{3,2,1,0:T(8,128)(2,1)}, bf16[2,4,128,128]{3,2,1,0:T(8,128)(2,1)S(1)}, u32[]{:S(2)}, u32[]{:S(2)}) collective-permute-start(bf16[2,4,128,128]{3,2,1,0:T(8,128)(2,1)} %get-tuple-element.24.refs_5_), channel_id=1, source_target_pairs={{0,1},{1,0},{2,3},{3,2},{4,5},{5,4},{6,7},{7,6},{8,9},{9,8},{10,11... | collective-permute-start | bytes 786440 | tf_op jit(solution)/shard_map/ppermute | solution.py:207
  21.6 12.0 %collective-permute-start.9 = (bf16[2,4,128,128]{3,2,1,0:T(8,128)(2,1)}, bf16[2,4,128,128]{3,2,1,0:T(8,128)(2,1)S(1)}, u32[]{:S(2)}, u32[]{:S(2)}) collective-permute-start(bf16[2,4,128,128]{3,2,1,0:T(8,128)(2,1)} %get-tuple-element.24.refs_5_), channel_id=1, source_target_pairs={{0,2},{1,3},{2,0},{3,1},{4,6},{5,7},{6,4},{7,5},{8,10},{9,11},{10,... | collective-permute-start | bytes 786440 | tf_op jit(solution)/shard_map/ppermute | solution.py:207
  22.1 14.0 %collective-permute-start.11 = (bf16[2,4,128,128]{3,2,1,0:T(8,128)(2,1)S(1)}, bf16[2,4,128,128]{3,2,1,0:T(8,128)(2,1)S(1)}, u32[]{:S(2)}, u32[]{:S(2)}) collective-permute-start(bf16[2,4,128,128]{3,2,1,0:T(8,128)(2,1)S(1)} %collective-permute-done.10.refs_8_), channel_id=1, source_target_pairs={{0,2},{1,3},{2,0},{3,1},{4,6},{5,7},{6,4},{7,5},{8,10},{9,11},{10,... | collective-permute-start | bytes 786440 | tf_op jit(solution)/shard_map/ppermute | solution.py:207
  24.6 13.9 %collective-permute-start.3 = (bf16[2,4,128,128]{3,2,1,0:T(8,128)(2,1)}, bf16[2,4,128,128]{3,2,1,0:T(8,128)(2,1)S(1)}, u32[]{:S(2)}, u32[]{:S(2)}) collective-permute-start(bf16[2,4,128,128]{3,2,1,0:T(8,128)(2,1)} %get-tuple-element.23), channel_id=1, source_target_pairs={{0,8},{1,9},{2,10},{3,11},{4,12},{5,13},{6,14},{7,15},{8,0},{9,1},... | collective-permute-start | bytes 786440 | tf_op jit(solution)/shard_map/ppermute | solution.py:207
  28.0 5.6 %collective-permute-start.2 = (bf16[4,80,128]{2,1,0:T(8,128)(2,1)}, bf16[4,80,128]{2,1,0:T(8,128)(2,1)S(1)}, u32[]{:S(2)}, u32[]{:S(2)}) collective-permute-start(bf16[4,80,128]{2,1,0:T(8,128)(2,1)} %get-tuple-element.21), channel_id=1, source_target_pairs={{0,4},{1,5},{2,6},{3,7},{4,0},{5,1},{6,2},{7,3},{8,12},{9,13},{10,... | collective-permute-start | bytes 245768 | tf_op jit(solution)/shard_map/ppermute | solution.py:207
  29.1 10.0 %copy-start.7 = (bf16[4,80,128]{2,1,0:T(8,128)(2,1)S(1)}, bf16[4,80,128]{2,1,0:T(8,128)(2,1)}, u32[]{:S(2)}) copy-start(bf16[4,80,128]{2,1,0:T(8,128)(2,1)} %get-tuple-element.20) | copy-start | bytes 245764
  29.1 17.8 %copy-start.3 = (bf16[4,80,128]{2,1,0:T(8,128)(2,1)S(1)}, bf16[4,80,128]{2,1,0:T(8,128)(2,1)}, u32[]{:S(2)}) copy-start(bf16[4,80,128]{2,1,0:T(8,128)(2,1)} %get-tuple-element.22.refs_3_) | copy-start | bytes 245764
  36.6 10.4 %copy-start.4 = (bf16[2,4,128,128]{3,2,1,0:T(8,128)(2,1)S(1)}, bf16[2,4,128,128]{3,2,1,0:T(8,128)(2,1)}, u32[]{:S(2)}) copy-start(bf16[2,4,128,128]{3,2,1,0:T(8,128)(2,1)} %get-tuple-element.24.refs_5_) | copy-start | bytes 786436
  36.6 10.3 %collective-permute-start.12 = (bf16[3,2,4,128,128]{4,3,2,1,0:T(8,128)(2,1)S(1)}, bf16[3,2,4,128,128]{4,3,2,1,0:T(8,128)(2,1)S(1)}, u32[]{:S(2)}, u32[]{:S(2)}) collective-permute-start(bf16[3,2,4,128,128]{4,3,2,1,0:T(8,128)(2,1)S(1)} %get-tuple-element.28.refs_7_), channel_id=1, source_target_pairs={{0,1},{1,0},{2,3},{3,2},{4,5},{5,4},{6,7},{7,6},{8,9},{9,8},{10,11... | collective-permute-start | bytes 2359304 | tf_op jit(solution)/shard_map/ppermute | solution.py:207
  38.5 8.2 %collective-permute-start.4 = (bf16[2,4,128,128]{3,2,1,0:T(8,128)(2,1)S(1)}, bf16[2,4,128,128]{3,2,1,0:T(8,128)(2,1)S(1)}, u32[]{:S(2)}, u32[]{:S(2)}) collective-permute-start(bf16[2,4,128,128]{3,2,1,0:T(8,128)(2,1)S(1)} %collective-permute-done.3.refs_1_), channel_id=1, source_target_pairs={{0,2},{1,3},{2,0},{3,1},{4,6},{5,7},{6,4},{7,5},{8,10},{9,11},{10,... | collective-permute-start | bytes 786440 | tf_op jit(solution)/shard_map/ppermute | solution.py:207
  39.0 7.7 %collective-permute-start.1 = (bf16[4,80,128]{2,1,0:T(8,128)(2,1)S(1)}, bf16[4,80,128]{2,1,0:T(8,128)(2,1)S(1)}, u32[]{:S(2)}, u32[]{:S(2)}) collective-permute-start(bf16[4,80,128]{2,1,0:T(8,128)(2,1)S(1)} %copy-done.7), channel_id=1, source_target_pairs={{0,8},{1,9},{2,10},{3,11},{4,12},{5,13},{6,14},{7,15},{8,0},{9,1},... | collective-permute-start | bytes 245768 | tf_op jit(solution)/shard_map/ppermute | solution.py:207
  42.3 4.6 %collective-permute-start.13 = (bf16[2,2,4,128,128]{4,3,2,1,0:T(8,128)(2,1)S(1)}, bf16[2,2,4,128,128]{4,3,2,1,0:T(8,128)(2,1)S(1)}, u32[]{:S(2)}, u32[]{:S(2)}) collective-permute-start(bf16[2,2,4,128,128]{4,3,2,1,0:T(8,128)(2,1)S(1)} %stack_far.1.refs_2_.refs_9_), channel_id=1, source_target_pairs={{0,1},{1,0},{2,3},{3,2},{4,5},{5,4},{6,7},{7,6},{8,9},{9,8},{10,11... | collective-permute-start | bytes 1572872 | tf_op jit(solution)/shard_map/ppermute | solution.py:207
  46.8 3.1 %collective-permute-start.5 = (bf16[2,2,4,128,128]{4,3,2,1,0:T(8,128)(2,1)S(1)}, bf16[2,2,4,128,128]{4,3,2,1,0:T(8,128)(2,1)S(1)}, u32[]{:S(2)}, u32[]{:S(2)}) collective-permute-start(bf16[2,2,4,128,128]{4,3,2,1,0:T(8,128)(2,1)S(1)} %stack_last.1.refs_4_), channel_id=1, source_target_pairs={{0,1},{1,0},{2,3},{3,2},{4,5},{5,4},{6,7},{7,6},{8,9},{9,8},{10,11... | collective-permute-start | bytes 1572872 | tf_op jit(solution)/shard_map/ppermute | solution.py:207
  49.9 5.5 %copy-start.6 = (s32[76]{0:T(128)S(1)}, s32[76]{0:T(128)}, u32[]{:S(2)}) copy-start(s32[76]{0:T(128)} %param.10) | copy-start | bytes 916
  49.9 12.4 %copy-start.2 = (bf16[128,2048]{1,0:T(8,128)(2,1)S(1)}, bf16[128,2048]{1,0:T(8,128)(2,1)}, u32[]{:S(2)}) copy-start(bf16[128,2048]{1,0:T(8,128)(2,1)} %refs_2_.1) | copy-start | bytes 1572868
  50.9 7.2 %collective-permute-start.14 = (bf16[4,80,128]{2,1,0:T(8,128)(2,1)S(1)}, bf16[4,80,128]{2,1,0:T(8,128)(2,1)S(1)}, u32[]{:S(2)}, u32[]{:S(2)}) collective-permute-start(bf16[4,80,128]{2,1,0:T(8,128)(2,1)S(1)} %get-tuple-element.29), channel_id=1, source_target_pairs={{0,12},{1,13},{2,14},{3,15},{4,8},{5,9},{6,10},{7,11},{8,4},{9,5},... | collective-permute-start | bytes 245768 | tf_op jit(solution)/shard_map/ppermute | solution.py:207
  51.6 10.6 %collective-permute-start.15 = (bf16[4,80,128]{2,1,0:T(8,128)(2,1)S(1)}, bf16[4,80,128]{2,1,0:T(8,128)(2,1)S(1)}, u32[]{:S(2)}, u32[]{:S(2)}) collective-permute-start(bf16[4,80,128]{2,1,0:T(8,128)(2,1)S(1)} %get-tuple-element.30), channel_id=1, source_target_pairs={{0,8},{1,9},{2,10},{3,11},{4,12},{5,13},{6,14},{7,15},{8,0},{9,1},... | collective-permute-start | bytes 245768 | tf_op jit(solution)/shard_map/ppermute | solution.py:207
  54.2 8.1 %collective-permute-start.16 = (bf16[4,80,128]{2,1,0:T(8,128)(2,1)S(1)}, bf16[4,80,128]{2,1,0:T(8,128)(2,1)S(1)}, u32[]{:S(2)}, u32[]{:S(2)}) collective-permute-start(bf16[4,80,128]{2,1,0:T(8,128)(2,1)S(1)} %get-tuple-element.31), channel_id=1, source_target_pairs={{0,4},{1,5},{2,6},{3,7},{4,0},{5,1},{6,2},{7,3},{8,12},{9,13},{10,... | collective-permute-start | bytes 245768 | tf_op jit(solution)/shard_map/ppermute | solution.py:207

commit v15 on v8

--- a/solution.py
+++ b/solution.py
@@ -163,7 +163,7 @@
 def add_shared(sums, queries, shared, head, tokens):
     for ref in shared:
         rows = ref.shape[2]
-        chunk = next(c * tokens for c in (4, 3, 2, 1) if rows % (c * tokens) == 0)
+        chunk = next(c * tokens for c in (7, 6, 5, 4, 3, 2, 1) if rows % (c * tokens) == 0)
         for first in range(0, rows, chunk):
             at = slice(first, first + chunk)
             sums = add_keys(sums, queries, ref[head, 0, at], ref[head, 1, at])

time: 62.9 us -> 60.7 us (0.965)
  Pallas kernels: 12 us -> 9.52 us
    pallas_call x1, Pallas kernels: 3.37 us -> 2.1 us  [shards(): pl.pallas_call(lambda *refs: attend_kernel(tokens, padded, *refs), out_sh...]
    pallas_call x1, Pallas kernels: 2.68 us -> 1.44 us  [complete(): pl.pallas_call(lambda *refs: complete_kernel(tokens, first, *refs), out_s...]
  transfers between devices with their start and end apart: 16 -> 16, of which waited for: 7 -> 8; matrix products, arithmetic and copies ran while one was open for 0% -> 0% of each run, Pallas kernels for 9% -> 7%
where the time goes in v15:
time: 60.7 us; the launch traced here: 60.5 us
  starting transfers between devices  29.7 us (49%)
  waiting for transfers between devices  18.7 us (31%)
  Pallas kernels  9.52 us (16%)
  local copies, waits for them, and re-layouts  2.49 us (4%)
    ppermute x16, starting transfers between devices, trade(): return lax.ppermute(block, 'seq', [(a, a ^ distance) for a in range(count)])  29.7 us
    ppermute x16, waiting for transfers between devices, trade(): return lax.ppermute(block, 'seq', [(a, a ^ distance) for a in range(count)])  18.7 us
    pallas_call x2, Pallas kernels, prepare(): pl.pallas_call(lambda *refs: prepare_kernel(plan, groups, per_group, padd...  4.74 us
    unnamed x22, local copies, waits for them, and re-layouts  2.48 us
    pallas_call x1, Pallas kernels, shards(): pl.pallas_call(lambda *refs: attend_kernel(tokens, padded, *refs), out_sh...  2.1 us
    pallas_call x1, Pallas kernels, complete(): pl.pallas_call(lambda *refs: complete_kernel(tokens, first, *refs), out_s...  1.44 us
  transfers between devices with their start and end apart: 16, of which 8 were waited for; matrix products, arithmetic and copies ran while one was open for 0% of the time, Pallas kernels for 7%

profile of v15, /device:TPU:0, one launch (start us, length us, event | category | flops | bytes accessed | tf_op | source)
XLA Modules:
  0.0 60.5 jit_solution(16956576451315108585)
XLA Ops:
  0.0 0.0 copy-start.2
  0.0 2.4 %prepare_first.1 = (bf16[2,336,128]{2,1,0:T(8,128)(2,1)}, bf16[2,256,128]{2,1,0:T(8,128)(2,1)}, bf16[2,80,128]{2,1,0:T(8,128)(2,1)}) custom-call(s32[1]{0:T(128)} %bitcast.refs_0_, s32[1,76]{1,0:T(1,128)} %bitcast.11, f32[1,128]{1,0:T(1,128)} %bitcast.7, f32[1,128]{1,0:T(1,128)} %bitcast.9, bf16[3,76,2048]{2,1,0:T(8,128)(2,1)} %bitcast.5, ...), custom_call_target="tpu_custom_call" | custom-call | tf_op jit(solution)/shard_map/prepare_first/pallas_call | solution.py:279
  2.4 0.5 collective-permute-start.1
  3.0 5.6 %collective-permute-start = (bf16[2,336,128]{2,1,0:T(8,128)(2,1)}, bf16[2,336,128]{2,1,0:T(8,128)(2,1)S(1)}, u32[]{:S(2)}, u32[]{:S(2)}) collective-permute-start(bf16[2,336,128]{2,1,0:T(8,128)(2,1)} %get-tuple-element.27), channel_id=1, source_target_pairs={{0,14},{1,15},{2,12},{3,13},{4,10},{5,11},{6,8},{7,9},{8,6},{9,7},... | collective-permute-start | bytes 516104 | tf_op jit(solution)/shard_map/ppermute | solution.py:236
  8.6 0.0 collective-permute-done.1.refs_9_.refs_8_
  8.6 0.0 copy-done.10
  8.6 0.0 copy-done.8
  8.6 0.0 copy-done.9
  8.6 0.0 copy-done
  8.7 0.0 copy-start.3
  8.7 1.2 %copy-done.3 = bf16[256,2048]{1,0:T(8,128)(2,1)S(1)} copy-done((bf16[256,2048]{1,0:T(8,128)(2,1)S(1)}, bf16[256,2048]{1,0:T(8,128)(2,1)}, u32[]{:S(2)}) %copy-start.3) | copy-done | bytes 1048600
  9.9 1.2 %copy-done.4 = bf16[256,2048]{1,0:T(8,128)(2,1)S(1)} copy-done((bf16[256,2048]{1,0:T(8,128)(2,1)S(1)}, bf16[256,2048]{1,0:T(8,128)(2,1)}, u32[]{:S(2)}) %copy-start.4) | copy-done | bytes 1048600
  11.1 2.3 %prepare_rest.1 = (bf16[2,336,128]{2,1,0:T(8,128)(2,1)S(1)}, bf16[2,336,128]{2,1,0:T(8,128)(2,1)S(1)}, bf16[2,336,128]{2,1,0:T(8,128)(2,1)S(1)}, bf16[2,336,128]...) custom-call(s32[1]{0:T(128)} %bitcast.refs_0_, ...), custom_call_target="tpu_custom_call" | custom-call | tf_op jit(solution)/shard_map/prepare_rest/pallas_call | solution.py:279
  13.5 0.6 collective-permute-start.2
  14.0 1.5 %collective-permute-start.3 = (bf16[2,336,128]{2,1,0:T(8,128)(2,1)S(1)}, bf16[2,336,128]{2,1,0:T(8,128)(2,1)S(1)}, u32[]{:S(2)}, u32[]{:S(2)}) collective-permute-start(bf16[2,336,128]{2,1,0:T(8,128)(2,1)S(1)} %get-tuple-element.30), channel_id=1, source_target_pairs={{0,2},{1,3},{2,0},{3,1},{4,6},{5,7},{6,4},{7,5},{8,10},{9,11},{10,... | collective-permute-start | bytes 516104 | tf_op jit(solution)/shard_map/ppermute | solution.py:236
  15.6 0.4 collective-permute-start.4
  16.0 3.4 %collective-permute-start.5 = (bf16[2,336,128]{2,1,0:T(8,128)(2,1)S(1)}, bf16[2,336,128]{2,1,0:T(8,128)(2,1)S(1)}, u32[]{:S(2)}, u32[]{:S(2)}) collective-permute-start(bf16[2,336,128]{2,1,0:T(8,128)(2,1)S(1)} %get-tuple-element.32), channel_id=1, source_target_pairs={{0,4},{1,5},{2,6},{3,7},{4,0},{5,1},{6,2},{7,3},{8,12},{9,13},{10,... | collective-permute-start | bytes 516104 | tf_op jit(solution)/shard_map/ppermute | solution.py:236
  19.4 0.0 collective-permute-done.refs_0_
  19.4 0.0 collective-permute-start.6
  19.4 3.3 %collective-permute-done.2.refs_1_ = bf16[2,336,128]{2,1,0:T(8,128)(2,1)S(1)} collective-permute-done((bf16[2,336,128]{2,1,0:T(8,128)(2,1)S(1)}, bf16[2,336,128]{2,1,0:T(8,128)(2,1)S(1)}, u32[]{:S(2)}, u32[]{:S(2)}) %collective-permute-start.2) | collective-permute-done | bytes 172064 | tf_op jit(solution)/shard_map/ppermute | solution.py:236
  22.6 6.0 %collective-permute-start.7 = (bf16[2,336,128]{2,1,0:T(8,128)(2,1)S(1)}, bf16[2,336,128]{2,1,0:T(8,128)(2,1)S(1)}, u32[]{:S(2)}, u32[]{:S(2)}) collective-permute-start(bf16[2,336,128]{2,1,0:T(8,128)(2,1)S(1)} %get-tuple-element.34), channel_id=1, source_target_pairs={{0,6},{1,7},{2,4},{3,5},{4,2},{5,3},{6,0},{7,1},{8,14},{9,15},{10,... | collective-permute-start | bytes 516104 | tf_op jit(solution)/shard_map/ppermute | solution.py:236
  28.7 0.0 collective-permute-done.3.refs_2_
  28.7 6.9 %collective-permute-done.4.refs_3_ = bf16[2,336,128]{2,1,0:T(8,128)(2,1)S(1)} collective-permute-done((bf16[2,336,128]{2,1,0:T(8,128)(2,1)S(1)}, bf16[2,336,128]{2,1,0:T(8,128)(2,1)S(1)}, u32[]{:S(2)}, u32[]{:S(2)}) %collective-permute-start.4) | collective-permute-done | bytes 172064 | tf_op jit(solution)/shard_map/ppermute | solution.py:236
  35.6 0.0 collective-permute-done.5.refs_4_
  35.6 3.3 %collective-permute-done.6.refs_5_ = bf16[2,336,128]{2,1,0:T(8,128)(2,1)S(1)} collective-permute-done((bf16[2,336,128]{2,1,0:T(8,128)(2,1)S(1)}, bf16[2,336,128]{2,1,0:T(8,128)(2,1)S(1)}, u32[]{:S(2)}, u32[]{:S(2)}) %collective-permute-start.6) | collective-permute-done | bytes 172064 | tf_op jit(solution)/shard_map/ppermute | solution.py:236
  38.9 0.0 collective-permute-done.7.refs_6_
  38.9 0.0 copy-done.6
  38.9 0.1 gather.1
  39.0 0.1 collective-permute-start.8
  39.1 2.1 %attend.1.refs_2_ = f32[2,640,256]{2,1,0:T(8,128)S(1)} custom-call(bf16[2,2,512,128]{3,2,1,0:T(8,128)(2,1)S(1)} %get-tuple-element.40.refs_0_, bf16[2,2,896,128]{3,2,1,0:T(8,128)(2,1)S(1)} %get-tuple-element.38.refs_1_, bf16[2,640,128]{2,1,0:T(8,128)(2,1)S(1)} %get-tuple-element.39.refs_2_.refs_1_), custom_call_target="tpu_custom_call" | custom-call | flops 5000000000 | bytes 15000000 | tf_op jit(solution)/shard_map/attend/pallas_call | solution.py:337
  41.2 0.0 copy-start.5
  41.2 0.3 collective-permute-done.8.refs_0_
  41.6 1.4 %complete.1 = (bf16[2,80,128]{2,1,0:T(8,128)(2,1)S(1)}, bf16[2,80,128]{2,1,0:T(8,128)(2,1)S(1)}, bf16[2,80,128]{2,1,0:T(8,128)(2,1)S(1)}, bf16[2,80,128]{2,1,0:T...) custom-call(bf16[2,2,896,128]{3,2,1,0:T(8,128)(2,1)S(1)} %collective, ...), custom_call_target="tpu_custom_call" | custom-call | tf_op jit(solution)/shard_map/complete/pallas_call | solution.py:350
  43.0 5.2 %collective-permute-start.10 = (bf16[2,80,128]{2,1,0:T(8,128)(2,1)S(1)}, bf16[2,80,128]{2,1,0:T(8,128)(2,1)S(1)}, u32[]{:S(2)}, u32[]{:S(2)}) collective-permute-start(bf16[2,80,128]{2,1,0:T(8,128)(2,1)S(1)} %get-tuple-element.42), channel_id=1, source_target_pairs={{0,14},{1,15},{2,12},{3,13},{4,10},{5,11},{6,8},{7,9},{8,6},{9,7},... | collective-permute-start | bytes 122888 | tf_op jit(solution)/shard_map/ppermute | solution.py:236
  48.3 0.8 %collective-permute-start.11 = (bf16[2,80,128]{2,1,0:T(8,128)(2,1)S(1)}, bf16[2,80,128]{2,1,0:T(8,128)(2,1)S(1)}, u32[]{:S(2)}, u32[]{:S(2)}) collective-permute-start(bf16[2,80,128]{2,1,0:T(8,128)(2,1)S(1)} %get-tuple-element.43), channel_id=1, source_target_pairs={{0,12},{1,13},{2,14},{3,15},{4,8},{5,9},{6,10},{7,11},{8,4},{9,5},... | collective-permute-start | bytes 122888 | tf_op jit(solution)/shard_map/ppermute | solution.py:236
  49.0 0.0 collective-permute-start.12
  49.0 2.2 %collective-permute-start.13 = (bf16[2,80,128]{2,1,0:T(8,128)(2,1)S(1)}, bf16[2,80,128]{2,1,0:T(8,128)(2,1)S(1)}, u32[]{:S(2)}, u32[]{:S(2)}) collective-permute-start(bf16[2,80,128]{2,1,0:T(8,128)(2,1)S(1)} %get-tuple-element.45), channel_id=1, source_target_pairs={{0,8},{1,9},{2,10},{3,11},{4,12},{5,13},{6,14},{7,15},{8,0},{9,1},... | collective-permute-start | bytes 122888 | tf_op jit(solution)/shard_map/ppermute | solution.py:236
  51.3 2.2 %collective-permute-start.14 = (bf16[2,80,128]{2,1,0:T(8,128)(2,1)S(1)}, bf16[2,80,128]{2,1,0:T(8,128)(2,1)S(1)}, u32[]{:S(2)}, u32[]{:S(2)}) collective-permute-start(bf16[2,80,128]{2,1,0:T(8,128)(2,1)S(1)} %get-tuple-element.46), channel_id=1, source_target_pairs={{0,2},{1,3},{2,0},{3,1},{4,6},{5,7},{6,4},{7,5},{8,10},{9,11},{10,... | collective-permute-start | bytes 122888 | tf_op jit(solution)/shard_map/ppermute | solution.py:236
  53.4 0.0 collective-permute-done.10.refs_4_
  53.4 0.7 %collective-permute-start.15 = (bf16[2,80,128]{2,1,0:T(8,128)(2,1)S(1)}, bf16[2,80,128]{2,1,0:T(8,128)(2,1)S(1)}, u32[]{:S(2)}, u32[]{:S(2)}) collective-permute-start(bf16[2,80,128]{2,1,0:T(8,128)(2,1)S(1)} %get-tuple-element.47), channel_id=1, source_target_pairs={{0,4},{1,5},{2,6},{3,7},{4,0},{5,1},{6,2},{7,3},{8,12},{9,13},{10,... | collective-permute-start | bytes 122888 | tf_op jit(solution)/shard_map/ppermute | solution.py:236
  54.1 0.4 collective-permute-done.11.refs_5_
  54.5 0.4 collective-permute-start.9
  54.9 0.0 collective-permute-done.12.refs_6_
  54.9 1.2 %collective-permute-done.13.refs_7_ = bf16[2,80,128]{2,1,0:T(8,128)(2,1)S(1)} collective-permute-done((bf16[2,80,128]{2,1,0:T(8,128)(2,1)S(1)}, bf16[2,80,128]{2,1,0:T(8,128)(2,1)S(1)}, u32[]{:S(2)}, u32[]{:S(2)}) %collective-permute-start.13) | collective-permute-done | bytes 40992 | tf_op jit(solution)/shard_map/ppermute | solution.py:236
  56.1 0.0 collective-permute-done.14.refs_8_
  56.1 1.3 %collective-permute-done.15.refs_9_ = bf16[2,80,128]{2,1,0:T(8,128)(2,1)S(1)} collective-permute-done((bf16[2,80,128]{2,1,0:T(8,128)(2,1)S(1)}, bf16[2,80,128]{2,1,0:T(8,128)(2,1)S(1)}, u32[]{:S(2)}, u32[]{:S(2)}) %collective-permute-start.15) | collective-permute-done | bytes 40992 | tf_op jit(solution)/shard_map/ppermute | solution.py:236
  57.4 2.0 %collective-permute-done.9.refs_3_ = bf16[2,80,128]{2,1,0:T(8,128)(2,1)S(1)} collective-permute-done((bf16[2,80,128]{2,1,0:T(8,128)(2,1)S(1)}, bf16[2,80,128]{2,1,0:T(8,128)(2,1)S(1)}, u32[]{:S(2)}, u32[]{:S(2)}) %collective-permute-start.9) | collective-permute-done | bytes 40992 | tf_op jit(solution)/shard_map/ppermute | solution.py:236
  59.4 1.1 %finish.1 = bf16[128,2048]{1,0:T(8,128)(2,1)} custom-call(s32[1]{0:T(128)} %bitcast.refs_0_, s32[1,80]{1,0:T(1,128)S(1)} %pad.4.refs_1_, bf16[128,2048]{1,0:T(8,128)(2,1)S(1)} %copy-done.5, bf16[2,80,128]{2,1,0:T(8,128)(2,1)S(1)} %collective-permute-done.9.refs_3_, bf16[2,80,128]{2,1,0:T(8,128)(2,1)S(1)} %collective-permute-done.10.refs_4_, ...), custom_call_target="tpu_custom_call" | custom-call | tf_op jit(solution)/shard_map/finish/pallas_call | solution.py:366
  (13 shorter events, 0.0 us)
Async XLA Ops:
  0.0 8.6 %copy-start.10 = (s32[76]{0:T(128)S(1)}, s32[76]{0:T(128)}, u32[]{:S(2)}) copy-start(s32[76]{0:T(128)} %param.10) | copy-start | bytes 916
  0.0 8.6 %copy-start.8 = (f32[128]{0:T(128)S(1)}, f32[128]{0:T(128)}, u32[]{:S(2)}) copy-start(f32[128]{0:T(128)} %param.16) | copy-start | bytes 1540
  0.0 8.6 %copy-start.9 = (f32[128]{0:T(128)S(1)}, f32[128]{0:T(128)}, u32[]{:S(2)}) copy-start(f32[128]{0:T(128)} %param.17) | copy-start | bytes 1540
  0.0 8.6 %copy-start = (bf16[76,3,2048]{2,0,1:T(8,128)(2,1)S(1)}, bf16[76,3,2048]{2,0,1:T(8,128)(2,1)}, u32[]{:S(2)}) copy-start(bf16[76,3,2048]{2,0,1:T(8,128)(2,1)} %param.9) | copy-start | bytes 2801668
  0.0 8.6 %copy-start.1 = (bf16[128,2048]{1,0:T(8,128)(2,1)S(1)}, bf16[128,2048]{1,0:T(8,128)(2,1)}, u32[]{:S(2)}) copy-start(bf16[128,2048]{1,0:T(8,128)(2,1)} %refs_5_.3) | copy-start | bytes 1572868
  0.0 8.6 %copy-start.2 = (bf16[128,2048]{1,0:T(8,128)(2,1)S(1)}, bf16[128,2048]{1,0:T(8,128)(2,1)}, u32[]{:S(2)}) copy-start(bf16[128,2048]{1,0:T(8,128)(2,1)} %refs_6_.3) | copy-start | bytes 1572868
  2.4 6.2 %collective-permute-start.1 = (bf16[2,256,128]{2,1,0:T(8,128)(2,1)}, bf16[2,256,128]{2,1,0:T(8,128)(2,1)S(1)}, u32[]{:S(2)}, u32[]{:S(2)}) collective-permute-start(bf16[2,256,128]{2,1,0:T(8,128)(2,1)} %get-tuple-element.28.refs_7_), channel_id=1, source_target_pairs={{0,1},{1,0},{2,3},{3,2},{4,5},{5,4},{6,7},{7,6},{8,9},{9,8},{10,11... | collective-permute-start | bytes 393224 | tf_op jit(solution)/shard_map/ppermute | solution.py:236
  3.0 16.4 %collective-permute-start = (bf16[2,336,128]{2,1,0:T(8,128)(2,1)}, bf16[2,336,128]{2,1,0:T(8,128)(2,1)S(1)}, u32[]{:S(2)}, u32[]{:S(2)}) collective-permute-start(bf16[2,336,128]{2,1,0:T(8,128)(2,1)} %get-tuple-element.27), channel_id=1, source_target_pairs={{0,14},{1,15},{2,12},{3,13},{4,10},{5,11},{6,8},{7,9},{8,6},{9,7},... | collective-permute-start | bytes 516104 | tf_op jit(solution)/shard_map/ppermute | solution.py:236
  8.7 1.2 %copy-start.3 = (bf16[256,2048]{1,0:T(8,128)(2,1)S(1)}, bf16[256,2048]{1,0:T(8,128)(2,1)}, u32[]{:S(2)}) copy-start(bf16[256,2048]{1,0:T(8,128)(2,1)} %refs_7_.1) | copy-start | bytes 3145732
  9.9 1.2 %copy-start.4 = (bf16[256,2048]{1,0:T(8,128)(2,1)S(1)}, bf16[256,2048]{1,0:T(8,128)(2,1)}, u32[]{:S(2)}) copy-start(bf16[256,2048]{1,0:T(8,128)(2,1)} %refs_8_.1) | copy-start | bytes 3145732
  11.1 27.8 %copy-start.6 = (bf16[2,256,128]{2,1,0:T(8,128)(2,1)S(1)}, bf16[2,256,128]{2,1,0:T(8,128)(2,1)}, u32[]{:S(2)}) copy-start(bf16[2,256,128]{2,1,0:T(8,128)(2,1)} %get-tuple-element.28.refs_7_) | copy-start | bytes 393220
  11.1 27.8 %copy-start.7 = (bf16[2,80,128]{2,1,0:T(8,128)(2,1)S(1)}, bf16[2,80,128]{2,1,0:T(8,128)(2,1)}, u32[]{:S(2)}) copy-start(bf16[2,80,128]{2,1,0:T(8,128)(2,1)} %get-tuple-element.37.refs_11_) | copy-start | bytes 122884
  13.5 9.2 %collective-permute-start.2 = (bf16[2,336,128]{2,1,0:T(8,128)(2,1)S(1)}, bf16[2,336,128]{2,1,0:T(8,128)(2,1)S(1)}, u32[]{:S(2)}, u32[]{:S(2)}) collective-permute-start(bf16[2,336,128]{2,1,0:T(8,128)(2,1)S(1)} %get-tuple-element.29), channel_id=1, source_target_pairs={{0,12},{1,13},{2,14},{3,15},{4,8},{5,9},{6,10},{7,11},{8,4},{9,5},... | collective-permute-start | bytes 516104 | tf_op jit(solution)/shard_map/ppermute | solution.py:236
  14.0 14.6 %collective-permute-start.3 = (bf16[2,336,128]{2,1,0:T(8,128)(2,1)S(1)}, bf16[2,336,128]{2,1,0:T(8,128)(2,1)S(1)}, u32[]{:S(2)}, u32[]{:S(2)}) collective-permute-start(bf16[2,336,128]{2,1,0:T(8,128)(2,1)S(1)} %get-tuple-element.30), channel_id=1, source_target_pairs={{0,2},{1,3},{2,0},{3,1},{4,6},{5,7},{6,4},{7,5},{8,10},{9,11},{10,... | collective-permute-start | bytes 516104 | tf_op jit(solution)/shard_map/ppermute | solution.py:236
  15.6 20.0 %collective-permute-start.4 = (bf16[2,336,128]{2,1,0:T(8,128)(2,1)S(1)}, bf16[2,336,128]{2,1,0:T(8,128)(2,1)S(1)}, u32[]{:S(2)}, u32[]{:S(2)}) collective-permute-start(bf16[2,336,128]{2,1,0:T(8,128)(2,1)S(1)} %get-tuple-element.31), channel_id=1, source_target_pairs={{0,10},{1,11},{2,8},{3,9},{4,14},{5,15},{6,12},{7,13},{8,2},{9,3},... | collective-permute-start | bytes 516104 | tf_op jit(solution)/shard_map/ppermute | solution.py:236
  16.0 19.6 %collective-permute-start.5 = (bf16[2,336,128]{2,1,0:T(8,128)(2,1)S(1)}, bf16[2,336,128]{2,1,0:T(8,128)(2,1)S(1)}, u32[]{:S(2)}, u32[]{:S(2)}) collective-permute-start(bf16[2,336,128]{2,1,0:T(8,128)(2,1)S(1)} %get-tuple-element.32), channel_id=1, source_target_pairs={{0,4},{1,5},{2,6},{3,7},{4,0},{5,1},{6,2},{7,3},{8,12},{9,13},{10,... | collective-permute-start | bytes 516104 | tf_op jit(solution)/shard_map/ppermute | solution.py:236
  19.4 19.5 %collective-permute-start.6 = (bf16[2,336,128]{2,1,0:T(8,128)(2,1)S(1)}, bf16[2,336,128]{2,1,0:T(8,128)(2,1)S(1)}, u32[]{:S(2)}, u32[]{:S(2)}) collective-permute-start(bf16[2,336,128]{2,1,0:T(8,128)(2,1)S(1)} %get-tuple-element.33), channel_id=1, source_target_pairs={{0,8},{1,9},{2,10},{3,11},{4,12},{5,13},{6,14},{7,15},{8,0},{9,1},... | collective-permute-start | bytes 516104 | tf_op jit(solution)/shard_map/ppermute | solution.py:236
  22.6 16.2 %collective-permute-start.7 = (bf16[2,336,128]{2,1,0:T(8,128)(2,1)S(1)}, bf16[2,336,128]{2,1,0:T(8,128)(2,1)S(1)}, u32[]{:S(2)}, u32[]{:S(2)}) collective-permute-start(bf16[2,336,128]{2,1,0:T(8,128)(2,1)S(1)} %get-tuple-element.34), channel_id=1, source_target_pairs={{0,6},{1,7},{2,4},{3,5},{4,2},{5,3},{6,0},{7,1},{8,14},{9,15},{10,... | collective-permute-start | bytes 516104 | tf_op jit(solution)/shard_map/ppermute | solution.py:236
  39.0 2.5 %collective-permute-start.8 = (bf16[2,2,896,128]{3,2,1,0:T(8,128)(2,1)S(1)}, bf16[2,2,896,128]{3,2,1,0:T(8,128)(2,1)S(1)}, u32[]{:S(2)}, u32[]{:S(2)}) collective-permute-start(bf16[2,2,896,128]{3,2,1,0:T(8,128)(2,1)S(1)} %get-tuple-element.38.refs_1_), channel_id=1, source_target_pairs={{0,1},{1,0},{2,3},{3,2},{4,5},{5,4},{6,7},{7,6},{8,9},{9,8},{10,11... | collective-permute-start | bytes 2752520 | tf_op jit(solution)/shard_map/ppermute | solution.py:236
  41.2 18.2 %copy-start.5 = (bf16[128,2048]{1,0:T(8,128)(2,1)S(1)}, bf16[128,2048]{1,0:T(8,128)(2,1)}, u32[]{:S(2)}) copy-start(bf16[128,2048]{1,0:T(8,128)(2,1)} %refs_2_.1) | copy-start | bytes 1572868
  43.0 10.4 %collective-permute-start.10 = (bf16[2,80,128]{2,1,0:T(8,128)(2,1)S(1)}, bf16[2,80,128]{2,1,0:T(8,128)(2,1)S(1)}, u32[]{:S(2)}, u32[]{:S(2)}) collective-permute-start(bf16[2,80,128]{2,1,0:T(8,128)(2,1)S(1)} %get-tuple-element.42), channel_id=1, source_target_pairs={{0,14},{1,15},{2,12},{3,13},{4,10},{5,11},{6,8},{7,9},{8,6},{9,7},... | collective-permute-start | bytes 122888 | tf_op jit(solution)/shard_map/ppermute | solution.py:236
  48.3 6.2 %collective-permute-start.11 = (bf16[2,80,128]{2,1,0:T(8,128)(2,1)S(1)}, bf16[2,80,128]{2,1,0:T(8,128)(2,1)S(1)}, u32[]{:S(2)}, u32[]{:S(2)}) collective-permute-start(bf16[2,80,128]{2,1,0:T(8,128)(2,1)S(1)} %get-tuple-element.43), channel_id=1, source_target_pairs={{0,12},{1,13},{2,14},{3,15},{4,8},{5,9},{6,10},{7,11},{8,4},{9,5},... | collective-permute-start | bytes 122888 | tf_op jit(solution)/shard_map/ppermute | solution.py:236
  49.0 5.9 %collective-permute-start.12 = (bf16[2,80,128]{2,1,0:T(8,128)(2,1)S(1)}, bf16[2,80,128]{2,1,0:T(8,128)(2,1)S(1)}, u32[]{:S(2)}, u32[]{:S(2)}) collective-permute-start(bf16[2,80,128]{2,1,0:T(8,128)(2,1)S(1)} %get-tuple-element.44), channel_id=1, source_target_pairs={{0,10},{1,11},{2,8},{3,9},{4,14},{5,15},{6,12},{7,13},{8,2},{9,3},... | collective-permute-start | bytes 122888 | tf_op jit(solution)/shard_map/ppermute | solution.py:236
  49.0 7.1 %collective-permute-start.13 = (bf16[2,80,128]{2,1,0:T(8,128)(2,1)S(1)}, bf16[2,80,128]{2,1,0:T(8,128)(2,1)S(1)}, u32[]{:S(2)}, u32[]{:S(2)}) collective-permute-start(bf16[2,80,128]{2,1,0:T(8,128)(2,1)S(1)} %get-tuple-element.45), channel_id=1, source_target_pairs={{0,8},{1,9},{2,10},{3,11},{4,12},{5,13},{6,14},{7,15},{8,0},{9,1},... | collective-permute-start | bytes 122888 | tf_op jit(solution)/shard_map/ppermute | solution.py:236
  51.3 4.8 %collective-permute-start.14 = (bf16[2,80,128]{2,1,0:T(8,128)(2,1)S(1)}, bf16[2,80,128]{2,1,0:T(8,128)(2,1)S(1)}, u32[]{:S(2)}, u32[]{:S(2)}) collective-permute-start(bf16[2,80,128]{2,1,0:T(8,128)(2,1)S(1)} %get-tuple-element.46), channel_id=1, source_target_pairs={{0,2},{1,3},{2,0},{3,1},{4,6},{5,7},{6,4},{7,5},{8,10},{9,11},{10,... | collective-permute-start | bytes 122888 | tf_op jit(solution)/shard_map/ppermute | solution.py:236
  53.4 4.0 %collective-permute-start.15 = (bf16[2,80,128]{2,1,0:T(8,128)(2,1)S(1)}, bf16[2,80,128]{2,1,0:T(8,128)(2,1)S(1)}, u32[]{:S(2)}, u32[]{:S(2)}) collective-permute-start(bf16[2,80,128]{2,1,0:T(8,128)(2,1)S(1)} %get-tuple-element.47), channel_id=1, source_target_pairs={{0,4},{1,5},{2,6},{3,7},{4,0},{5,1},{6,2},{7,3},{8,12},{9,13},{10,... | collective-permute-start | bytes 122888 | tf_op jit(solution)/shard_map/ppermute | solution.py:236
  54.5 4.9 %collective-permute-start.9 = (bf16[2,80,128]{2,1,0:T(8,128)(2,1)S(1)}, bf16[2,80,128]{2,1,0:T(8,128)(2,1)S(1)}, u32[]{:S(2)}, u32[]{:S(2)}) collective-permute-start(bf16[2,80,128]{2,1,0:T(8,128)(2,1)S(1)} %get-tuple-element.41), channel_id=1, source_target_pairs={{0,6},{1,7},{2,4},{3,5},{4,2},{5,3},{6,0},{7,1},{8,14},{9,15},{10,... | collective-permute-start | bytes 122888 | tf_op jit(solution)/shard_map/ppermute | solution.py:236

commit v16 on v11

--- a/solution.py
+++ b/solution.py
@@ -8,7 +8,7 @@
 from jax.sharding import PartitionSpec as P
 
 LOG2E = math.log2(math.e)
-FIRST_HEADS = [15, 14, 1]
+FIRST_HEADS = [15, 14, 13, 1]
 
 
 def round_up(count, step):
@@ -183,7 +183,7 @@
     near = list(reversed(range(1, half)))
     order = far[:3]
     for turn in range(max(len(far) - 3, len(near))):
-        order += far[turn + 3 : turn + 4] + near[turn : turn + 1]
+        order += near[turn : turn + 1] + far[turn + 3 : turn + 4]
     names = sorted(range(count - 1), key=lambda number: str(number) if number else "")
     return [0] + [order[names.index(number)] for number in range(count - 1)]
 

time: 59.4 us -> 58.8 us (0.990)
  starting transfers between devices: 33.3 us -> 31.8 us
  waiting for transfers between devices: 17.5 us -> 18.2 us
    all_to_all x1, starting transfers between devices: 4.75 us -> 3.67 us  [shards(): lax.all_to_all(result, 'seq', split_axis=0, concat_axis=0, tiled=True)]
    ppermute x15, waiting for transfers between devices: 6.4 us -> 7.18 us  [trade(): return lax.ppermute(block, 'seq', [(a, a ^ step) for a in range(count)])]
  transfers between devices with their start and end apart: 16 -> 16, of which waited for: 6 -> 3; matrix products, arithmetic and copies ran while one was open for 0% -> 0% of each run, Pallas kernels for 2% -> 1%
where the time goes in v16:
time: 58.8 us; the launch traced here: 58.6 us
  starting transfers between devices  31.8 us (54%)
  waiting for transfers between devices  18.2 us (31%)
  Pallas kernels  7.13 us (12%)
  local copies, waits for them, and re-layouts  1.26 us (2%)
    ppermute x15, starting transfers between devices, trade(): return lax.ppermute(block, 'seq', [(a, a ^ step) for a in range(count)])  28.1 us
    all_to_all x1, waiting for transfers between devices, shards(): lax.all_to_all(result, 'seq', split_axis=0, concat_axis=0, tiled=True)  11 us
    ppermute x15, waiting for transfers between devices, trade(): return lax.ppermute(block, 'seq', [(a, a ^ step) for a in range(count)])  7.18 us
    all_to_all x1, starting transfers between devices, shards(): lax.all_to_all(result, 'seq', split_axis=0, concat_axis=0, tiled=True)  3.67 us
    pallas_call x1, Pallas kernels, shards(): pl.pallas_call(lambda *refs: attend_kernel(tokens, per_group, query_rows,...  2.95 us
    pallas_call x1, Pallas kernels, shards(): pl.pallas_call(lambda *refs: prepare_kernel(per_group, padded, early, Tru...  2.22 us
    unnamed x18, local copies, waits for them, and re-layouts  1.25 us
  transfers between devices with their start and end apart: 16, of which 3 were waited for; matrix products, arithmetic and copies ran while one was open for 0% of the time, Pallas kernels for 1%

profile of v16, /device:TPU:0, one launch (start us, length us, event | category | flops | bytes accessed | tf_op | source)
XLA Modules:
  0.0 58.6 jit_solution(12943418575188959653)
XLA Ops:
  0.0 0.0 copy-start.1
  0.0 0.0 copy-start.2
  0.0 2.2 %prepare_first.1 = (bf16[336,128]{1,0:T(8,128)(2,1)}, bf16[336,128]{1,0:T(8,128)(2,1)}, bf16[336,128]{1,0:T(8,128)(2,1)}, bf16[336,128]{1,0:T(8,128)(2,1)}) custom-call(s32[1]{0:T(128)} %bitcast.1.refs_0_, s32[1,76]{1,0:T(1,128)} %bitcast.14, f32[1,128]{1,0:T(1,128)} %bitcast.10, f32[1,128]{1,0:T(1,128)} %bitcast.12, bf16[3,76,2048]{2,1,0:T(8,128)(2,1)} %bitcast.5, ...), custom_call_target="tpu_custom_call" | custom-call | tf_op jit(solution)/shard_map/prepare_first/pallas_call | solution.py:238
  2.2 0.5 collective-permute-start
  2.7 5.7 %collective-permute-start.1 = (bf16[336,128]{1,0:T(8,128)(2,1)}, bf16[336,128]{1,0:T(8,128)(2,1)S(1)}, u32[]{:S(2)}, u32[]{:S(2)}) collective-permute-start(bf16[336,128]{1,0:T(8,128)(2,1)} %get-tuple-element.25), channel_id=1, source_target_pairs={{0,15},{1,14},{2,13},{3,12},{4,11},{5,10},{6,9},{7,8},{8,7},{9,6},... | collective-permute-start | bytes 258056 | tf_op jit(solution)/shard_map/ppermute | solution.py:195
  8.4 0.0 collective-permute-start.10
  8.4 3.4 %collective-permute-start.2 = (bf16[336,128]{1,0:T(8,128)(2,1)}, bf16[336,128]{1,0:T(8,128)(2,1)S(1)}, u32[]{:S(2)}, u32[]{:S(2)}) collective-permute-start(bf16[336,128]{1,0:T(8,128)(2,1)} %get-tuple-element.26), channel_id=1, source_target_pairs={{0,14},{1,15},{2,12},{3,13},{4,10},{5,11},{6,8},{7,9},{8,6},{9,7},... | collective-permute-start | bytes 258056 | tf_op jit(solution)/shard_map/ppermute | solution.py:195
  11.8 0.0 collective-permute-done.refs_9_.refs_11_
  11.8 0.0 copy-done
  11.8 0.0 copy-done.1
  11.8 0.0 copy-done.2
  11.8 0.0 copy-done.3
  11.8 0.0 copy-done.6
  11.9 0.0 copy-done.7
  11.9 0.0 copy-done.8
  11.9 0.0 copy-start.4
  11.9 1.2 %copy-done.4 = bf16[256,2048]{1,0:T(8,128)(2,1)S(1)} copy-done((bf16[256,2048]{1,0:T(8,128)(2,1)S(1)}, bf16[256,2048]{1,0:T(8,128)(2,1)}, u32[]{:S(2)}) %copy-start.4) | copy-done | bytes 1048600
  13.1 0.9 %prepare_rest.1 = (bf16[336,128]{1,0:T(8,128)(2,1)S(1)}, bf16[336,128]{1,0:T(8,128)(2,1)S(1)}, bf16[336,128]{1,0:T(8,128)(2,1)S(1)}, bf16[336,128]{1,0:T(8,128)(...) custom-call(s32[1]{0:T(128)} %bitcast.1.refs_0_, ...), custom_call_target="tpu_custom_call" | custom-call | tf_op jit(solution)/shard_map/prepare_rest/pallas_call | solution.py:255
  14.0 0.1 collective-permute-start.11
  14.1 0.6 collective-permute-start.12
  14.6 0.0 collective-permute-done.1.refs_2_
  14.6 2.1 %collective-permute-start.13 = (bf16[336,128]{1,0:T(8,128)(2,1)S(1)}, bf16[336,128]{1,0:T(8,128)(2,1)S(1)}, u32[]{:S(2)}, u32[]{:S(2)}) collective-permute-start(bf16[336,128]{1,0:T(8,128)(2,1)S(1)} %get-tuple-element.37), channel_id=1, source_target_pairs={{0,6},{1,7},{2,4},{3,5},{4,2},{5,3},{6,0},{7,1},{8,14},{9,15},{10,... | collective-permute-start | bytes 258056 | tf_op jit(solution)/shard_map/ppermute | solution.py:195
  16.8 0.0 collective-permute-done.10.refs_12_
  16.8 3.2 %collective-permute-start.14 = (bf16[336,128]{1,0:T(8,128)(2,1)S(1)}, bf16[336,128]{1,0:T(8,128)(2,1)S(1)}, u32[]{:S(2)}, u32[]{:S(2)}) collective-permute-start(bf16[336,128]{1,0:T(8,128)(2,1)S(1)} %get-tuple-element.38), channel_id=1, source_target_pairs={{0,11},{1,10},{2,9},{3,8},{4,15},{5,14},{6,13},{7,12},{8,3},{9,2},... | collective-permute-start | bytes 258056 | tf_op jit(solution)/shard_map/ppermute | solution.py:195
  19.9 0.0 collective-permute-done.2.refs_3_
  20.0 1.0 %collective-permute-start.3 = (bf16[336,128]{1,0:T(8,128)(2,1)S(1)}, bf16[336,128]{1,0:T(8,128)(2,1)S(1)}, u32[]{:S(2)}, u32[]{:S(2)}) collective-permute-start(bf16[336,128]{1,0:T(8,128)(2,1)S(1)} %get-tuple-element.27), channel_id=1, source_target_pairs={{0,5},{1,4},{2,7},{3,6},{4,1},{5,0},{6,3},{7,2},{8,13},{9,12},{10,... | collective-permute-start | bytes 258056 | tf_op jit(solution)/shard_map/ppermute | solution.py:195
  20.9 0.0 collective-permute-done.11.refs_13_
  20.9 6.9 %collective-permute-start.4 = (bf16[336,128]{1,0:T(8,128)(2,1)S(1)}, bf16[336,128]{1,0:T(8,128)(2,1)S(1)}, u32[]{:S(2)}, u32[]{:S(2)}) collective-permute-start(bf16[336,128]{1,0:T(8,128)(2,1)S(1)} %get-tuple-element.28), channel_id=1, source_target_pairs={{0,10},{1,11},{2,8},{3,9},{4,14},{5,15},{6,12},{7,13},{8,2},{9,3},... | collective-permute-start | bytes 258056 | tf_op jit(solution)/shard_map/ppermute | solution.py:195
  27.8 0.0 collective-permute-done.12.refs_14_
  27.8 0.0 collective-permute-start.5
  27.9 0.0 collective-permute-done.13.refs_15_
  27.9 0.1 collective-permute-start.6
  27.9 0.0 collective-permute-done.14.refs_16_
  27.9 0.4 collective-permute-start.7
  28.4 0.0 collective-permute-done.3.refs_4_
  28.4 3.7 %collective-permute-start.8 = (bf16[336,128]{1,0:T(8,128)(2,1)S(1)}, bf16[336,128]{1,0:T(8,128)(2,1)S(1)}, u32[]{:S(2)}, u32[]{:S(2)}) collective-permute-start(bf16[336,128]{1,0:T(8,128)(2,1)S(1)} %get-tuple-element.32), channel_id=1, source_target_pairs={{0,8},{1,9},{2,10},{3,11},{4,12},{5,13},{6,14},{7,15},{8,0},{9,1},... | collective-permute-start | bytes 258056 | tf_op jit(solution)/shard_map/ppermute | solution.py:195
  32.0 0.0 collective-permute-done.4.refs_5_
  32.0 0.6 collective-permute-start.9
  32.6 1.6 %collective-permute-done.5.refs_6_ = bf16[336,128]{1,0:T(8,128)(2,1)S(1)} collective-permute-done((bf16[336,128]{1,0:T(8,128)(2,1)S(1)}, bf16[336,128]{1,0:T(8,128)(2,1)S(1)}, u32[]{:S(2)}, u32[]{:S(2)}) %collective-permute-start.5) | collective-permute-done | bytes 86048 | tf_op jit(solution)/shard_map/ppermute | solution.py:195
  34.2 0.0 collective-permute-done.6.refs_7_
  34.2 0.0 collective-permute-done.7.refs_8_
  34.2 5.6 %collective-permute-done.8.refs_9_ = bf16[336,128]{1,0:T(8,128)(2,1)S(1)} collective-permute-done((bf16[336,128]{1,0:T(8,128)(2,1)S(1)}, bf16[336,128]{1,0:T(8,128)(2,1)S(1)}, u32[]{:S(2)}, u32[]{:S(2)}) %collective-permute-start.8) | collective-permute-done | bytes 86048 | tf_op jit(solution)/shard_map/ppermute | solution.py:195
  39.8 0.0 collective-permute-done.9.refs_10_
  39.8 3.0 %attend.1 = bf16[16,80,128]{2,1,0:T(8,128)(2,1)} custom-call(s32[1]{0:T(128)} %bitcast.1.refs_0_, bf16[336,128]{1,0:T(8,128)(2,1)S(1)} %get-tuple-element.24.refs_1_, bf16[336,128]{1,0:T(8,128)(2,1)S(1)} %collective-permute-done.1.refs_2_, bf16[336,128]{1,0:T(8,128)(2,1)S(1)} %collective-permute-done.2.refs_3_, ...), custom_call_target="tpu_custom_call" | custom-call | tf_op jit(solution)/shard_map/attend/pallas_call | solution.py:288
  42.7 3.7 %all-to-all-start = ((bf16[16,80,128]{2,1,0:T(8,128)(2,1)}), bf16[16,80,128]{2,1,0:T(8,128)(2,1)S(1)}, u32[]{:S(2)}, u32[]{:S(2)}) async-start(bf16[16,80,128]{2,1,0:T(8,128)(2,1)} %attend.1), calls=%async_computation | async-start | bytes 655360 | tf_op jit(solution)/shard_map/all_to_all | solution.py:310
  46.4 11.0 %all-to-all-done.refs_1_ = bf16[16,80,128]{2,1,0:T(8,128)(2,1)S(1)} async-done(((bf16[16,80,128]{2,1,0:T(8,128)(2,1)}), bf16[16,80,128]{2,1,0:T(8,128)(2,1)S(1)}, u32[]{:S(2)}, u32[]{:S(2)}) %all-to-all-start) | async-done | bytes 327712 | tf_op jit(solution)/shard_map/all_to_all | solution.py:310
  57.5 0.0 copy-done.5
  57.5 1.1 %finish.1 = bf16[128,2048]{1,0:T(8,128)(2,1)} custom-call(s32[1,80]{1,0:T(1,128)S(1)} %pad.4.refs_0_, bf16[16,80,128]{2,1,0:T(8,128)(2,1)S(1)} %all-to-all-done.refs_1_, bf16[128,2048]{1,0:T(8,128)(2,1)S(1)} %copy-done.5), custom_call_target="tpu_custom_call" | custom-call | tf_op jit(solution)/shard_map/finish/pallas_call | solution.py:313
  (7 shorter events, 0.0 us)
Async XLA Ops:
  0.0 11.8 %copy-start = (bf16[76,3,2048]{2,0,1:T(8,128)(2,1)S(1)}, bf16[76,3,2048]{2,0,1:T(8,128)(2,1)}, u32[]{:S(2)}) copy-start(bf16[76,3,2048]{2,0,1:T(8,128)(2,1)} %param.9) | copy-start | bytes 2801668
  0.0 11.8 %copy-start.1 = (bf16[128,2048]{1,0:T(8,128)(2,1)S(1)}, bf16[128,2048]{1,0:T(8,128)(2,1)}, u32[]{:S(2)}) copy-start(bf16[128,2048]{1,0:T(8,128)(2,1)} %refs_5_.3) | copy-start | bytes 1572868
  0.0 11.8 %copy-start.2 = (bf16[128,2048]{1,0:T(8,128)(2,1)S(1)}, bf16[128,2048]{1,0:T(8,128)(2,1)}, u32[]{:S(2)}) copy-start(bf16[128,2048]{1,0:T(8,128)(2,1)} %refs_6_.3) | copy-start | bytes 1572868
  0.0 11.8 %copy-start.3 = (bf16[256,2048]{1,0:T(8,128)(2,1)S(1)}, bf16[256,2048]{1,0:T(8,128)(2,1)}, u32[]{:S(2)}) copy-start(bf16[256,2048]{1,0:T(8,128)(2,1)} %refs_7_.1) | copy-start | bytes 3145732
  2.2 9.6 %collective-permute-start = (bf16[336,128]{1,0:T(8,128)(2,1)}, bf16[336,128]{1,0:T(8,128)(2,1)S(1)}, u32[]{:S(2)}, u32[]{:S(2)}) collective-permute-start(bf16[336,128]{1,0:T(8,128)(2,1)} %get-tuple-element.23), channel_id=1, source_target_pairs={{0,1},{1,0},{2,3},{3,2},{4,5},{5,4},{6,7},{7,6},{8,9},{9,8},{10,11... | collective-permute-start | bytes 258056 | tf_op jit(solution)/shard_map/ppermute | solution.py:195
  2.7 11.9 %collective-permute-start.1 = (bf16[336,128]{1,0:T(8,128)(2,1)}, bf16[336,128]{1,0:T(8,128)(2,1)S(1)}, u32[]{:S(2)}, u32[]{:S(2)}) collective-permute-start(bf16[336,128]{1,0:T(8,128)(2,1)} %get-tuple-element.25), channel_id=1, source_target_pairs={{0,15},{1,14},{2,13},{3,12},{4,11},{5,10},{6,9},{7,8},{8,7},{9,6},... | collective-permute-start | bytes 258056 | tf_op jit(solution)/shard_map/ppermute | solution.py:195
  8.4 3.5 %copy-start.6 = (f32[128]{0:T(128)S(1)}, f32[128]{0:T(128)}, u32[]{:S(2)}) copy-start(f32[128]{0:T(128)} %param.16) | copy-start | bytes 1540
  8.4 3.5 %copy-start.7 = (f32[128]{0:T(128)S(1)}, f32[128]{0:T(128)}, u32[]{:S(2)}) copy-start(f32[128]{0:T(128)} %param.17) | copy-start | bytes 1540
  8.4 3.5 %copy-start.8 = (s32[76]{0:T(128)S(1)}, s32[76]{0:T(128)}, u32[]{:S(2)}) copy-start(s32[76]{0:T(128)} %param.10) | copy-start | bytes 916
  8.4 8.4 %collective-permute-start.10 = (bf16[336,128]{1,0:T(8,128)(2,1)}, bf16[336,128]{1,0:T(8,128)(2,1)S(1)}, u32[]{:S(2)}, u32[]{:S(2)}) collective-permute-start(bf16[336,128]{1,0:T(8,128)(2,1)} %get-tuple-element.34), channel_id=1, source_target_pairs={{0,13},{1,12},{2,15},{3,14},{4,9},{5,8},{6,11},{7,10},{8,5},{9,4},... | collective-permute-start | bytes 258056 | tf_op jit(solution)/shard_map/ppermute | solution.py:195
  8.4 11.6 %collective-permute-start.2 = (bf16[336,128]{1,0:T(8,128)(2,1)}, bf16[336,128]{1,0:T(8,128)(2,1)S(1)}, u32[]{:S(2)}, u32[]{:S(2)}) collective-permute-start(bf16[336,128]{1,0:T(8,128)(2,1)} %get-tuple-element.26), channel_id=1, source_target_pairs={{0,14},{1,15},{2,12},{3,13},{4,10},{5,11},{6,8},{7,9},{8,6},{9,7},... | collective-permute-start | bytes 258056 | tf_op jit(solution)/shard_map/ppermute | solution.py:195
  11.9 1.2 %copy-start.4 = (bf16[256,2048]{1,0:T(8,128)(2,1)S(1)}, bf16[256,2048]{1,0:T(8,128)(2,1)}, u32[]{:S(2)}) copy-start(bf16[256,2048]{1,0:T(8,128)(2,1)} %refs_8_.3) | copy-start | bytes 3145732
  14.0 6.9 %collective-permute-start.11 = (bf16[336,128]{1,0:T(8,128)(2,1)S(1)}, bf16[336,128]{1,0:T(8,128)(2,1)S(1)}, u32[]{:S(2)}, u32[]{:S(2)}) collective-permute-start(bf16[336,128]{1,0:T(8,128)(2,1)S(1)} %get-tuple-element.35), channel_id=1, source_target_pairs={{0,7},{1,6},{2,5},{3,4},{4,3},{5,2},{6,1},{7,0},{8,15},{9,14},{10,... | collective-permute-start | bytes 258056 | tf_op jit(solution)/shard_map/ppermute | solution.py:195
  14.1 13.8 %collective-permute-start.12 = (bf16[336,128]{1,0:T(8,128)(2,1)S(1)}, bf16[336,128]{1,0:T(8,128)(2,1)S(1)}, u32[]{:S(2)}, u32[]{:S(2)}) collective-permute-start(bf16[336,128]{1,0:T(8,128)(2,1)S(1)} %get-tuple-element.36), channel_id=1, source_target_pairs={{0,12},{1,13},{2,14},{3,15},{4,8},{5,9},{6,10},{7,11},{8,4},{9,5},... | collective-permute-start | bytes 258056 | tf_op jit(solution)/shard_map/ppermute | solution.py:195
  14.6 13.2 %collective-permute-start.13 = (bf16[336,128]{1,0:T(8,128)(2,1)S(1)}, bf16[336,128]{1,0:T(8,128)(2,1)S(1)}, u32[]{:S(2)}, u32[]{:S(2)}) collective-permute-start(bf16[336,128]{1,0:T(8,128)(2,1)S(1)} %get-tuple-element.37), channel_id=1, source_target_pairs={{0,6},{1,7},{2,4},{3,5},{4,2},{5,3},{6,0},{7,1},{8,14},{9,15},{10,... | collective-permute-start | bytes 258056 | tf_op jit(solution)/shard_map/ppermute | solution.py:195
  16.8 11.2 %collective-permute-start.14 = (bf16[336,128]{1,0:T(8,128)(2,1)S(1)}, bf16[336,128]{1,0:T(8,128)(2,1)S(1)}, u32[]{:S(2)}, u32[]{:S(2)}) collective-permute-start(bf16[336,128]{1,0:T(8,128)(2,1)S(1)} %get-tuple-element.38), channel_id=1, source_target_pairs={{0,11},{1,10},{2,9},{3,8},{4,15},{5,14},{6,13},{7,12},{8,3},{9,2},... | collective-permute-start | bytes 258056 | tf_op jit(solution)/shard_map/ppermute | solution.py:195
  20.0 8.4 %collective-permute-start.3 = (bf16[336,128]{1,0:T(8,128)(2,1)S(1)}, bf16[336,128]{1,0:T(8,128)(2,1)S(1)}, u32[]{:S(2)}, u32[]{:S(2)}) collective-permute-start(bf16[336,128]{1,0:T(8,128)(2,1)S(1)} %get-tuple-element.27), channel_id=1, source_target_pairs={{0,5},{1,4},{2,7},{3,6},{4,1},{5,0},{6,3},{7,2},{8,13},{9,12},{10,... | collective-permute-start | bytes 258056 | tf_op jit(solution)/shard_map/ppermute | solution.py:195
  20.9 11.1 %collective-permute-start.4 = (bf16[336,128]{1,0:T(8,128)(2,1)S(1)}, bf16[336,128]{1,0:T(8,128)(2,1)S(1)}, u32[]{:S(2)}, u32[]{:S(2)}) collective-permute-start(bf16[336,128]{1,0:T(8,128)(2,1)S(1)} %get-tuple-element.28), channel_id=1, source_target_pairs={{0,10},{1,11},{2,8},{3,9},{4,14},{5,15},{6,12},{7,13},{8,2},{9,3},... | collective-permute-start | bytes 258056 | tf_op jit(solution)/shard_map/ppermute | solution.py:195
  27.8 6.3 %collective-permute-start.5 = (bf16[336,128]{1,0:T(8,128)(2,1)S(1)}, bf16[336,128]{1,0:T(8,128)(2,1)S(1)}, u32[]{:S(2)}, u32[]{:S(2)}) collective-permute-start(bf16[336,128]{1,0:T(8,128)(2,1)S(1)} %get-tuple-element.29), channel_id=1, source_target_pairs={{0,4},{1,5},{2,6},{3,7},{4,0},{5,1},{6,2},{7,3},{8,12},{9,13},{10,... | collective-permute-start | bytes 258056 | tf_op jit(solution)/shard_map/ppermute | solution.py:195
  27.9 6.3 %collective-permute-start.6 = (bf16[336,128]{1,0:T(8,128)(2,1)S(1)}, bf16[336,128]{1,0:T(8,128)(2,1)S(1)}, u32[]{:S(2)}, u32[]{:S(2)}) collective-permute-start(bf16[336,128]{1,0:T(8,128)(2,1)S(1)} %get-tuple-element.30), channel_id=1, source_target_pairs={{0,9},{1,8},{2,11},{3,10},{4,13},{5,12},{6,15},{7,14},{8,1},{9,0},... | collective-permute-start | bytes 258056 | tf_op jit(solution)/shard_map/ppermute | solution.py:195
  27.9 6.2 %collective-permute-start.7 = (bf16[336,128]{1,0:T(8,128)(2,1)S(1)}, bf16[336,128]{1,0:T(8,128)(2,1)S(1)}, u32[]{:S(2)}, u32[]{:S(2)}) collective-permute-start(bf16[336,128]{1,0:T(8,128)(2,1)S(1)} %get-tuple-element.31), channel_id=1, source_target_pairs={{0,3},{1,2},{2,1},{3,0},{4,7},{5,6},{6,5},{7,4},{8,11},{9,10},{10,... | collective-permute-start | bytes 258056 | tf_op jit(solution)/shard_map/ppermute | solution.py:195
  28.4 11.4 %collective-permute-start.8 = (bf16[336,128]{1,0:T(8,128)(2,1)S(1)}, bf16[336,128]{1,0:T(8,128)(2,1)S(1)}, u32[]{:S(2)}, u32[]{:S(2)}) collective-permute-start(bf16[336,128]{1,0:T(8,128)(2,1)S(1)} %get-tuple-element.32), channel_id=1, source_target_pairs={{0,8},{1,9},{2,10},{3,11},{4,12},{5,13},{6,14},{7,15},{8,0},{9,1},... | collective-permute-start | bytes 258056 | tf_op jit(solution)/shard_map/ppermute | solution.py:195
  32.0 7.7 %collective-permute-start.9 = (bf16[336,128]{1,0:T(8,128)(2,1)S(1)}, bf16[336,128]{1,0:T(8,128)(2,1)S(1)}, u32[]{:S(2)}, u32[]{:S(2)}) collective-permute-start(bf16[336,128]{1,0:T(8,128)(2,1)S(1)} %get-tuple-element.33), channel_id=1, source_target_pairs={{0,2},{1,3},{2,0},{3,1},{4,6},{5,7},{6,4},{7,5},{8,10},{9,11},{10,... | collective-permute-start | bytes 258056 | tf_op jit(solution)/shard_map/ppermute | solution.py:195
  42.7 14.7 %copy-start.5 = (bf16[128,2048]{1,0:T(8,128)(2,1)S(1)}, bf16[128,2048]{1,0:T(8,128)(2,1)}, u32[]{:S(2)}) copy-start(bf16[128,2048]{1,0:T(8,128)(2,1)} %refs_2_.1) | copy-start | bytes 1572868
  42.7 14.7 %all-to-all-start = ((bf16[16,80,128]{2,1,0:T(8,128)(2,1)}), bf16[16,80,128]{2,1,0:T(8,128)(2,1)S(1)}, u32[]{:S(2)}, u32[]{:S(2)}) async-start(bf16[16,80,128]{2,1,0:T(8,128)(2,1)} %attend.1), calls=%async_computation | async-start | bytes 655360 | tf_op jit(solution)/shard_map/all_to_all | solution.py:310

commit v17 on v16

--- a/solution.py
+++ b/solution.py
@@ -181,9 +181,7 @@
     half = count // 2
     far = list(reversed(range(half, count)))
     near = list(reversed(range(1, half)))
-    order = far[:3]
-    for turn in range(max(len(far) - 3, len(near))):
-        order += near[turn : turn + 1] + far[turn + 3 : turn + 4]
+    order = far[:3] + near[:1] + far[3:4] + near[1:2] + far[4:6] + near[2:3] + far[6:] + near[3:]
     names = sorted(range(count - 1), key=lambda number: str(number) if number else "")
     return [0] + [order[names.index(number)] for number in range(count - 1)]
 

time: 58.8 us -> 61.7 us (1.049)
  starting transfers between devices: 31.8 us -> 33.5 us
  waiting for transfers between devices: 18.2 us -> 19.4 us
    all_to_all x1, starting transfers between devices: 3.67 us -> 5.47 us  [shards(): lax.all_to_all(result, 'seq', split_axis=0, concat_axis=0, tiled=True)]
    ppermute x15, waiting for transfers between devices: 7.18 us -> 8.3 us  [trade(): return lax.ppermute(block, 'seq', [(a, a ^ step) for a in range(count)])]
  transfers between devices with their start and end apart: 16 -> 16, of which waited for: 3 -> 6; matrix products, arithmetic and copies ran while one was open for 0% -> 0% of each run, Pallas kernels for 1% -> 1%
where the time goes in v17:
time: 61.7 us; the launch traced here: 61.4 us
  starting transfers between devices  33.5 us (54%)
  waiting for transfers between devices  19.4 us (31%)
  Pallas kernels  7.13 us (12%)
  local copies, waits for them, and re-layouts  1.26 us (2%)
    ppermute x15, starting transfers between devices, trade(): return lax.ppermute(block, 'seq', [(a, a ^ step) for a in range(count)])  28.1 us
    all_to_all x1, waiting for transfers between devices, shards(): lax.all_to_all(result, 'seq', split_axis=0, concat_axis=0, tiled=True)  11.1 us
    ppermute x15, waiting for transfers between devices, trade(): return lax.ppermute(block, 'seq', [(a, a ^ step) for a in range(count)])  8.3 us
    all_to_all x1, starting transfers between devices, shards(): lax.all_to_all(result, 'seq', split_axis=0, concat_axis=0, tiled=True)  5.47 us
    pallas_call x1, Pallas kernels, shards(): pl.pallas_call(lambda *refs: attend_kernel(tokens, per_group, query_rows,...  2.95 us
    pallas_call x1, Pallas kernels, shards(): pl.pallas_call(lambda *refs: prepare_kernel(per_group, padded, early, Tru...  2.22 us
    unnamed x18, local copies, waits for them, and re-layouts  1.25 us
  transfers between devices with their start and end apart: 16, of which 6 were waited for; matrix products, arithmetic and copies ran while one was open for 0% of the time, Pallas kernels for 1%

profile of v17, /device:TPU:0, one launch (start us, length us, event | category | flops | bytes accessed | tf_op | source)
XLA Modules:
  0.0 61.4 jit_solution(104810974563032223)
XLA Ops:
  0.0 0.0 copy-start
  0.0 0.0 copy-start.1
  0.0 2.2 %prepare_first.1 = (bf16[336,128]{1,0:T(8,128)(2,1)}, bf16[336,128]{1,0:T(8,128)(2,1)}, bf16[336,128]{1,0:T(8,128)(2,1)}, bf16[336,128]{1,0:T(8,128)(2,1)}) custom-call(s32[1]{0:T(128)} %bitcast.1.refs_0_, s32[1,76]{1,0:T(1,128)} %bitcast.14, f32[1,128]{1,0:T(1,128)} %bitcast.10, f32[1,128]{1,0:T(1,128)} %bitcast.12, bf16[3,76,2048]{2,1,0:T(8,128)(2,1)} %bitcast.5, ...), custom_call_target="tpu_custom_call" | custom-call | tf_op jit(solution)/shard_map/prepare_first/pallas_call | solution.py:236
  2.2 0.5 collective-permute-start
  2.7 5.7 %collective-permute-start.1 = (bf16[336,128]{1,0:T(8,128)(2,1)}, bf16[336,128]{1,0:T(8,128)(2,1)S(1)}, u32[]{:S(2)}, u32[]{:S(2)}) collective-permute-start(bf16[336,128]{1,0:T(8,128)(2,1)} %get-tuple-element.25), channel_id=1, source_target_pairs={{0,15},{1,14},{2,13},{3,12},{4,11},{5,10},{6,9},{7,8},{8,7},{9,6},... | collective-permute-start | bytes 258056 | tf_op jit(solution)/shard_map/ppermute | solution.py:193
  8.4 0.0 collective-permute-start.10
  8.4 3.4 %collective-permute-start.2 = (bf16[336,128]{1,0:T(8,128)(2,1)}, bf16[336,128]{1,0:T(8,128)(2,1)S(1)}, u32[]{:S(2)}, u32[]{:S(2)}) collective-permute-start(bf16[336,128]{1,0:T(8,128)(2,1)} %get-tuple-element.26), channel_id=1, source_target_pairs={{0,14},{1,15},{2,12},{3,13},{4,10},{5,11},{6,8},{7,9},{8,6},{9,7},... | collective-permute-start | bytes 258056 | tf_op jit(solution)/shard_map/ppermute | solution.py:193
  11.8 0.0 collective-permute-done.refs_9_.refs_11_
  11.8 0.0 copy-done
  11.8 0.0 copy-done.1
  11.8 0.0 copy-done.2
  11.8 0.0 copy-done.3
  11.8 0.0 copy-done.6
  11.9 0.0 copy-done.7
  11.9 0.0 copy-done.8
  11.9 0.0 copy-start.4
  11.9 1.2 %copy-done.4 = bf16[256,2048]{1,0:T(8,128)(2,1)S(1)} copy-done((bf16[256,2048]{1,0:T(8,128)(2,1)S(1)}, bf16[256,2048]{1,0:T(8,128)(2,1)}, u32[]{:S(2)}) %copy-start.4) | copy-done | bytes 1048600
  13.1 0.9 %prepare_rest.1 = (bf16[336,128]{1,0:T(8,128)(2,1)S(1)}, bf16[336,128]{1,0:T(8,128)(2,1)S(1)}, bf16[336,128]{1,0:T(8,128)(2,1)S(1)}, bf16[336,128]{1,0:T(8,128)(...) custom-call(s32[1]{0:T(128)} %bitcast.1.refs_0_, ...), custom_call_target="tpu_custom_call" | custom-call | tf_op jit(solution)/shard_map/prepare_rest/pallas_call | solution.py:253
  14.0 0.1 collective-permute-start.11
  14.1 0.6 collective-permute-start.12
  14.6 0.0 collective-permute-done.1.refs_2_
  14.6 2.1 %collective-permute-start.13 = (bf16[336,128]{1,0:T(8,128)(2,1)S(1)}, bf16[336,128]{1,0:T(8,128)(2,1)S(1)}, u32[]{:S(2)}, u32[]{:S(2)}) collective-permute-start(bf16[336,128]{1,0:T(8,128)(2,1)S(1)} %get-tuple-element.37), channel_id=1, source_target_pairs={{0,6},{1,7},{2,4},{3,5},{4,2},{5,3},{6,0},{7,1},{8,14},{9,15},{10,... | collective-permute-start | bytes 258056 | tf_op jit(solution)/shard_map/ppermute | solution.py:193
  16.8 0.0 collective-permute-done.10.refs_12_
  16.8 3.2 %collective-permute-start.14 = (bf16[336,128]{1,0:T(8,128)(2,1)S(1)}, bf16[336,128]{1,0:T(8,128)(2,1)S(1)}, u32[]{:S(2)}, u32[]{:S(2)}) collective-permute-start(bf16[336,128]{1,0:T(8,128)(2,1)S(1)} %get-tuple-element.38), channel_id=1, source_target_pairs={{0,11},{1,10},{2,9},{3,8},{4,15},{5,14},{6,13},{7,12},{8,3},{9,2},... | collective-permute-start | bytes 258056 | tf_op jit(solution)/shard_map/ppermute | solution.py:193
  19.9 0.0 collective-permute-done.2.refs_3_
  20.0 7.9 %collective-permute-start.3 = (bf16[336,128]{1,0:T(8,128)(2,1)S(1)}, bf16[336,128]{1,0:T(8,128)(2,1)S(1)}, u32[]{:S(2)}, u32[]{:S(2)}) collective-permute-start(bf16[336,128]{1,0:T(8,128)(2,1)S(1)} %get-tuple-element.27), channel_id=1, source_target_pairs={{0,10},{1,11},{2,8},{3,9},{4,14},{5,15},{6,12},{7,13},{8,2},{9,3},... | collective-permute-start | bytes 258056 | tf_op jit(solution)/shard_map/ppermute | solution.py:193
  27.8 0.0 collective-permute-done.11.refs_13_
  27.8 0.0 collective-permute-start.4
  27.8 0.0 collective-permute-done.12.refs_14_
  27.9 0.1 collective-permute-start.5
  27.9 0.0 collective-permute-done.13.refs_15_
  27.9 1.8 %collective-permute-start.6 = (bf16[336,128]{1,0:T(8,128)(2,1)S(1)}, bf16[336,128]{1,0:T(8,128)(2,1)S(1)}, u32[]{:S(2)}, u32[]{:S(2)}) collective-permute-start(bf16[336,128]{1,0:T(8,128)(2,1)S(1)} %get-tuple-element.30), channel_id=1, source_target_pairs={{0,8},{1,9},{2,10},{3,11},{4,12},{5,13},{6,14},{7,15},{8,0},{9,1},... | collective-permute-start | bytes 258056 | tf_op jit(solution)/shard_map/ppermute | solution.py:193
  29.7 0.0 collective-permute-done.14.refs_16_
  29.7 2.8 %collective-permute-start.7 = (bf16[336,128]{1,0:T(8,128)(2,1)S(1)}, bf16[336,128]{1,0:T(8,128)(2,1)S(1)}, u32[]{:S(2)}, u32[]{:S(2)}) collective-permute-start(bf16[336,128]{1,0:T(8,128)(2,1)S(1)} %get-tuple-element.31), channel_id=1, source_target_pairs={{0,4},{1,5},{2,6},{3,7},{4,0},{5,1},{6,2},{7,3},{8,12},{9,13},{10,... | collective-permute-start | bytes 258056 | tf_op jit(solution)/shard_map/ppermute | solution.py:193
  32.5 2.9 %collective-permute-done.3.refs_4_ = bf16[336,128]{1,0:T(8,128)(2,1)S(1)} collective-permute-done((bf16[336,128]{1,0:T(8,128)(2,1)S(1)}, bf16[336,128]{1,0:T(8,128)(2,1)S(1)}, u32[]{:S(2)}, u32[]{:S(2)}) %collective-permute-start.3) | collective-permute-done | bytes 86048 | tf_op jit(solution)/shard_map/ppermute | solution.py:193
  35.4 0.0 collective-permute-start.8
  35.4 0.0 collective-permute-done.4.refs_5_
  35.4 0.0 collective-permute-start.9
  35.5 0.8 %collective-permute-done.5.refs_6_ = bf16[336,128]{1,0:T(8,128)(2,1)S(1)} collective-permute-done((bf16[336,128]{1,0:T(8,128)(2,1)S(1)}, bf16[336,128]{1,0:T(8,128)(2,1)S(1)}, u32[]{:S(2)}, u32[]{:S(2)}) %collective-permute-start.5) | collective-permute-done | bytes 86048 | tf_op jit(solution)/shard_map/ppermute | solution.py:193
  36.3 2.1 %collective-permute-done.6.refs_7_ = bf16[336,128]{1,0:T(8,128)(2,1)S(1)} collective-permute-done((bf16[336,128]{1,0:T(8,128)(2,1)S(1)}, bf16[336,128]{1,0:T(8,128)(2,1)S(1)}, u32[]{:S(2)}, u32[]{:S(2)}) %collective-permute-start.6) | collective-permute-done | bytes 86048 | tf_op jit(solution)/shard_map/ppermute | solution.py:193
  38.4 0.0 collective-permute-done.7.refs_8_
  38.4 1.3 %collective-permute-done.8.refs_9_ = bf16[336,128]{1,0:T(8,128)(2,1)S(1)} collective-permute-done((bf16[336,128]{1,0:T(8,128)(2,1)S(1)}, bf16[336,128]{1,0:T(8,128)(2,1)S(1)}, u32[]{:S(2)}, u32[]{:S(2)}) %collective-permute-start.8) | collective-permute-done | bytes 86048 | tf_op jit(solution)/shard_map/ppermute | solution.py:193
  39.7 1.1 %collective-permute-done.9.refs_10_ = bf16[336,128]{1,0:T(8,128)(2,1)S(1)} collective-permute-done((bf16[336,128]{1,0:T(8,128)(2,1)S(1)}, bf16[336,128]{1,0:T(8,128)(2,1)S(1)}, u32[]{:S(2)}, u32[]{:S(2)}) %collective-permute-start.9) | collective-permute-done | bytes 86048 | tf_op jit(solution)/shard_map/ppermute | solution.py:193
  40.8 3.0 %attend.1 = bf16[16,80,128]{2,1,0:T(8,128)(2,1)} custom-call(s32[1]{0:T(128)} %bitcast.1.refs_0_, bf16[336,128]{1,0:T(8,128)(2,1)S(1)} %get-tuple-element.24.refs_1_, bf16[336,128]{1,0:T(8,128)(2,1)S(1)} %collective-permute-done.1.refs_2_, bf16[336,128]{1,0:T(8,128)(2,1)S(1)} %collective-permute-done.2.refs_3_, ...), custom_call_target="tpu_custom_call" | custom-call | tf_op jit(solution)/shard_map/attend/pallas_call | solution.py:286
  43.8 5.5 %all-to-all-start = ((bf16[16,80,128]{2,1,0:T(8,128)(2,1)}), bf16[16,80,128]{2,1,0:T(8,128)(2,1)S(1)}, u32[]{:S(2)}, u32[]{:S(2)}) async-start(bf16[16,80,128]{2,1,0:T(8,128)(2,1)} %attend.1), calls=%async_computation | async-start | bytes 655360 | tf_op jit(solution)/shard_map/all_to_all | solution.py:308
  49.3 11.1 %all-to-all-done.refs_1_ = bf16[16,80,128]{2,1,0:T(8,128)(2,1)S(1)} async-done(((bf16[16,80,128]{2,1,0:T(8,128)(2,1)}), bf16[16,80,128]{2,1,0:T(8,128)(2,1)S(1)}, u32[]{:S(2)}, u32[]{:S(2)}) %all-to-all-start) | async-done | bytes 327712 | tf_op jit(solution)/shard_map/all_to_all | solution.py:308
  60.4 0.0 copy-done.5
  60.4 1.1 %finish.1 = bf16[128,2048]{1,0:T(8,128)(2,1)} custom-call(s32[1,80]{1,0:T(1,128)S(1)} %pad.4.refs_0_, bf16[16,80,128]{2,1,0:T(8,128)(2,1)S(1)} %all-to-all-done.refs_1_, bf16[128,2048]{1,0:T(8,128)(2,1)S(1)} %copy-done.5), custom_call_target="tpu_custom_call" | custom-call | tf_op jit(solution)/shard_map/finish/pallas_call | solution.py:311
  (7 shorter events, 0.0 us)
Async XLA Ops:
  0.0 11.8 %copy-start = (bf16[76,3,2048]{2,0,1:T(8,128)(2,1)S(1)}, bf16[76,3,2048]{2,0,1:T(8,128)(2,1)}, u32[]{:S(2)}) copy-start(bf16[76,3,2048]{2,0,1:T(8,128)(2,1)} %param.9) | copy-start | bytes 2801668
  0.0 11.8 %copy-start.1 = (bf16[128,2048]{1,0:T(8,128)(2,1)S(1)}, bf16[128,2048]{1,0:T(8,128)(2,1)}, u32[]{:S(2)}) copy-start(bf16[128,2048]{1,0:T(8,128)(2,1)} %refs_5_.3) | copy-start | bytes 1572868
  0.0 11.8 %copy-start.2 = (bf16[128,2048]{1,0:T(8,128)(2,1)S(1)}, bf16[128,2048]{1,0:T(8,128)(2,1)}, u32[]{:S(2)}) copy-start(bf16[128,2048]{1,0:T(8,128)(2,1)} %refs_6_.3) | copy-start | bytes 1572868
  0.0 11.8 %copy-start.3 = (bf16[256,2048]{1,0:T(8,128)(2,1)S(1)}, bf16[256,2048]{1,0:T(8,128)(2,1)}, u32[]{:S(2)}) copy-start(bf16[256,2048]{1,0:T(8,128)(2,1)} %refs_7_.1) | copy-start | bytes 3145732
  2.2 9.6 %collective-permute-start = (bf16[336,128]{1,0:T(8,128)(2,1)}, bf16[336,128]{1,0:T(8,128)(2,1)S(1)}, u32[]{:S(2)}, u32[]{:S(2)}) collective-permute-start(bf16[336,128]{1,0:T(8,128)(2,1)} %get-tuple-element.23), channel_id=1, source_target_pairs={{0,1},{1,0},{2,3},{3,2},{4,5},{5,4},{6,7},{7,6},{8,9},{9,8},{10,11... | collective-permute-start | bytes 258056 | tf_op jit(solution)/shard_map/ppermute | solution.py:193
  2.7 11.9 %collective-permute-start.1 = (bf16[336,128]{1,0:T(8,128)(2,1)}, bf16[336,128]{1,0:T(8,128)(2,1)S(1)}, u32[]{:S(2)}, u32[]{:S(2)}) collective-permute-start(bf16[336,128]{1,0:T(8,128)(2,1)} %get-tuple-element.25), channel_id=1, source_target_pairs={{0,15},{1,14},{2,13},{3,12},{4,11},{5,10},{6,9},{7,8},{8,7},{9,6},... | collective-permute-start | bytes 258056 | tf_op jit(solution)/shard_map/ppermute | solution.py:193
  8.4 3.5 %copy-start.6 = (f32[128]{0:T(128)S(1)}, f32[128]{0:T(128)}, u32[]{:S(2)}) copy-start(f32[128]{0:T(128)} %param.16) | copy-start | bytes 1540
  8.4 3.5 %copy-start.7 = (f32[128]{0:T(128)S(1)}, f32[128]{0:T(128)}, u32[]{:S(2)}) copy-start(f32[128]{0:T(128)} %param.17) | copy-start | bytes 1540
  8.4 3.5 %copy-start.8 = (s32[76]{0:T(128)S(1)}, s32[76]{0:T(128)}, u32[]{:S(2)}) copy-start(s32[76]{0:T(128)} %param.10) | copy-start | bytes 916
  8.4 8.4 %collective-permute-start.10 = (bf16[336,128]{1,0:T(8,128)(2,1)}, bf16[336,128]{1,0:T(8,128)(2,1)S(1)}, u32[]{:S(2)}, u32[]{:S(2)}) collective-permute-start(bf16[336,128]{1,0:T(8,128)(2,1)} %get-tuple-element.34), channel_id=1, source_target_pairs={{0,13},{1,12},{2,15},{3,14},{4,9},{5,8},{6,11},{7,10},{8,5},{9,4},... | collective-permute-start | bytes 258056 | tf_op jit(solution)/shard_map/ppermute | solution.py:193
  8.4 11.6 %collective-permute-start.2 = (bf16[336,128]{1,0:T(8,128)(2,1)}, bf16[336,128]{1,0:T(8,128)(2,1)S(1)}, u32[]{:S(2)}, u32[]{:S(2)}) collective-permute-start(bf16[336,128]{1,0:T(8,128)(2,1)} %get-tuple-element.26), channel_id=1, source_target_pairs={{0,14},{1,15},{2,12},{3,13},{4,10},{5,11},{6,8},{7,9},{8,6},{9,7},... | collective-permute-start | bytes 258056 | tf_op jit(solution)/shard_map/ppermute | solution.py:193
  11.9 1.2 %copy-start.4 = (bf16[256,2048]{1,0:T(8,128)(2,1)S(1)}, bf16[256,2048]{1,0:T(8,128)(2,1)}, u32[]{:S(2)}) copy-start(bf16[256,2048]{1,0:T(8,128)(2,1)} %refs_8_.3) | copy-start | bytes 3145732
  14.0 13.9 %collective-permute-start.11 = (bf16[336,128]{1,0:T(8,128)(2,1)S(1)}, bf16[336,128]{1,0:T(8,128)(2,1)S(1)}, u32[]{:S(2)}, u32[]{:S(2)}) collective-permute-start(bf16[336,128]{1,0:T(8,128)(2,1)S(1)} %get-tuple-element.35), channel_id=1, source_target_pairs={{0,7},{1,6},{2,5},{3,4},{4,3},{5,2},{6,1},{7,0},{8,15},{9,14},{10,... | collective-permute-start | bytes 258056 | tf_op jit(solution)/shard_map/ppermute | solution.py:193
  14.1 13.8 %collective-permute-start.12 = (bf16[336,128]{1,0:T(8,128)(2,1)S(1)}, bf16[336,128]{1,0:T(8,128)(2,1)S(1)}, u32[]{:S(2)}, u32[]{:S(2)}) collective-permute-start(bf16[336,128]{1,0:T(8,128)(2,1)S(1)} %get-tuple-element.36), channel_id=1, source_target_pairs={{0,12},{1,13},{2,14},{3,15},{4,8},{5,9},{6,10},{7,11},{8,4},{9,5},... | collective-permute-start | bytes 258056 | tf_op jit(solution)/shard_map/ppermute | solution.py:193
  14.6 13.3 %collective-permute-start.13 = (bf16[336,128]{1,0:T(8,128)(2,1)S(1)}, bf16[336,128]{1,0:T(8,128)(2,1)S(1)}, u32[]{:S(2)}, u32[]{:S(2)}) collective-permute-start(bf16[336,128]{1,0:T(8,128)(2,1)S(1)} %get-tuple-element.37), channel_id=1, source_target_pairs={{0,6},{1,7},{2,4},{3,5},{4,2},{5,3},{6,0},{7,1},{8,14},{9,15},{10,... | collective-permute-start | bytes 258056 | tf_op jit(solution)/shard_map/ppermute | solution.py:193
  16.8 13.0 %collective-permute-start.14 = (bf16[336,128]{1,0:T(8,128)(2,1)S(1)}, bf16[336,128]{1,0:T(8,128)(2,1)S(1)}, u32[]{:S(2)}, u32[]{:S(2)}) collective-permute-start(bf16[336,128]{1,0:T(8,128)(2,1)S(1)} %get-tuple-element.38), channel_id=1, source_target_pairs={{0,11},{1,10},{2,9},{3,8},{4,15},{5,14},{6,13},{7,12},{8,3},{9,2},... | collective-permute-start | bytes 258056 | tf_op jit(solution)/shard_map/ppermute | solution.py:193
  20.0 15.5 %collective-permute-start.3 = (bf16[336,128]{1,0:T(8,128)(2,1)S(1)}, bf16[336,128]{1,0:T(8,128)(2,1)S(1)}, u32[]{:S(2)}, u32[]{:S(2)}) collective-permute-start(bf16[336,128]{1,0:T(8,128)(2,1)S(1)} %get-tuple-element.27), channel_id=1, source_target_pairs={{0,10},{1,11},{2,8},{3,9},{4,14},{5,15},{6,12},{7,13},{8,2},{9,3},... | collective-permute-start | bytes 258056 | tf_op jit(solution)/shard_map/ppermute | solution.py:193
  27.8 7.6 %collective-permute-start.4 = (bf16[336,128]{1,0:T(8,128)(2,1)S(1)}, bf16[336,128]{1,0:T(8,128)(2,1)S(1)}, u32[]{:S(2)}, u32[]{:S(2)}) collective-permute-start(bf16[336,128]{1,0:T(8,128)(2,1)S(1)} %get-tuple-element.28), channel_id=1, source_target_pairs={{0,5},{1,4},{2,7},{3,6},{4,1},{5,0},{6,3},{7,2},{8,13},{9,12},{10,... | collective-permute-start | bytes 258056 | tf_op jit(solution)/shard_map/ppermute | solution.py:193
  27.9 8.4 %collective-permute-start.5 = (bf16[336,128]{1,0:T(8,128)(2,1)S(1)}, bf16[336,128]{1,0:T(8,128)(2,1)S(1)}, u32[]{:S(2)}, u32[]{:S(2)}) collective-permute-start(bf16[336,128]{1,0:T(8,128)(2,1)S(1)} %get-tuple-element.29), channel_id=1, source_target_pairs={{0,9},{1,8},{2,11},{3,10},{4,13},{5,12},{6,15},{7,14},{8,1},{9,0},... | collective-permute-start | bytes 258056 | tf_op jit(solution)/shard_map/ppermute | solution.py:193
  27.9 10.5 %collective-permute-start.6 = (bf16[336,128]{1,0:T(8,128)(2,1)S(1)}, bf16[336,128]{1,0:T(8,128)(2,1)S(1)}, u32[]{:S(2)}, u32[]{:S(2)}) collective-permute-start(bf16[336,128]{1,0:T(8,128)(2,1)S(1)} %get-tuple-element.30), channel_id=1, source_target_pairs={{0,8},{1,9},{2,10},{3,11},{4,12},{5,13},{6,14},{7,15},{8,0},{9,1},... | collective-permute-start | bytes 258056 | tf_op jit(solution)/shard_map/ppermute | solution.py:193
  29.7 8.7 %collective-permute-start.7 = (bf16[336,128]{1,0:T(8,128)(2,1)S(1)}, bf16[336,128]{1,0:T(8,128)(2,1)S(1)}, u32[]{:S(2)}, u32[]{:S(2)}) collective-permute-start(bf16[336,128]{1,0:T(8,128)(2,1)S(1)} %get-tuple-element.31), channel_id=1, source_target_pairs={{0,4},{1,5},{2,6},{3,7},{4,0},{5,1},{6,2},{7,3},{8,12},{9,13},{10,... | collective-permute-start | bytes 258056 | tf_op jit(solution)/shard_map/ppermute | solution.py:193
  35.4 4.3 %collective-permute-start.8 = (bf16[336,128]{1,0:T(8,128)(2,1)S(1)}, bf16[336,128]{1,0:T(8,128)(2,1)S(1)}, u32[]{:S(2)}, u32[]{:S(2)}) collective-permute-start(bf16[336,128]{1,0:T(8,128)(2,1)S(1)} %get-tuple-element.32), channel_id=1, source_target_pairs={{0,3},{1,2},{2,1},{3,0},{4,7},{5,6},{6,5},{7,4},{8,11},{9,10},{10,... | collective-permute-start | bytes 258056 | tf_op jit(solution)/shard_map/ppermute | solution.py:193
  35.4 5.4 %collective-permute-start.9 = (bf16[336,128]{1,0:T(8,128)(2,1)S(1)}, bf16[336,128]{1,0:T(8,128)(2,1)S(1)}, u32[]{:S(2)}, u32[]{:S(2)}) collective-permute-start(bf16[336,128]{1,0:T(8,128)(2,1)S(1)} %get-tuple-element.33), channel_id=1, source_target_pairs={{0,2},{1,3},{2,0},{3,1},{4,6},{5,7},{6,4},{7,5},{8,10},{9,11},{10,... | collective-permute-start | bytes 258056 | tf_op jit(solution)/shard_map/ppermute | solution.py:193
  43.8 16.6 %copy-start.5 = (bf16[128,2048]{1,0:T(8,128)(2,1)S(1)}, bf16[128,2048]{1,0:T(8,128)(2,1)}, u32[]{:S(2)}) copy-start(bf16[128,2048]{1,0:T(8,128)(2,1)} %refs_2_.1) | copy-start | bytes 1572868
  43.8 16.6 %all-to-all-start = ((bf16[16,80,128]{2,1,0:T(8,128)(2,1)}), bf16[16,80,128]{2,1,0:T(8,128)(2,1)S(1)}, u32[]{:S(2)}, u32[]{:S(2)}) async-start(bf16[16,80,128]{2,1,0:T(8,128)(2,1)} %attend.1), calls=%async_computation | async-start | bytes 655360 | tf_op jit(solution)/shard_map/all_to_all | solution.py:308

commit v18 on v16

--- a/solution.py
+++ b/solution.py
@@ -281,7 +281,7 @@
     arrived = [arrived[step] for step in steps]
 
     all_fresh = seq_count * slot_count // 2
-    query_rows = 4 * slot_count
+    query_rows = 8 * slot_count
     turns = -(-all_fresh // query_rows) if groups == 1 else None
     packed_rows = seq_count * padded + query_rows + padded
     all_keys = text + seq_count * tokens

time: 58.8 us -> 59.2 us (level)
  no operation moved by 1% of the time
where the time goes in v18:
time: 59.2 us; the launch traced here: 58.9 us
  starting transfers between devices  31.8 us (54%)
  waiting for transfers between devices  18.2 us (31%)
  Pallas kernels  7.49 us (13%)
  local copies, waits for them, and re-layouts  1.26 us (2%)
    ppermute x15, starting transfers between devices, trade(): return lax.ppermute(block, 'seq', [(a, a ^ step) for a in range(count)])  28.1 us
    all_to_all x1, waiting for transfers between devices, shards(): lax.all_to_all(result, 'seq', split_axis=0, concat_axis=0, tiled=True)  11 us
    ppermute x15, waiting for transfers between devices, trade(): return lax.ppermute(block, 'seq', [(a, a ^ step) for a in range(count)])  7.18 us
    all_to_all x1, starting transfers between devices, shards(): lax.all_to_all(result, 'seq', split_axis=0, concat_axis=0, tiled=True)  3.67 us
    pallas_call x1, Pallas kernels, shards(): pl.pallas_call(lambda *refs: attend_kernel(tokens, per_group, query_rows,...  3.31 us
    pallas_call x1, Pallas kernels, shards(): pl.pallas_call(lambda *refs: prepare_kernel(per_group, padded, early, Tru...  2.22 us
    unnamed x18, local copies, waits for them, and re-layouts  1.25 us
  transfers between devices with their start and end apart: 16, of which 3 were waited for; matrix products, arithmetic and copies ran while one was open for 0% of the time, Pallas kernels for 1%

profile of v18, /device:TPU:0, one launch (start us, length us, event | category | flops | bytes accessed | tf_op | source)
XLA Modules:
  0.0 58.9 jit_solution(13326419977542806927)
XLA Ops:
  0.0 0.0 copy-start
  0.0 0.0 copy-start.1
  0.0 2.2 %prepare_first.1 = (bf16[336,128]{1,0:T(8,128)(2,1)}, bf16[336,128]{1,0:T(8,128)(2,1)}, bf16[336,128]{1,0:T(8,128)(2,1)}, bf16[336,128]{1,0:T(8,128)(2,1)}) custom-call(s32[1]{0:T(128)} %bitcast.1.refs_0_, s32[1,76]{1,0:T(1,128)} %bitcast.14, f32[1,128]{1,0:T(1,128)} %bitcast.10, f32[1,128]{1,0:T(1,128)} %bitcast.12, bf16[3,76,2048]{2,1,0:T(8,128)(2,1)} %bitcast.5, ...), custom_call_target="tpu_custom_call" | custom-call | tf_op jit(solution)/shard_map/prepare_first/pallas_call | solution.py:238
  2.2 0.5 collective-permute-start
  2.7 5.7 %collective-permute-start.1 = (bf16[336,128]{1,0:T(8,128)(2,1)}, bf16[336,128]{1,0:T(8,128)(2,1)S(1)}, u32[]{:S(2)}, u32[]{:S(2)}) collective-permute-start(bf16[336,128]{1,0:T(8,128)(2,1)} %get-tuple-element.25), channel_id=1, source_target_pairs={{0,15},{1,14},{2,13},{3,12},{4,11},{5,10},{6,9},{7,8},{8,7},{9,6},... | collective-permute-start | bytes 258056 | tf_op jit(solution)/shard_map/ppermute | solution.py:195
  8.4 0.0 collective-permute-start.10
  8.4 3.4 %collective-permute-start.2 = (bf16[336,128]{1,0:T(8,128)(2,1)}, bf16[336,128]{1,0:T(8,128)(2,1)S(1)}, u32[]{:S(2)}, u32[]{:S(2)}) collective-permute-start(bf16[336,128]{1,0:T(8,128)(2,1)} %get-tuple-element.26), channel_id=1, source_target_pairs={{0,14},{1,15},{2,12},{3,13},{4,10},{5,11},{6,8},{7,9},{8,6},{9,7},... | collective-permute-start | bytes 258056 | tf_op jit(solution)/shard_map/ppermute | solution.py:195
  11.8 0.0 collective-permute-done.refs_9_.refs_11_
  11.8 0.0 copy-done
  11.8 0.0 copy-done.1
  11.8 0.0 copy-done.2
  11.8 0.0 copy-done.3
  11.8 0.0 copy-done.6
  11.9 0.0 copy-done.7
  11.9 0.0 copy-done.8
  11.9 0.0 copy-start.4
  11.9 1.2 %copy-done.4 = bf16[256,2048]{1,0:T(8,128)(2,1)S(1)} copy-done((bf16[256,2048]{1,0:T(8,128)(2,1)S(1)}, bf16[256,2048]{1,0:T(8,128)(2,1)}, u32[]{:S(2)}) %copy-start.4) | copy-done | bytes 1048600
  13.1 0.9 %prepare_rest.1 = (bf16[336,128]{1,0:T(8,128)(2,1)S(1)}, bf16[336,128]{1,0:T(8,128)(2,1)S(1)}, bf16[336,128]{1,0:T(8,128)(2,1)S(1)}, bf16[336,128]{1,0:T(8,128)(...) custom-call(s32[1]{0:T(128)} %bitcast.1.refs_0_, ...), custom_call_target="tpu_custom_call" | custom-call | tf_op jit(solution)/shard_map/prepare_rest/pallas_call | solution.py:255
  14.0 0.1 collective-permute-start.11
  14.1 0.6 collective-permute-start.12
  14.6 0.0 collective-permute-done.1.refs_2_
  14.6 2.1 %collective-permute-start.13 = (bf16[336,128]{1,0:T(8,128)(2,1)S(1)}, bf16[336,128]{1,0:T(8,128)(2,1)S(1)}, u32[]{:S(2)}, u32[]{:S(2)}) collective-permute-start(bf16[336,128]{1,0:T(8,128)(2,1)S(1)} %get-tuple-element.37), channel_id=1, source_target_pairs={{0,6},{1,7},{2,4},{3,5},{4,2},{5,3},{6,0},{7,1},{8,14},{9,15},{10,... | collective-permute-start | bytes 258056 | tf_op jit(solution)/shard_map/ppermute | solution.py:195
  16.8 0.0 collective-permute-done.10.refs_12_
  16.8 3.2 %collective-permute-start.14 = (bf16[336,128]{1,0:T(8,128)(2,1)S(1)}, bf16[336,128]{1,0:T(8,128)(2,1)S(1)}, u32[]{:S(2)}, u32[]{:S(2)}) collective-permute-start(bf16[336,128]{1,0:T(8,128)(2,1)S(1)} %get-tuple-element.38), channel_id=1, source_target_pairs={{0,11},{1,10},{2,9},{3,8},{4,15},{5,14},{6,13},{7,12},{8,3},{9,2},... | collective-permute-start | bytes 258056 | tf_op jit(solution)/shard_map/ppermute | solution.py:195
  19.9 0.0 collective-permute-done.2.refs_3_
  20.0 1.0 %collective-permute-start.3 = (bf16[336,128]{1,0:T(8,128)(2,1)S(1)}, bf16[336,128]{1,0:T(8,128)(2,1)S(1)}, u32[]{:S(2)}, u32[]{:S(2)}) collective-permute-start(bf16[336,128]{1,0:T(8,128)(2,1)S(1)} %get-tuple-element.27), channel_id=1, source_target_pairs={{0,5},{1,4},{2,7},{3,6},{4,1},{5,0},{6,3},{7,2},{8,13},{9,12},{10,... | collective-permute-start | bytes 258056 | tf_op jit(solution)/shard_map/ppermute | solution.py:195
  20.9 0.0 collective-permute-done.11.refs_13_
  20.9 6.9 %collective-permute-start.4 = (bf16[336,128]{1,0:T(8,128)(2,1)S(1)}, bf16[336,128]{1,0:T(8,128)(2,1)S(1)}, u32[]{:S(2)}, u32[]{:S(2)}) collective-permute-start(bf16[336,128]{1,0:T(8,128)(2,1)S(1)} %get-tuple-element.28), channel_id=1, source_target_pairs={{0,10},{1,11},{2,8},{3,9},{4,14},{5,15},{6,12},{7,13},{8,2},{9,3},... | collective-permute-start | bytes 258056 | tf_op jit(solution)/shard_map/ppermute | solution.py:195
  27.8 0.0 collective-permute-done.12.refs_14_
  27.8 0.0 collective-permute-start.5
  27.9 0.0 collective-permute-done.13.refs_15_
  27.9 0.1 collective-permute-start.6
  27.9 0.0 collective-permute-done.14.refs_16_
  27.9 0.4 collective-permute-start.7
  28.4 0.0 collective-permute-done.3.refs_4_
  28.4 3.7 %collective-permute-start.8 = (bf16[336,128]{1,0:T(8,128)(2,1)S(1)}, bf16[336,128]{1,0:T(8,128)(2,1)S(1)}, u32[]{:S(2)}, u32[]{:S(2)}) collective-permute-start(bf16[336,128]{1,0:T(8,128)(2,1)S(1)} %get-tuple-element.32), channel_id=1, source_target_pairs={{0,8},{1,9},{2,10},{3,11},{4,12},{5,13},{6,14},{7,15},{8,0},{9,1},... | collective-permute-start | bytes 258056 | tf_op jit(solution)/shard_map/ppermute | solution.py:195
  32.0 0.0 collective-permute-done.4.refs_5_
  32.0 0.6 collective-permute-start.9
  32.6 1.6 %collective-permute-done.5.refs_6_ = bf16[336,128]{1,0:T(8,128)(2,1)S(1)} collective-permute-done((bf16[336,128]{1,0:T(8,128)(2,1)S(1)}, bf16[336,128]{1,0:T(8,128)(2,1)S(1)}, u32[]{:S(2)}, u32[]{:S(2)}) %collective-permute-start.5) | collective-permute-done | bytes 86048 | tf_op jit(solution)/shard_map/ppermute | solution.py:195
  34.2 0.0 collective-permute-done.6.refs_7_
  34.2 0.0 collective-permute-done.7.refs_8_
  34.2 5.6 %collective-permute-done.8.refs_9_ = bf16[336,128]{1,0:T(8,128)(2,1)S(1)} collective-permute-done((bf16[336,128]{1,0:T(8,128)(2,1)S(1)}, bf16[336,128]{1,0:T(8,128)(2,1)S(1)}, u32[]{:S(2)}, u32[]{:S(2)}) %collective-permute-start.8) | collective-permute-done | bytes 86048 | tf_op jit(solution)/shard_map/ppermute | solution.py:195
  39.8 0.0 collective-permute-done.9.refs_10_
  39.8 3.3 %attend.1 = bf16[16,80,128]{2,1,0:T(8,128)(2,1)} custom-call(s32[1]{0:T(128)} %bitcast.1.refs_0_, bf16[336,128]{1,0:T(8,128)(2,1)S(1)} %get-tuple-element.24.refs_1_, bf16[336,128]{1,0:T(8,128)(2,1)S(1)} %collective-permute-done.1.refs_2_, bf16[336,128]{1,0:T(8,128)(2,1)S(1)} %collective-permute-done.2.refs_3_, ...), custom_call_target="tpu_custom_call" | custom-call | tf_op jit(solution)/shard_map/attend/pallas_call | solution.py:288
  43.1 3.7 %all-to-all-start = ((bf16[16,80,128]{2,1,0:T(8,128)(2,1)}), bf16[16,80,128]{2,1,0:T(8,128)(2,1)S(1)}, u32[]{:S(2)}, u32[]{:S(2)}) async-start(bf16[16,80,128]{2,1,0:T(8,128)(2,1)} %attend.1), calls=%async_computation | async-start | bytes 655360 | tf_op jit(solution)/shard_map/all_to_all | solution.py:310
  46.8 11.0 %all-to-all-done.refs_1_ = bf16[16,80,128]{2,1,0:T(8,128)(2,1)S(1)} async-done(((bf16[16,80,128]{2,1,0:T(8,128)(2,1)}), bf16[16,80,128]{2,1,0:T(8,128)(2,1)S(1)}, u32[]{:S(2)}, u32[]{:S(2)}) %all-to-all-start) | async-done | bytes 327712 | tf_op jit(solution)/shard_map/all_to_all | solution.py:310
  57.8 0.0 copy-done.5
  57.8 1.1 %finish.1 = bf16[128,2048]{1,0:T(8,128)(2,1)} custom-call(s32[1,80]{1,0:T(1,128)S(1)} %pad.4.refs_0_, bf16[16,80,128]{2,1,0:T(8,128)(2,1)S(1)} %all-to-all-done.refs_1_, bf16[128,2048]{1,0:T(8,128)(2,1)S(1)} %copy-done.5), custom_call_target="tpu_custom_call" | custom-call | tf_op jit(solution)/shard_map/finish/pallas_call | solution.py:313
  (7 shorter events, 0.0 us)
Async XLA Ops:
  0.0 11.8 %copy-start = (bf16[76,3,2048]{2,0,1:T(8,128)(2,1)S(1)}, bf16[76,3,2048]{2,0,1:T(8,128)(2,1)}, u32[]{:S(2)}) copy-start(bf16[76,3,2048]{2,0,1:T(8,128)(2,1)} %param.9) | copy-start | bytes 2801668
  0.0 11.8 %copy-start.1 = (bf16[128,2048]{1,0:T(8,128)(2,1)S(1)}, bf16[128,2048]{1,0:T(8,128)(2,1)}, u32[]{:S(2)}) copy-start(bf16[128,2048]{1,0:T(8,128)(2,1)} %refs_5_.3) | copy-start | bytes 1572868
  0.0 11.8 %copy-start.2 = (bf16[128,2048]{1,0:T(8,128)(2,1)S(1)}, bf16[128,2048]{1,0:T(8,128)(2,1)}, u32[]{:S(2)}) copy-start(bf16[128,2048]{1,0:T(8,128)(2,1)} %refs_6_.3) | copy-start | bytes 1572868
  0.0 11.8 %copy-start.3 = (bf16[256,2048]{1,0:T(8,128)(2,1)S(1)}, bf16[256,2048]{1,0:T(8,128)(2,1)}, u32[]{:S(2)}) copy-start(bf16[256,2048]{1,0:T(8,128)(2,1)} %refs_7_.1) | copy-start | bytes 3145732
  2.2 9.6 %collective-permute-start = (bf16[336,128]{1,0:T(8,128)(2,1)}, bf16[336,128]{1,0:T(8,128)(2,1)S(1)}, u32[]{:S(2)}, u32[]{:S(2)}) collective-permute-start(bf16[336,128]{1,0:T(8,128)(2,1)} %get-tuple-element.23), channel_id=1, source_target_pairs={{0,1},{1,0},{2,3},{3,2},{4,5},{5,4},{6,7},{7,6},{8,9},{9,8},{10,11... | collective-permute-start | bytes 258056 | tf_op jit(solution)/shard_map/ppermute | solution.py:195
  2.7 11.9 %collective-permute-start.1 = (bf16[336,128]{1,0:T(8,128)(2,1)}, bf16[336,128]{1,0:T(8,128)(2,1)S(1)}, u32[]{:S(2)}, u32[]{:S(2)}) collective-permute-start(bf16[336,128]{1,0:T(8,128)(2,1)} %get-tuple-element.25), channel_id=1, source_target_pairs={{0,15},{1,14},{2,13},{3,12},{4,11},{5,10},{6,9},{7,8},{8,7},{9,6},... | collective-permute-start | bytes 258056 | tf_op jit(solution)/shard_map/ppermute | solution.py:195
  8.4 3.5 %copy-start.6 = (f32[128]{0:T(128)S(1)}, f32[128]{0:T(128)}, u32[]{:S(2)}) copy-start(f32[128]{0:T(128)} %param.16) | copy-start | bytes 1540
  8.4 3.5 %copy-start.7 = (f32[128]{0:T(128)S(1)}, f32[128]{0:T(128)}, u32[]{:S(2)}) copy-start(f32[128]{0:T(128)} %param.17) | copy-start | bytes 1540
  8.4 3.5 %copy-start.8 = (s32[76]{0:T(128)S(1)}, s32[76]{0:T(128)}, u32[]{:S(2)}) copy-start(s32[76]{0:T(128)} %param.10) | copy-start | bytes 916
  8.4 8.4 %collective-permute-start.10 = (bf16[336,128]{1,0:T(8,128)(2,1)}, bf16[336,128]{1,0:T(8,128)(2,1)S(1)}, u32[]{:S(2)}, u32[]{:S(2)}) collective-permute-start(bf16[336,128]{1,0:T(8,128)(2,1)} %get-tuple-element.34), channel_id=1, source_target_pairs={{0,13},{1,12},{2,15},{3,14},{4,9},{5,8},{6,11},{7,10},{8,5},{9,4},... | collective-permute-start | bytes 258056 | tf_op jit(solution)/shard_map/ppermute | solution.py:195
  8.4 11.6 %collective-permute-start.2 = (bf16[336,128]{1,0:T(8,128)(2,1)}, bf16[336,128]{1,0:T(8,128)(2,1)S(1)}, u32[]{:S(2)}, u32[]{:S(2)}) collective-permute-start(bf16[336,128]{1,0:T(8,128)(2,1)} %get-tuple-element.26), channel_id=1, source_target_pairs={{0,14},{1,15},{2,12},{3,13},{4,10},{5,11},{6,8},{7,9},{8,6},{9,7},... | collective-permute-start | bytes 258056 | tf_op jit(solution)/shard_map/ppermute | solution.py:195
  11.9 1.2 %copy-start.4 = (bf16[256,2048]{1,0:T(8,128)(2,1)S(1)}, bf16[256,2048]{1,0:T(8,128)(2,1)}, u32[]{:S(2)}) copy-start(bf16[256,2048]{1,0:T(8,128)(2,1)} %refs_8_.3) | copy-start | bytes 3145732
  14.0 6.9 %collective-permute-start.11 = (bf16[336,128]{1,0:T(8,128)(2,1)S(1)}, bf16[336,128]{1,0:T(8,128)(2,1)S(1)}, u32[]{:S(2)}, u32[]{:S(2)}) collective-permute-start(bf16[336,128]{1,0:T(8,128)(2,1)S(1)} %get-tuple-element.35), channel_id=1, source_target_pairs={{0,7},{1,6},{2,5},{3,4},{4,3},{5,2},{6,1},{7,0},{8,15},{9,14},{10,... | collective-permute-start | bytes 258056 | tf_op jit(solution)/shard_map/ppermute | solution.py:195
  14.1 13.8 %collective-permute-start.12 = (bf16[336,128]{1,0:T(8,128)(2,1)S(1)}, bf16[336,128]{1,0:T(8,128)(2,1)S(1)}, u32[]{:S(2)}, u32[]{:S(2)}) collective-permute-start(bf16[336,128]{1,0:T(8,128)(2,1)S(1)} %get-tuple-element.36), channel_id=1, source_target_pairs={{0,12},{1,13},{2,14},{3,15},{4,8},{5,9},{6,10},{7,11},{8,4},{9,5},... | collective-permute-start | bytes 258056 | tf_op jit(solution)/shard_map/ppermute | solution.py:195
  14.6 13.2 %collective-permute-start.13 = (bf16[336,128]{1,0:T(8,128)(2,1)S(1)}, bf16[336,128]{1,0:T(8,128)(2,1)S(1)}, u32[]{:S(2)}, u32[]{:S(2)}) collective-permute-start(bf16[336,128]{1,0:T(8,128)(2,1)S(1)} %get-tuple-element.37), channel_id=1, source_target_pairs={{0,6},{1,7},{2,4},{3,5},{4,2},{5,3},{6,0},{7,1},{8,14},{9,15},{10,... | collective-permute-start | bytes 258056 | tf_op jit(solution)/shard_map/ppermute | solution.py:195
  16.8 11.2 %collective-permute-start.14 = (bf16[336,128]{1,0:T(8,128)(2,1)S(1)}, bf16[336,128]{1,0:T(8,128)(2,1)S(1)}, u32[]{:S(2)}, u32[]{:S(2)}) collective-permute-start(bf16[336,128]{1,0:T(8,128)(2,1)S(1)} %get-tuple-element.38), channel_id=1, source_target_pairs={{0,11},{1,10},{2,9},{3,8},{4,15},{5,14},{6,13},{7,12},{8,3},{9,2},... | collective-permute-start | bytes 258056 | tf_op jit(solution)/shard_map/ppermute | solution.py:195
  20.0 8.4 %collective-permute-start.3 = (bf16[336,128]{1,0:T(8,128)(2,1)S(1)}, bf16[336,128]{1,0:T(8,128)(2,1)S(1)}, u32[]{:S(2)}, u32[]{:S(2)}) collective-permute-start(bf16[336,128]{1,0:T(8,128)(2,1)S(1)} %get-tuple-element.27), channel_id=1, source_target_pairs={{0,5},{1,4},{2,7},{3,6},{4,1},{5,0},{6,3},{7,2},{8,13},{9,12},{10,... | collective-permute-start | bytes 258056 | tf_op jit(solution)/shard_map/ppermute | solution.py:195
  20.9 11.1 %collective-permute-start.4 = (bf16[336,128]{1,0:T(8,128)(2,1)S(1)}, bf16[336,128]{1,0:T(8,128)(2,1)S(1)}, u32[]{:S(2)}, u32[]{:S(2)}) collective-permute-start(bf16[336,128]{1,0:T(8,128)(2,1)S(1)} %get-tuple-element.28), channel_id=1, source_target_pairs={{0,10},{1,11},{2,8},{3,9},{4,14},{5,15},{6,12},{7,13},{8,2},{9,3},... | collective-permute-start | bytes 258056 | tf_op jit(solution)/shard_map/ppermute | solution.py:195
  27.8 6.3 %collective-permute-start.5 = (bf16[336,128]{1,0:T(8,128)(2,1)S(1)}, bf16[336,128]{1,0:T(8,128)(2,1)S(1)}, u32[]{:S(2)}, u32[]{:S(2)}) collective-permute-start(bf16[336,128]{1,0:T(8,128)(2,1)S(1)} %get-tuple-element.29), channel_id=1, source_target_pairs={{0,4},{1,5},{2,6},{3,7},{4,0},{5,1},{6,2},{7,3},{8,12},{9,13},{10,... | collective-permute-start | bytes 258056 | tf_op jit(solution)/shard_map/ppermute | solution.py:195
  27.9 6.3 %collective-permute-start.6 = (bf16[336,128]{1,0:T(8,128)(2,1)S(1)}, bf16[336,128]{1,0:T(8,128)(2,1)S(1)}, u32[]{:S(2)}, u32[]{:S(2)}) collective-permute-start(bf16[336,128]{1,0:T(8,128)(2,1)S(1)} %get-tuple-element.30), channel_id=1, source_target_pairs={{0,9},{1,8},{2,11},{3,10},{4,13},{5,12},{6,15},{7,14},{8,1},{9,0},... | collective-permute-start | bytes 258056 | tf_op jit(solution)/shard_map/ppermute | solution.py:195
  27.9 6.2 %collective-permute-start.7 = (bf16[336,128]{1,0:T(8,128)(2,1)S(1)}, bf16[336,128]{1,0:T(8,128)(2,1)S(1)}, u32[]{:S(2)}, u32[]{:S(2)}) collective-permute-start(bf16[336,128]{1,0:T(8,128)(2,1)S(1)} %get-tuple-element.31), channel_id=1, source_target_pairs={{0,3},{1,2},{2,1},{3,0},{4,7},{5,6},{6,5},{7,4},{8,11},{9,10},{10,... | collective-permute-start | bytes 258056 | tf_op jit(solution)/shard_map/ppermute | solution.py:195
  28.4 11.4 %collective-permute-start.8 = (bf16[336,128]{1,0:T(8,128)(2,1)S(1)}, bf16[336,128]{1,0:T(8,128)(2,1)S(1)}, u32[]{:S(2)}, u32[]{:S(2)}) collective-permute-start(bf16[336,128]{1,0:T(8,128)(2,1)S(1)} %get-tuple-element.32), channel_id=1, source_target_pairs={{0,8},{1,9},{2,10},{3,11},{4,12},{5,13},{6,14},{7,15},{8,0},{9,1},... | collective-permute-start | bytes 258056 | tf_op jit(solution)/shard_map/ppermute | solution.py:195
  32.0 7.7 %collective-permute-start.9 = (bf16[336,128]{1,0:T(8,128)(2,1)S(1)}, bf16[336,128]{1,0:T(8,128)(2,1)S(1)}, u32[]{:S(2)}, u32[]{:S(2)}) collective-permute-start(bf16[336,128]{1,0:T(8,128)(2,1)S(1)} %get-tuple-element.33), channel_id=1, source_target_pairs={{0,2},{1,3},{2,0},{3,1},{4,6},{5,7},{6,4},{7,5},{8,10},{9,11},{10,... | collective-permute-start | bytes 258056 | tf_op jit(solution)/shard_map/ppermute | solution.py:195
  43.1 14.7 %copy-start.5 = (bf16[128,2048]{1,0:T(8,128)(2,1)S(1)}, bf16[128,2048]{1,0:T(8,128)(2,1)}, u32[]{:S(2)}) copy-start(bf16[128,2048]{1,0:T(8,128)(2,1)} %refs_2_.1) | copy-start | bytes 1572868
  43.1 14.7 %all-to-all-start = ((bf16[16,80,128]{2,1,0:T(8,128)(2,1)}), bf16[16,80,128]{2,1,0:T(8,128)(2,1)S(1)}, u32[]{:S(2)}, u32[]{:S(2)}) async-start(bf16[16,80,128]{2,1,0:T(8,128)(2,1)} %attend.1), calls=%async_computation | async-start | bytes 655360 | tf_op jit(solution)/shard_map/all_to_all | solution.py:310
